TPU v7x, 128 devices: a whole 4x4x4 slice. The times are simulated.
128 devices in a mesh: sp: 16 (over x, y_hi, core), fl: 8 (over z, y_lo).
Axes of the slice: x: 4, y: 4 (y_hi: 2, y_lo: 2; y = y_hi * 2 + y_lo), z: 4, core: 2. Of those that a mesh axis runs over, the one named last changes fastest.
Arguments:
- inputs: bfloat16 [32, 64, 32, 256], P('sp', 'fl'), may hold values from -6 to 6
- weight_fine: bfloat16 [27, 256, 256], replicated, may hold values from -0.078125 to 0.078125
- weight_coarse: bfloat16 [27, 256, 512], P(None, None, 'fl'), may hold values from -0.078125 to 0.078125
- cotangent: bfloat16 [16, 32, 16, 512], P('sp', None, None, 'fl'), may hold values from -24 to 24
Outputs:
- coarse_out: bfloat16 [16, 32, 16, 512], P('sp', None, None, 'fl')
- grad_input: bfloat16 [32, 64, 32, 256], P('sp', 'fl')
- grad_fine: float32 [1769472], P(('sp', 'fl'))
- grad_coarse: float32 [6912, 512], P('sp', 'fl')
All inputs are finite; a program needn't handle non-finite values.
Results may differ from a plain program's by a relative error of at most 0.022.
Values may be sent and summed in bfloat16 or wider, within the bound.
No kernel may reach another device: no remote copies, remote signals or barrier semaphores. Data moves between devices by JAX's collectives and lax.ppermute only.
A program may use at most 128 MiB of HBM per device.

v0:
```python
import math

import jax
import jax.numpy as jnp
from jax import lax
from jax.sharding import PartitionSpec as P


def padded_2(cells, sides, width):
    for axis, dim in sides:
        count = lax.axis_size(axis)
        ends = count - 1
        head = lax.slice_in_dim(cells, 0, width, axis=dim)
        tail = lax.slice_in_dim(cells, cells.shape[dim] - width, cells.shape[dim], axis=dim)
        cells = jnp.concatenate(
            [
                lax.ppermute(tail, axis, [(i, (i + 1) % count) for i in range(ends)]),
                cells,
                lax.ppermute(head, axis, [((i + 1) % count, i) for i in range(ends)]),
            ],
            axis=dim,
        )
    return cells


def tap_offsets():
    return [
        (first, second, third) for first in range(3) for second in range(3) for third in range(3)
    ]


def forward_taps(padded, weight, extent):
    rows_x, rows_y, depth = extent
    total = jnp.zeros((rows_x * rows_y * depth, weight.shape[2]), jnp.float32)
    for number, (first, second, third) in enumerate(tap_offsets()):
        window = padded[first : first + rows_x, second : second + rows_y, third : third + depth, :]
        total = total + jnp.dot(
            window.reshape(-1, window.shape[-1]), weight[number], preferred_element_type=jnp.float32
        )
    return total.reshape(rows_x, rows_y, depth, weight.shape[2])


def backward_taps(padded, weight, extent):
    rows_x, rows_y, depth = extent
    total = jnp.zeros((rows_x * rows_y * depth, weight.shape[1]), jnp.float32)
    for number, (first, second, third) in enumerate(tap_offsets()):
        window = padded[
            2 - first : 2 - first + rows_x,
            2 - second : 2 - second + rows_y,
            2 - third : 2 - third + depth,
            :,
        ]
        total = total + lax.dot_general(
            window.reshape(-1, window.shape[-1]),
            weight[number],
            (((1,), (1,)), ((), ())),
            preferred_element_type=jnp.float32,
        )
    return total.reshape(rows_x, rows_y, depth, weight.shape[1])


def weight_taps(padded, grads, extent):
    rows_x, rows_y, depth = extent
    flat_grads = grads.reshape(-1, grads.shape[-1])
    pieces = []
    for first, second, third in tap_offsets():
        window = padded[first : first + rows_x, second : second + rows_y, third : third + depth, :]
        pieces.append(
            lax.dot_general(
                window.reshape(-1, window.shape[-1]),
                flat_grads,
                (((0,), (0,)), ((), ())),
                preferred_element_type=jnp.float32,
            )
        )
    return jnp.stack(pieces)


def pool_cells(values):
    rows_x, rows_y, depth, width = values.shape
    blocks = values.astype(jnp.float32).reshape(
        rows_x // 2, 2, rows_y // 2, 2, depth // 2, 2, width
    )
    return jnp.mean(blocks, axis=(1, 3, 5)).astype(jnp.bfloat16)


def spread_cells(values):
    rows_x, rows_y, depth, width = values.shape
    wide = jnp.broadcast_to(
        values[:, None, :, None, :, None, :], (rows_x, 2, rows_y, 2, depth, 2, width)
    )
    return wide.reshape(rows_x * 2, rows_y * 2, depth * 2, width)


def silu_slope(values):
    sigma = jax.nn.sigmoid(values)
    return sigma * (1.0 + values * (1.0 - sigma))


def fine_rim(values):
    extended = padded_2(values, (("sp", 0), ("fl", 1)), 1)
    return jnp.pad(extended, ((0, 0), (0, 0), (1, 1), (0, 0)))


def coarse_rim_pad(extended):
    return jnp.pad(extended, ((0, 0), (1, 1), (1, 1), (0, 0)))


def body(inputs, weight_fine, weight_coarse, cotangent):
    rows_x, rows_y, depth, width = inputs.shape
    fine_extent = (rows_x, rows_y, depth)
    cells = rows_x * lax.axis_size("sp") * rows_y * lax.axis_size("fl") * depth
    padded_in = fine_rim(inputs)
    fine_pre = forward_taps(padded_in, weight_fine, fine_extent)
    fine_act = (fine_pre * jax.nn.sigmoid(fine_pre)).astype(jnp.bfloat16)
    pooled = pool_cells(fine_act)
    gathered = lax.all_gather(pooled, "fl", axis=1, tiled=True)
    coarse_extent = gathered.shape[:3]
    padded_pool = coarse_rim_pad(padded_2(gathered, (("sp", 0),), 1))
    coarse_out = forward_taps(padded_pool, weight_coarse, coarse_extent).astype(jnp.bfloat16)
    coarse_terms = weight_taps(padded_pool, cotangent, coarse_extent).reshape(
        -1, cotangent.shape[-1]
    )
    grad_coarse = lax.psum_scatter(
        coarse_terms.astype(jnp.bfloat16), "sp", scatter_dimension=0, tiled=True
    ).astype(jnp.float32) * (1.0 / math.sqrt(cells // 8))
    padded_cot = coarse_rim_pad(padded_2(cotangent, (("sp", 0),), 1))
    partial_grad = backward_taps(padded_cot, weight_coarse, coarse_extent)
    pooled_grad = lax.psum_scatter(
        partial_grad.astype(jnp.bfloat16), "fl", scatter_dimension=1, tiled=True
    )
    fine_grad = (
        spread_cells(pooled_grad.astype(jnp.float32)) * 0.125 * silu_slope(fine_pre)
    ).astype(jnp.bfloat16)
    fine_terms = weight_taps(padded_in, fine_grad, fine_extent).reshape(-1)
    summed = lax.psum_scatter(fine_terms, ("sp", "fl"), scatter_dimension=0, tiled=True)
    grad_fine = summed * (1.0 / math.sqrt(cells))
    grad_input = backward_taps(fine_rim(fine_grad), weight_fine, fine_extent).astype(jnp.bfloat16)
    return (coarse_out, grad_input, grad_fine, grad_coarse)


def solution(mesh):
    return jax.shard_map(
        body,
        mesh=mesh,
        in_specs=(P("sp", "fl", None, None), P(), P(None, None, "fl"), P("sp", None, None, "fl")),
        out_specs=(
            P("sp", None, None, "fl"),
            P("sp", "fl", None, None),
            P(("sp", "fl")),
            P("sp", "fl"),
        ),
        check_vma=False,
    )
```

profile of v0, /device:TPU:1, one launch (start us, length us, event | category | flops | bytes accessed | tf_op | source)
XLA Modules:
  0.0 401.4 jit_solution(3515070865083290961)
XLA Ops:
  7.2 3.3 collective-permute-start.7
  10.5 4.8 %collective-permute-start.6 = (bf16[1,32,16,64]{3,2,1,0:T(8,128)(2,1)}, bf16[1,32,16,64]{3,2,1,0:T(8,128)(2,1)S(1)}, u32[]{:S(2)}, u32[]{:S(2)}) collective-permute-start(bf16[1,32,16,64]{3,2,1,0:T(8,128)(2,1)} %param.7), channel_id=1, source_target_pairs={{0,8},{8,16},{16,24},{24,32},{32,40},{40,48},{48,56},{56,64},{64,7... | collective-permute-start | bytes 196616 | tf_op jit(solution)/shard_map/ppermute | solution.py:17
  16.4 1.9 collective-permute-start.1
  18.3 5.1 %collective-permute-start = (bf16[1,8,32,256]{3,2,1,0:T(8,128)(2,1)S(1)}, bf16[1,8,32,256]{3,2,1,0:T(8,128)(2,1)S(1)}, u32[]{:S(2)}, u32[]{:S(2)}) collective-permute-start(bf16[1,8,32,256]{3,2,1,0:T(8,128)(2,1)S(1)} %get-tuple-element.121), channel_id=1, source_target_pairs={{0,8},{8,16},{16,24},{24,32},{32,40},{40,48},{48,56},{56,64},{64,7... | collective-permute-start | bytes 393224 | tf_op jit(solution)/shard_map/ppermute | solution.py:17
  30.8 3.0 collective-permute-start.2
  37.1 2.0 collective-permute-done.3
  40.2 1.3 copy-done
  48.6 25.5 %reduce-scatter.5.cloned.1.call-done = bf16[1,4,16,256]{3,2,1,0:T(8,128)(2,1)} async-done(((bf16[1,32,16,256]{3,2,1,0:T(8,128)(2,1)}), bf16[1,4,16,256]{3,2,1,0:T(8,128)(2,1)}) %reduce-scatter.5.cloned.1.call-update) | async-done | bytes 32784 | tf_op jit(solution)/shard_map/reduce_scatter | solution.py:129
  75.1 2.2 fusion.132
  79.6 22.3 %all-gather = bf16[32,16,256]{2,1,0:T(8,128)(2,1)S(1)} all-gather(bf16[4,16,256]{2,1,0:T(8,128)(2,1)S(1)} %multiply_convert_fusion.2), channel_id=2, replica_groups=mesh['sp'=16,'fl'=8] {'fl'}, dimensions={0}, use_global_device_ids=true | all-gather | bytes 294912 | tf_op jit(solution)/shard_map/all_gather | solution.py:117
  102.0 14.2 %collective-permute-start.5 = (bf16[1,32,16,256]{3,1,2,0:T(8,128)(2,1)S(1)}, bf16[1,32,16,256]{3,1,2,0:T(8,128)(2,1)S(1)}, u32[]{:S(2)}, u32[]{:S(2)}) collective-permute-start(bf16[1,32,16,256]{3,1,2,0:T(8,128)(2,1)S(1)} %bitcast.1268), channel_id=1, source_target_pairs={{8,0},{16,8},{24,16},{32,24},{40,32},{48,40},{56,48},{64,56},{72,6... | collective-permute-start | bytes 786440 | tf_op jit(solution)/shard_map/ppermute | solution.py:19
  116.2 4.2 %collective-permute-start.4 = (bf16[1,32,16,256]{3,1,2,0:T(8,128)(2,1)S(1)}, bf16[1,32,16,256]{3,1,2,0:T(8,128)(2,1)S(1)}, u32[]{:S(2)}, u32[]{:S(2)}) collective-permute-start(bf16[1,32,16,256]{3,1,2,0:T(8,128)(2,1)S(1)} %bitcast.1269), channel_id=1, source_target_pairs={{0,8},{8,16},{16,24},{24,32},{32,40},{40,48},{48,56},{56,64},{64,7... | collective-permute-start | bytes 786440 | tf_op jit(solution)/shard_map/ppermute | solution.py:17
  121.6 2.4 collective-permute-start.8
  124.0 2.7 collective-permute-start.9
  133.4 2.8 copy-done.2
  159.4 2.6 copy.298
  163.1 1.9 fusion.15
  168.9 9.7 %copy.301 = f32[864,2,8,128]{3,1,2,0:T(2,128)} copy(f32[864,2,8,128]{3,2,1,0:T(8,128)} %bitcast.1157) | data formatting | bytes 14155776
  180.8 1.5 collective-permute-start.11
  183.4 3.1 collective-permute-done.11
  186.4 1.4 select_maximum_fusion.2
  210.8 16.8 %reduce-scatter.7.cloned.1.call-done = bf16[432,64]{1,0:T(8,128)(2,1)} async-done(((bf16[6912,64]{1,0:T(8,128)(2,1)}), bf16[432,64]{1,0:T(8,128)(2,1)}) %reduce-scatter.7.cloned.1.call-update) | async-done | bytes 55312
  229.2 164.1 %all-reduce.7.cloned.1.call-done = f32[1769472]{0:T(1024)} async-done(((f32[1769472]{0:T(1024)}), f32[1769472]{0:T(1024)}) %all-reduce.7.cloned.1.call-update) | async-done | bytes 7077904
  393.3 1.5 dynamic-slice_multiply_fusion
  (273 shorter events, 85.6 us)
Async XLA Ops:
  7.2 66.9 %reduce-scatter.5.cloned.1.call-start = ((), (), s32[]{:S(2)}) async-start(), calls=%async_computation.2 | async-start | bytes 294912 | tf_op jit(solution)/shard_map/reduce_scatter | solution.py:129
  7.2 16.2 %collective-permute-start.7 = (bf16[1,32,16,64]{3,2,1,0:T(8,128)(2,1)}, bf16[1,32,16,64]{3,2,1,0:T(8,128)(2,1)S(1)}, u32[]{:S(2)}, u32[]{:S(2)}) collective-permute-start(bf16[1,32,16,64]{3,2,1,0:T(8,128)(2,1)} %param.7), channel_id=1, source_target_pairs={{8,0},{16,8},{24,16},{32,24},{40,32},{48,40},{56,48},{64,56},{72,6... | collective-permute-start | bytes 196616 | tf_op jit(solution)/shard_map/ppermute | solution.py:19
  10.5 12.9 %collective-permute-start.6 = (bf16[1,32,16,64]{3,2,1,0:T(8,128)(2,1)}, bf16[1,32,16,64]{3,2,1,0:T(8,128)(2,1)S(1)}, u32[]{:S(2)}, u32[]{:S(2)}) collective-permute-start(bf16[1,32,16,64]{3,2,1,0:T(8,128)(2,1)} %param.7), channel_id=1, source_target_pairs={{0,8},{8,16},{16,24},{24,32},{32,40},{40,48},{48,56},{56,64},{64,7... | collective-permute-start | bytes 196616 | tf_op jit(solution)/shard_map/ppermute | solution.py:17
  16.4 14.4 %collective-permute-start.1 = (bf16[1,8,32,256]{3,2,1,0:T(8,128)(2,1)S(1)}, bf16[1,8,32,256]{3,2,1,0:T(8,128)(2,1)S(1)}, u32[]{:S(2)}, u32[]{:S(2)}) collective-permute-start(bf16[1,8,32,256]{3,2,1,0:T(8,128)(2,1)S(1)} %get-tuple-element.120), channel_id=1, source_target_pairs={{8,0},{16,8},{24,16},{32,24},{40,32},{48,40},{56,48},{64,56},{72,6... | collective-permute-start | bytes 393224 | tf_op jit(solution)/shard_map/ppermute | solution.py:19
  18.3 12.4 %collective-permute-start = (bf16[1,8,32,256]{3,2,1,0:T(8,128)(2,1)S(1)}, bf16[1,8,32,256]{3,2,1,0:T(8,128)(2,1)S(1)}, u32[]{:S(2)}, u32[]{:S(2)}) collective-permute-start(bf16[1,8,32,256]{3,2,1,0:T(8,128)(2,1)S(1)} %get-tuple-element.121), channel_id=1, source_target_pairs={{0,8},{8,16},{16,24},{24,32},{32,40},{40,48},{48,56},{56,64},{64,7... | collective-permute-start | bytes 393224 | tf_op jit(solution)/shard_map/ppermute | solution.py:17
  30.8 5.3 %copy-start.15 = (bf16[3,8,32,256]{3,2,1,0:T(8,128)(2,1)}, bf16[3,8,32,256]{3,2,1,0:T(8,128)(2,1)S(1)}, u32[]{:S(2)}) copy-start(bf16[3,8,32,256]{3,2,1,0:T(8,128)(2,1)S(1)} %get-tuple-element.118) | copy-start | bytes 1179652
  30.8 9.4 %copy-start.14 = (bf16[3,8,32,256]{3,2,1,0:T(8,128)(2,1)}, bf16[3,8,32,256]{3,2,1,0:T(8,128)(2,1)S(1)}, u32[]{:S(2)}) copy-start(bf16[3,8,32,256]{3,2,1,0:T(8,128)(2,1)S(1)} %get-tuple-element.122) | copy-start | bytes 1179652
  30.8 11.2 %copy-start.5 = (bf16[4,8,32,256]{3,2,1,0:T(8,128)(2,1)}, bf16[4,8,32,256]{3,2,1,0:T(8,128)(2,1)S(1)}, u32[]{:S(2)}) copy-start(bf16[4,8,32,256]{3,2,1,0:T(8,128)(2,1)S(1)} %get-tuple-element.123) | copy-start | bytes 1572868
  30.8 6.3 %collective-permute-start.2 = (bf16[4,1,32,256]{3,2,1,0:T(8,128)(2,1)S(1)}, bf16[4,1,32,256]{3,2,1,0:T(8,128)(2,1)S(1)}, u32[]{:S(2)}, u32[]{:S(2)}) collective-permute-start(bf16[4,1,32,256]{3,2,1,0:T(8,128)(2,1)S(1)} %get-tuple-element.111), channel_id=1, source_target_pairs={{0,1},{1,2},{2,3},{3,4},{4,5},{5,6},{6,7},{8,9},{9,10},{10,11},{11... | collective-permute-start | bytes 196616 | tf_op jit(solution)/shard_map/ppermute | solution.py:17
  33.8 5.3 %collective-permute-start.3 = (bf16[4,1,32,256]{3,2,1,0:T(8,128)(2,1)S(1)}, bf16[4,1,32,256]{3,2,1,0:T(8,128)(2,1)S(1)}, u32[]{:S(2)}, u32[]{:S(2)}) collective-permute-start(bf16[4,1,32,256]{3,2,1,0:T(8,128)(2,1)S(1)} %get-tuple-element.112), channel_id=1, source_target_pairs={{1,0},{2,1},{3,2},{4,3},{5,4},{6,5},{7,6},{9,8},{10,9},{11,10},{12... | collective-permute-start | bytes 196616 | tf_op jit(solution)/shard_map/ppermute | solution.py:19
  36.1 191.5 %reduce-scatter.7.cloned.1.call-start = ((), (), s32[]{:S(2)}) async-start(), calls=%async_computation.3 | async-start | bytes 1880064
  37.1 4.9 %copy-start.17 = (bf16[4,1,32,256]{3,2,1,0:T(8,128)(2,1)}, bf16[4,1,32,256]{3,2,1,0:T(8,128)(2,1)S(1)}, u32[]{:S(2)}) copy-start(bf16[4,1,32,256]{3,2,1,0:T(8,128)(2,1)S(1)} %collective-permute-done.2) | copy-start | bytes 196612
  102.0 31.5 %collective-permute-start.5 = (bf16[1,32,16,256]{3,1,2,0:T(8,128)(2,1)S(1)}, bf16[1,32,16,256]{3,1,2,0:T(8,128)(2,1)S(1)}, u32[]{:S(2)}, u32[]{:S(2)}) collective-permute-start(bf16[1,32,16,256]{3,1,2,0:T(8,128)(2,1)S(1)} %bitcast.1268), channel_id=1, source_target_pairs={{8,0},{16,8},{24,16},{32,24},{40,32},{48,40},{56,48},{64,56},{72,6... | collective-permute-start | bytes 786440 | tf_op jit(solution)/shard_map/ppermute | solution.py:19
  116.2 20.0 %collective-permute-start.4 = (bf16[1,32,16,256]{3,1,2,0:T(8,128)(2,1)S(1)}, bf16[1,32,16,256]{3,1,2,0:T(8,128)(2,1)S(1)}, u32[]{:S(2)}, u32[]{:S(2)}) collective-permute-start(bf16[1,32,16,256]{3,1,2,0:T(8,128)(2,1)S(1)} %bitcast.1269), channel_id=1, source_target_pairs={{0,8},{8,16},{16,24},{24,32},{32,40},{40,48},{48,56},{56,64},{64,7... | collective-permute-start | bytes 786440 | tf_op jit(solution)/shard_map/ppermute | solution.py:17
  121.3 7.2 %copy-start.16 = (bf16[3,8,32,256]{3,2,1,0:T(8,128)(2,1)S(1)}, bf16[3,8,32,256]{3,2,1,0:T(8,128)(2,1)}, u32[]{:S(2)}) copy-start(bf16[3,8,32,256]{3,2,1,0:T(8,128)(2,1)} %copy-done.15) | copy-start | bytes 1179652
  121.6 57.1 %collective-permute-start.8 = (bf16[1,8,32,256]{3,2,1,0:T(8,128)(2,1)}, bf16[1,8,32,256]{3,2,1,0:T(8,128)(2,1)}, u32[]{:S(2)}, u32[]{:S(2)}) collective-permute-start(bf16[1,8,32,256]{3,2,1,0:T(8,128)(2,1)} %get-tuple-element.115), channel_id=1, source_target_pairs={{0,8},{8,16},{16,24},{24,32},{32,40},{40,48},{48,56},{56,64},{64,7... | collective-permute-start | bytes 393224 | tf_op jit(solution)/shard_map/ppermute | solution.py:17
  124.0 54.7 %collective-permute-start.9 = (bf16[1,8,32,256]{3,2,1,0:T(8,128)(2,1)}, bf16[1,8,32,256]{3,2,1,0:T(8,128)(2,1)}, u32[]{:S(2)}, u32[]{:S(2)}) collective-permute-start(bf16[1,8,32,256]{3,2,1,0:T(8,128)(2,1)} %get-tuple-element.116), channel_id=1, source_target_pairs={{8,0},{16,8},{24,16},{32,24},{40,32},{48,40},{56,48},{64,56},{72,6... | collective-permute-start | bytes 393224 | tf_op jit(solution)/shard_map/ppermute | solution.py:19
  133.4 2.8 copy-start.2
  136.3 18.9 %copy-start.9 = (bf16[1,32,16,256]{3,1,2,0:T(8,128)(2,1)}, bf16[1,32,16,256]{3,1,2,0:T(8,128)(2,1)S(1)}, u32[]{:S(2)}) copy-start(bf16[1,32,16,256]{3,1,2,0:T(8,128)(2,1)S(1)} %collective-permute-done.5) | copy-start | bytes 786436
  136.3 8.0 %copy-start.11 = (bf16[1,32,16,256]{3,1,2,0:T(8,128)(2,1)}, bf16[1,32,16,256]{3,1,2,0:T(8,128)(2,1)S(1)}, u32[]{:S(2)}) copy-start(bf16[1,32,16,256]{3,1,2,0:T(8,128)(2,1)S(1)} %collective-permute-done.4) | copy-start | bytes 786436
  162.0 231.3 %all-reduce.7.cloned.1.call-start = ((), (), s32[]{:S(2)}) async-start(), calls=%async_computation.4 | async-start | bytes 14155776
  162.1 4.9 %copy-start.7 = (bf16[4,8,32,256]{3,2,1,0:T(8,128)(2,1)S(1)}, bf16[4,8,32,256]{3,2,1,0:T(8,128)(2,1)}, u32[]{:S(2)}) copy-start(bf16[4,8,32,256]{3,2,1,0:T(8,128)(2,1)} %copy-done.5) | copy-start | bytes 1572868
  179.5 3.8 collective-permute-start.10
  180.8 5.6 %collective-permute-start.11 = (bf16[4,1,32,256]{3,2,1,0:T(8,128)(2,1)S(1)}, bf16[4,1,32,256]{3,2,1,0:T(8,128)(2,1)S(1)}, u32[]{:S(2)}, u32[]{:S(2)}) collective-permute-start(bf16[4,1,32,256]{3,2,1,0:T(8,128)(2,1)S(1)} %get-tuple-element.107), channel_id=1, source_target_pairs={{1,0},{2,1},{3,2},{4,3},{5,4},{6,5},{7,6},{9,8},{10,9},{11,10},{12... | collective-permute-start | bytes 196616 | tf_op jit(solution)/shard_map/ppermute | solution.py:19
  (10 other events, 16.6 us)
Sparse Core Ops, SparseCore 0:
  36.2 37.8 reduce-scatter.4
  162.2 65.3 reduce-scatter.6
  233.4 159.8 all-reduce.6
where the time goes:
time: 402 us; the launch traced here: 401 us
  waiting for transfers between devices  211 us (52%)
  matrix products  64.6 us (16%)
  starting transfers between devices  46 us (11%)
  local copies, waits for them, and re-layouts  30.8 us (8%)
  blocking collectives  22.3 us (6%)
  between operations  15.1 us (4%)
  other arithmetic  11.1 us (3%)
    unnamed x5, waiting for transfers between devices  181 us
    dot_general x54, matrix products, weight_taps(): lax.dot_general(window.reshape(-1, window.shape[-1]), flat_grads, (((0,),...  36.1 us
    reduce_scatter x1, waiting for transfers between devices, body(): lax.psum_scatter(partial_grad.astype(jnp.bfloat16), 'fl', scatter_dimensi...  25.5 us
    ppermute x6, starting transfers between devices, padded_2(): lax.ppermute(head, axis, [((i + 1) % count, i) for i in range(ends)])  25 us
    all_gather x1, blocking collectives, body(): gathered = lax.all_gather(pooled, 'fl', axis=1, tiled=True)  22.3 us
    ppermute x6, starting transfers between devices, padded_2(): lax.ppermute(tail, axis, [(i, (i + 1) % count) for i in range(ends)])  20.8 us
    unnamed x43, local copies, waits for them, and re-layouts  19 us
    dot_general x54, matrix products, forward_taps(): jnp.dot(window.reshape(-1, window.shape[-1]), weight[number], preferred_e...  14.6 us
  transfers between devices with their start and end apart: 15, of which 5 were waited for; matrix products, arithmetic and copies ran while one was open for 23% of the time, Pallas kernels for 0%

commit v1 on v0

--- a/solution.py
+++ b/solution.py
@@ -98,7 +98,7 @@
 
 
 def fine_rim(values):
-    extended = padded_2(values, (("sp", 0), ("fl", 1)), 1)
+    extended = padded_2(values, ((SP, 0), (FL, 1)), 1)
     return jnp.pad(extended, ((0, 0), (0, 0), (1, 1), (0, 0)))
 
 
@@ -109,46 +109,74 @@
 def body(inputs, weight_fine, weight_coarse, cotangent):
     rows_x, rows_y, depth, width = inputs.shape
     fine_extent = (rows_x, rows_y, depth)
-    cells = rows_x * lax.axis_size("sp") * rows_y * lax.axis_size("fl") * depth
+    cells = rows_x * 16 * rows_y * 8 * depth
+    core = lax.axis_index("c")
+    padded_cot = coarse_rim_pad(padded_2(cotangent, ((SP, 0),), 1))
     padded_in = fine_rim(inputs)
+    coarse_extent = cotangent.shape[:3]
+    partial_grad = backward_taps(padded_cot, weight_coarse, coarse_extent).astype(jnp.bfloat16)
     fine_pre = forward_taps(padded_in, weight_fine, fine_extent)
     fine_act = (fine_pre * jax.nn.sigmoid(fine_pre)).astype(jnp.bfloat16)
     pooled = pool_cells(fine_act)
-    gathered = lax.all_gather(pooled, "fl", axis=1, tiled=True)
-    coarse_extent = gathered.shape[:3]
-    padded_pool = coarse_rim_pad(padded_2(gathered, (("sp", 0),), 1))
-    coarse_out = forward_taps(padded_pool, weight_coarse, coarse_extent).astype(jnp.bfloat16)
-    coarse_terms = weight_taps(padded_pool, cotangent, coarse_extent).reshape(
-        -1, cotangent.shape[-1]
-    )
-    grad_coarse = lax.psum_scatter(
-        coarse_terms.astype(jnp.bfloat16), "sp", scatter_dimension=0, tiled=True
-    ).astype(jnp.float32) * (1.0 / math.sqrt(cells // 8))
-    padded_cot = coarse_rim_pad(padded_2(cotangent, (("sp", 0),), 1))
-    partial_grad = backward_taps(padded_cot, weight_coarse, coarse_extent)
-    pooled_grad = lax.psum_scatter(
-        partial_grad.astype(jnp.bfloat16), "fl", scatter_dimension=1, tiled=True
+    half = pooled.reshape(-1, width)
+    parts = partial_grad.reshape(8, -1, width)
+    sent = jnp.concatenate([jnp.broadcast_to(half[None], parts.shape), parts], axis=1)
+    got = lax.all_to_all(sent, FL, 0, 0, tiled=True)
+    gathered = got[:, : half.shape[0]].reshape(coarse_extent + (width,))
+    pooled_grad = (
+        got[:, half.shape[0] :].astype(jnp.float32).sum(0).astype(jnp.bfloat16).reshape(pooled.shape)
     )
     fine_grad = (
         spread_cells(pooled_grad.astype(jnp.float32)) * 0.125 * silu_slope(fine_pre)
     ).astype(jnp.bfloat16)
-    fine_terms = weight_taps(padded_in, fine_grad, fine_extent).reshape(-1)
-    summed = lax.psum_scatter(fine_terms, ("sp", "fl"), scatter_dimension=0, tiled=True)
-    grad_fine = summed * (1.0 / math.sqrt(cells))
+    fine_terms = weight_taps(padded_in, fine_grad, fine_extent).astype(jnp.bfloat16)
+    fine_terms = fine_terms.reshape(8, 2, 8, -1, width)
+    theirs = jnp.where(core == 0, fine_terms[:, 1], fine_terms[:, 0])
+    mine = jnp.where(core == 0, fine_terms[:, 0], fine_terms[:, 1])
+    arrived = lax.ppermute(theirs, "c", [(0, 1), (1, 0)])
+    pair = (mine.astype(jnp.float32) + arrived.astype(jnp.float32)).astype(jnp.bfloat16)
+    spread = lax.all_to_all(
+        pair.reshape((64,) + pair.shape[2:]), ("x", "yh", "z", "yl"), 0, 0, tiled=True
+    )
+    grad_fine = spread.astype(jnp.float32).sum(0).reshape(-1) * (1.0 / math.sqrt(cells))
     grad_input = backward_taps(fine_rim(fine_grad), weight_fine, fine_extent).astype(jnp.bfloat16)
+
+    flat = gathered.reshape(-1, width)
+    pieces = []
+    for first, second, third in tap_offsets():
+        window = padded_cot[
+            2 - first : 2 - first + 1, 2 - second : 2 - second + 32, 2 - third : 2 - third + 16, :
+        ]
+        pieces.append(
+            lax.dot_general(
+                flat,
+                window.reshape(-1, window.shape[-1]),
+                (((0,), (0,)), ((), ())),
+                preferred_element_type=jnp.float32,
+            )
+        )
+    coarse_terms = jnp.stack(pieces).astype(jnp.bfloat16).reshape(8, 2, -1, cotangent.shape[-1])
+    theirs = jnp.where(core == 0, coarse_terms[:, 1], coarse_terms[:, 0])
+    mine = jnp.where(core == 0, coarse_terms[:, 0], coarse_terms[:, 1])
+    arrived = lax.ppermute(theirs, "c", [(0, 1), (1, 0)])
+    pair = (mine.astype(jnp.float32) + arrived.astype(jnp.float32)).astype(jnp.bfloat16)
+    spread = lax.all_to_all(pair, ("x", "yh"), 0, 0, tiled=True)
+    grad_coarse = spread.astype(jnp.float32).sum(0) * (1.0 / math.sqrt(cells // 8))
+    padded_pool = coarse_rim_pad(padded_2(gathered, ((SP, 0),), 1))
+    coarse_out = forward_taps(padded_pool, weight_coarse, coarse_extent).astype(jnp.bfloat16)
     return (coarse_out, grad_input, grad_fine, grad_coarse)
 
 
+SP = ("x", "yh", "c")
+FL = ("z", "yl")
+
+
 def solution(mesh):
+    fine_mesh = jax.sharding.Mesh(mesh.devices.reshape(4, 2, 2, 4, 2), SP + FL)
     return jax.shard_map(
         body,
-        mesh=mesh,
-        in_specs=(P("sp", "fl", None, None), P(), P(None, None, "fl"), P("sp", None, None, "fl")),
-        out_specs=(
-            P("sp", None, None, "fl"),
-            P("sp", "fl", None, None),
-            P(("sp", "fl")),
-            P("sp", "fl"),
-        ),
+        mesh=fine_mesh,
+        in_specs=(P(SP, FL, None, None), P(), P(None, None, FL), P(SP, None, None, FL)),
+        out_specs=(P(SP, None, None, FL), P(SP, FL, None, None), P(SP + FL), P(SP, FL)),
         check_vma=False,
     )

time: 402 us -> 230 us (0.57)
  waiting for transfers between devices: 211 us -> 44.3 us
  blocking collectives: 22.3 us -> 0 us
  matrix products: 64.6 us -> 79.9 us
  starting transfers between devices: 46 us -> 60.3 us
  between operations: 15.1 us -> 2.34 us
  local copies, waits for them, and re-layouts: 30.8 us -> 23.2 us
  other arithmetic: 11.1 us -> 18.7 us
    unnamed x5 -> x0, waiting for transfers between devices: 181 us -> none
    all_to_all x0 -> x3, waiting for transfers between devices: none -> 31.6 us  [the longest x1 17.7 us: body(): lax.all_to_all(pair.reshape((64,) + pair.shape[2:]), ('x', 'yh', 'z', 'yl...]
    reduce_scatter x1 -> x0, waiting for transfers between devices: 25.5 us -> none  [body(): lax.psum_scatter(partial_grad.astype(jnp.bfloat16), 'fl', scatter_dimensi...]
    all_gather x1 -> x0, blocking collectives: 22.3 us -> none  [body(): gathered = lax.all_gather(pooled, 'fl', axis=1, tiled=True)]
    all_to_all x0 -> x3, starting transfers between devices: none -> 21.8 us  [the longest x1 8.69 us: body(): spread = lax.all_to_all(pair, ('x', 'yh'), 0, 0, tiled=True)]
    dot_general x54, matrix products: 14.6 us -> 31.5 us  [forward_taps(): jnp.dot(window.reshape(-1, window.shape[-1]), weight[number], preferred_e...]
    unnamed x43 -> x120, local copies, waits for them, and re-layouts: 19 us -> 3.16 us
    ppermute x6, starting transfers between devices: 25 us -> 10.6 us  [padded_2(): lax.ppermute(head, axis, [((i + 1) % count, i) for i in range(ends)])]
  transfers between devices with their start and end apart: 15 -> 17, of which waited for: 5 -> 6; matrix products, arithmetic and copies ran while one was open for 23% -> 46% of each run, Pallas kernels for 0% -> 0%
where the time goes in v1:
time: 230 us; the launch traced here: 229 us
  matrix products  79.9 us (35%)
  starting transfers between devices  60.3 us (26%)
  waiting for transfers between devices  44.3 us (19%)
  local copies, waits for them, and re-layouts  23.2 us (10%)
  other arithmetic  18.7 us (8%)
  between operations  2.34 us (1%)
    dot_general x54, matrix products, forward_taps(): jnp.dot(window.reshape(-1, window.shape[-1]), weight[number], preferred_e...  31.5 us
    ppermute x6, starting transfers between devices, padded_2(): lax.ppermute(tail, axis, [(i, (i + 1) % count) for i in range(ends)])  27.6 us
    dot_general x27, matrix products, weight_taps(): lax.dot_general(window.reshape(-1, window.shape[-1]), flat_grads, (((0,),...  25.2 us
    all_to_all x1, waiting for transfers between devices, body(): lax.all_to_all(pair.reshape((64,) + pair.shape[2:]), ('x', 'yh', 'z', 'yl...  17.7 us
    dot_general x54, matrix products, backward_taps(): lax.dot_general(window.reshape(-1, window.shape[-1]), weight[number], (((...  13.8 us
    ppermute x6, waiting for transfers between devices, padded_2(): lax.ppermute(head, axis, [((i + 1) % count, i) for i in range(ends)])  12.7 us
    ppermute x6, starting transfers between devices, padded_2(): lax.ppermute(head, axis, [((i + 1) % count, i) for i in range(ends)])  10.6 us
    dot_general x27, matrix products, body(): lax.dot_general(flat, window.reshape(-1, window.shape[-1]), (((0,), (0,))...  9.41 us
  transfers between devices with their start and end apart: 17, of which 6 were waited for; matrix products, arithmetic and copies ran while one was open for 46% of the time, Pallas kernels for 0%

profile of v1, /device:TPU:1, one launch (start us, length us, event | category | flops | bytes accessed | tf_op | source)
XLA Modules:
  0.0 228.7 jit_solution(7109964646152069766)
XLA Ops:
  0.6 6.2 %collective-permute-start.4 = (bf16[1,32,16,64]{3,2,1,0:T(8,128)(2,1)}, bf16[1,32,16,64]{3,2,1,0:T(8,128)(2,1)S(1)}, u32[]{:S(2)}, u32[]{:S(2)}) collective-permute-start(bf16[1,32,16,64]{3,2,1,0:T(8,128)(2,1)} %param.7), channel_id=1, source_target_pairs={{0,8},{8,16},{16,24},{24,32},{32,40},{40,48},{48,56},{56,64},{64,7... | collective-permute-start | bytes 196616 | tf_op jit(solution)/shard_map/ppermute | solution.py:17
  6.9 1.9 collective-permute-start.5
  9.8 5.1 %collective-permute-start = (bf16[1,8,32,256]{3,2,1,0:T(8,128)(2,1)S(1)}, bf16[1,8,32,256]{3,2,1,0:T(8,128)(2,1)S(1)}, u32[]{:S(2)}, u32[]{:S(2)}) collective-permute-start(bf16[1,8,32,256]{3,2,1,0:T(8,128)(2,1)S(1)} %get-tuple-element.125), channel_id=1, source_target_pairs={{0,8},{8,16},{16,24},{24,32},{32,40},{40,48},{48,56},{56,64},{64,7... | collective-permute-start | bytes 393224 | tf_op jit(solution)/shard_map/ppermute | solution.py:17
  14.9 2.1 collective-permute-start.1
  24.8 2.3 %collective-permute-start.2 = (bf16[4,1,32,256]{3,2,1,0:T(8,128)(2,1)S(1)}, bf16[4,1,32,256]{3,2,1,0:T(8,128)(2,1)S(1)}, u32[]{:S(2)}, u32[]{:S(2)}) collective-permute-start(bf16[4,1,32,256]{3,2,1,0:T(8,128)(2,1)S(1)} %get-tuple-element.115), channel_id=1, source_target_pairs={{0,1},{1,2},{2,3},{3,4},{4,5},{5,6},{6,7},{8,9},{9,10},{10,11},{11... | collective-permute-start | bytes 196616 | tf_op jit(solution)/shard_map/ppermute | solution.py:17
  29.4 3.7 %collective-permute-done.3 = bf16[4,1,32,256]{3,2,1,0:T(8,128)(2,1)S(1)} collective-permute-done((bf16[4,1,32,256]{3,2,1,0:T(8,128)(2,1)S(1)}, bf16[4,1,32,256]{3,2,1,0:T(8,128)(2,1)S(1)}, u32[]{:S(2)}, u32[]{:S(2)}) %collective-permute-start.3) | collective-permute-done | bytes 65568 | tf_op jit(solution)/shard_map/ppermute | solution.py:19
  44.3 6.6 %all-to-all-start = ((bf16[8,128,256]{2,1,0:T(8,128)(2,1)}), bf16[8,128,256]{2,1,0:T(8,128)(2,1)S(1)}, u32[]{:S(2)}, u32[]{:S(2)}) async-start(bf16[8,128,256]{2,1,0:T(8,128)(2,1)} %pad_maximum_fusion.3), calls=%async_computation | async-start | bytes 1048576 | tf_op jit(solution)/shard_map/all_to_all | solution.py:124
  50.9 9.2 %all-to-all-done = bf16[8,128,256]{2,1,0:T(8,128)(2,1)S(1)} async-done(((bf16[8,128,256]{2,1,0:T(8,128)(2,1)}), bf16[8,128,256]{2,1,0:T(8,128)(2,1)S(1)}, u32[]{:S(2)}, u32[]{:S(2)}) %all-to-all-start) | async-done | bytes 524320 | tf_op jit(solution)/shard_map/all_to_all | solution.py:124
  63.2 6.4 %collective-permute-start.6 = (bf16[1,32,16,256]{3,2,1,0:T(8,128)(2,1)S(1)}, bf16[1,32,16,256]{3,2,1,0:T(8,128)(2,1)}, u32[]{:S(2)}, u32[]{:S(2)}) collective-permute-start(bf16[1,32,16,256]{3,2,1,0:T(8,128)(2,1)S(1)} %bitcast.1084), channel_id=1, source_target_pairs={{0,8},{8,16},{16,24},{24,32},{32,40},{40,48},{48,56},{56,64},{64,7... | collective-permute-start | bytes 786440 | tf_op jit(solution)/shard_map/ppermute | solution.py:17
  69.6 2.1 collective-permute-start.7
  81.8 2.5 %convert_element_type.145 = bf16[8,2,432,64]{2,1,0,3:T(2,128)(2,1)S(1)} reshape(bf16[27,256,64]{1,0,2:T(8,128)(2,1)S(1)} %copy.53) | data formatting | bytes 1769472 | tf_op jit(solution)/shard_map/convert_element_type | solution.py:158
  84.3 2.2 broadcast_select_fusion
  111.7 6.2 %convert_element_type.139 = bf16[8,2,8,54,256]{4,3,2,1,0:T(8,128)(2,1)} reshape(bf16[27,256,256]{2,1,0:T(8,128)(2,1)} %fusion.50) | data formatting | bytes 7077888 | tf_op jit(solution)/shard_map/convert_element_type | solution.py:132
  118.0 2.3 %select_bitcast_fusion = bf16[8,8,54,256]{3,2,1,0:T(8,128)(2,1)S(1)} fusion(pred[]{:T(512)S(6)} %eq.2, bf16[8,2,8,54,256]{4,3,2,1,0:T(8,128)(2,1)} %convert_element_type.139), kind=kLoop, calls=%fused_computation.18 | loop fusion | flops 884736 | bytes 5308417 | tf_op jit(solution)/shard_map/jit(_where)/select_n | solution.py:134
  122.0 5.1 %collective-permute-start.8 = (bf16[1,8,32,256]{3,2,1,0:T(8,128)(2,1)S(1)}, bf16[1,8,32,256]{3,2,1,0:T(8,128)(2,1)S(1)}, u32[]{:S(2)}, u32[]{:S(2)}) collective-permute-start(bf16[1,8,32,256]{3,2,1,0:T(8,128)(2,1)S(1)} %copy-done.58), channel_id=1, source_target_pairs={{0,8},{8,16},{16,24},{24,32},{32,40},{40,48},{48,56},{56,64},{64,7... | collective-permute-start | bytes 393224 | tf_op jit(solution)/shard_map/ppermute | solution.py:17
  127.1 1.9 collective-permute-start.9
  129.3 5.6 %collective-permute-done.9 = bf16[1,8,32,256]{3,2,1,0:T(8,128)(2,1)S(1)} collective-permute-done((bf16[1,8,32,256]{3,2,1,0:T(8,128)(2,1)S(1)}, bf16[1,8,32,256]{3,2,1,0:T(8,128)(2,1)S(1)}, u32[]{:S(2)}, u32[]{:S(2)}) %collective-permute-start.9) | collective-permute-done | bytes 131104 | tf_op jit(solution)/shard_map/ppermute | solution.py:19
  134.9 2.4 %collective-permute-start.10 = (bf16[4,1,32,256]{3,2,1,0:T(8,128)(2,1)S(1)}, bf16[4,1,32,256]{3,2,1,0:T(8,128)(2,1)S(1)}, u32[]{:S(2)}, u32[]{:S(2)}) collective-permute-start(bf16[4,1,32,256]{3,2,1,0:T(8,128)(2,1)S(1)} %get-tuple-element.108), channel_id=1, source_target_pairs={{0,1},{1,2},{2,3},{3,4},{4,5},{5,6},{6,7},{8,9},{9,10},{10,11},{11... | collective-permute-start | bytes 196616 | tf_op jit(solution)/shard_map/ppermute | solution.py:17
  139.0 3.3 %collective-permute-done.11 = bf16[4,1,32,256]{3,2,1,0:T(8,128)(2,1)S(1)} collective-permute-done((bf16[4,1,32,256]{3,2,1,0:T(8,128)(2,1)S(1)}, bf16[4,1,32,256]{3,2,1,0:T(8,128)(2,1)S(1)}, u32[]{:S(2)}, u32[]{:S(2)}) %collective-permute-start.11) | collective-permute-done | bytes 65568 | tf_op jit(solution)/shard_map/ppermute | solution.py:19
  176.7 8.7 %all-to-all-start.2 = ((bf16[8,432,64]{1,2,0:T(8,128)(2,1)}), bf16[8,432,64]{1,2,0:T(8,128)(2,1)S(1)}, u32[]{:S(2)}, u32[]{:S(2)}) async-start(bf16[8,432,64]{1,2,0:T(8,128)(2,1)} %copy.56), calls=%async_computation.2 | async-start | bytes 1048576 | tf_op jit(solution)/shard_map/all_to_all | solution.py:163
  185.4 4.7 %fusion = bf16[8,8,54,256]{3,2,1,0:T(8,128)(2,1)} fusion(bf16[8,8,54,256]{3,1,2,0:T(8,128)(2,1)} %collective-permute-done.12, pred[]{:T(512)S(6)} %eq.2, bf16[8,2,8,54,256]{4,3,2,1,0:T(8,128)(2,1)} %convert_element_type.139), kind=kLoop, calls=%fused_computation.5 | loop fusion | flops 4423680 | bytes 7077889 | tf_op jit(solution)/shard_map/convert_element_type | solution.py:137
  190.2 4.7 %all-to-all-done.2 = bf16[8,432,64]{1,2,0:T(8,128)(2,1)S(1)} async-done(((bf16[8,432,64]{1,2,0:T(8,128)(2,1)}), bf16[8,432,64]{1,2,0:T(8,128)(2,1)S(1)}, u32[]{:S(2)}, u32[]{:S(2)}) %all-to-all-start.2) | async-done | bytes 442400 | tf_op jit(solution)/shard_map/all_to_all | solution.py:163
  194.8 6.5 %all-to-all-start.1 = ((bf16[64,54,256]{2,1,0:T(8,128)(2,1)}), bf16[64,54,256]{2,1,0:T(8,128)(2,1)S(1)}, u32[]{:S(2)}, u32[]{:S(2)}) async-start(bf16[64,54,256]{2,1,0:T(8,128)(2,1)} %bitcast.253), calls=%async_computation.1 | async-start | bytes 3670016 | tf_op jit(solution)/shard_map/all_to_all | solution.py:138
  210.1 17.7 %all-to-all-done.1 = bf16[64,54,256]{2,1,0:T(8,128)(2,1)S(1)} async-done(((bf16[64,54,256]{2,1,0:T(8,128)(2,1)}), bf16[64,54,256]{2,1,0:T(8,128)(2,1)S(1)}, u32[]{:S(2)}, u32[]{:S(2)}) %all-to-all-start.1) | async-done | bytes 1769504 | tf_op jit(solution)/shard_map/all_to_all | solution.py:138
  (340 shorter events, 106.7 us)
Async XLA Ops:
  0.6 16.4 %collective-permute-start.4 = (bf16[1,32,16,64]{3,2,1,0:T(8,128)(2,1)}, bf16[1,32,16,64]{3,2,1,0:T(8,128)(2,1)S(1)}, u32[]{:S(2)}, u32[]{:S(2)}) collective-permute-start(bf16[1,32,16,64]{3,2,1,0:T(8,128)(2,1)} %param.7), channel_id=1, source_target_pairs={{0,8},{8,16},{16,24},{24,32},{32,40},{40,48},{48,56},{56,64},{64,7... | collective-permute-start | bytes 196616 | tf_op jit(solution)/shard_map/ppermute | solution.py:17
  6.9 10.2 %collective-permute-start.5 = (bf16[1,32,16,64]{3,2,1,0:T(8,128)(2,1)}, bf16[1,32,16,64]{3,2,1,0:T(8,128)(2,1)S(1)}, u32[]{:S(2)}, u32[]{:S(2)}) collective-permute-start(bf16[1,32,16,64]{3,2,1,0:T(8,128)(2,1)} %param.7), channel_id=1, source_target_pairs={{8,0},{16,8},{24,16},{32,24},{40,32},{48,40},{56,48},{64,56},{72,6... | collective-permute-start | bytes 196616 | tf_op jit(solution)/shard_map/ppermute | solution.py:19
  9.8 14.8 %collective-permute-start = (bf16[1,8,32,256]{3,2,1,0:T(8,128)(2,1)S(1)}, bf16[1,8,32,256]{3,2,1,0:T(8,128)(2,1)S(1)}, u32[]{:S(2)}, u32[]{:S(2)}) collective-permute-start(bf16[1,8,32,256]{3,2,1,0:T(8,128)(2,1)S(1)} %get-tuple-element.125), channel_id=1, source_target_pairs={{0,8},{8,16},{16,24},{24,32},{32,40},{40,48},{48,56},{56,64},{64,7... | collective-permute-start | bytes 393224 | tf_op jit(solution)/shard_map/ppermute | solution.py:17
  14.9 9.8 %collective-permute-start.1 = (bf16[1,8,32,256]{3,2,1,0:T(8,128)(2,1)S(1)}, bf16[1,8,32,256]{3,2,1,0:T(8,128)(2,1)S(1)}, u32[]{:S(2)}, u32[]{:S(2)}) collective-permute-start(bf16[1,8,32,256]{3,2,1,0:T(8,128)(2,1)S(1)} %get-tuple-element.124), channel_id=1, source_target_pairs={{8,0},{16,8},{24,16},{32,24},{40,32},{48,40},{56,48},{64,56},{72,6... | collective-permute-start | bytes 393224 | tf_op jit(solution)/shard_map/ppermute | solution.py:19
  24.8 4.6 %collective-permute-start.2 = (bf16[4,1,32,256]{3,2,1,0:T(8,128)(2,1)S(1)}, bf16[4,1,32,256]{3,2,1,0:T(8,128)(2,1)S(1)}, u32[]{:S(2)}, u32[]{:S(2)}) collective-permute-start(bf16[4,1,32,256]{3,2,1,0:T(8,128)(2,1)S(1)} %get-tuple-element.115), channel_id=1, source_target_pairs={{0,1},{1,2},{2,3},{3,4},{4,5},{5,6},{6,7},{8,9},{9,10},{10,11},{11... | collective-permute-start | bytes 196616 | tf_op jit(solution)/shard_map/ppermute | solution.py:17
  27.1 6.0 %collective-permute-start.3 = (bf16[4,1,32,256]{3,2,1,0:T(8,128)(2,1)S(1)}, bf16[4,1,32,256]{3,2,1,0:T(8,128)(2,1)S(1)}, u32[]{:S(2)}, u32[]{:S(2)}) collective-permute-start(bf16[4,1,32,256]{3,2,1,0:T(8,128)(2,1)S(1)} %get-tuple-element.116), channel_id=1, source_target_pairs={{1,0},{2,1},{3,2},{4,3},{5,4},{6,5},{7,6},{9,8},{10,9},{11,10},{12... | collective-permute-start | bytes 196616 | tf_op jit(solution)/shard_map/ppermute | solution.py:19
  44.3 15.8 %all-to-all-start = ((bf16[8,128,256]{2,1,0:T(8,128)(2,1)}), bf16[8,128,256]{2,1,0:T(8,128)(2,1)S(1)}, u32[]{:S(2)}, u32[]{:S(2)}) async-start(bf16[8,128,256]{2,1,0:T(8,128)(2,1)} %pad_maximum_fusion.3), calls=%async_computation | async-start | bytes 1048576 | tf_op jit(solution)/shard_map/all_to_all | solution.py:124
  60.2 16.2 %copy-start.33 = (bf16[1,32,16,64]{3,2,1,0:T(8,128)(2,1)S(1)}, bf16[1,32,16,64]{3,2,1,0:T(8,128)(2,1)}, u32[]{:S(2)}) copy-start(bf16[1,32,16,64]{3,2,1,0:T(8,128)(2,1)} %copy-done.32) | copy-start | bytes 196612
  60.4 16.2 %copy-start.25 = (bf16[1,32,16,64]{3,2,1,0:T(8,128)(2,1)S(1)}, bf16[1,32,16,64]{3,2,1,0:T(8,128)(2,1)}, u32[]{:S(2)}) copy-start(bf16[1,32,16,64]{3,2,1,0:T(8,128)(2,1)} %copy-done.24) | copy-start | bytes 196612
  60.4 16.4 %copy-start.23 = (bf16[1,32,16,64]{3,2,1,0:T(8,128)(2,1)S(1)}, bf16[1,32,16,64]{3,2,1,0:T(8,128)(2,1)}, u32[]{:S(2)}) copy-start(bf16[1,32,16,64]{3,2,1,0:T(8,128)(2,1)} %copy-done.22) | copy-start | bytes 196612
  61.6 16.2 %copy-start.15 = (bf16[1,32,16,64]{3,2,1,0:T(8,128)(2,1)S(1)}, bf16[1,32,16,64]{3,2,1,0:T(8,128)(2,1)}, u32[]{:S(2)}) copy-start(bf16[1,32,16,64]{3,2,1,0:T(8,128)(2,1)} %copy-done.14) | copy-start | bytes 196612
  61.6 16.4 %copy-start.13 = (bf16[1,32,16,64]{3,2,1,0:T(8,128)(2,1)S(1)}, bf16[1,32,16,64]{3,2,1,0:T(8,128)(2,1)}, u32[]{:S(2)}) copy-start(bf16[1,32,16,64]{3,2,1,0:T(8,128)(2,1)} %copy-done.12) | copy-start | bytes 196612
  61.6 16.6 %copy-start.36 = (bf16[1,32,16,64]{3,2,1,0:T(8,128)(2,1)S(1)}, bf16[1,32,16,64]{3,2,1,0:T(8,128)(2,1)}, u32[]{:S(2)}) copy-start(bf16[1,32,16,64]{3,2,1,0:T(8,128)(2,1)} %param.7) | copy-start | bytes 196612
  62.5 16.1 %copy-start.9 = (bf16[1,32,16,64]{3,2,1,0:T(8,128)(2,1)S(1)}, bf16[1,32,16,64]{3,2,1,0:T(8,128)(2,1)}, u32[]{:S(2)}) copy-start(bf16[1,32,16,64]{3,2,1,0:T(8,128)(2,1)} %copy-done.8) | copy-start | bytes 196612
  63.2 89.8 %collective-permute-start.6 = (bf16[1,32,16,256]{3,2,1,0:T(8,128)(2,1)S(1)}, bf16[1,32,16,256]{3,2,1,0:T(8,128)(2,1)}, u32[]{:S(2)}, u32[]{:S(2)}) collective-permute-start(bf16[1,32,16,256]{3,2,1,0:T(8,128)(2,1)S(1)} %bitcast.1084), channel_id=1, source_target_pairs={{0,8},{8,16},{16,24},{24,32},{32,40},{40,48},{48,56},{56,64},{64,7... | collective-permute-start | bytes 786440 | tf_op jit(solution)/shard_map/ppermute | solution.py:17
  69.6 83.5 %collective-permute-start.7 = (bf16[1,32,16,256]{3,2,1,0:T(8,128)(2,1)S(1)}, bf16[1,32,16,256]{3,2,1,0:T(8,128)(2,1)}, u32[]{:S(2)}, u32[]{:S(2)}) collective-permute-start(bf16[1,32,16,256]{3,2,1,0:T(8,128)(2,1)S(1)} %bitcast.1085), channel_id=1, source_target_pairs={{8,0},{16,8},{24,16},{32,24},{40,32},{48,40},{56,48},{64,56},{72,6... | collective-permute-start | bytes 786440 | tf_op jit(solution)/shard_map/ppermute | solution.py:19
  87.5 87.0 %collective-permute-start.13 = (bf16[8,432,64]{1,0,2:T(8,128)(2,1)}, bf16[8,432,64]{1,0,2:T(8,128)(2,1)}, u32[]{:S(2)}, u32[]{:S(2)}) collective-permute-start(bf16[8,432,64]{1,0,2:T(8,128)(2,1)} %bitcast.1083), channel_id=1, source_target_pairs={{0,8},{8,0},{1,9},{9,1},{2,10},{10,2},{3,11},{11,3},{4,12},{12,4},... | collective-permute-start | bytes 1327112 | tf_op jit(solution)/shard_map/ppermute | solution.py:161
  122.0 7.3 %collective-permute-start.8 = (bf16[1,8,32,256]{3,2,1,0:T(8,128)(2,1)S(1)}, bf16[1,8,32,256]{3,2,1,0:T(8,128)(2,1)S(1)}, u32[]{:S(2)}, u32[]{:S(2)}) collective-permute-start(bf16[1,8,32,256]{3,2,1,0:T(8,128)(2,1)S(1)} %copy-done.58), channel_id=1, source_target_pairs={{0,8},{8,16},{16,24},{24,32},{32,40},{40,48},{48,56},{56,64},{64,7... | collective-permute-start | bytes 393224 | tf_op jit(solution)/shard_map/ppermute | solution.py:17
  127.1 7.8 %collective-permute-start.9 = (bf16[1,8,32,256]{3,2,1,0:T(8,128)(2,1)S(1)}, bf16[1,8,32,256]{3,2,1,0:T(8,128)(2,1)S(1)}, u32[]{:S(2)}, u32[]{:S(2)}) collective-permute-start(bf16[1,8,32,256]{3,2,1,0:T(8,128)(2,1)S(1)} %copy-done.57), channel_id=1, source_target_pairs={{8,0},{16,8},{24,16},{32,24},{40,32},{48,40},{56,48},{64,56},{72,6... | collective-permute-start | bytes 393224 | tf_op jit(solution)/shard_map/ppermute | solution.py:19
  134.9 3.8 %collective-permute-start.10 = (bf16[4,1,32,256]{3,2,1,0:T(8,128)(2,1)S(1)}, bf16[4,1,32,256]{3,2,1,0:T(8,128)(2,1)S(1)}, u32[]{:S(2)}, u32[]{:S(2)}) collective-permute-start(bf16[4,1,32,256]{3,2,1,0:T(8,128)(2,1)S(1)} %get-tuple-element.108), channel_id=1, source_target_pairs={{0,1},{1,2},{2,3},{3,4},{4,5},{5,6},{6,7},{8,9},{9,10},{10,11},{11... | collective-permute-start | bytes 196616 | tf_op jit(solution)/shard_map/ppermute | solution.py:17
  137.4 5.0 %collective-permute-start.11 = (bf16[4,1,32,256]{3,2,1,0:T(8,128)(2,1)S(1)}, bf16[4,1,32,256]{3,2,1,0:T(8,128)(2,1)S(1)}, u32[]{:S(2)}, u32[]{:S(2)}) collective-permute-start(bf16[4,1,32,256]{3,2,1,0:T(8,128)(2,1)S(1)} %get-tuple-element.109), channel_id=1, source_target_pairs={{1,0},{2,1},{3,2},{4,3},{5,4},{6,5},{7,6},{9,8},{10,9},{11,10},{12... | collective-permute-start | bytes 196616 | tf_op jit(solution)/shard_map/ppermute | solution.py:19
  138.7 46.7 %collective-permute-start.12 = (bf16[8,8,54,256]{3,1,2,0:T(8,128)(2,1)}, bf16[8,8,54,256]{3,1,2,0:T(8,128)(2,1)}, u32[]{:S(2)}, u32[]{:S(2)}) collective-permute-start(bf16[8,8,54,256]{3,1,2,0:T(8,128)(2,1)} %copy.51), channel_id=1, source_target_pairs={{0,8},{8,0},{1,9},{9,1},{2,10},{10,2},{3,11},{11,3},{4,12},{12,4},... | collective-permute-start | bytes 5308424 | tf_op jit(solution)/shard_map/ppermute | solution.py:136
  176.7 18.1 %all-to-all-start.2 = ((bf16[8,432,64]{1,2,0:T(8,128)(2,1)}), bf16[8,432,64]{1,2,0:T(8,128)(2,1)S(1)}, u32[]{:S(2)}, u32[]{:S(2)}) async-start(bf16[8,432,64]{1,2,0:T(8,128)(2,1)} %copy.56), calls=%async_computation.2 | async-start | bytes 1048576 | tf_op jit(solution)/shard_map/all_to_all | solution.py:163
  194.8 32.9 %all-to-all-start.1 = ((bf16[64,54,256]{2,1,0:T(8,128)(2,1)}), bf16[64,54,256]{2,1,0:T(8,128)(2,1)S(1)}, u32[]{:S(2)}, u32[]{:S(2)}) async-start(bf16[64,54,256]{2,1,0:T(8,128)(2,1)} %bitcast.253), calls=%async_computation.1 | async-start | bytes 3670016 | tf_op jit(solution)/shard_map/all_to_all | solution.py:138
  (52 other events, 277.3 us)

commit v2 on v0

v2 whole, which is shorter than its diff:
```python
import functools
import math

import jax
import jax.numpy as jnp
from jax import lax
from jax.experimental import pallas as pl
from jax.experimental.pallas import tpu as pltpu
from jax.sharding import PartitionSpec as P

SP = ("x", "yh", "c")
FL = ("z", "yl")
BF = jnp.bfloat16
F32 = jnp.float32
VMEM = pl.BlockSpec(memory_space=pltpu.VMEM)
SMEM = pl.BlockSpec(memory_space=pltpu.SMEM)
ANY = pl.BlockSpec(memory_space=pl.ANY)


def call(kernel, out_shape, in_specs, scratch=(), flops=0, moved=0, limit=24):
    return pl.pallas_call(
        kernel,
        out_shape=out_shape,
        in_specs=in_specs,
        out_specs=jax.tree.map(lambda _: VMEM, out_shape),
        scratch_shapes=list(scratch),
        compiler_params=pltpu.CompilerParams(vmem_limit_bytes=limit * 2**20),
        cost_estimate=pl.CostEstimate(flops=flops, bytes_accessed=moved, transcendentals=0),
    )


def along_depth(rows, order):
    count, depth, width = rows.shape
    flat = rows.astype(F32).reshape(count * depth, width)
    place = lax.broadcasted_iota(jnp.int32, flat.shape, 0) & (depth - 1)
    before = jnp.where(place == 0, 0.0, pltpu.roll(flat, 1, 0)).astype(BF)
    after = jnp.where(place == depth - 1, 0.0, pltpu.roll(flat, count * depth - 1, 0)).astype(BF)
    middle = flat.astype(BF)
    trio = (before, middle, after) if order > 0 else (after, middle, before)
    return jnp.concatenate(trio, axis=1).reshape(count, depth, 3 * width)


def fetch(source, target, sems):
    copies = [
        pltpu.make_async_copy(source.at[k], target.at[k], sems.at[k]) for k in range(sems.shape[0])
    ]
    for copy in copies:
        copy.start()
    return copies


def assemble(own, xlo, xhi, ylo, yhi, wide, order):
    planes = (xlo[0], own[0], own[1], xhi[0])
    for x in range(4):
        rows = jnp.concatenate([ylo[x : x + 1], planes[x], yhi[x : x + 1]], axis=0)
        wide[x] = along_depth(rows, order)


def fine_forward_kernel(own, xlo, xhi, ylo, yhi, w_hbm, pooled, slope, wide, w, pre, sums, sems):
    copies = fetch(w_hbm, w, sems)
    assemble(own, xlo, xhi, ylo, yhi, wide, 1)
    for k in range(9):
        a, b = divmod(k, 3)
        copies[k].wait()
        window = wide[a : a + 2, b : b + 8].reshape(512, 768)
        term = jnp.dot(window, w[k], preferred_element_type=F32)
        pre[...] = term if k == 0 else pre[...] + term
    for y in range(4):
        total = jnp.zeros((32, 256), F32)
        for x in range(2):
            for half in range(2):
                at = x * 256 + (2 * y + half) * 32
                value = pre[at : at + 32]
                sigma = 1.0 / (1.0 + jnp.exp(-value))
                total = total + (value * sigma).astype(BF).astype(F32)
                slope[at : at + 32] = 0.125 * sigma * (1.0 + value * (1.0 - sigma))
        sums[0, y * 32 : y * 32 + 32] = total[:, :128]
        sums[1, y * 32 : y * 32 + 32] = total[:, 128:]
    for side in range(2):
        even = sums[side, pl.ds(0, 64, stride=2)]
        odd = sums[side, pl.ds(1, 64, stride=2)]
        pooled[:, side * 128 : side * 128 + 128] = ((even + odd) * 0.125).astype(BF)


def fine_forward(own, xlo, xhi, ylo, yhi, weight):
    return call(
        fine_forward_kernel,
        (jax.ShapeDtypeStruct((64, 256), BF), jax.ShapeDtypeStruct((512, 256), F32)),
        [VMEM] * 5 + [ANY],
        [
            pltpu.VMEM((4, 10, 32, 768), BF),
            pltpu.VMEM((9, 768, 256), BF),
            pltpu.VMEM((512, 256), F32),
            pltpu.VMEM((2, 128, 128), F32),
            pltpu.SemaphoreType.DMA((9,)),
        ],
        flops=2 * 512 * 6912 * 256,
        moved=5 * 2**20,
    )(own, xlo, xhi, ylo, yhi, weight.reshape(9, 768, 256))


def turn_kernel(own, xlo, xhi, ylo, yhi, turned):
    planes = (xlo[0], own[0], own[1], xhi[0])
    for x in range(4):
        rows = jnp.concatenate([ylo[x : x + 1], planes[x], yhi[x : x + 1]], axis=0)
        wide = along_depth(rows, 1)
        for b in range(3):
            for c in range(3):
                window = wide[b : b + 8, :, c * 256 : c * 256 + 256].reshape(256, 256)
                turned[b * 3 + c, :, x * 256 : x * 256 + 256] = window.T


def turn(own, xlo, xhi, ylo, yhi):
    return call(
        turn_kernel,
        jax.ShapeDtypeStruct((9, 256, 1024), BF),
        [VMEM] * 5,
        flops=2 * 512 * 6912 * 64,
        moved=6 * 2**20,
    )(own, xlo, xhi, ylo, yhi)


def fine_weight_kernel(core, parts, slope, turned, grad, terms, spread, total):
    summed = parts[0].astype(F32)
    for k in range(1, 8):
        summed = summed + parts[k].astype(F32)
    summed = summed.astype(BF).astype(F32)
    for side in range(2):
        half = summed[:, side * 128 : side * 128 + 128]
        spread[side, pl.ds(0, 64, stride=2)] = half
        spread[side, pl.ds(1, 64, stride=2)] = half
    for y in range(4):
        wide = jnp.concatenate([spread[0, y * 32 : y * 32 + 32], spread[1, y * 32 : y * 32 + 32]], axis=1)
        for x in range(2):
            for half in range(2):
                at = x * 256 + (2 * y + half) * 32
                grad[at : at + 32] = (wide * slope[at : at + 32]).astype(BF)
    right = grad[...]
    me = core[0]
    done = 0
    for tap in range(27):
        a, bc = divmod(tap, 9)
        total[tap * 256 : tap * 256 + 256] = jnp.dot(
            turned[bc, :, a * 256 : a * 256 + 512], right, preferred_element_type=F32
        )
        while done < 128 and (done + 1) * 54 <= (tap + 1) * 256:
            block, f = divmod(done, 8)
            k, c = divmod(block, 2)
            value = total[done * 54 : done * 54 + 54].astype(BF)
            terms[lax.rem(me + c, 2), k * 8 + f] = value
            done += 1


def fine_weight(core, parts, slope, turned):
    return call(
        fine_weight_kernel,
        (jax.ShapeDtypeStruct((512, 256), BF), jax.ShapeDtypeStruct((2, 64, 54, 256), BF)),
        [SMEM] + [VMEM] * 3,
        [pltpu.VMEM((2, 128, 128), F32), pltpu.VMEM((6912, 256), F32)],
        flops=2 * 512 * 6912 * 256,
        moved=9 * 2**20,
        limit=32,
    )(core, parts, slope, turned)


def fine_back_kernel(own, xlo, xhi, ylo, yhi, w_hbm, out, wide, w, total, sems):
    copies = fetch(w_hbm, w, sems)
    assemble(own, xlo, xhi, ylo, yhi, wide, -1)
    for k in range(9):
        a, b = divmod(k, 3)
        copies[k].wait()
        window = wide[2 - a : 4 - a, 2 - b : 10 - b].reshape(512, 768)
        right = jnp.concatenate([w[k, 0], w[k, 1], w[k, 2]], axis=1)
        term = lax.dot_general(window, right, (((1,), (1,)), ((), ())), preferred_element_type=F32)
        total[...] = term if k == 0 else total[...] + term
    out[...] = total[...].astype(BF)


def fine_back(own, xlo, xhi, ylo, yhi, weight):
    return call(
        fine_back_kernel,
        jax.ShapeDtypeStruct((512, 256), BF),
        [VMEM] * 5 + [ANY],
        [
            pltpu.VMEM((4, 10, 32, 768), BF),
            pltpu.VMEM((9, 3, 256, 256), BF),
            pltpu.VMEM((512, 256), F32),
            pltpu.SemaphoreType.DMA((9,)),
        ],
        flops=2 * 512 * 6912 * 256,
        moved=5 * 2**20,
    )(own, xlo, xhi, ylo, yhi, weight.reshape(9, 3, 256, 256))


def pad_rows(plane):
    edge = jnp.zeros((1,) + plane.shape[1:], plane.dtype)
    return jnp.concatenate([edge, plane, edge], axis=0)


def coarse_back_kernel(own, xlo, xhi, w, partial, wide):
    for x, plane in enumerate((xlo, own, xhi)):
        wide[x] = along_depth(pad_rows(plane[0]), -1)
    total = None
    for k in range(9):
        a, b = divmod(k, 3)
        window = wide[2 - a, 2 - b : 34 - b].reshape(512, 192)
        term = jnp.dot(window, w[k], preferred_element_type=F32)
        total = term if k == 0 else total + term
    partial[...] = total.astype(BF)


def coarse_back(own, xlo, xhi, weight):
    turned = jnp.swapaxes(weight, 1, 2).reshape(9, 192, 256)
    return call(
        coarse_back_kernel,
        (jax.ShapeDtypeStruct((512, 256), BF), jax.ShapeDtypeStruct((3, 34, 16, 192), BF)),
        [VMEM] * 4,
        flops=2 * 512 * 1728 * 256,
        moved=3 * 2**20,
    )(own, xlo, xhi, turned)


def coarse_weight_kernel(core, pooled, wide, terms, total):
    left = pooled[...].T
    for k in range(9):
        a, b = divmod(k, 3)
        window = wide[2 - a, 2 - b : 34 - b].reshape(512, 192)
        term = jnp.dot(left, window, preferred_element_type=F32)
        for c in range(3):
            at = (3 * k + c) * 256
            total[at : at + 256] = term[:, c * 64 : c * 64 + 64]
    me = core[0]
    for block in range(16):
        k, c = divmod(block, 2)
        at = block * 432
        upper = total[at : at + 224]
        lower = jnp.concatenate([total[at + 224 : at + 432], jnp.zeros((16, 64), F32)], axis=0)
        terms[lax.rem(me + c, 2), k] = jnp.concatenate([upper, lower], axis=1).astype(BF)


def coarse_weight(core, pooled, wide):
    return call(
        coarse_weight_kernel,
        jax.ShapeDtypeStruct((2, 8, 224, 128), BF),
        [SMEM, VMEM, VMEM],
        [pltpu.VMEM((6912, 64), F32)],
        flops=2 * 512 * 1728 * 256,
        moved=3 * 2**20,
    )(core, pooled, wide)


def coarse_forward_kernel(own, xlo, xhi, w, out, wide):
    for x, plane in enumerate((xlo, own, xhi)):
        wide[x] = along_depth(pad_rows(plane[...]), 1)
    total = None
    for k in range(9):
        a, b = divmod(k, 3)
        window = wide[a, b : b + 32].reshape(512, 768)
        term = jnp.dot(window, w[k], preferred_element_type=F32)
        total = term if k == 0 else total + term
    out[...] = total.astype(BF)


def coarse_forward(own, xlo, xhi, weight):
    return call(
        coarse_forward_kernel,
        jax.ShapeDtypeStruct((512, 64), BF),
        [VMEM] * 4,
        [pltpu.VMEM((3, 34, 16, 768), BF)],
        flops=2 * 512 * 6912 * 128,
        moved=3 * 2**20,
    )(own, xlo, xhi, weight.reshape(9, 768, 64))


def fine_sum_kernel(scale, parts, out):
    total = parts[0].astype(F32)
    for k in range(1, 64):
        total = total + parts[k].astype(F32)
    out[...] = total * scale


def coarse_sum_kernel(scale, parts, out):
    total = parts[0].astype(F32)
    for k in range(1, 8):
        total = total + parts[k].astype(F32)
    total = total * scale
    out[:224] = total[:, :64]
    out[224:] = total[:208, 64:]


def halo(block, axis, dim):
    count = lax.axis_size(axis)
    size = block.shape[dim]
    low = lax.slice_in_dim(block, 0, 1, axis=dim)
    high = lax.slice_in_dim(block, size - 1, size, axis=dim)
    return (
        lax.ppermute(high, axis, [(i, i + 1) for i in range(count - 1)]),
        lax.ppermute(low, axis, [(i + 1, i) for i in range(count - 1)]),
    )


def fine_halo(block):
    xlo, xhi = halo(block, SP, 0)
    low = jnp.concatenate([xlo[:, :1], block[:, :1], xhi[:, :1]], axis=0)
    high = jnp.concatenate([xlo[:, -1:], block[:, -1:], xhi[:, -1:]], axis=0)
    count = lax.axis_size(FL)
    ylo = lax.ppermute(high, FL, [(i, i + 1) for i in range(count - 1)])
    yhi = lax.ppermute(low, FL, [(i + 1, i) for i in range(count - 1)])
    return block, xlo, xhi, ylo[:, 0], yhi[:, 0]


def pair_sum(terms):
    arrived = lax.ppermute(terms[1], "c", [(0, 1), (1, 0)])
    return (terms[0].astype(F32) + arrived.astype(F32)).astype(BF)


def body(inputs, weight_fine, weight_coarse, cotangent):
    cells = 65536
    core = lax.axis_index("c").astype(jnp.int32).reshape(1)
    cot_lo, cot_hi = halo(cotangent, SP, 0)
    blocks = fine_halo(inputs)
    partial, wide_cot = coarse_back(cotangent, cot_lo, cot_hi, weight_coarse)
    pooled, slope = fine_forward(*blocks, weight_fine)
    sent = jnp.concatenate(
        [jnp.broadcast_to(pooled[None], (8, 64, 256)), partial.reshape(8, 64, 256)], axis=1
    )
    got = lax.all_to_all(sent, FL, 0, 0, tiled=True)
    turned = turn(*blocks)
    grad, terms = fine_weight(core, got[:, 64:], slope, turned)
    spread = lax.all_to_all(pair_sum(terms), ("x", "yh", "z", "yl"), 0, 0, tiled=True)

    gathered = got[:, :64].reshape(512, 256)
    coarse_terms = coarse_weight(core, gathered, wide_cot)
    coarse_spread = lax.all_to_all(pair_sum(coarse_terms), ("x", "yh"), 0, 0, tiled=True)
    grad_input = fine_back(*fine_halo(grad.reshape(2, 8, 32, 256)), weight_fine)
    slab = gathered.reshape(32, 16, 256)
    pool_lo, pool_hi = halo(slab[None], SP, 0)
    coarse_out = coarse_forward(slab, pool_lo[0], pool_hi[0], weight_coarse)
    grad_coarse = call(
        functools.partial(coarse_sum_kernel, 1.0 / math.sqrt(cells // 8)),
        jax.ShapeDtypeStruct((432, 64), F32),
        [VMEM],
    )(coarse_spread)
    grad_fine = call(
        functools.partial(fine_sum_kernel, 1.0 / math.sqrt(cells)),
        jax.ShapeDtypeStruct((54, 256), F32),
        [VMEM],
    )(spread)
    return (
        coarse_out.reshape(1, 32, 16, 64),
        grad_input.reshape(2, 8, 32, 256),
        grad_fine.reshape(-1),
        grad_coarse,
    )


def solution(mesh):
    fine_mesh = jax.sharding.Mesh(mesh.devices.reshape(4, 2, 2, 4, 2), SP + FL)
    return jax.shard_map(
        body,
        mesh=fine_mesh,
        in_specs=(P(SP, FL, None, None), P(), P(None, None, FL), P(SP, None, None, FL)),
        out_specs=(P(SP, None, None, FL), P(SP, FL, None, None), P(SP + FL), P(SP, FL)),
        check_vma=False,
    )
```

time: 402 us -> 151 us (0.38)
  the two profiles are of different devices: /device:TPU:1 before, /device:TPU:15 now
where the time goes in v2:
time: 151 us; the launch traced here: 150 us
  starting transfers between devices  62.5 us (41%)
  waiting for transfers between devices  30.9 us (20%)
  local copies, waits for them, and re-layouts  24.3 us (16%)
  Pallas kernels  23.8 us (16%)
  other arithmetic  7.49 us (5%)
    unnamed x37, local copies, waits for them, and re-layouts  22.1 us
    ppermute x4, starting transfers between devices, halo(): lax.ppermute(high, axis, [(i, i + 1) for i in range(count - 1)])  14.3 us
    ppermute x4, starting transfers between devices, halo(): lax.ppermute(low, axis, [(i + 1, i) for i in range(count - 1)])  11.6 us
    ppermute x4, waiting for transfers between devices, halo(): lax.ppermute(high, axis, [(i, i + 1) for i in range(count - 1)])  11 us
    all_to_all x1, starting transfers between devices, body(): lax.all_to_all(pair_sum(terms), ('x', 'yh', 'z', 'yl'), 0, 0, tiled=True)  8.68 us
    ppermute x2, starting transfers between devices, fine_halo(): ylo = lax.ppermute(high, FL, [(i, i + 1) for i in range(count - 1)])  8.34 us
    pallas_call x1, Pallas kernels, fine_back(): call(fine_back_kernel, jax.ShapeDtypeStruct((512, 256), BF), [VMEM] * 5 +...  8.03 us
    ppermute x4, waiting for transfers between devices, halo(): lax.ppermute(low, axis, [(i + 1, i) for i in range(count - 1)])  7.52 us
  transfers between devices with their start and end apart: 17, of which 8 were waited for; matrix products, arithmetic and copies ran while one was open for 8% of the time, Pallas kernels for 10%

profile of v2, /device:TPU:15, one launch (start us, length us, event | category | flops | bytes accessed | tf_op | source)
XLA Modules:
  0.0 150.0 jit_solution(17730700636290401769)
XLA Ops:
  0.6 4.6 %collective-permute-start.4 = (bf16[1,32,16,64]{3,2,1,0:T(8,128)(2,1)}, bf16[1,32,16,64]{3,2,1,0:T(8,128)(2,1)S(1)}, u32[]{:S(2)}, u32[]{:S(2)}) collective-permute-start(bf16[1,32,16,64]{3,2,1,0:T(8,128)(2,1)} %own.4), channel_id=1, source_target_pairs={{0,8},{8,16},{16,24},{24,32},{32,40},{40,48},{48,56},{56,64},{64,7... | collective-permute-start | bytes 196616 | tf_op jit(solution)/shard_map/ppermute | solution.py:297
  8.2 4.1 %collective-permute-start.1 = (bf16[1,8,32,256]{3,2,0,1:T(8,128)(2,1)S(1)}, bf16[1,8,32,256]{3,2,0,1:T(8,128)(2,1)S(1)}, u32[]{:S(2)}, u32[]{:S(2)}) collective-permute-start(bf16[1,8,32,256]{3,2,0,1:T(8,128)(2,1)S(1)} %get-tuple-element.36), channel_id=1, source_target_pairs={{8,0},{16,8},{24,16},{32,24},{40,32},{48,40},{56,48},{64,56},{72,6... | collective-permute-start | bytes 393224 | tf_op jit(solution)/shard_map/ppermute | solution.py:298
  12.3 2.9 %collective-permute-start = (bf16[1,8,32,256]{3,2,0,1:T(8,128)(2,1)S(1)}, bf16[1,8,32,256]{3,2,0,1:T(8,128)(2,1)S(1)}, u32[]{:S(2)}, u32[]{:S(2)}) collective-permute-start(bf16[1,8,32,256]{3,2,0,1:T(8,128)(2,1)S(1)} %get-tuple-element.37), channel_id=1, source_target_pairs={{0,8},{8,16},{16,24},{24,32},{32,40},{40,48},{48,56},{56,64},{64,7... | collective-permute-start | bytes 393224 | tf_op jit(solution)/shard_map/ppermute | solution.py:297
  17.2 4.3 %collective-permute-start.2 = (bf16[4,1,32,256]{3,2,0,1:T(8,128)(2,1)S(1)}, bf16[4,1,32,256]{3,2,0,1:T(8,128)(2,1)S(1)}, u32[]{:S(2)}, u32[]{:S(2)}) collective-permute-start(bf16[4,1,32,256]{3,2,0,1:T(8,128)(2,1)S(1)} %pad_maximum_fusion.1), channel_id=1, source_target_pairs={{0,1},{1,2},{2,3},{3,4},{4,5},{5,6},{6,7},{8,9},{9,10},{10,11},{11... | collective-permute-start | bytes 196616 | tf_op jit(solution)/shard_map/ppermute | solution.py:307
  29.9 6.2 %shard_map.75 = (bf16[64,256]{1,0:T(8,128)(2,1)S(1)}, f32[512,256]{1,0:T(8,128)S(1)}) custom-call(bf16[2,8,32,256]{3,2,1,0:T(8,128)(2,1)S(1)} %copy-done.4, bf16[1,8,32,256]{3,2,1,0:T(8,128)(2,1)S(1)} %bitcast.61, bf16[1,8,32,256]{3,2,1,0:T(8,128)(2,1)S(1)} %bitcast.59, bf16[4,32,256]{2,1,0:T(8,128)(2,1)S(1)} %bitcast.63, bf16[4,32,256]{2,1,0:T(8,128)(2,1)S(1)} %bitcast.65, ...), custom_call_target="tpu_custom_call" | custom-call | flops 1811939328 | bytes 5242880 | tf_op jit(solution)/shard_map/pallas_call | solution.py:86
  37.0 5.8 %all-to-all-start = ((bf16[8,128,256]{2,1,0:T(8,128)(2,1)}), bf16[8,128,256]{2,1,0:T(8,128)(2,1)S(1)}, u32[]{:S(2)}, u32[]{:S(2)}) async-start(bf16[8,128,256]{2,1,0:T(8,128)(2,1)} %pad_maximum_fusion), calls=%async_computation | async-start | bytes 1048576 | tf_op jit(solution)/shard_map/all_to_all | solution.py:327
  46.2 3.2 %all-to-all-done = bf16[8,128,256]{2,1,0:T(8,128)(2,1)S(1)} async-done(((bf16[8,128,256]{2,1,0:T(8,128)(2,1)}), bf16[8,128,256]{2,1,0:T(8,128)(2,1)S(1)}, u32[]{:S(2)}, u32[]{:S(2)}) %all-to-all-start) | async-done | bytes 524320 | tf_op jit(solution)/shard_map/all_to_all | solution.py:327
  49.5 2.3 %copy-done.1 = bf16[9,256,1024]{2,1,0:T(8,128)(2,1)S(1)} copy-done((bf16[9,256,1024]{2,1,0:T(8,128)(2,1)S(1)}, bf16[9,256,1024]{2,1,0:T(8,128)(2,1)}, u32[]{:S(2)}) %copy-start.1) | copy-done | bytes 4718616
  51.8 2.2 %shard_map.79 = (bf16[512,256]{1,0:T(8,128)(2,1)S(1)}, bf16[2,64,54,256]{3,2,1,0:T(8,128)(2,1)S(1)}) custom-call(s32[1]{0:T(128)} %bitcast.14.core, bf16[8,64,256]{2,1,0:T(8,128)(2,1)S(1)} %get-tuple-element.28.parts, f32[512,256]{1,0:T(8,128)S(1)} %get-tuple-element.12.slope, bf16[9,256,1024]{2,1,0:T(8,128)(2,1)S(1)} %copy-done.1), custom_call_target="tpu_custom_call" | custom-call | flops 1811939328 | bytes 9437184 | tf_op jit(solution)/shard_map/pallas_call | solution.py:155
  56.9 5.5 %collective-permute-start.12 = (bf16[64,54,256]{2,0,1:T(8,128)(2,1)S(1)}, bf16[64,54,256]{2,0,1:T(8,128)(2,1)}, u32[]{:S(2)}, u32[]{:S(2)}) collective-permute-start(bf16[64,54,256]{2,0,1:T(8,128)(2,1)S(1)} %copy.48), channel_id=1, source_target_pairs={{0,8},{8,0},{1,9},{9,1},{2,10},{10,2},{3,11},{11,3},{4,12},{12,4},... | collective-permute-start | bytes 5308424 | tf_op jit(solution)/shard_map/ppermute | solution.py:313
  63.7 2.7 %collective-permute-done.13 = bf16[8,224,128]{2,1,0:T(8,128)(2,1)S(1)} collective-permute-done((bf16[8,224,128]{2,1,0:T(8,128)(2,1)S(1)}, bf16[8,224,128]{2,1,0:T(8,128)(2,1)S(1)}, u32[]{:S(2)}, u32[]{:S(2)}) %collective-permute-start.13) | collective-permute-done | bytes 458784 | tf_op jit(solution)/shard_map/ppermute | solution.py:313
  67.3 4.4 %all-to-all-start.2 = ((bf16[8,224,128]{2,1,0:T(8,128)(2,1)}), bf16[8,224,128]{2,1,0:T(8,128)(2,1)S(1)}, u32[]{:S(2)}, u32[]{:S(2)}) async-start(bf16[8,224,128]{2,1,0:T(8,128)(2,1)} %fusion.1), calls=%async_computation.2 | async-start | bytes 917504 | tf_op jit(solution)/shard_map/all_to_all | solution.py:334
  71.8 4.4 %fusion = bf16[64,54,256]{2,1,0:T(8,128)(2,1)} fusion(bf16[64,54,256]{2,0,1:T(8,128)(2,1)} %collective-permute-done.12, bf16[2,64,54,256]{3,2,1,0:T(8,128)(2,1)} %copy-done.2), kind=kLoop, calls=%fused_computation.1 | loop fusion | flops 3538944 | bytes 5308416 | tf_op jit(solution)/shard_map/convert_element_type | solution.py:314
  76.2 2.6 %all-to-all-done.2.parts = bf16[8,224,128]{2,1,0:T(8,128)(2,1)S(1)} async-done(((bf16[8,224,128]{2,1,0:T(8,128)(2,1)}), bf16[8,224,128]{2,1,0:T(8,128)(2,1)S(1)}, u32[]{:S(2)}, u32[]{:S(2)}) %all-to-all-start.2) | async-done | bytes 458784 | tf_op jit(solution)/shard_map/all_to_all | solution.py:334
  78.7 8.7 %all-to-all-start.1 = ((bf16[64,54,256]{2,1,0:T(8,128)(2,1)}), bf16[64,54,256]{2,1,0:T(8,128)(2,1)S(1)}, u32[]{:S(2)}, u32[]{:S(2)}) async-start(bf16[64,54,256]{2,1,0:T(8,128)(2,1)} %fusion), calls=%async_computation.1 | async-start | bytes 3670016 | tf_op jit(solution)/shard_map/all_to_all | solution.py:330
  87.4 3.6 %collective-permute-start.7 = (bf16[1,32,16,256]{3,2,1,0:T(8,128)(2,1)S(1)}, bf16[1,32,16,256]{3,2,1,0:T(8,128)(2,1)}, u32[]{:S(2)}, u32[]{:S(2)}) collective-permute-start(bf16[1,32,16,256]{3,2,1,0:T(8,128)(2,1)S(1)} %bitcast.52), channel_id=1, source_target_pairs={{8,0},{16,8},{24,16},{32,24},{40,32},{48,40},{56,48},{64,56},{72,6... | collective-permute-start | bytes 786440 | tf_op jit(solution)/shard_map/ppermute | solution.py:298
  91.0 3.7 %collective-permute-start.6 = (bf16[1,32,16,256]{3,2,1,0:T(8,128)(2,1)S(1)}, bf16[1,32,16,256]{3,2,1,0:T(8,128)(2,1)}, u32[]{:S(2)}, u32[]{:S(2)}) collective-permute-start(bf16[1,32,16,256]{3,2,1,0:T(8,128)(2,1)S(1)} %bitcast.53), channel_id=1, source_target_pairs={{0,8},{8,16},{16,24},{24,32},{32,40},{40,48},{48,56},{56,64},{64,7... | collective-permute-start | bytes 786440 | tf_op jit(solution)/shard_map/ppermute | solution.py:297
  95.7 3.1 %collective-permute-start.8 = (bf16[1,8,32,256]{3,2,0,1:T(8,128)(2,1)S(1)}, bf16[1,8,32,256]{3,2,0,1:T(8,128)(2,1)S(1)}, u32[]{:S(2)}, u32[]{:S(2)}) collective-permute-start(bf16[1,8,32,256]{3,2,0,1:T(8,128)(2,1)S(1)} %bitcast.73), channel_id=1, source_target_pairs={{0,8},{8,16},{16,24},{24,32},{32,40},{40,48},{48,56},{56,64},{64,7... | collective-permute-start | bytes 393224 | tf_op jit(solution)/shard_map/ppermute | solution.py:297
  101.5 9.9 %collective-permute-done.8 = bf16[1,8,32,256]{3,2,0,1:T(8,128)(2,1)S(1)} collective-permute-done((bf16[1,8,32,256]{3,2,0,1:T(8,128)(2,1)S(1)}, bf16[1,8,32,256]{3,2,0,1:T(8,128)(2,1)S(1)}, u32[]{:S(2)}, u32[]{:S(2)}) %collective-permute-start.8) | collective-permute-done | bytes 131104 | tf_op jit(solution)/shard_map/ppermute | solution.py:297
  112.0 7.5 %collective-permute-done.9 = bf16[1,8,32,256]{3,2,0,1:T(8,128)(2,1)S(1)} collective-permute-done((bf16[1,8,32,256]{3,2,0,1:T(8,128)(2,1)S(1)}, bf16[1,8,32,256]{3,2,0,1:T(8,128)(2,1)S(1)}, u32[]{:S(2)}, u32[]{:S(2)}) %collective-permute-start.9) | collective-permute-done | bytes 131104 | tf_op jit(solution)/shard_map/ppermute | solution.py:298
  120.8 4.0 %collective-permute-start.10 = (bf16[4,1,32,256]{3,2,0,1:T(8,128)(2,1)}, bf16[4,1,32,256]{3,2,0,1:T(8,128)(2,1)S(1)}, u32[]{:S(2)}, u32[]{:S(2)}) collective-permute-start(bf16[4,1,32,256]{3,2,0,1:T(8,128)(2,1)} %pad_maximum_fusion.3), channel_id=1, source_target_pairs={{0,1},{1,2},{2,3},{3,4},{4,5},{5,6},{6,7},{8,9},{9,10},{10,11},{11... | collective-permute-start | bytes 196616 | tf_op jit(solution)/shard_map/ppermute | solution.py:307
  129.2 2.5 %collective-permute-done.11 = bf16[4,1,32,256]{3,2,0,1:T(8,128)(2,1)} collective-permute-done((bf16[4,1,32,256]{3,2,0,1:T(8,128)(2,1)}, bf16[4,1,32,256]{3,2,0,1:T(8,128)(2,1)}, u32[]{:S(2)}, u32[]{:S(2)}) %collective-permute-start.11) | collective-permute-done | bytes 65568 | tf_op jit(solution)/shard_map/ppermute | solution.py:308
  136.5 8.0 %shard_map.80 = bf16[512,256]{1,0:T(8,128)(2,1)} custom-call(bf16[2,8,32,256]{3,2,1,0:T(8,128)(2,1)S(1)} %bitcast.57, bf16[1,8,32,256]{3,2,1,0:T(8,128)(2,1)S(1)} %bitcast.67, bf16[1,8,32,256]{3,2,1,0:T(8,128)(2,1)S(1)} %bitcast.68, bf16[4,32,256]{2,1,0:T(8,128)(2,1)S(1)} %bitcast.71, bf16[4,32,256]{2,1,0:T(8,128)(2,1)} %bitcast.21.yhi, ...), custom_call_target="tpu_custom_call" | custom-call | flops 1811939328 | bytes 5242880 | tf_op jit(solution)/shard_map/pallas_call | solution.py:180
  144.5 3.7 %shard_map.77 = bf16[512,64]{1,0:T(8,128)(2,1)} custom-call(bf16[32,16,256]{2,1,0:T(8,128)(2,1)S(1)} %bitcast.54, bf16[32,16,256]{2,1,0:T(8,128)(2,1)} %bitcast.10.xlo, bf16[32,16,256]{2,1,0:T(8,128)(2,1)} %bitcast.11.xhi, bf16[9,768,64]{2,1,0:T(8,128)(2,1)S(1)} %bitcast.50), custom_call_target="tpu_custom_call" | custom-call | flops 905969664 | bytes 3145728 | tf_op jit(solution)/shard_map/pallas_call | solution.py:265
  (74 shorter events, 39.1 us)
Async XLA Ops:
  0.6 27.2 %copy-start.4 = (bf16[2,8,32,256]{3,2,1,0:T(8,128)(2,1)S(1)}, bf16[2,8,32,256]{3,2,1,0:T(8,128)(2,1)}, u32[]{:S(2)}) copy-start(bf16[2,8,32,256]{3,2,1,0:T(8,128)(2,1)} %own.5) | copy-start | bytes 786436
  0.6 22.9 %collective-permute-start.4 = (bf16[1,32,16,64]{3,2,1,0:T(8,128)(2,1)}, bf16[1,32,16,64]{3,2,1,0:T(8,128)(2,1)S(1)}, u32[]{:S(2)}, u32[]{:S(2)}) collective-permute-start(bf16[1,32,16,64]{3,2,1,0:T(8,128)(2,1)} %own.4), channel_id=1, source_target_pairs={{0,8},{8,16},{16,24},{24,32},{32,40},{40,48},{48,56},{56,64},{64,7... | collective-permute-start | bytes 196616 | tf_op jit(solution)/shard_map/ppermute | solution.py:297
  5.3 18.2 %collective-permute-start.5 = (bf16[1,32,16,64]{3,2,1,0:T(8,128)(2,1)}, bf16[1,32,16,64]{3,2,1,0:T(8,128)(2,1)S(1)}, u32[]{:S(2)}, u32[]{:S(2)}) collective-permute-start(bf16[1,32,16,64]{3,2,1,0:T(8,128)(2,1)} %own.4), channel_id=1, source_target_pairs={{8,0},{16,8},{24,16},{32,24},{40,32},{48,40},{56,48},{64,56},{72,6... | collective-permute-start | bytes 196616 | tf_op jit(solution)/shard_map/ppermute | solution.py:298
  8.2 7.9 %collective-permute-start.1 = (bf16[1,8,32,256]{3,2,0,1:T(8,128)(2,1)S(1)}, bf16[1,8,32,256]{3,2,0,1:T(8,128)(2,1)S(1)}, u32[]{:S(2)}, u32[]{:S(2)}) collective-permute-start(bf16[1,8,32,256]{3,2,0,1:T(8,128)(2,1)S(1)} %get-tuple-element.36), channel_id=1, source_target_pairs={{8,0},{16,8},{24,16},{32,24},{40,32},{48,40},{56,48},{64,56},{72,6... | collective-permute-start | bytes 393224 | tf_op jit(solution)/shard_map/ppermute | solution.py:298
  12.3 4.9 %collective-permute-start = (bf16[1,8,32,256]{3,2,0,1:T(8,128)(2,1)S(1)}, bf16[1,8,32,256]{3,2,0,1:T(8,128)(2,1)S(1)}, u32[]{:S(2)}, u32[]{:S(2)}) collective-permute-start(bf16[1,8,32,256]{3,2,0,1:T(8,128)(2,1)S(1)} %get-tuple-element.37), channel_id=1, source_target_pairs={{0,8},{8,16},{16,24},{24,32},{32,40},{40,48},{48,56},{56,64},{64,7... | collective-permute-start | bytes 393224 | tf_op jit(solution)/shard_map/ppermute | solution.py:297
  17.2 9.2 %collective-permute-start.2 = (bf16[4,1,32,256]{3,2,0,1:T(8,128)(2,1)S(1)}, bf16[4,1,32,256]{3,2,0,1:T(8,128)(2,1)S(1)}, u32[]{:S(2)}, u32[]{:S(2)}) collective-permute-start(bf16[4,1,32,256]{3,2,0,1:T(8,128)(2,1)S(1)} %pad_maximum_fusion.1), channel_id=1, source_target_pairs={{0,1},{1,2},{2,3},{3,4},{4,5},{5,6},{6,7},{8,9},{9,10},{10,11},{11... | collective-permute-start | bytes 196616 | tf_op jit(solution)/shard_map/ppermute | solution.py:307
  21.6 6.3 %collective-permute-start.3 = (bf16[4,1,32,256]{3,2,0,1:T(8,128)(2,1)S(1)}, bf16[4,1,32,256]{3,2,0,1:T(8,128)(2,1)S(1)}, u32[]{:S(2)}, u32[]{:S(2)}) collective-permute-start(bf16[4,1,32,256]{3,2,0,1:T(8,128)(2,1)S(1)} %pad_maximum_fusion.2), channel_id=1, source_target_pairs={{1,0},{2,1},{3,2},{4,3},{5,4},{6,5},{7,6},{9,8},{10,9},{11,10},{12... | collective-permute-start | bytes 196616 | tf_op jit(solution)/shard_map/ppermute | solution.py:308
  27.9 2.0 %copy-start.13 = (bf16[27,256,256]{2,1,0:T(8,128)(2,1)S(1)}, bf16[27,256,256]{2,1,0:T(8,128)(2,1)}, u32[]{:S(2)}) copy-start(bf16[27,256,256]{2,1,0:T(8,128)(2,1)} %param.5) | copy-start | bytes 10616836
  37.0 12.4 %all-to-all-start = ((bf16[8,128,256]{2,1,0:T(8,128)(2,1)}), bf16[8,128,256]{2,1,0:T(8,128)(2,1)S(1)}, u32[]{:S(2)}, u32[]{:S(2)}) async-start(bf16[8,128,256]{2,1,0:T(8,128)(2,1)} %pad_maximum_fusion), calls=%async_computation | async-start | bytes 1048576 | tf_op jit(solution)/shard_map/all_to_all | solution.py:327
  44.1 2.2 %copy-start = (bf16[9,256,1024]{2,1,0:T(8,128)(2,1)}, bf16[9,256,1024]{2,1,0:T(8,128)(2,1)S(1)}, u32[]{:S(2)}) copy-start(bf16[9,256,1024]{2,1,0:T(8,128)(2,1)S(1)} %shard_map.78.turned) | copy-start | bytes 14155780
  49.4 2.3 %copy-start.1 = (bf16[9,256,1024]{2,1,0:T(8,128)(2,1)S(1)}, bf16[9,256,1024]{2,1,0:T(8,128)(2,1)}, u32[]{:S(2)}) copy-start(bf16[9,256,1024]{2,1,0:T(8,128)(2,1)} %copy-done) | copy-start | bytes 14155780
  56.9 14.9 %collective-permute-start.12 = (bf16[64,54,256]{2,0,1:T(8,128)(2,1)S(1)}, bf16[64,54,256]{2,0,1:T(8,128)(2,1)}, u32[]{:S(2)}, u32[]{:S(2)}) collective-permute-start(bf16[64,54,256]{2,0,1:T(8,128)(2,1)S(1)} %copy.48), channel_id=1, source_target_pairs={{0,8},{8,0},{1,9},{9,1},{2,10},{10,2},{3,11},{11,3},{4,12},{12,4},... | collective-permute-start | bytes 5308424 | tf_op jit(solution)/shard_map/ppermute | solution.py:313
  63.6 2.8 %collective-permute-start.13 = (bf16[8,224,128]{2,1,0:T(8,128)(2,1)S(1)}, bf16[8,224,128]{2,1,0:T(8,128)(2,1)S(1)}, u32[]{:S(2)}, u32[]{:S(2)}) collective-permute-start(bf16[8,224,128]{2,1,0:T(8,128)(2,1)S(1)} %slice_bitcast_fusion.1), channel_id=1, source_target_pairs={{0,8},{8,0},{1,9},{9,1},{2,10},{10,2},{3,11},{11,3},{4,12},{12,4},... | collective-permute-start | bytes 1376264 | tf_op jit(solution)/shard_map/ppermute | solution.py:313
  67.3 11.4 %all-to-all-start.2 = ((bf16[8,224,128]{2,1,0:T(8,128)(2,1)}), bf16[8,224,128]{2,1,0:T(8,128)(2,1)S(1)}, u32[]{:S(2)}, u32[]{:S(2)}) async-start(bf16[8,224,128]{2,1,0:T(8,128)(2,1)} %fusion.1), calls=%async_computation.2 | async-start | bytes 917504 | tf_op jit(solution)/shard_map/all_to_all | solution.py:334
  76.2 51.2 %copy-start.6 = (bf16[27,256,64]{1,2,0:T(8,128)(2,1)S(1)}, bf16[27,256,64]{1,2,0:T(8,128)(2,1)}, u32[]{:S(2)}) copy-start(bf16[27,256,64]{1,2,0:T(8,128)(2,1)} %param.6) | copy-start | bytes 2654212
  78.7 70.4 %all-to-all-start.1 = ((bf16[64,54,256]{2,1,0:T(8,128)(2,1)}), bf16[64,54,256]{2,1,0:T(8,128)(2,1)S(1)}, u32[]{:S(2)}, u32[]{:S(2)}) async-start(bf16[64,54,256]{2,1,0:T(8,128)(2,1)} %fusion), calls=%async_computation.1 | async-start | bytes 3670016 | tf_op jit(solution)/shard_map/all_to_all | solution.py:330
  87.4 57.1 %collective-permute-start.7 = (bf16[1,32,16,256]{3,2,1,0:T(8,128)(2,1)S(1)}, bf16[1,32,16,256]{3,2,1,0:T(8,128)(2,1)}, u32[]{:S(2)}, u32[]{:S(2)}) collective-permute-start(bf16[1,32,16,256]{3,2,1,0:T(8,128)(2,1)S(1)} %bitcast.52), channel_id=1, source_target_pairs={{8,0},{16,8},{24,16},{32,24},{40,32},{48,40},{56,48},{64,56},{72,6... | collective-permute-start | bytes 786440 | tf_op jit(solution)/shard_map/ppermute | solution.py:298
  91.0 53.5 %collective-permute-start.6 = (bf16[1,32,16,256]{3,2,1,0:T(8,128)(2,1)S(1)}, bf16[1,32,16,256]{3,2,1,0:T(8,128)(2,1)}, u32[]{:S(2)}, u32[]{:S(2)}) collective-permute-start(bf16[1,32,16,256]{3,2,1,0:T(8,128)(2,1)S(1)} %bitcast.53), channel_id=1, source_target_pairs={{0,8},{8,16},{16,24},{24,32},{32,40},{40,48},{48,56},{56,64},{64,7... | collective-permute-start | bytes 786440 | tf_op jit(solution)/shard_map/ppermute | solution.py:297
  95.7 15.7 %collective-permute-start.8 = (bf16[1,8,32,256]{3,2,0,1:T(8,128)(2,1)S(1)}, bf16[1,8,32,256]{3,2,0,1:T(8,128)(2,1)S(1)}, u32[]{:S(2)}, u32[]{:S(2)}) collective-permute-start(bf16[1,8,32,256]{3,2,0,1:T(8,128)(2,1)S(1)} %bitcast.73), channel_id=1, source_target_pairs={{0,8},{8,16},{16,24},{24,32},{32,40},{40,48},{48,56},{56,64},{64,7... | collective-permute-start | bytes 393224 | tf_op jit(solution)/shard_map/ppermute | solution.py:297
  98.8 20.8 %collective-permute-start.9 = (bf16[1,8,32,256]{3,2,0,1:T(8,128)(2,1)S(1)}, bf16[1,8,32,256]{3,2,0,1:T(8,128)(2,1)S(1)}, u32[]{:S(2)}, u32[]{:S(2)}) collective-permute-start(bf16[1,8,32,256]{3,2,0,1:T(8,128)(2,1)S(1)} %bitcast.72), channel_id=1, source_target_pairs={{8,0},{16,8},{24,16},{32,24},{40,32},{48,40},{56,48},{64,56},{72,6... | collective-permute-start | bytes 393224 | tf_op jit(solution)/shard_map/ppermute | solution.py:298
  120.8 8.3 %collective-permute-start.10 = (bf16[4,1,32,256]{3,2,0,1:T(8,128)(2,1)}, bf16[4,1,32,256]{3,2,0,1:T(8,128)(2,1)S(1)}, u32[]{:S(2)}, u32[]{:S(2)}) collective-permute-start(bf16[4,1,32,256]{3,2,0,1:T(8,128)(2,1)} %pad_maximum_fusion.3), channel_id=1, source_target_pairs={{0,1},{1,2},{2,3},{3,4},{4,5},{5,6},{6,7},{8,9},{9,10},{10,11},{11... | collective-permute-start | bytes 196616 | tf_op jit(solution)/shard_map/ppermute | solution.py:307
  125.5 6.2 %collective-permute-start.11 = (bf16[4,1,32,256]{3,2,0,1:T(8,128)(2,1)}, bf16[4,1,32,256]{3,2,0,1:T(8,128)(2,1)}, u32[]{:S(2)}, u32[]{:S(2)}) collective-permute-start(bf16[4,1,32,256]{3,2,0,1:T(8,128)(2,1)} %pad_maximum_fusion.4), channel_id=1, source_target_pairs={{1,0},{2,1},{3,2},{4,3},{5,4},{6,5},{7,6},{9,8},{10,9},{11,10},{12... | collective-permute-start | bytes 196616 | tf_op jit(solution)/shard_map/ppermute | solution.py:308
  134.4 2.0 %copy-start.14 = (bf16[27,256,256]{2,1,0:T(8,128)(2,1)S(1)}, bf16[27,256,256]{2,1,0:T(8,128)(2,1)}, u32[]{:S(2)}) copy-start(bf16[27,256,256]{2,1,0:T(8,128)(2,1)} %param.5) | copy-start | bytes 10616836
  136.4 8.1 %copy-start.3 = (bf16[27,256,64]{2,1,0:T(8,128)(2,1)S(1)}, bf16[27,256,64]{2,1,0:T(8,128)(2,1)}, u32[]{:S(2)}) copy-start(bf16[27,256,64]{2,1,0:T(8,128)(2,1)} %copy.41) | copy-start | bytes 2654212
  (9 other events, 8.6 us)

commit v3 on v2

v3 whole, which is shorter than its diff:
```python
import functools
import math

import jax
import jax.numpy as jnp
from jax import lax
from jax.experimental import pallas as pl
from jax.experimental.pallas import tpu as pltpu
from jax.sharding import PartitionSpec as P

SP = ("x", "yh", "c")
FL = ("z", "yl")
BF = jnp.bfloat16
F32 = jnp.float32
VMEM = pl.BlockSpec(memory_space=pltpu.VMEM)
SMEM = pl.BlockSpec(memory_space=pltpu.SMEM)
SWAP = [(0, 1), (1, 0)]


def call(kernel, out_shape, in_specs, scratch=(), limit=12, flops=2**20):
    return pl.pallas_call(
        kernel,
        out_shape=out_shape,
        in_specs=in_specs,
        out_specs=jax.tree.map(lambda _: VMEM, out_shape),
        scratch_shapes=list(scratch),
        compiler_params=pltpu.CompilerParams(vmem_limit_bytes=limit * 2**20),
        cost_estimate=pl.CostEstimate(flops=flops, bytes_accessed=2**16, transcendentals=0),
    )


def array(*shape, dtype=BF):
    return jax.ShapeDtypeStruct(shape, dtype)


def along_depth(rows, order):
    count, depth, width = rows.shape
    flat = rows.astype(F32).reshape(count * depth, width)
    place = lax.broadcasted_iota(jnp.int32, flat.shape, 0) & (depth - 1)
    before = jnp.where(place == 0, 0.0, pltpu.roll(flat, 1, 0)).astype(BF)
    after = jnp.where(place == depth - 1, 0.0, pltpu.roll(flat, count * depth - 1, 0)).astype(BF)
    middle = flat.astype(BF)
    trio = (before, middle, after) if order > 0 else (after, middle, before)
    return jnp.concatenate(trio, axis=1).reshape(count, depth, 3 * width)


def pad_rows(plane):
    edge = jnp.zeros((1,) + plane.shape[1:], plane.dtype)
    return jnp.concatenate([edge, plane, edge], axis=0)


def unpacked(block):
    strips = [block[:, 64 * k : 64 * k + 64] for k in range(4)]
    return jnp.concatenate(strips, axis=0).reshape(32, 16, 64)


def pack_kernel(own, cot, up, down):
    flat = cot[0].reshape(512, 64)
    packed = jnp.concatenate([flat[128 * k : 128 * k + 128] for k in range(4)], axis=1)
    up[:256] = own[1].reshape(256, 256)
    down[:256] = own[0].reshape(256, 256)
    up[256:] = packed
    down[256:] = packed


def plane_of(own, lo, hi, x):
    if x == 0 or x == 3:
        return (lo if x == 0 else hi)[:256].reshape(8, 32, 256)
    return own[x - 1]


def edge_kernel(own, lo, hi, low, high):
    for x in range(4):
        plane = plane_of(own, lo, hi, x)
        low[32 * x : 32 * x + 32] = plane[0]
        high[32 * x : 32 * x + 32] = plane[7]


def whole_plane(own, lo, hi, ylo, yhi, x):
    rows = slice(32 * x, 32 * x + 32)
    return jnp.concatenate([ylo[rows][None], plane_of(own, lo, hi, x), yhi[rows][None]], axis=0)


def coarse_back_kernel(cot, lo, hi, w, partial, wide):
    planes = (unpacked(lo[256:384]), cot[0], unpacked(hi[256:384]))
    for x in range(3):
        wide[x] = along_depth(pad_rows(planes[x]), -1)
    total = None
    for k in range(9):
        a, b = divmod(k, 3)
        window = wide[2 - a, 2 - b : 34 - b].reshape(512, 192)
        term = jnp.dot(window, w[k], preferred_element_type=F32)
        total = term if k == 0 else total + term
    partial[...] = total.astype(BF)


def fine_forward_kernel(place, own, lo, hi, ylo, yhi, w, pooled, slope, far, wide, pre, sums):
    for x in range(4):
        plane = whole_plane(own, lo, hi, ylo, yhi, x)
        wide[x] = along_depth(plane, 1)

        @pl.when(place[0] == x // 2)
        def _():
            far[320 * (x % 2) : 320 * (x % 2) + 320] = plane.reshape(320, 256)

    far[640:] = jnp.where(place[0] == 0, lo[256:384], hi[256:384])
    for k in range(9):
        a, b = divmod(k, 3)
        window = wide[a : a + 2, b : b + 8].reshape(512, 768)
        term = jnp.dot(window, w[k], preferred_element_type=F32)
        pre[...] = term if k == 0 else pre[...] + term
    for y in range(4):
        total = jnp.zeros((32, 256), F32)
        for x in range(2):
            for half in range(2):
                at = x * 256 + (2 * y + half) * 32
                value = pre[at : at + 32]
                sigma = 1.0 / (1.0 + jnp.exp(-value))
                total = total + (value * sigma).astype(BF).astype(F32)
                slope[at : at + 32] = 0.125 * sigma * (1.0 + value * (1.0 - sigma))
        sums[0, y * 32 : y * 32 + 32] = total[:, :128]
        sums[1, y * 32 : y * 32 + 32] = total[:, 128:]
    for side in range(2):
        even = sums[side, pl.ds(0, 64, stride=2)]
        odd = sums[side, pl.ds(1, 64, stride=2)]
        pooled[:, side * 128 : side * 128 + 128] = ((even + odd) * 0.125).astype(BF)


def fine_grad_kernel(place, parts, slope, pooled, grad, sent, spread):
    summed = parts[0].astype(F32)
    for k in range(1, 8):
        summed = summed + parts[k].astype(F32)
    summed = summed.astype(BF).astype(F32)
    for side in range(2):
        half = summed[:, side * 128 : side * 128 + 128]
        spread[side, pl.ds(0, 64, stride=2)] = half
        spread[side, pl.ds(1, 64, stride=2)] = half
    for y in range(4):
        wide = jnp.concatenate([spread[0, y * 32 : y * 32 + 32], spread[1, y * 32 : y * 32 + 32]], axis=1)
        for x in range(2):
            for half in range(2):
                at = x * 256 + (2 * y + half) * 32
                grad[at : at + 32] = (wide * slope[at : at + 32]).astype(BF)
    low = jnp.concatenate([grad[0:32], grad[256:288]], axis=0)
    high = jnp.concatenate([grad[224:256], grad[480:512]], axis=0)
    for k in range(8):
        sent[k, :64] = pooled[...]
        sent[k, 64:] = jnp.where(k < place[3], low, high)


def fine_weight_kernel(
    place, own, lo, hi, ylo, yhi, far, grad, other, terms, wide, turned, total
):
    for core in range(2):

        @pl.when(place[0] == core)
        def _():
            planes, windows = set(), set()

            def prepare(bc, slot):
                if (bc, slot) in windows:
                    return
                windows.add((bc, slot))
                if slot not in planes:
                    planes.add(slot)
                    x = slot - 2 * core
                    if 0 <= x < 4:
                        rows = whole_plane(own, lo, hi, ylo, yhi, x)
                    else:
                        at = 320 * (slot % 2)
                        rows = far[at : at + 320].reshape(10, 32, 256)
                    wide[slot] = along_depth(rows, 1)
                b, c = divmod(bc, 3)
                window = wide[slot, b : b + 8, :, c * 256 : c * 256 + 256]
                turned[bc, slot] = window.reshape(256, 256).T

            pair = (grad, other) if core == 0 else (other, grad)
            right = jnp.concatenate([pair[0][...], pair[1][...]], axis=0)
            for k in range(8):
                at = 432 * (2 * k + core)
                end = at + 432
                pieces = []
                while at < end:
                    tap, low = divmod(at, 256)
                    high = min(256, low + end - at)
                    a, bc = divmod(tap, 9)
                    for plane in range(4):
                        prepare(bc, a + plane)
                    strips = [turned[bc, a + plane, low:high] for plane in range(4)]
                    pieces.append(jnp.concatenate(strips, axis=1))
                    at += high - low
                left = jnp.concatenate(pieces, axis=0)
                total[k % 2] = jnp.dot(left, right, preferred_element_type=F32)
                for f in range(8):
                    terms[k * 8 + f] = total[k % 2, f * 54 : f * 54 + 54].astype(BF)


def grad_plane(place, grad, got, x):
    below = got[jnp.maximum(place[3] - 1, 0), 64 + 32 * x : 96 + 32 * x]
    above = got[jnp.minimum(place[3] + 1, 7), 64 + 32 * x : 96 + 32 * x]
    below = jnp.where(place[3] > 0, below, jnp.zeros_like(below))
    above = jnp.where(place[3] < 7, above, jnp.zeros_like(above))
    middle = grad[256 * x : 256 * x + 256].reshape(8, 32, 256)
    return jnp.concatenate([below[None], middle, above[None]], axis=0)


def ship_kernel(place, grad, got, up, down, slab):
    down[:320] = grad_plane(place, grad, got, 0).reshape(320, 256)
    up[:320] = grad_plane(place, grad, got, 1).reshape(320, 256)
    for k in range(8):
        up[320 + 64 * k : 384 + 64 * k] = got[k, :64]
        down[320 + 64 * k : 384 + 64 * k] = got[k, :64]
        slab[64 * k : 64 * k + 64] = got[k, :64]


def fine_back_kernel(up, down, lo, hi, w, out, wide, total):
    for x, plane in enumerate((lo, down, up, hi)):
        wide[x] = along_depth(plane[:320].reshape(10, 32, 256), -1)
    for k in range(9):
        a, b = divmod(k, 3)
        window = wide[2 - a : 4 - a, 2 - b : 10 - b].reshape(512, 768)
        right = jnp.concatenate([w[k, 0], w[k, 1], w[k, 2]], axis=1)
        term = lax.dot_general(window, right, (((1,), (1,)), ((), ())), preferred_element_type=F32)
        total[...] = term if k == 0 else total[...] + term
    out[...] = total[...].astype(BF)


def coarse_weight_kernel(place, slab, other, wide, far, terms, outer, total):
    outer[...] = along_depth(pad_rows(unpacked(far[640:768])), -1)
    left = jnp.concatenate([slab[...].T, other[...].T], axis=1)
    for core in range(2):

        @pl.when(place[0] == core)
        def _():
            for k in range(9):
                a, b = divmod(k, 3)
                rows = slice(2 - b, 34 - b)
                at = 2 - a + (1 if core == 0 else -1)
                across = wide[at, rows] if 0 <= at < 3 else outer[rows]
                right = jnp.concatenate(
                    [wide[2 - a, rows].reshape(512, 192), across.reshape(512, 192)], axis=0
                )
                term = jnp.dot(left, right, preferred_element_type=F32)
                for c in range(3):
                    row = (3 * k + c) * 256
                    total[row : row + 256] = term[:, c * 64 : c * 64 + 64]
            for block in range(8):
                x, yh = divmod(block, 2)
                row = (2 * block + core) * 432
                upper = total[row : row + 224]
                lower = jnp.concatenate(
                    [total[row + 224 : row + 432], jnp.zeros((16, 64), F32)], axis=0
                )
                at = lax.rem(4 + x - place[2], 4) * 2 + lax.rem(place[1] + yh, 2)
                terms[at] = jnp.concatenate([upper, lower], axis=1).astype(BF)


def coarse_forward_kernel(slab, lo, hi, w, out, wide):
    for x, plane in enumerate((lo, slab, hi)):
        wide[x] = along_depth(pad_rows(plane[320:832].reshape(32, 16, 256)), 1)
    total = None
    for k in range(9):
        a, b = divmod(k, 3)
        window = wide[a, b : b + 32].reshape(512, 768)
        turned = w[k].T
        right = jnp.concatenate([turned[:, 64 * c : 64 * c + 64] for c in range(3)], axis=0)
        term = jnp.dot(window, right, preferred_element_type=F32)
        total = term if k == 0 else total + term
    out[...] = total.astype(BF)


def fine_sum_kernel(scale, parts, out):
    total = parts[0].astype(F32)
    for k in range(1, 64):
        total = total + parts[k].astype(F32)
    total = total * scale
    out[pl.ds(0, 54, stride=2)] = total[:, :128]
    out[pl.ds(1, 54, stride=2)] = total[:, 128:]


def quad_kernel(own, first, second, third, out):
    total = own[...].astype(F32) + first[...].astype(F32)
    total = total + second[...].astype(F32) + third[...].astype(F32)
    out[...] = total.astype(BF)


def coarse_sum_kernel(scale, own, other, out):
    total = own[:224].astype(F32) + other[...].astype(F32)
    total = total * scale
    out[...] = jnp.concatenate([total[:, :64], total[:208, 64:]], axis=0).T


def swap_sides(up, down, axis):
    steps = range(lax.axis_size(axis) - 1)
    return (
        lax.ppermute(up, axis, [(i, i + 1) for i in steps]),
        lax.ppermute(down, axis, [(i + 1, i) for i in steps]),
    )


def body(inputs, weight_fine, weight_coarse, cotangent):
    cells = 65536
    place = [lax.axis_index(name) for name in ("c", "yh", "x", FL)]
    place = jnp.stack(place).astype(jnp.int32)
    turned_coarse = jnp.swapaxes(weight_coarse, 1, 2).reshape(9, 192, 256)

    pack = call(pack_kernel, (array(384, 256), array(384, 256)), [VMEM] * 2, limit=60)
    lo, hi = swap_sides(*pack(inputs, cotangent), SP)
    edge = call(edge_kernel, (array(128, 256), array(128, 256)), [VMEM] * 3)
    low, high = edge(inputs, lo, hi)
    ylo, yhi = swap_sides(high, low, FL)
    partial, wide_cot = call(
        coarse_back_kernel,
        (array(512, 256), array(3, 34, 16, 192)),
        [VMEM] * 4,
        limit=60,
    )(cotangent, lo, hi, turned_coarse)
    parts = lax.all_to_all(partial.reshape(8, 64, 256), FL, 0, 0, tiled=True)
    parts, ylo, yhi = lax.optimization_barrier((parts, ylo, yhi))
    blocks = (inputs, lo, hi, ylo, yhi)
    pooled, slope, far = call(
        fine_forward_kernel,
        (array(64, 256), array(512, 256, dtype=F32), array(768, 256)),
        [SMEM] + [VMEM] * 6,
        [
            pltpu.VMEM((4, 10, 32, 768), BF),
            pltpu.VMEM((512, 256), F32),
            pltpu.VMEM((2, 128, 128), F32),
        ],
    )(place, *blocks, weight_fine.reshape(9, 768, 256))
    grad, sent = call(
        fine_grad_kernel,
        (array(512, 256), array(8, 128, 256)),
        [SMEM] + [VMEM] * 3,
        [pltpu.VMEM((2, 128, 128), F32)],
    )(place, parts, slope, pooled)
    far = lax.ppermute(far, "c", SWAP)
    got = lax.all_to_all(sent, FL, 0, 0, tiled=True)
    terms = call(
        fine_weight_kernel,
        array(64, 54, 256),
        [SMEM] + [VMEM] * 8,
        [
            pltpu.VMEM((6, 10, 32, 768), BF),
            pltpu.VMEM((9, 6, 256, 256), BF),
            pltpu.VMEM((2, 432, 256), F32),
        ],
        limit=24,
    )(place, *blocks, far, grad, lax.ppermute(grad, "c", SWAP))
    terms, got = lax.optimization_barrier((terms, got))
    shapes = (array(832, 256), array(832, 256), array(512, 256))
    up, down, slab = call(ship_kernel, shapes, [SMEM] + [VMEM] * 2)(place, grad, got)
    terms, up, down, slab = lax.optimization_barrier((terms, up, down, slab))
    across = lax.ppermute(slab, "c", SWAP)
    lo, hi = swap_sides(up, down, SP)
    spread = lax.all_to_all(terms, ("x", "yh", "z", "yl"), 0, 0, tiled=True)

    coarse_terms = call(
        coarse_weight_kernel,
        array(8, 224, 128),
        [SMEM] + [VMEM] * 4,
        [pltpu.VMEM((34, 16, 192), BF), pltpu.VMEM((6912, 64), F32)],
    )(place, slab, across, wide_cot, far)
    coarse_terms = coarse_terms.reshape(4, 448, 128)
    arrived = [
        lax.ppermute(coarse_terms[step], "x", [(i, (i + step) % 4) for i in range(4)])
        for step in range(1, 4)
    ]
    coarse_terms = call(quad_kernel, array(448, 128), [VMEM] * 4)(coarse_terms[0], *arrived)
    arrived = lax.ppermute(coarse_terms[224:], "yh", SWAP)
    grad_input = call(
        fine_back_kernel,
        array(512, 256),
        [VMEM] * 5,
        [pltpu.VMEM((4, 10, 32, 768), BF), pltpu.VMEM((512, 256), F32)],
        flops=2**31,
    )(up, down, lo, hi, weight_fine.reshape(9, 3, 256, 256))
    coarse_out = call(
        coarse_forward_kernel,
        array(512, 64),
        [VMEM] * 4,
        [pltpu.VMEM((3, 34, 16, 768), BF)],
        flops=2**31,
    )(up, lo, hi, turned_coarse)
    grad_coarse = call(
        functools.partial(coarse_sum_kernel, 1.0 / math.sqrt(cells // 8)),
        array(64, 432, dtype=F32),
        [VMEM] * 2,
    )(coarse_terms, arrived)
    grad_fine = call(
        functools.partial(fine_sum_kernel, 1.0 / math.sqrt(cells)),
        array(108, 128, dtype=F32),
        [VMEM],
    )(spread)
    return (
        coarse_out.reshape(1, 32, 16, 64),
        grad_input.reshape(2, 8, 32, 256),
        grad_fine.reshape(-1),
        grad_coarse.T,
    )


def solution(mesh):
    fine_mesh = jax.sharding.Mesh(mesh.devices.reshape(4, 2, 2, 4, 2), SP + FL)
    return jax.shard_map(
        body,
        mesh=fine_mesh,
        in_specs=(P(SP, FL, None, None), P(), P(None, None, FL), P(SP, None, None, FL)),
        out_specs=(P(SP, None, None, FL), P(SP, FL, None, None), P(SP + FL), P(SP, FL)),
        check_vma=False,
    )
```

time: 151 us -> 114 us (0.75)
  the two profiles are of different devices: /device:TPU:15 before, /device:TPU:1 now
where the time goes in v3:
time: 114 us; the launch traced here: 113 us
  starting transfers between devices  53.3 us (47%)
  waiting for transfers between devices  26.4 us (23%)
  Pallas kernels  23 us (20%)
  local copies, waits for them, and re-layouts  9.22 us (8%)
    ppermute x3, starting transfers between devices, swap_sides(): lax.ppermute(up, axis, [(i, i + 1) for i in steps])  14.2 us
    ppermute x3, waiting for transfers between devices, body(): lax.ppermute(coarse_terms[step], 'x', [(i, (i + step) % 4) for i in range...  12.8 us
    all_to_all x1, starting transfers between devices, body(): spread = lax.all_to_all(terms, ('x', 'yh', 'z', 'yl'), 0, 0, tiled=True)  10.8 us
    ppermute x3, waiting for transfers between devices, swap_sides(): lax.ppermute(down, axis, [(i + 1, i) for i in steps])  9.42 us
    unnamed x36, local copies, waits for them, and re-layouts  9.18 us
    ppermute x1, starting transfers between devices, body(): arrived = lax.ppermute(coarse_terms[224:], 'yh', SWAP)  6.64 us
    all_to_all x1, starting transfers between devices, body(): got = lax.all_to_all(sent, FL, 0, 0, tiled=True)  5.47 us
    all_to_all x1, starting transfers between devices, body(): parts = lax.all_to_all(partial.reshape(8, 64, 256), FL, 0, 0, tiled=True)  5.15 us
  transfers between devices with their start and end apart: 16, of which 8 were waited for; matrix products, arithmetic and copies ran while one was open for 0% of the time, Pallas kernels for 11%

profile of v3, /device:TPU:1, one launch (start us, length us, event | category | flops | bytes accessed | tf_op | source)
XLA Modules:
  0.0 112.8 jit_solution(11850697484829535293)
XLA Ops:
  0.6 1.9 %shard_map.75 = (bf16[384,256]{1,0:T(8,128)(2,1)}, bf16[384,256]{1,0:T(8,128)(2,1)}) custom-call(bf16[2,8,32,256]{3,2,1,0:T(8,128)(2,1)} %own.7, bf16[1,32,16,64]{3,2,1,0:T(8,128)(2,1)} %cot.3), custom_call_target="tpu_custom_call" | custom-call | flops 1048576 | bytes 65536 | tf_op jit(solution)/shard_map/pallas_call | solution.py:308
  2.5 6.2 %collective-permute-start = (bf16[384,256]{1,0:T(8,128)(2,1)}, bf16[384,256]{1,0:T(8,128)(2,1)S(1)}, u32[]{:S(2)}, u32[]{:S(2)}) collective-permute-start(bf16[384,256]{1,0:T(8,128)(2,1)} %get-tuple-element.27), channel_id=1, source_target_pairs={{0,8},{8,16},{16,24},{24,32},{32,40},{40,48},{48,56},{56,64},{64,7... | collective-permute-start | bytes 589832 | tf_op jit(solution)/shard_map/ppermute | solution.py:296
  8.7 1.9 %collective-permute-start.1 = (bf16[384,256]{1,0:T(8,128)(2,1)}, bf16[384,256]{1,0:T(8,128)(2,1)S(1)}, u32[]{:S(2)}, u32[]{:S(2)}) collective-permute-start(bf16[384,256]{1,0:T(8,128)(2,1)} %get-tuple-element.28), channel_id=1, source_target_pairs={{8,0},{16,8},{24,16},{32,24},{40,32},{48,40},{56,48},{64,56},{72,6... | collective-permute-start | bytes 589832 | tf_op jit(solution)/shard_map/ppermute | solution.py:297
  11.6 5.8 %collective-permute-done.1.hi = bf16[384,256]{1,0:T(8,128)(2,1)S(1)} collective-permute-done((bf16[384,256]{1,0:T(8,128)(2,1)}, bf16[384,256]{1,0:T(8,128)(2,1)S(1)}, u32[]{:S(2)}, u32[]{:S(2)}) %collective-permute-start.1) | collective-permute-done | bytes 196640 | tf_op jit(solution)/shard_map/ppermute | solution.py:297
  18.1 3.1 %shard_map.76 = (bf16[512,256]{1,0:T(8,128)(2,1)}, bf16[3,34,16,192]{3,2,1,0:T(8,128)(2,1)}) custom-call(bf16[1,32,16,64]{3,2,1,0:T(8,128)(2,1)} %cot.3, bf16[384,256]{1,0:T(8,128)(2,1)} %copy-done.4, bf16[384,256]{1,0:T(8,128)(2,1)} %copy-done.8, bf16[9,192,256]{2,1,0:T(8,128)(2,1)} %bitcast.20), custom_call_target="tpu_custom_call" | custom-call | flops 1048576 | bytes 65536 | tf_op jit(solution)/shard_map/pallas_call | solution.py:312
  21.1 5.1 %all-to-all-start = ((bf16[8,64,256]{2,1,0:T(8,128)(2,1)}), bf16[8,64,256]{2,1,0:T(8,128)(2,1)S(1)}, u32[]{:S(2)}, u32[]{:S(2)}) async-start(bf16[8,64,256]{2,1,0:T(8,128)(2,1)} %bitcast.23), calls=%async_computation | async-start | bytes 524288 | tf_op jit(solution)/shard_map/all_to_all | solution.py:318
  28.2 3.4 %collective-permute-start.2 = (bf16[128,256]{1,0:T(8,128)(2,1)S(1)}, bf16[128,256]{1,0:T(8,128)(2,1)S(1)}, u32[]{:S(2)}, u32[]{:S(2)}) collective-permute-start(bf16[128,256]{1,0:T(8,128)(2,1)S(1)} %get-tuple-element.30), channel_id=1, source_target_pairs={{0,1},{1,2},{2,3},{3,4},{4,5},{5,6},{6,7},{8,9},{9,10},{10,11},{11... | collective-permute-start | bytes 196616 | tf_op jit(solution)/shard_map/ppermute | solution.py:296
  32.9 3.6 %collective-permute-done.3.yhi = bf16[128,256]{1,0:T(8,128)(2,1)S(1)} collective-permute-done((bf16[128,256]{1,0:T(8,128)(2,1)S(1)}, bf16[128,256]{1,0:T(8,128)(2,1)S(1)}, u32[]{:S(2)}, u32[]{:S(2)}) %collective-permute-start.3) | collective-permute-done | bytes 65568 | tf_op jit(solution)/shard_map/ppermute | solution.py:297
  36.6 2.0 %copy-done.2 = bf16[27,256,256]{2,1,0:T(8,128)(2,1)S(1)} copy-done((bf16[27,256,256]{2,1,0:T(8,128)(2,1)S(1)}, bf16[27,256,256]{2,1,0:T(8,128)(2,1)}, u32[]{:S(2)}) %copy-start.2) | copy-done | bytes 3538968
  40.4 3.0 %shard_map.78 = (bf16[64,256]{1,0:T(8,128)(2,1)S(1)}, f32[512,256]{1,0:T(8,128)S(1)}, bf16[768,256]{1,0:T(8,128)(2,1)S(1)}) custom-call(s32[4]{0:T(128)S(1)} %pad_add_fusion.place, bf16[2,8,32,256]{3,2,1,0:T(8,128)(2,1)S(1)} %copy-done.1, bf16[384,256]{1,0:T(8,128)(2,1)S(1)} %copy-done.6, bf16[384,256]{1,0:T(8,128)(2,1)S(1)} %copy-done.10, ...), custom_call_target="tpu_custom_call" | custom-call | flops 1048576 | bytes 65536 | tf_op jit(solution)/shard_map/pallas_call | solution.py:321
  44.9 5.5 %all-to-all-start.1 = ((bf16[8,128,256]{2,1,0:T(8,128)(2,1)}), bf16[8,128,256]{2,1,0:T(8,128)(2,1)S(1)}, u32[]{:S(2)}, u32[]{:S(2)}) async-start(bf16[8,128,256]{2,1,0:T(8,128)(2,1)} %get-tuple-element.39), calls=%async_computation.1 | async-start | bytes 1048576 | tf_op jit(solution)/shard_map/all_to_all | solution.py:338
  50.9 1.6 %collective-permute-done.5.other = bf16[512,256]{1,0:T(8,128)(2,1)S(1)} collective-permute-done((bf16[512,256]{1,0:T(8,128)(2,1)S(1)}, bf16[512,256]{1,0:T(8,128)(2,1)S(1)}, u32[]{:S(2)}, u32[]{:S(2)}) %collective-permute-start.5) | collective-permute-done | bytes 262176 | tf_op jit(solution)/shard_map/ppermute | solution.py:349
  52.5 3.0 %shard_map.80 = bf16[64,54,256]{2,1,0:T(8,128)(2,1)S(1)} custom-call(s32[4]{0:T(128)S(1)} %pad_add_fusion.place, bf16[2,8,32,256]{3,2,1,0:T(8,128)(2,1)S(1)} %copy-done.1, bf16[384,256]{1,0:T(8,128)(2,1)S(1)} %copy-done.7, bf16[384,256]{1,0:T(8,128)(2,1)S(1)} %copy-done.11, bf16[128,256]{1,0:T(8,128)(2,1)S(1)} %collective-permute-done.2.ylo, ...), custom_call_target="tpu_custom_call" | custom-call | flops 1048576 | bytes 65536 | tf_op jit(solution)/shard_map/pallas_call | solution.py:339
  56.7 1.6 %all-to-all-done.1.got = bf16[8,128,256]{2,1,0:T(8,128)(2,1)S(1)} async-done(((bf16[8,128,256]{2,1,0:T(8,128)(2,1)}), bf16[8,128,256]{2,1,0:T(8,128)(2,1)S(1)}, u32[]{:S(2)}, u32[]{:S(2)}) %all-to-all-start.1) | async-done | bytes 524320 | tf_op jit(solution)/shard_map/all_to_all | solution.py:338
  60.5 10.8 %all-to-all-start.2 = ((bf16[64,54,256]{2,1,0:T(8,128)(2,1)}), bf16[64,54,256]{2,1,0:T(8,128)(2,1)S(1)}, u32[]{:S(2)}, u32[]{:S(2)}) async-start(bf16[64,54,256]{2,1,0:T(8,128)(2,1)} %copy-done), calls=%async_computation.2 | async-start | bytes 3670016 | tf_op jit(solution)/shard_map/all_to_all | solution.py:356
  72.3 4.6 %collective-permute-start.6 = (bf16[832,256]{1,0:T(8,128)(2,1)}, bf16[832,256]{1,0:T(8,128)(2,1)S(1)}, u32[]{:S(2)}, u32[]{:S(2)}) collective-permute-start(bf16[832,256]{1,0:T(8,128)(2,1)} %copy-done.14), channel_id=1, source_target_pairs={{0,8},{8,16},{16,24},{24,32},{32,40},{40,48},{48,56},{56,64},{64,7... | collective-permute-start | bytes 1277960 | tf_op jit(solution)/shard_map/ppermute | solution.py:296
  76.9 1.9 %collective-permute-start.7 = (bf16[832,256]{1,0:T(8,128)(2,1)}, bf16[832,256]{1,0:T(8,128)(2,1)S(1)}, u32[]{:S(2)}, u32[]{:S(2)}) collective-permute-start(bf16[832,256]{1,0:T(8,128)(2,1)} %copy-done.16), channel_id=1, source_target_pairs={{8,0},{16,8},{24,16},{32,24},{40,32},{48,40},{56,48},{64,56},{72,6... | collective-permute-start | bytes 1277960 | tf_op jit(solution)/shard_map/ppermute | solution.py:297
  78.9 2.6 %shard_map.85 = bf16[8,224,128]{2,1,0:T(8,128)(2,1)S(1)} custom-call(s32[4]{0:T(128)S(1)} %pad_add_fusion.place, bf16[512,256]{1,0:T(8,128)(2,1)S(1)} %get-tuple-element.48.slab, bf16[512,256]{1,0:T(8,128)(2,1)S(1)} %collective-permute-done.8.other, bf16[3,34,16,192]{3,2,1,0:T(8,128)(2,1)S(1)} %copy-done.13, bf16[768,256]{1,0:T(8,128)(2,1)S(1)} %collective-permute-done.4.far), custom_call_target="tpu_custom_call" | custom-call | flops 1048576 | bytes 65536 | tf_op jit(solution)/shard_map/pallas_call | solution.py:358
  81.6 2.9 %collective-permute-start.10 = (bf16[448,128]{1,0:T(8,128)(2,1)S(1)}, bf16[448,128]{1,0:T(8,128)(2,1)S(1)}, u32[]{:S(2)}, u32[]{:S(2)}) collective-permute-start(bf16[448,128]{1,0:T(8,128)(2,1)S(1)} %bitcast.27), channel_id=1, source_target_pairs={{0,64},{32,96},{64,0},{96,32},{1,65},{33,97},{65,1},{97,33},{2,66}... | collective-permute-start | bytes 344072 | tf_op jit(solution)/shard_map/ppermute | solution.py:366
  86.0 9.6 %collective-permute-done.10.second = bf16[448,128]{1,0:T(8,128)(2,1)S(1)} collective-permute-done((bf16[448,128]{1,0:T(8,128)(2,1)S(1)}, bf16[448,128]{1,0:T(8,128)(2,1)S(1)}, u32[]{:S(2)}, u32[]{:S(2)}) %collective-permute-start.10) | collective-permute-done | bytes 114720 | tf_op jit(solution)/shard_map/ppermute | solution.py:366
  96.4 2.3 %collective-permute-done.9.first = bf16[448,128]{1,0:T(8,128)(2,1)S(1)} collective-permute-done((bf16[448,128]{1,0:T(8,128)(2,1)S(1)}, bf16[448,128]{1,0:T(8,128)(2,1)S(1)}, u32[]{:S(2)}, u32[]{:S(2)}) %collective-permute-start.9) | collective-permute-done | bytes 114720 | tf_op jit(solution)/shard_map/ppermute | solution.py:366
  98.9 6.6 %collective-permute-start.12 = (bf16[224,128]{1,0:T(8,128)(2,1)S(1)}, bf16[224,128]{1,0:T(8,128)(2,1)S(1)}, u32[]{:S(2)}, u32[]{:S(2)}) collective-permute-start(bf16[224,128]{1,0:T(8,128)(2,1)S(1)} %slice.28), channel_id=1, source_target_pairs={{0,16},{16,0},{1,17},{17,1},{2,18},{18,2},{3,19},{19,3},{4,20},{20... | collective-permute-start | bytes 172040 | tf_op jit(solution)/shard_map/ppermute | solution.py:370
  105.5 2.8 %shard_map.82 = bf16[512,64]{1,0:T(8,128)(2,1)} custom-call(bf16[832,256]{1,0:T(8,128)(2,1)S(1)} %copy-done.15, bf16[832,256]{1,0:T(8,128)(2,1)S(1)} %collective-permute-done.6.lo, bf16[832,256]{1,0:T(8,128)(2,1)S(1)} %collective-permute-done.7.hi, bf16[9,192,256]{2,1,0:T(8,128)(2,1)S(1)} %bitcast.21), custom_call_target="tpu_custom_call" | custom-call | flops 2147483648 | bytes 65536 | tf_op jit(solution)/shard_map/pallas_call | solution.py:378
  108.3 2.8 %shard_map.83 = bf16[512,256]{1,0:T(8,128)(2,1)} custom-call(bf16[832,256]{1,0:T(8,128)(2,1)S(1)} %copy-done.15, bf16[832,256]{1,0:T(8,128)(2,1)S(1)} %copy-done.17, bf16[832,256]{1,0:T(8,128)(2,1)S(1)} %collective-permute-done.6.lo, bf16[832,256]{1,0:T(8,128)(2,1)S(1)} %collective-permute-done.7.hi, bf16[9,3,256,256]{3,2,1,0:T(8,128)(2,1)S(1)} %bitcast.19), custom_call_target="tpu_custom_call" | custom-call | flops 2147483648 | bytes 65536 | tf_op jit(solution)/shard_map/pallas_call | solution.py:371
  (60 shorter events, 17.4 us)
Async XLA Ops:
  0.6 25.7 %copy-start.1 = (bf16[2,8,32,256]{3,2,1,0:T(8,128)(2,1)S(1)}, bf16[2,8,32,256]{3,2,1,0:T(8,128)(2,1)}, u32[]{:S(2)}) copy-start(bf16[2,8,32,256]{3,2,1,0:T(8,128)(2,1)} %own.7) | copy-start | bytes 786436
  2.5 9.1 %collective-permute-start = (bf16[384,256]{1,0:T(8,128)(2,1)}, bf16[384,256]{1,0:T(8,128)(2,1)S(1)}, u32[]{:S(2)}, u32[]{:S(2)}) collective-permute-start(bf16[384,256]{1,0:T(8,128)(2,1)} %get-tuple-element.27), channel_id=1, source_target_pairs={{0,8},{8,16},{16,24},{24,32},{32,40},{40,48},{48,56},{56,64},{64,7... | collective-permute-start | bytes 589832 | tf_op jit(solution)/shard_map/ppermute | solution.py:296
  8.7 8.7 %collective-permute-start.1 = (bf16[384,256]{1,0:T(8,128)(2,1)}, bf16[384,256]{1,0:T(8,128)(2,1)S(1)}, u32[]{:S(2)}, u32[]{:S(2)}) collective-permute-start(bf16[384,256]{1,0:T(8,128)(2,1)} %get-tuple-element.28), channel_id=1, source_target_pairs={{8,0},{16,8},{24,16},{32,24},{40,32},{48,40},{56,48},{64,56},{72,6... | collective-permute-start | bytes 589832 | tf_op jit(solution)/shard_map/ppermute | solution.py:297
  21.1 15.4 %all-to-all-start = ((bf16[8,64,256]{2,1,0:T(8,128)(2,1)}), bf16[8,64,256]{2,1,0:T(8,128)(2,1)S(1)}, u32[]{:S(2)}, u32[]{:S(2)}) async-start(bf16[8,64,256]{2,1,0:T(8,128)(2,1)} %bitcast.23), calls=%async_computation | async-start | bytes 524288 | tf_op jit(solution)/shard_map/all_to_all | solution.py:318
  28.2 4.8 %collective-permute-start.2 = (bf16[128,256]{1,0:T(8,128)(2,1)S(1)}, bf16[128,256]{1,0:T(8,128)(2,1)S(1)}, u32[]{:S(2)}, u32[]{:S(2)}) collective-permute-start(bf16[128,256]{1,0:T(8,128)(2,1)S(1)} %get-tuple-element.30), channel_id=1, source_target_pairs={{0,1},{1,2},{2,3},{3,4},{4,5},{5,6},{6,7},{8,9},{9,10},{10,11},{11... | collective-permute-start | bytes 196616 | tf_op jit(solution)/shard_map/ppermute | solution.py:296
  31.5 5.0 %collective-permute-start.3 = (bf16[128,256]{1,0:T(8,128)(2,1)S(1)}, bf16[128,256]{1,0:T(8,128)(2,1)S(1)}, u32[]{:S(2)}, u32[]{:S(2)}) collective-permute-start(bf16[128,256]{1,0:T(8,128)(2,1)S(1)} %get-tuple-element.31), channel_id=1, source_target_pairs={{1,0},{2,1},{3,2},{4,3},{5,4},{6,5},{7,6},{9,8},{10,9},{11,10},{12... | collective-permute-start | bytes 196616 | tf_op jit(solution)/shard_map/ppermute | solution.py:297
  43.4 9.0 %copy-start.7 = (bf16[384,256]{1,0:T(8,128)(2,1)S(1)}, bf16[384,256]{1,0:T(8,128)(2,1)}, u32[]{:S(2)}) copy-start(bf16[384,256]{1,0:T(8,128)(2,1)} %copy-done.4) | copy-start | bytes 589828
  43.4 9.0 %copy-start.11 = (bf16[384,256]{1,0:T(8,128)(2,1)S(1)}, bf16[384,256]{1,0:T(8,128)(2,1)}, u32[]{:S(2)}) copy-start(bf16[384,256]{1,0:T(8,128)(2,1)} %copy-done.8) | copy-start | bytes 589828
  44.9 13.4 %all-to-all-start.1 = ((bf16[8,128,256]{2,1,0:T(8,128)(2,1)}), bf16[8,128,256]{2,1,0:T(8,128)(2,1)S(1)}, u32[]{:S(2)}, u32[]{:S(2)}) async-start(bf16[8,128,256]{2,1,0:T(8,128)(2,1)} %get-tuple-element.39), calls=%async_computation.1 | async-start | bytes 1048576 | tf_op jit(solution)/shard_map/all_to_all | solution.py:338
  50.4 2.1 %collective-permute-start.4 = (bf16[768,256]{1,0:T(8,128)(2,1)S(1)}, bf16[768,256]{1,0:T(8,128)(2,1)S(1)}, u32[]{:S(2)}, u32[]{:S(2)}) collective-permute-start(bf16[768,256]{1,0:T(8,128)(2,1)S(1)} %get-tuple-element.34), channel_id=1, source_target_pairs={{0,8},{8,0},{1,9},{9,1},{2,10},{10,2},{3,11},{11,3},{4,12},{12,4},... | collective-permute-start | bytes 1179656 | tf_op jit(solution)/shard_map/ppermute | solution.py:337
  50.4 2.1 %collective-permute-start.5 = (bf16[512,256]{1,0:T(8,128)(2,1)S(1)}, bf16[512,256]{1,0:T(8,128)(2,1)S(1)}, u32[]{:S(2)}, u32[]{:S(2)}) collective-permute-start(bf16[512,256]{1,0:T(8,128)(2,1)S(1)} %get-tuple-element.38.grad), channel_id=1, source_target_pairs={{0,8},{8,0},{1,9},{9,1},{2,10},{10,2},{3,11},{11,3},{4,12},{12,4},... | collective-permute-start | bytes 786440 | tf_op jit(solution)/shard_map/ppermute | solution.py:349
  60.4 18.4 %copy-start.13 = (bf16[3,34,16,192]{3,2,1,0:T(8,128)(2,1)S(1)}, bf16[3,34,16,192]{3,2,1,0:T(8,128)(2,1)}, u32[]{:S(2)}) copy-start(bf16[3,34,16,192]{3,2,1,0:T(8,128)(2,1)} %get-tuple-element.49.wide) | copy-start | bytes 1880068
  60.5 51.5 %all-to-all-start.2 = ((bf16[64,54,256]{2,1,0:T(8,128)(2,1)}), bf16[64,54,256]{2,1,0:T(8,128)(2,1)S(1)}, u32[]{:S(2)}, u32[]{:S(2)}) async-start(bf16[64,54,256]{2,1,0:T(8,128)(2,1)} %copy-done), calls=%async_computation.2 | async-start | bytes 3670016 | tf_op jit(solution)/shard_map/all_to_all | solution.py:356
  71.3 7.6 %collective-permute-start.8 = (bf16[512,256]{1,0:T(8,128)(2,1)S(1)}, bf16[512,256]{1,0:T(8,128)(2,1)S(1)}, u32[]{:S(2)}, u32[]{:S(2)}) collective-permute-start(bf16[512,256]{1,0:T(8,128)(2,1)S(1)} %get-tuple-element.48.slab), channel_id=1, source_target_pairs={{0,8},{8,0},{1,9},{9,1},{2,10},{10,2},{3,11},{11,3},{4,12},{12,4},... | collective-permute-start | bytes 786440 | tf_op jit(solution)/shard_map/ppermute | solution.py:354
  72.3 33.2 %collective-permute-start.6 = (bf16[832,256]{1,0:T(8,128)(2,1)}, bf16[832,256]{1,0:T(8,128)(2,1)S(1)}, u32[]{:S(2)}, u32[]{:S(2)}) collective-permute-start(bf16[832,256]{1,0:T(8,128)(2,1)} %copy-done.14), channel_id=1, source_target_pairs={{0,8},{8,16},{16,24},{24,32},{32,40},{40,48},{48,56},{56,64},{64,7... | collective-permute-start | bytes 1277960 | tf_op jit(solution)/shard_map/ppermute | solution.py:296
  76.9 28.6 %collective-permute-start.7 = (bf16[832,256]{1,0:T(8,128)(2,1)}, bf16[832,256]{1,0:T(8,128)(2,1)S(1)}, u32[]{:S(2)}, u32[]{:S(2)}) collective-permute-start(bf16[832,256]{1,0:T(8,128)(2,1)} %copy-done.16), channel_id=1, source_target_pairs={{8,0},{16,8},{24,16},{32,24},{40,32},{48,40},{56,48},{64,56},{72,6... | collective-permute-start | bytes 1277960 | tf_op jit(solution)/shard_map/ppermute | solution.py:297
  78.9 26.6 %copy-start.12 = (bf16[27,256,64]{1,2,0:T(8,128)(2,1)S(1)}, bf16[27,256,64]{1,2,0:T(8,128)(2,1)}, u32[]{:S(2)}) copy-start(bf16[27,256,64]{1,2,0:T(8,128)(2,1)} %param.6) | copy-start | bytes 2654212
  78.9 26.6 %copy-start.15 = (bf16[832,256]{1,0:T(8,128)(2,1)S(1)}, bf16[832,256]{1,0:T(8,128)(2,1)}, u32[]{:S(2)}) copy-start(bf16[832,256]{1,0:T(8,128)(2,1)} %copy-done.14) | copy-start | bytes 1277956
  81.6 14.0 %collective-permute-start.10 = (bf16[448,128]{1,0:T(8,128)(2,1)S(1)}, bf16[448,128]{1,0:T(8,128)(2,1)S(1)}, u32[]{:S(2)}, u32[]{:S(2)}) collective-permute-start(bf16[448,128]{1,0:T(8,128)(2,1)S(1)} %bitcast.27), channel_id=1, source_target_pairs={{0,64},{32,96},{64,0},{96,32},{1,65},{33,97},{65,1},{97,33},{2,66}... | collective-permute-start | bytes 344072 | tf_op jit(solution)/shard_map/ppermute | solution.py:366
  84.5 11.9 %collective-permute-start.11 = (bf16[448,128]{1,0:T(8,128)(2,1)S(1)}, bf16[448,128]{1,0:T(8,128)(2,1)S(1)}, u32[]{:S(2)}, u32[]{:S(2)}) collective-permute-start(bf16[448,128]{1,0:T(8,128)(2,1)S(1)} %bitcast.26), channel_id=1, source_target_pairs={{0,96},{32,0},{64,32},{96,64},{1,97},{33,1},{65,33},{97,65},{2,98}... | collective-permute-start | bytes 344072 | tf_op jit(solution)/shard_map/ppermute | solution.py:366
  85.3 13.5 %collective-permute-start.9 = (bf16[448,128]{1,0:T(8,128)(2,1)S(1)}, bf16[448,128]{1,0:T(8,128)(2,1)S(1)}, u32[]{:S(2)}, u32[]{:S(2)}) collective-permute-start(bf16[448,128]{1,0:T(8,128)(2,1)S(1)} %bitcast.25), channel_id=1, source_target_pairs={{0,32},{32,64},{64,96},{96,0},{1,33},{33,65},{65,97},{97,1},{2,34}... | collective-permute-start | bytes 344072 | tf_op jit(solution)/shard_map/ppermute | solution.py:366
  98.9 9.5 %copy-start.3 = (bf16[27,256,256]{2,1,0:T(8,128)(2,1)S(1)}, bf16[27,256,256]{2,1,0:T(8,128)(2,1)}, u32[]{:S(2)}) copy-start(bf16[27,256,256]{2,1,0:T(8,128)(2,1)} %param.5) | copy-start | bytes 10616836
  98.9 9.5 %copy-start.17 = (bf16[832,256]{1,0:T(8,128)(2,1)S(1)}, bf16[832,256]{1,0:T(8,128)(2,1)}, u32[]{:S(2)}) copy-start(bf16[832,256]{1,0:T(8,128)(2,1)} %copy-done.16) | copy-start | bytes 1277956
  98.9 12.2 %collective-permute-start.12 = (bf16[224,128]{1,0:T(8,128)(2,1)S(1)}, bf16[224,128]{1,0:T(8,128)(2,1)S(1)}, u32[]{:S(2)}, u32[]{:S(2)}) collective-permute-start(bf16[224,128]{1,0:T(8,128)(2,1)S(1)} %slice.28), channel_id=1, source_target_pairs={{0,16},{16,0},{1,17},{17,1},{2,18},{18,2},{3,19},{19,3},{4,20},{20... | collective-permute-start | bytes 172040 | tf_op jit(solution)/shard_map/ppermute | solution.py:370
  (10 other events, 15.0 us)

commit v4 on v3

--- a/solution.py
+++ b/solution.py
@@ -72,13 +72,14 @@
 def edge_kernel(own, lo, hi, low, high):
     for x in range(4):
         plane = plane_of(own, lo, hi, x)
-        low[32 * x : 32 * x + 32] = plane[0]
-        high[32 * x : 32 * x + 32] = plane[7]
+        low[64 * x : 64 * x + 64] = plane[:2].reshape(64, 256)
+        high[64 * x : 64 * x + 64] = plane[6:].reshape(64, 256)
 
 
 def whole_plane(own, lo, hi, ylo, yhi, x):
-    rows = slice(32 * x, 32 * x + 32)
-    return jnp.concatenate([ylo[rows][None], plane_of(own, lo, hi, x), yhi[rows][None]], axis=0)
+    below = ylo[64 * x : 64 * x + 64].reshape(2, 32, 256)
+    above = yhi[64 * x : 64 * x + 64].reshape(2, 32, 256)
+    return jnp.concatenate([below, plane_of(own, lo, hi, x), above], axis=0)
 
 
 def coarse_back_kernel(cot, lo, hi, w, partial, wide):
@@ -94,58 +95,78 @@
     partial[...] = total.astype(BF)
 
 
-def fine_forward_kernel(place, own, lo, hi, ylo, yhi, w, pooled, slope, far, wide, pre, sums):
+def fine_forward_kernel(
+    place, own, lo, hi, ylo, yhi, partial, w, sent, slope, far, wide, pre, sums, padded
+):
     for x in range(4):
         plane = whole_plane(own, lo, hi, ylo, yhi, x)
         wide[x] = along_depth(plane, 1)
 
         @pl.when(place[0] == x // 2)
         def _():
-            far[320 * (x % 2) : 320 * (x % 2) + 320] = plane.reshape(320, 256)
+            far[320 * (x % 2) : 320 * (x % 2) + 320] = plane[1:11].reshape(320, 256)
 
     far[640:] = jnp.where(place[0] == 0, lo[256:384], hi[256:384])
     for k in range(9):
         a, b = divmod(k, 3)
-        window = wide[a : a + 2, b : b + 8].reshape(512, 768)
+        window = wide[a : a + 2, b : b + 10].reshape(640, 768)
         term = jnp.dot(window, w[k], preferred_element_type=F32)
         pre[...] = term if k == 0 else pre[...] + term
-    for y in range(4):
+    for y in range(6):
         total = jnp.zeros((32, 256), F32)
         for x in range(2):
-            for half in range(2):
-                at = x * 256 + (2 * y + half) * 32
-                value = pre[at : at + 32]
-                sigma = 1.0 / (1.0 + jnp.exp(-value))
-                total = total + (value * sigma).astype(BF).astype(F32)
-                slope[at : at + 32] = 0.125 * sigma * (1.0 + value * (1.0 - sigma))
-        sums[0, y * 32 : y * 32 + 32] = total[:, :128]
-        sums[1, y * 32 : y * 32 + 32] = total[:, 128:]
+            for row in (2 * y - 1, 2 * y):
+                if 0 <= row < 10:
+                    at = x * 320 + row * 32
+                    value = pre[at : at + 32]
+                    sigma = 1.0 / (1.0 + jnp.exp(-value))
+                    total = total + (value * sigma).astype(BF).astype(F32)
+                    slope[at : at + 32] = 0.125 * sigma * (1.0 + value * (1.0 - sigma))
+        if 0 < y < 5:
+            sums[0, y * 32 - 32 : y * 32] = total[:, :128]
+            sums[1, y * 32 - 32 : y * 32] = total[:, 128:]
+    pooled = []
     for side in range(2):
         even = sums[side, pl.ds(0, 64, stride=2)]
         odd = sums[side, pl.ds(1, 64, stride=2)]
-        pooled[:, side * 128 : side * 128 + 128] = ((even + odd) * 0.125).astype(BF)
-
-
-def fine_grad_kernel(place, parts, slope, pooled, grad, sent, spread):
-    summed = parts[0].astype(F32)
-    for k in range(1, 8):
-        summed = summed + parts[k].astype(F32)
-    summed = summed.astype(BF).astype(F32)
-    for side in range(2):
-        half = summed[:, side * 128 : side * 128 + 128]
-        spread[side, pl.ds(0, 64, stride=2)] = half
-        spread[side, pl.ds(1, 64, stride=2)] = half
-    for y in range(4):
-        wide = jnp.concatenate([spread[0, y * 32 : y * 32 + 32], spread[1, y * 32 : y * 32 + 32]], axis=1)
-        for x in range(2):
-            for half in range(2):
-                at = x * 256 + (2 * y + half) * 32
-                grad[at : at + 32] = (wide * slope[at : at + 32]).astype(BF)
-    low = jnp.concatenate([grad[0:32], grad[256:288]], axis=0)
-    high = jnp.concatenate([grad[224:256], grad[480:512]], axis=0)
+        pooled.append(((even + odd) * 0.125).astype(BF))
+    pooled = jnp.concatenate(pooled, axis=1)
+    padded[:16] = jnp.zeros((16, 256), BF)
+    padded[16:528] = partial[...]
+    padded[528:] = jnp.zeros((16, 256), BF)
     for k in range(8):
-        sent[k, :64] = pooled[...]
-        sent[k, 64:] = jnp.where(k < place[3], low, high)
+        sent[k, :64] = pooled
+        sent[k, 64:] = padded[64 * k : 64 * k + 96]
+
+
+def fine_grad_kernel(place, got, slope, grad, up, down, slab, spread):
+    for y in range(6):
+        rows = slice(64 + 16 * y, 80 + 16 * y)
+        total = got[0, rows].astype(F32)
+        for k in range(1, 8):
+            total = total + got[k, rows].astype(F32)
+        total = total.astype(BF).astype(F32)
+        if y == 0:
+            total = jnp.where(place[3] > 0, total, 0.0)
+        if y == 5:
+            total = jnp.where(place[3] < 7, total, 0.0)
+        for side in range(2):
+            half = total[:, side * 128 : side * 128 + 128]
+            spread[side, pl.ds(32 * y, 16, stride=2)] = half
+            spread[side, pl.ds(32 * y + 1, 16, stride=2)] = half
+        at = slice(y * 32, y * 32 + 32)
+        wide = jnp.concatenate([spread[0, at], spread[1, at]], axis=1)
+        for x, out in enumerate((down, up)):
+            for row in (2 * y - 1, 2 * y):
+                if 0 <= row < 10:
+                    at = x * 320 + row * 32
+                    value = (wide * slope[at : at + 32]).astype(BF)
+                    out[row * 32 : row * 32 + 32] = value
+                    if 0 < row < 9:
+                        at = x * 256 + row * 32 - 32
+                        grad[at : at + 32] = value
+    for k in range(8):
+        slab[64 * k : 64 * k + 64] = got[k, :64]
 
 
 def fine_weight_kernel(
@@ -165,7 +186,7 @@
                     planes.add(slot)
                     x = slot - 2 * core
                     if 0 <= x < 4:
-                        rows = whole_plane(own, lo, hi, ylo, yhi, x)
+                        rows = whole_plane(own, lo, hi, ylo, yhi, x)[1:11]
                     else:
                         at = 320 * (slot % 2)
                         rows = far[at : at + 320].reshape(10, 32, 256)
@@ -195,27 +216,9 @@
                     terms[k * 8 + f] = total[k % 2, f * 54 : f * 54 + 54].astype(BF)
 
 
-def grad_plane(place, grad, got, x):
-    below = got[jnp.maximum(place[3] - 1, 0), 64 + 32 * x : 96 + 32 * x]
-    above = got[jnp.minimum(place[3] + 1, 7), 64 + 32 * x : 96 + 32 * x]
-    below = jnp.where(place[3] > 0, below, jnp.zeros_like(below))
-    above = jnp.where(place[3] < 7, above, jnp.zeros_like(above))
-    middle = grad[256 * x : 256 * x + 256].reshape(8, 32, 256)
-    return jnp.concatenate([below[None], middle, above[None]], axis=0)
-
-
-def ship_kernel(place, grad, got, up, down, slab):
-    down[:320] = grad_plane(place, grad, got, 0).reshape(320, 256)
-    up[:320] = grad_plane(place, grad, got, 1).reshape(320, 256)
-    for k in range(8):
-        up[320 + 64 * k : 384 + 64 * k] = got[k, :64]
-        down[320 + 64 * k : 384 + 64 * k] = got[k, :64]
-        slab[64 * k : 64 * k + 64] = got[k, :64]
-
-
 def fine_back_kernel(up, down, lo, hi, w, out, wide, total):
     for x, plane in enumerate((lo, down, up, hi)):
-        wide[x] = along_depth(plane[:320].reshape(10, 32, 256), -1)
+        wide[x] = along_depth(plane[...].reshape(10, 32, 256), -1)
     for k in range(9):
         a, b = divmod(k, 3)
         window = wide[2 - a : 4 - a, 2 - b : 10 - b].reshape(512, 768)
@@ -255,18 +258,34 @@
                 terms[at] = jnp.concatenate([upper, lower], axis=1).astype(BF)
 
 
-def coarse_forward_kernel(slab, lo, hi, w, out, wide):
-    for x, plane in enumerate((lo, slab, hi)):
-        wide[x] = along_depth(pad_rows(plane[320:832].reshape(32, 16, 256)), 1)
+def packed(plane):
+    return jnp.concatenate([plane[128 * k : 128 * k + 128] for k in range(4)], axis=1)
+
+
+def coarse_forward_kernel(slab, w, own, up, down, wide):
+    wide[...] = along_depth(pad_rows(slab[...].reshape(32, 16, 256)), 1)
     total = None
-    for k in range(9):
-        a, b = divmod(k, 3)
-        window = wide[a, b : b + 32].reshape(512, 768)
-        turned = w[k].T
-        right = jnp.concatenate([turned[:, 64 * c : 64 * c + 64] for c in range(3)], axis=0)
+    for b in range(3):
+        columns = []
+        for a in range(3):
+            turned = w[3 * a + b].T
+            columns.append(
+                jnp.concatenate([turned[:, 64 * c : 64 * c + 64] for c in range(3)], axis=0)
+            )
+        right = jnp.concatenate(columns, axis=1)
+        window = wide[b : b + 32].reshape(512, 768)
         term = jnp.dot(window, right, preferred_element_type=F32)
-        total = term if k == 0 else total + term
-    out[...] = total.astype(BF)
+        total = term if b == 0 else total + term
+    up[...] = packed(total[:, :64]).astype(BF)
+    own[...] = total[:, 64:128]
+    down[...] = packed(total[:, 128:]).astype(BF)
+
+
+def coarse_out_kernel(own, lo, hi, out):
+    for k in range(4):
+        rows, columns = slice(128 * k, 128 * k + 128), slice(64 * k, 64 * k + 64)
+        total = own[rows] + lo[:, columns].astype(F32) + hi[:, columns].astype(F32)
+        out[rows] = total.astype(BF)
 
 
 def fine_sum_kernel(scale, parts, out):
@@ -306,36 +325,37 @@
 
     pack = call(pack_kernel, (array(384, 256), array(384, 256)), [VMEM] * 2, limit=60)
     lo, hi = swap_sides(*pack(inputs, cotangent), SP)
-    edge = call(edge_kernel, (array(128, 256), array(128, 256)), [VMEM] * 3)
+    edge = call(edge_kernel, (array(256, 256), array(256, 256)), [VMEM] * 3)
     low, high = edge(inputs, lo, hi)
     ylo, yhi = swap_sides(high, low, FL)
     partial, wide_cot = call(
         coarse_back_kernel,
         (array(512, 256), array(3, 34, 16, 192)),
         [VMEM] * 4,
-        limit=60,
     )(cotangent, lo, hi, turned_coarse)
-    parts = lax.all_to_all(partial.reshape(8, 64, 256), FL, 0, 0, tiled=True)
-    parts, ylo, yhi = lax.optimization_barrier((parts, ylo, yhi))
     blocks = (inputs, lo, hi, ylo, yhi)
-    pooled, slope, far = call(
+    sent, slope, far = call(
         fine_forward_kernel,
-        (array(64, 256), array(512, 256, dtype=F32), array(768, 256)),
-        [SMEM] + [VMEM] * 6,
+        (array(8, 160, 256), array(640, 256, dtype=F32), array(768, 256)),
+        [SMEM] + [VMEM] * 7,
         [
-            pltpu.VMEM((4, 10, 32, 768), BF),
-            pltpu.VMEM((512, 256), F32),
+            pltpu.VMEM((4, 12, 32, 768), BF),
+            pltpu.VMEM((640, 256), F32),
             pltpu.VMEM((2, 128, 128), F32),
+            pltpu.VMEM((544, 256), BF),
         ],
-    )(place, *blocks, weight_fine.reshape(9, 768, 256))
-    grad, sent = call(
-        fine_grad_kernel,
-        (array(512, 256), array(8, 128, 256)),
-        [SMEM] + [VMEM] * 3,
-        [pltpu.VMEM((2, 128, 128), F32)],
-    )(place, parts, slope, pooled)
+    )(place, *blocks, partial, weight_fine.reshape(9, 768, 256))
     far = lax.ppermute(far, "c", SWAP)
     got = lax.all_to_all(sent, FL, 0, 0, tiled=True)
+    grad, up, down, slab = call(
+        fine_grad_kernel,
+        (array(512, 256), array(320, 256), array(320, 256), array(512, 256)),
+        [SMEM] + [VMEM] * 2,
+        [pltpu.VMEM((2, 192, 128), F32)],
+    )(place, got, slope)
+    other = lax.ppermute(grad, "c", SWAP)
+    lo, hi = swap_sides(up, down, SP)
+    across = lax.ppermute(slab, "c", SWAP)
     terms = call(
         fine_weight_kernel,
         array(64, 54, 256),
@@ -346,13 +366,8 @@
             pltpu.VMEM((2, 432, 256), F32),
         ],
         limit=24,
-    )(place, *blocks, far, grad, lax.ppermute(grad, "c", SWAP))
-    terms, got = lax.optimization_barrier((terms, got))
-    shapes = (array(832, 256), array(832, 256), array(512, 256))
-    up, down, slab = call(ship_kernel, shapes, [SMEM] + [VMEM] * 2)(place, grad, got)
-    terms, up, down, slab = lax.optimization_barrier((terms, up, down, slab))
-    across = lax.ppermute(slab, "c", SWAP)
-    lo, hi = swap_sides(up, down, SP)
+    )(place, *blocks, far, grad, other)
+    terms, lo, hi = lax.optimization_barrier((terms, lo, hi))
     spread = lax.all_to_all(terms, ("x", "yh", "z", "yl"), 0, 0, tiled=True)
 
     coarse_terms = call(
@@ -367,7 +382,6 @@
         for step in range(1, 4)
     ]
     coarse_terms = call(quad_kernel, array(448, 128), [VMEM] * 4)(coarse_terms[0], *arrived)
-    arrived = lax.ppermute(coarse_terms[224:], "yh", SWAP)
     grad_input = call(
         fine_back_kernel,
         array(512, 256),
@@ -375,13 +389,16 @@
         [pltpu.VMEM((4, 10, 32, 768), BF), pltpu.VMEM((512, 256), F32)],
         flops=2**31,
     )(up, down, lo, hi, weight_fine.reshape(9, 3, 256, 256))
-    coarse_out = call(
+    grad_input, coarse_terms = lax.optimization_barrier((grad_input, coarse_terms))
+    arrived = lax.ppermute(coarse_terms[224:], "yh", SWAP)
+    centre, up, down = call(
         coarse_forward_kernel,
-        array(512, 64),
-        [VMEM] * 4,
-        [pltpu.VMEM((3, 34, 16, 768), BF)],
-        flops=2**31,
-    )(up, lo, hi, turned_coarse)
+        (array(512, 64, dtype=F32), array(128, 256), array(128, 256)),
+        [VMEM] * 2,
+        [pltpu.VMEM((34, 16, 768), BF)],
+    )(slab, turned_coarse)
+    lo, hi = swap_sides(up, down, SP)
+    coarse_out = call(coarse_out_kernel, array(512, 64), [VMEM] * 3)(centre, lo, hi)
     grad_coarse = call(
         functools.partial(coarse_sum_kernel, 1.0 / math.sqrt(cells // 8)),
         array(64, 432, dtype=F32),
@@ -391,6 +408,7 @@
         functools.partial(fine_sum_kernel, 1.0 / math.sqrt(cells)),
         array(108, 128, dtype=F32),
         [VMEM],
+        flops=2**31,
     )(spread)
     return (
         coarse_out.reshape(1, 32, 16, 64),

time: 114 us -> 110 us (0.965)
  starting transfers between devices: 53.3 us -> 49 us
  waiting for transfers between devices: 26.4 us -> 29.2 us
  Pallas kernels: 23 us -> 21.3 us
    all_to_all x1, waiting for transfers between devices: 1.57 us -> 9.72 us  [body(): got = lax.all_to_all(sent, FL, 0, 0, tiled=True)]
    ppermute x3 -> x4, starting transfers between devices: 14.2 us -> 20.2 us  [swap_sides(): lax.ppermute(up, axis, [(i, i + 1) for i in steps])]
    all_to_all x1 -> x0, starting transfers between devices: 5.15 us -> none  [body(): parts = lax.all_to_all(partial.reshape(8, 64, 256), FL, 0, 0, tiled=True)]
    ppermute x1, starting transfers between devices: 6.64 us -> 2.82 us  [body(): arrived = lax.ppermute(coarse_terms[224:], 'yh', SWAP)]
    ppermute x3, waiting for transfers between devices: 12.8 us -> 9.03 us  [body(): lax.ppermute(coarse_terms[step], 'x', [(i, (i + step) % 4) for i in range...]
    all_to_all x1, starting transfers between devices: 10.8 us -> 7.77 us  [body(): spread = lax.all_to_all(terms, ('x', 'yh', 'z', 'yl'), 0, 0, tiled=True)]
    pallas_call x1, Pallas kernels: 3.07 us -> 0.91 us  [body(): call(coarse_back_kernel, (array(512, 256), array(3, 34, 16, 192)), [VMEM]...]
    ppermute x3 -> x4, starting transfers between devices: 5.13 us -> 7.05 us  [swap_sides(): lax.ppermute(down, axis, [(i + 1, i) for i in steps])]
  transfers between devices with their start and end apart: 16 -> 17, of which waited for: 8 -> 9; matrix products, arithmetic and copies ran while one was open for 0% -> 0% of each run, Pallas kernels for 11% -> 13%
where the time goes in v4:
time: 110 us; the launch traced here: 109 us
  starting transfers between devices  49 us (45%)
  waiting for transfers between devices  29.2 us (27%)
  Pallas kernels  21.3 us (19%)
  local copies, waits for them, and re-layouts  8.44 us (8%)
    ppermute x4, starting transfers between devices, swap_sides(): lax.ppermute(up, axis, [(i, i + 1) for i in steps])  20.2 us
    all_to_all x1, waiting for transfers between devices, body(): got = lax.all_to_all(sent, FL, 0, 0, tiled=True)  9.72 us
    ppermute x3, waiting for transfers between devices, body(): lax.ppermute(coarse_terms[step], 'x', [(i, (i + step) % 4) for i in range...  9.03 us
    ppermute x4, waiting for transfers between devices, swap_sides(): lax.ppermute(down, axis, [(i + 1, i) for i in steps])  8.44 us
    unnamed x30, local copies, waits for them, and re-layouts  8.4 us
    all_to_all x1, starting transfers between devices, body(): spread = lax.all_to_all(terms, ('x', 'yh', 'z', 'yl'), 0, 0, tiled=True)  7.77 us
    ppermute x4, starting transfers between devices, swap_sides(): lax.ppermute(down, axis, [(i + 1, i) for i in steps])  7.05 us
    all_to_all x1, starting transfers between devices, body(): got = lax.all_to_all(sent, FL, 0, 0, tiled=True)  6.65 us
  transfers between devices with their start and end apart: 17, of which 9 were waited for; matrix products, arithmetic and copies ran while one was open for 0% of the time, Pallas kernels for 13%

profile of v4, /device:TPU:1, one launch (start us, length us, event | category | flops | bytes accessed | tf_op | source)
XLA Modules:
  0.0 109.0 jit_solution(15607344830536468333)
XLA Ops:
  0.6 1.9 %shard_map.75 = (bf16[384,256]{1,0:T(8,128)(2,1)}, bf16[384,256]{1,0:T(8,128)(2,1)}) custom-call(bf16[2,8,32,256]{3,2,1,0:T(8,128)(2,1)} %own.7, bf16[1,32,16,64]{3,2,1,0:T(8,128)(2,1)} %cot.3), custom_call_target="tpu_custom_call" | custom-call | flops 1048576 | bytes 65536 | tf_op jit(solution)/shard_map/pallas_call | solution.py:327
  2.5 6.2 %collective-permute-start = (bf16[384,256]{1,0:T(8,128)(2,1)}, bf16[384,256]{1,0:T(8,128)(2,1)S(1)}, u32[]{:S(2)}, u32[]{:S(2)}) collective-permute-start(bf16[384,256]{1,0:T(8,128)(2,1)} %get-tuple-element.25), channel_id=1, source_target_pairs={{0,8},{8,16},{16,24},{24,32},{32,40},{40,48},{48,56},{56,64},{64,7... | collective-permute-start | bytes 589832 | tf_op jit(solution)/shard_map/ppermute | solution.py:315
  8.7 1.9 %collective-permute-start.1 = (bf16[384,256]{1,0:T(8,128)(2,1)}, bf16[384,256]{1,0:T(8,128)(2,1)S(1)}, u32[]{:S(2)}, u32[]{:S(2)}) collective-permute-start(bf16[384,256]{1,0:T(8,128)(2,1)} %get-tuple-element.26), channel_id=1, source_target_pairs={{8,0},{16,8},{24,16},{32,24},{40,32},{48,40},{56,48},{64,56},{72,6... | collective-permute-start | bytes 589832 | tf_op jit(solution)/shard_map/ppermute | solution.py:316
  11.6 5.8 %collective-permute-done.1.hi = bf16[384,256]{1,0:T(8,128)(2,1)S(1)} collective-permute-done((bf16[384,256]{1,0:T(8,128)(2,1)}, bf16[384,256]{1,0:T(8,128)(2,1)S(1)}, u32[]{:S(2)}, u32[]{:S(2)}) %collective-permute-start.1) | collective-permute-done | bytes 196640 | tf_op jit(solution)/shard_map/ppermute | solution.py:316
  18.4 2.3 %collective-permute-start.2 = (bf16[256,256]{1,0:T(8,128)(2,1)S(1)}, bf16[256,256]{1,0:T(8,128)(2,1)S(1)}, u32[]{:S(2)}, u32[]{:S(2)}) collective-permute-start(bf16[256,256]{1,0:T(8,128)(2,1)S(1)} %get-tuple-element.27), channel_id=1, source_target_pairs={{0,1},{1,2},{2,3},{3,4},{4,5},{5,6},{6,7},{8,9},{9,10},{10,11},{11... | collective-permute-start | bytes 393224 | tf_op jit(solution)/shard_map/ppermute | solution.py:315
  20.7 1.3 %collective-permute-start.3 = (bf16[256,256]{1,0:T(8,128)(2,1)S(1)}, bf16[256,256]{1,0:T(8,128)(2,1)S(1)}, u32[]{:S(2)}, u32[]{:S(2)}) collective-permute-start(bf16[256,256]{1,0:T(8,128)(2,1)S(1)} %get-tuple-element.28), channel_id=1, source_target_pairs={{1,0},{2,1},{3,2},{4,3},{5,4},{6,5},{7,6},{9,8},{10,9},{11,10},{12... | collective-permute-start | bytes 393224 | tf_op jit(solution)/shard_map/ppermute | solution.py:316
  26.0 1.4 %collective-permute-done.3.yhi = bf16[256,256]{1,0:T(8,128)(2,1)S(1)} collective-permute-done((bf16[256,256]{1,0:T(8,128)(2,1)S(1)}, bf16[256,256]{1,0:T(8,128)(2,1)S(1)}, u32[]{:S(2)}, u32[]{:S(2)}) %collective-permute-start.3) | collective-permute-done | bytes 131104 | tf_op jit(solution)/shard_map/ppermute | solution.py:316
  27.4 2.0 %copy-done.2 = bf16[27,256,256]{2,1,0:T(8,128)(2,1)S(1)} copy-done((bf16[27,256,256]{2,1,0:T(8,128)(2,1)S(1)}, bf16[27,256,256]{2,1,0:T(8,128)(2,1)}, u32[]{:S(2)}) %copy-start.2) | copy-done | bytes 3538968
  29.4 4.5 %shard_map.78 = (bf16[8,160,256]{2,1,0:T(8,128)(2,1)}, f32[640,256]{1,0:T(8,128)S(1)}, bf16[768,256]{1,0:T(8,128)(2,1)}) custom-call(s32[4]{0:T(128)S(1)} %pad_add_fusion.place, bf16[2,8,32,256]{3,2,1,0:T(8,128)(2,1)S(1)} %copy-done.1, bf16[384,256]{1,0:T(8,128)(2,1)S(1)} %collective-permute-done.lo, bf16[384,256]{1,0:T(8,128)(2,1)S(1)} %collective-permute-done.1.hi, ...), custom_call_target="tpu_custom_call" | custom-call | flops 1048576 | bytes 65536 | tf_op jit(solution)/shard_map/pallas_call | solution.py:337
  33.9 6.6 %all-to-all-start = ((bf16[8,160,256]{2,1,0:T(8,128)(2,1)}), bf16[8,160,256]{2,1,0:T(8,128)(2,1)S(1)}, u32[]{:S(2)}, u32[]{:S(2)}) async-start(bf16[8,160,256]{2,1,0:T(8,128)(2,1)} %get-tuple-element.30), calls=%async_computation | async-start | bytes 1310720 | tf_op jit(solution)/shard_map/all_to_all | solution.py:349
  40.5 9.7 %all-to-all-done.got = bf16[8,160,256]{2,1,0:T(8,128)(2,1)S(1)} async-done(((bf16[8,160,256]{2,1,0:T(8,128)(2,1)}), bf16[8,160,256]{2,1,0:T(8,128)(2,1)S(1)}, u32[]{:S(2)}, u32[]{:S(2)}) %all-to-all-start) | async-done | bytes 655392 | tf_op jit(solution)/shard_map/all_to_all | solution.py:349
  51.0 6.9 %collective-permute-start.8 = (bf16[320,256]{1,0:T(8,128)(2,1)S(1)}, bf16[320,256]{1,0:T(8,128)(2,1)S(1)}, u32[]{:S(2)}, u32[]{:S(2)}) collective-permute-start(bf16[320,256]{1,0:T(8,128)(2,1)S(1)} %get-tuple-element.36.up), channel_id=1, source_target_pairs={{0,8},{8,16},{16,24},{24,32},{32,40},{40,48},{48,56},{56,64},{64,7... | collective-permute-start | bytes 491528 | tf_op jit(solution)/shard_map/ppermute | solution.py:315
  57.9 1.9 %collective-permute-start.9 = (bf16[320,256]{1,0:T(8,128)(2,1)S(1)}, bf16[320,256]{1,0:T(8,128)(2,1)S(1)}, u32[]{:S(2)}, u32[]{:S(2)}) collective-permute-start(bf16[320,256]{1,0:T(8,128)(2,1)S(1)} %get-tuple-element.37.down), channel_id=1, source_target_pairs={{8,0},{16,8},{24,16},{32,24},{40,32},{48,40},{56,48},{64,56},{72,6... | collective-permute-start | bytes 491528 | tf_op jit(solution)/shard_map/ppermute | solution.py:316
  59.8 4.3 %shard_map.82 = bf16[64,54,256]{2,1,0:T(8,128)(2,1)} custom-call(s32[4]{0:T(128)S(1)} %pad_add_fusion.place, bf16[2,8,32,256]{3,2,1,0:T(8,128)(2,1)S(1)} %copy-done.1, bf16[384,256]{1,0:T(8,128)(2,1)S(1)} %collective-permute-done.lo, bf16[384,256]{1,0:T(8,128)(2,1)S(1)} %collective-permute-done.1.hi, bf16[256,256]{1,0:T(8,128)(2,1)S(1)} %collective-permute-done.2.ylo, ...), custom_call_target="tpu_custom_call" | custom-call | flops 1048576 | bytes 65536 | tf_op jit(solution)/shard_map/pallas_call | solution.py:359
  64.8 1.2 %collective-permute-done.9.hi = bf16[320,256]{1,0:T(8,128)(2,1)S(1)} collective-permute-done((bf16[320,256]{1,0:T(8,128)(2,1)S(1)}, bf16[320,256]{1,0:T(8,128)(2,1)S(1)}, u32[]{:S(2)}, u32[]{:S(2)}) %collective-permute-start.9) | collective-permute-done | bytes 163872 | tf_op jit(solution)/shard_map/ppermute | solution.py:316
  66.7 7.8 %all-to-all-start.1 = ((bf16[64,54,256]{2,1,0:T(8,128)(2,1)}), bf16[64,54,256]{2,1,0:T(8,128)(2,1)S(1)}, u32[]{:S(2)}, u32[]{:S(2)}) async-start(bf16[64,54,256]{2,1,0:T(8,128)(2,1)} %shard_map.82), calls=%async_computation.1 | async-start | bytes 3670016 | tf_op jit(solution)/shard_map/all_to_all | solution.py:371
  74.6 1.2 %shard_map.80 = (f32[512,64]{1,0:T(8,128)S(1)}, bf16[128,256]{1,0:T(8,128)(2,1)S(1)}, bf16[128,256]{1,0:T(8,128)(2,1)S(1)}) custom-call(bf16[512,256]{1,0:T(8,128)(2,1)S(1)} %get-tuple-element.32.slab, bf16[9,192,256]{2,1,0:T(8,128)(2,1)S(1)} %bitcast.20), custom_call_target="tpu_custom_call" | custom-call | flops 1048576 | bytes 65536 | tf_op jit(solution)/shard_map/pallas_call | solution.py:394
  75.8 4.8 %collective-permute-start.4 = (bf16[128,256]{1,0:T(8,128)(2,1)S(1)}, bf16[128,256]{1,0:T(8,128)(2,1)S(1)}, u32[]{:S(2)}, u32[]{:S(2)}) collective-permute-start(bf16[128,256]{1,0:T(8,128)(2,1)S(1)} %get-tuple-element.34), channel_id=1, source_target_pairs={{0,8},{8,16},{16,24},{24,32},{32,40},{40,48},{48,56},{56,64},{64,7... | collective-permute-start | bytes 196616 | tf_op jit(solution)/shard_map/ppermute | solution.py:315
  80.6 1.9 %collective-permute-start.5 = (bf16[128,256]{1,0:T(8,128)(2,1)S(1)}, bf16[128,256]{1,0:T(8,128)(2,1)S(1)}, u32[]{:S(2)}, u32[]{:S(2)}) collective-permute-start(bf16[128,256]{1,0:T(8,128)(2,1)S(1)} %get-tuple-element.35), channel_id=1, source_target_pairs={{8,0},{16,8},{24,16},{32,24},{40,32},{48,40},{56,48},{64,56},{72,6... | collective-permute-start | bytes 196616 | tf_op jit(solution)/shard_map/ppermute | solution.py:316
  83.7 2.6 %shard_map.84 = bf16[8,224,128]{2,1,0:T(8,128)(2,1)S(1)} custom-call(s32[4]{0:T(128)S(1)} %pad_add_fusion.place, bf16[512,256]{1,0:T(8,128)(2,1)S(1)} %get-tuple-element.32.slab, bf16[512,256]{1,0:T(8,128)(2,1)S(1)} %collective-permute-done.10.other, bf16[3,34,16,192]{3,2,1,0:T(8,128)(2,1)S(1)} %copy-done.7, bf16[768,256]{1,0:T(8,128)(2,1)S(1)} %collective-permute-done.6.far), custom_call_target="tpu_custom_call" | custom-call | flops 1048576 | bytes 65536 | tf_op jit(solution)/shard_map/pallas_call | solution.py:373
  86.4 2.9 %collective-permute-start.12 = (bf16[448,128]{1,0:T(8,128)(2,1)S(1)}, bf16[448,128]{1,0:T(8,128)(2,1)S(1)}, u32[]{:S(2)}, u32[]{:S(2)}) collective-permute-start(bf16[448,128]{1,0:T(8,128)(2,1)S(1)} %bitcast.26), channel_id=1, source_target_pairs={{0,64},{32,96},{64,0},{96,32},{1,65},{33,97},{65,1},{97,33},{2,66}... | collective-permute-start | bytes 344072 | tf_op jit(solution)/shard_map/ppermute | solution.py:381
  90.7 2.7 %shard_map.83 = bf16[512,256]{1,0:T(8,128)(2,1)} custom-call(bf16[320,256]{1,0:T(8,128)(2,1)S(1)} %get-tuple-element.36.up, bf16[320,256]{1,0:T(8,128)(2,1)S(1)} %copy-done.10, bf16[320,256]{1,0:T(8,128)(2,1)S(1)} %copy-done.12, bf16[320,256]{1,0:T(8,128)(2,1)S(1)} %copy-done.14, bf16[9,3,256,256]{3,2,1,0:T(8,128)(2,1)S(1)} %bitcast.18), custom_call_target="tpu_custom_call" | custom-call | flops 2147483648 | bytes 65536 | tf_op jit(solution)/shard_map/pallas_call | solution.py:385
  93.5 6.9 %collective-permute-done.12.second = bf16[448,128]{1,0:T(8,128)(2,1)S(1)} collective-permute-done((bf16[448,128]{1,0:T(8,128)(2,1)S(1)}, bf16[448,128]{1,0:T(8,128)(2,1)S(1)}, u32[]{:S(2)}, u32[]{:S(2)}) %collective-permute-start.12) | collective-permute-done | bytes 114720 | tf_op jit(solution)/shard_map/ppermute | solution.py:381
  102.6 2.8 %collective-permute-start.14 = (bf16[224,128]{1,0:T(8,128)(2,1)S(1)}, bf16[224,128]{1,0:T(8,128)(2,1)S(1)}, u32[]{:S(2)}, u32[]{:S(2)}) collective-permute-start(bf16[224,128]{1,0:T(8,128)(2,1)S(1)} %slice.23), channel_id=1, source_target_pairs={{0,16},{16,0},{1,17},{17,1},{2,18},{18,2},{3,19},{19,3},{4,20},{20... | collective-permute-start | bytes 172040 | tf_op jit(solution)/shard_map/ppermute | solution.py:393
  (56 shorter events, 16.4 us)
Async XLA Ops:
  0.6 26.7 %copy-start.1 = (bf16[2,8,32,256]{3,2,1,0:T(8,128)(2,1)S(1)}, bf16[2,8,32,256]{3,2,1,0:T(8,128)(2,1)}, u32[]{:S(2)}) copy-start(bf16[2,8,32,256]{3,2,1,0:T(8,128)(2,1)} %own.7) | copy-start | bytes 786436
  2.5 9.1 %collective-permute-start = (bf16[384,256]{1,0:T(8,128)(2,1)}, bf16[384,256]{1,0:T(8,128)(2,1)S(1)}, u32[]{:S(2)}, u32[]{:S(2)}) collective-permute-start(bf16[384,256]{1,0:T(8,128)(2,1)} %get-tuple-element.25), channel_id=1, source_target_pairs={{0,8},{8,16},{16,24},{24,32},{32,40},{40,48},{48,56},{56,64},{64,7... | collective-permute-start | bytes 589832 | tf_op jit(solution)/shard_map/ppermute | solution.py:315
  8.7 8.7 %collective-permute-start.1 = (bf16[384,256]{1,0:T(8,128)(2,1)}, bf16[384,256]{1,0:T(8,128)(2,1)S(1)}, u32[]{:S(2)}, u32[]{:S(2)}) collective-permute-start(bf16[384,256]{1,0:T(8,128)(2,1)} %get-tuple-element.26), channel_id=1, source_target_pairs={{8,0},{16,8},{24,16},{32,24},{40,32},{48,40},{56,48},{64,56},{72,6... | collective-permute-start | bytes 589832 | tf_op jit(solution)/shard_map/ppermute | solution.py:316
  18.4 7.6 %collective-permute-start.2 = (bf16[256,256]{1,0:T(8,128)(2,1)S(1)}, bf16[256,256]{1,0:T(8,128)(2,1)S(1)}, u32[]{:S(2)}, u32[]{:S(2)}) collective-permute-start(bf16[256,256]{1,0:T(8,128)(2,1)S(1)} %get-tuple-element.27), channel_id=1, source_target_pairs={{0,1},{1,2},{2,3},{3,4},{4,5},{5,6},{6,7},{8,9},{9,10},{10,11},{11... | collective-permute-start | bytes 393224 | tf_op jit(solution)/shard_map/ppermute | solution.py:315
  20.7 6.7 %collective-permute-start.3 = (bf16[256,256]{1,0:T(8,128)(2,1)S(1)}, bf16[256,256]{1,0:T(8,128)(2,1)S(1)}, u32[]{:S(2)}, u32[]{:S(2)}) collective-permute-start(bf16[256,256]{1,0:T(8,128)(2,1)S(1)} %get-tuple-element.28), channel_id=1, source_target_pairs={{1,0},{2,1},{3,2},{4,3},{5,4},{6,5},{7,6},{9,8},{10,9},{11,10},{12... | collective-permute-start | bytes 393224 | tf_op jit(solution)/shard_map/ppermute | solution.py:316
  33.9 16.4 %all-to-all-start = ((bf16[8,160,256]{2,1,0:T(8,128)(2,1)}), bf16[8,160,256]{2,1,0:T(8,128)(2,1)S(1)}, u32[]{:S(2)}, u32[]{:S(2)}) async-start(bf16[8,160,256]{2,1,0:T(8,128)(2,1)} %get-tuple-element.30), calls=%async_computation | async-start | bytes 1310720 | tf_op jit(solution)/shard_map/all_to_all | solution.py:349
  40.5 19.3 %collective-permute-start.6 = (bf16[768,256]{1,0:T(8,128)(2,1)}, bf16[768,256]{1,0:T(8,128)(2,1)S(1)}, u32[]{:S(2)}, u32[]{:S(2)}) collective-permute-start(bf16[768,256]{1,0:T(8,128)(2,1)} %get-tuple-element.38), channel_id=1, source_target_pairs={{0,8},{8,0},{1,9},{9,1},{2,10},{10,2},{3,11},{11,3},{4,12},{12,4},... | collective-permute-start | bytes 1179656 | tf_op jit(solution)/shard_map/ppermute | solution.py:348
  50.9 13.2 %copy-start.9 = (bf16[320,256]{1,0:T(8,128)(2,1)}, bf16[320,256]{1,0:T(8,128)(2,1)S(1)}, u32[]{:S(2)}) copy-start(bf16[320,256]{1,0:T(8,128)(2,1)S(1)} %get-tuple-element.37.down) | copy-start | bytes 491524
  50.9 8.9 %collective-permute-start.7 = (bf16[512,256]{1,0:T(8,128)(2,1)S(1)}, bf16[512,256]{1,0:T(8,128)(2,1)S(1)}, u32[]{:S(2)}, u32[]{:S(2)}) collective-permute-start(bf16[512,256]{1,0:T(8,128)(2,1)S(1)} %get-tuple-element.39.grad), channel_id=1, source_target_pairs={{0,8},{8,0},{1,9},{9,1},{2,10},{10,2},{3,11},{11,3},{4,12},{12,4},... | collective-permute-start | bytes 786440 | tf_op jit(solution)/shard_map/ppermute | solution.py:356
  51.0 13.1 %collective-permute-start.8 = (bf16[320,256]{1,0:T(8,128)(2,1)S(1)}, bf16[320,256]{1,0:T(8,128)(2,1)S(1)}, u32[]{:S(2)}, u32[]{:S(2)}) collective-permute-start(bf16[320,256]{1,0:T(8,128)(2,1)S(1)} %get-tuple-element.36.up), channel_id=1, source_target_pairs={{0,8},{8,16},{16,24},{24,32},{32,40},{40,48},{48,56},{56,64},{64,7... | collective-permute-start | bytes 491528 | tf_op jit(solution)/shard_map/ppermute | solution.py:315
  57.9 8.1 %collective-permute-start.9 = (bf16[320,256]{1,0:T(8,128)(2,1)S(1)}, bf16[320,256]{1,0:T(8,128)(2,1)S(1)}, u32[]{:S(2)}, u32[]{:S(2)}) collective-permute-start(bf16[320,256]{1,0:T(8,128)(2,1)S(1)} %get-tuple-element.37.down), channel_id=1, source_target_pairs={{8,0},{16,8},{24,16},{32,24},{40,32},{48,40},{56,48},{64,56},{72,6... | collective-permute-start | bytes 491528 | tf_op jit(solution)/shard_map/ppermute | solution.py:316
  64.1 10.4 %copy-start.5 = (bf16[27,256,64]{1,2,0:T(8,128)(2,1)S(1)}, bf16[27,256,64]{1,2,0:T(8,128)(2,1)}, u32[]{:S(2)}) copy-start(bf16[27,256,64]{1,2,0:T(8,128)(2,1)} %param.6) | copy-start | bytes 2654212
  66.7 41.4 %all-to-all-start.1 = ((bf16[64,54,256]{2,1,0:T(8,128)(2,1)}), bf16[64,54,256]{2,1,0:T(8,128)(2,1)S(1)}, u32[]{:S(2)}, u32[]{:S(2)}) async-start(bf16[64,54,256]{2,1,0:T(8,128)(2,1)} %shard_map.82), calls=%async_computation.1 | async-start | bytes 3670016 | tf_op jit(solution)/shard_map/all_to_all | solution.py:371
  74.5 8.1 %collective-permute-start.10 = (bf16[512,256]{1,0:T(8,128)(2,1)S(1)}, bf16[512,256]{1,0:T(8,128)(2,1)S(1)}, u32[]{:S(2)}, u32[]{:S(2)}) collective-permute-start(bf16[512,256]{1,0:T(8,128)(2,1)S(1)} %get-tuple-element.32.slab), channel_id=1, source_target_pairs={{0,8},{8,0},{1,9},{9,1},{2,10},{10,2},{3,11},{11,3},{4,12},{12,4},... | collective-permute-start | bytes 786440 | tf_op jit(solution)/shard_map/ppermute | solution.py:358
  74.6 16.2 %copy-start.3 = (bf16[27,256,256]{2,1,0:T(8,128)(2,1)S(1)}, bf16[27,256,256]{2,1,0:T(8,128)(2,1)}, u32[]{:S(2)}) copy-start(bf16[27,256,256]{2,1,0:T(8,128)(2,1)} %param.5) | copy-start | bytes 10616836
  75.8 29.6 %collective-permute-start.4 = (bf16[128,256]{1,0:T(8,128)(2,1)S(1)}, bf16[128,256]{1,0:T(8,128)(2,1)S(1)}, u32[]{:S(2)}, u32[]{:S(2)}) collective-permute-start(bf16[128,256]{1,0:T(8,128)(2,1)S(1)} %get-tuple-element.34), channel_id=1, source_target_pairs={{0,8},{8,16},{16,24},{24,32},{32,40},{40,48},{48,56},{56,64},{64,7... | collective-permute-start | bytes 196616 | tf_op jit(solution)/shard_map/ppermute | solution.py:315
  80.6 24.8 %collective-permute-start.5 = (bf16[128,256]{1,0:T(8,128)(2,1)S(1)}, bf16[128,256]{1,0:T(8,128)(2,1)S(1)}, u32[]{:S(2)}, u32[]{:S(2)}) collective-permute-start(bf16[128,256]{1,0:T(8,128)(2,1)S(1)} %get-tuple-element.35), channel_id=1, source_target_pairs={{8,0},{16,8},{24,16},{32,24},{40,32},{48,40},{56,48},{64,56},{72,6... | collective-permute-start | bytes 196616 | tf_op jit(solution)/shard_map/ppermute | solution.py:316
  83.7 7.1 %copy-start.10 = (bf16[320,256]{1,0:T(8,128)(2,1)S(1)}, bf16[320,256]{1,0:T(8,128)(2,1)}, u32[]{:S(2)}) copy-start(bf16[320,256]{1,0:T(8,128)(2,1)} %copy-done.9) | copy-start | bytes 491524
  83.7 7.1 %copy-start.12 = (bf16[320,256]{1,0:T(8,128)(2,1)S(1)}, bf16[320,256]{1,0:T(8,128)(2,1)}, u32[]{:S(2)}) copy-start(bf16[320,256]{1,0:T(8,128)(2,1)} %copy-done.11) | copy-start | bytes 491524
  83.7 7.1 %copy-start.14 = (bf16[320,256]{1,0:T(8,128)(2,1)S(1)}, bf16[320,256]{1,0:T(8,128)(2,1)}, u32[]{:S(2)}) copy-start(bf16[320,256]{1,0:T(8,128)(2,1)} %copy-done.13) | copy-start | bytes 491524
  86.4 14.1 %collective-permute-start.12 = (bf16[448,128]{1,0:T(8,128)(2,1)S(1)}, bf16[448,128]{1,0:T(8,128)(2,1)S(1)}, u32[]{:S(2)}, u32[]{:S(2)}) collective-permute-start(bf16[448,128]{1,0:T(8,128)(2,1)S(1)} %bitcast.26), channel_id=1, source_target_pairs={{0,64},{32,96},{64,0},{96,32},{1,65},{33,97},{65,1},{97,33},{2,66}... | collective-permute-start | bytes 344072 | tf_op jit(solution)/shard_map/ppermute | solution.py:381
  89.3 12.2 %collective-permute-start.13 = (bf16[448,128]{1,0:T(8,128)(2,1)S(1)}, bf16[448,128]{1,0:T(8,128)(2,1)S(1)}, u32[]{:S(2)}, u32[]{:S(2)}) collective-permute-start(bf16[448,128]{1,0:T(8,128)(2,1)S(1)} %bitcast.25), channel_id=1, source_target_pairs={{0,96},{32,0},{64,32},{96,64},{1,97},{33,1},{65,33},{97,65},{2,98}... | collective-permute-start | bytes 344072 | tf_op jit(solution)/shard_map/ppermute | solution.py:381
  90.0 12.5 %collective-permute-start.11 = (bf16[448,128]{1,0:T(8,128)(2,1)S(1)}, bf16[448,128]{1,0:T(8,128)(2,1)S(1)}, u32[]{:S(2)}, u32[]{:S(2)}) collective-permute-start(bf16[448,128]{1,0:T(8,128)(2,1)S(1)} %bitcast.24), channel_id=1, source_target_pairs={{0,32},{32,64},{64,96},{96,0},{1,33},{33,65},{65,97},{97,1},{2,34}... | collective-permute-start | bytes 344072 | tf_op jit(solution)/shard_map/ppermute | solution.py:381
  102.6 4.6 %collective-permute-start.14 = (bf16[224,128]{1,0:T(8,128)(2,1)S(1)}, bf16[224,128]{1,0:T(8,128)(2,1)S(1)}, u32[]{:S(2)}, u32[]{:S(2)}) collective-permute-start(bf16[224,128]{1,0:T(8,128)(2,1)S(1)} %slice.23), channel_id=1, source_target_pairs={{0,16},{16,0},{1,17},{17,1},{2,18},{18,2},{3,19},{19,3},{4,20},{20... | collective-permute-start | bytes 172040 | tf_op jit(solution)/shard_map/ppermute | solution.py:393
  (8 other events, 8.4 us)

commit v5 on v4

--- a/solution.py
+++ b/solution.py
@@ -54,38 +54,49 @@
     return jnp.concatenate(strips, axis=0).reshape(32, 16, 64)
 
 
-def pack_kernel(own, cot, up, down):
+def packed(plane):
+    return jnp.concatenate([plane[128 * k : 128 * k + 128] for k in range(4)], axis=1)
+
+
+def ordered(first, inner, outer):
+    return jnp.where(first, outer, inner), jnp.where(first, inner, outer)
+
+
+def pack_kernel(place, own, cot, inner, outer):
+    first = place[0] == 0
+    low, high = own[0].reshape(256, 256), own[1].reshape(256, 256)
+    inner[:256] = jnp.where(first, high, low)
+    outer[:256] = jnp.where(first, low, high)
     flat = cot[0].reshape(512, 64)
-    packed = jnp.concatenate([flat[128 * k : 128 * k + 128] for k in range(4)], axis=1)
-    up[:256] = own[1].reshape(256, 256)
-    down[:256] = own[0].reshape(256, 256)
-    up[256:] = packed
-    down[256:] = packed
-
-
-def plane_of(own, lo, hi, x):
-    if x == 0 or x == 3:
-        return (lo if x == 0 else hi)[:256].reshape(8, 32, 256)
-    return own[x - 1]
-
-
-def edge_kernel(own, lo, hi, low, high):
-    for x in range(4):
-        plane = plane_of(own, lo, hi, x)
-        low[64 * x : 64 * x + 64] = plane[:2].reshape(64, 256)
-        high[64 * x : 64 * x + 64] = plane[6:].reshape(64, 256)
-
-
-def whole_plane(own, lo, hi, ylo, yhi, x):
-    below = ylo[64 * x : 64 * x + 64].reshape(2, 32, 256)
-    above = yhi[64 * x : 64 * x + 64].reshape(2, 32, 256)
-    return jnp.concatenate([below, plane_of(own, lo, hi, x), above], axis=0)
-
-
-def coarse_back_kernel(cot, lo, hi, w, partial, wide):
-    planes = (unpacked(lo[256:384]), cot[0], unpacked(hi[256:384]))
-    for x in range(3):
-        wide[x] = along_depth(pad_rows(planes[x]), -1)
+    inner[256:] = packed(flat)
+    outer[256:] = packed(flat)
+
+
+def planes_of(place, own, inner, outer):
+    lo, hi = ordered(place[0] == 0, inner[:256], outer[:256])
+    return lo.reshape(8, 32, 256), own[0], own[1], hi.reshape(8, 32, 256)
+
+
+def edge_kernel(place, own, inner, outer, yinner, youter):
+    first = lax.rem(place[3], 2) == 0
+    for x, plane in enumerate(planes_of(place, own, inner, outer)):
+        low, high = plane[:2].reshape(64, 256), plane[6:].reshape(64, 256)
+        yinner[64 * x : 64 * x + 64] = jnp.where(first, high, low)
+        youter[64 * x : 64 * x + 64] = jnp.where(first, low, high)
+
+
+def whole_plane(place, plane, yinner, youter, x):
+    rows = slice(64 * x, 64 * x + 64)
+    below, above = ordered(lax.rem(place[3], 2) == 0, yinner[rows], youter[rows])
+    return jnp.concatenate(
+        [below.reshape(2, 32, 256), plane, above.reshape(2, 32, 256)], axis=0
+    )
+
+
+def coarse_back_kernel(place, cot, inner, outer, w, partial, wide):
+    lo, hi = ordered(place[0] == 0, inner[256:], outer[256:])
+    for x, plane in enumerate((unpacked(lo), cot[0], unpacked(hi))):
+        wide[x] = along_depth(pad_rows(plane), -1)
     total = None
     for k in range(9):
         a, b = divmod(k, 3)
@@ -96,17 +107,18 @@
 
 
 def fine_forward_kernel(
-    place, own, lo, hi, ylo, yhi, partial, w, sent, slope, far, wide, pre, sums, padded
+    place, own, inner, outer, yinner, youter, partial, w,
+    sent, slope, far, wide, pre, sums, padded,
 ):
-    for x in range(4):
-        plane = whole_plane(own, lo, hi, ylo, yhi, x)
+    for x, plane in enumerate(planes_of(place, own, inner, outer)):
+        plane = whole_plane(place, plane, yinner, youter, x)
         wide[x] = along_depth(plane, 1)
 
         @pl.when(place[0] == x // 2)
         def _():
             far[320 * (x % 2) : 320 * (x % 2) + 320] = plane[1:11].reshape(320, 256)
 
-    far[640:] = jnp.where(place[0] == 0, lo[256:384], hi[256:384])
+    far[640:] = outer[256:]
     for k in range(9):
         a, b = divmod(k, 3)
         window = wide[a : a + 2, b : b + 10].reshape(640, 768)
@@ -139,7 +151,7 @@
         sent[k, 64:] = padded[64 * k : 64 * k + 96]
 
 
-def fine_grad_kernel(place, got, slope, grad, up, down, slab, spread):
+def fine_grad_kernel(place, got, slope, grad, slab, spread):
     for y in range(6):
         rows = slice(64 + 16 * y, 80 + 16 * y)
         total = got[0, rows].astype(F32)
@@ -156,27 +168,25 @@
             spread[side, pl.ds(32 * y + 1, 16, stride=2)] = half
         at = slice(y * 32, y * 32 + 32)
         wide = jnp.concatenate([spread[0, at], spread[1, at]], axis=1)
-        for x, out in enumerate((down, up)):
+        for x in range(2):
             for row in (2 * y - 1, 2 * y):
                 if 0 <= row < 10:
                     at = x * 320 + row * 32
-                    value = (wide * slope[at : at + 32]).astype(BF)
-                    out[row * 32 : row * 32 + 32] = value
-                    if 0 < row < 9:
-                        at = x * 256 + row * 32 - 32
-                        grad[at : at + 32] = value
+                    grad[at : at + 32] = (wide * slope[at : at + 32]).astype(BF)
     for k in range(8):
         slab[64 * k : 64 * k + 64] = got[k, :64]
 
 
 def fine_weight_kernel(
-    place, own, lo, hi, ylo, yhi, far, grad, other, terms, wide, turned, total
+    place, own, inner, outer, yinner, youter, far, grad, other, terms, wide, turned, total
 ):
     for core in range(2):
 
         @pl.when(place[0] == core)
         def _():
             planes, windows = set(), set()
+            sides = [side[:256].reshape(8, 32, 256) for side in (inner, outer)]
+            blocks = (sides[1 - core], own[0], own[1], sides[core])
 
             def prepare(bc, slot):
                 if (bc, slot) in windows:
@@ -186,7 +196,7 @@
                     planes.add(slot)
                     x = slot - 2 * core
                     if 0 <= x < 4:
-                        rows = whole_plane(own, lo, hi, ylo, yhi, x)[1:11]
+                        rows = whole_plane(place, blocks[x], yinner, youter, x)[1:11]
                     else:
                         at = 320 * (slot % 2)
                         rows = far[at : at + 320].reshape(10, 32, 256)
@@ -196,7 +206,9 @@
                 turned[bc, slot] = window.reshape(256, 256).T
 
             pair = (grad, other) if core == 0 else (other, grad)
-            right = jnp.concatenate([pair[0][...], pair[1][...]], axis=0)
+            right = jnp.concatenate(
+                [side[at : at + 256] for side in pair for at in (32, 352)], axis=0
+            )
             for k in range(8):
                 at = 432 * (2 * k + core)
                 end = at + 432
@@ -216,16 +228,41 @@
                     terms[k * 8 + f] = total[k % 2, f * 54 : f * 54 + 54].astype(BF)
 
 
-def fine_back_kernel(up, down, lo, hi, w, out, wide, total):
-    for x, plane in enumerate((lo, down, up, hi)):
-        wide[x] = along_depth(plane[...].reshape(10, 32, 256), -1)
+def fine_back_kernel(place, grad, other, w, total, rest, wide):
+    first = place[0] == 0
+    none = jnp.zeros((320, 256), BF)
+    planes = (
+        jnp.where(first, none, other[320:]),
+        grad[:320],
+        grad[320:],
+        jnp.where(first, other[:320], none),
+    )
+    for x, plane in enumerate(planes):
+        wide[x] = along_depth(plane.reshape(10, 32, 256), -1)
     for k in range(9):
         a, b = divmod(k, 3)
         window = wide[2 - a : 4 - a, 2 - b : 10 - b].reshape(512, 768)
         right = jnp.concatenate([w[k, 0], w[k, 1], w[k, 2]], axis=1)
         term = lax.dot_general(window, right, (((1,), (1,)), ((), ())), preferred_element_type=F32)
         total[...] = term if k == 0 else total[...] + term
-    out[...] = total[...].astype(BF)
+    for b in range(3):
+        for c in range(3):
+            at = slice(256 * c, 256 * c + 256)
+            rest[b, :, at] = jnp.where(first, w[6 + b, c], w[b, c])
+
+
+def fine_rest_kernel(place, total, outer, rest, out):
+    wide = along_depth(outer[:320].reshape(10, 32, 256), -1)
+    more = None
+    for b in range(3):
+        window = wide[2 - b : 10 - b].reshape(256, 768)
+        term = lax.dot_general(
+            window, rest[b], (((1,), (1,)), ((), ())), preferred_element_type=F32
+        )
+        more = term if b == 0 else more + term
+    first = place[0] == 0
+    out[:256] = (total[:256] + jnp.where(first, more, 0.0)).astype(BF)
+    out[256:] = (total[256:] + jnp.where(first, 0.0, more)).astype(BF)
 
 
 def coarse_weight_kernel(place, slab, other, wide, far, terms, outer, total):
@@ -258,11 +295,9 @@
                 terms[at] = jnp.concatenate([upper, lower], axis=1).astype(BF)
 
 
-def packed(plane):
-    return jnp.concatenate([plane[128 * k : 128 * k + 128] for k in range(4)], axis=1)
-
-
-def coarse_forward_kernel(slab, w, own, up, down, wide):
+def coarse_forward_kernel(place, slab, w, grad, own, inner, outer, wide):
+    first = place[0] == 0
+    outer[:320] = jnp.where(first, grad[:320], grad[320:])
     wide[...] = along_depth(pad_rows(slab[...].reshape(32, 16, 256)), 1)
     total = None
     for b in range(3):
@@ -276,15 +311,16 @@
         window = wide[b : b + 32].reshape(512, 768)
         term = jnp.dot(window, right, preferred_element_type=F32)
         total = term if b == 0 else total + term
-    up[...] = packed(total[:, :64]).astype(BF)
     own[...] = total[:, 64:128]
-    down[...] = packed(total[:, 128:]).astype(BF)
-
-
-def coarse_out_kernel(own, lo, hi, out):
+    up, down = packed(total[:, :64]).astype(BF), packed(total[:, 128:]).astype(BF)
+    inner[...] = jnp.where(first, up, down)
+    outer[320:] = jnp.where(first, down, up)
+
+
+def coarse_out_kernel(own, inner, outer, out):
     for k in range(4):
         rows, columns = slice(128 * k, 128 * k + 128), slice(64 * k, 64 * k + 64)
-        total = own[rows] + lo[:, columns].astype(F32) + hi[:, columns].astype(F32)
+        total = own[rows] + inner[:, columns].astype(F32) + outer[320:, columns].astype(F32)
         out[rows] = total.astype(BF)
 
 
@@ -309,12 +345,11 @@
     out[...] = jnp.concatenate([total[:, :64], total[:208, 64:]], axis=0).T
 
 
-def swap_sides(up, down, axis):
-    steps = range(lax.axis_size(axis) - 1)
-    return (
-        lax.ppermute(up, axis, [(i, i + 1) for i in steps]),
-        lax.ppermute(down, axis, [(i + 1, i) for i in steps]),
-    )
+def swap(inner, outer, axis):
+    partner = axis[-1]
+    pairs = [(i, i + 1) for i in range(1, lax.axis_size(axis) - 1, 2)]
+    pairs += [(j, i) for i, j in pairs]
+    return lax.ppermute(inner, partner, SWAP), lax.ppermute(outer, axis, pairs)
 
 
 def body(inputs, weight_fine, weight_coarse, cotangent):
@@ -323,17 +358,16 @@
     place = jnp.stack(place).astype(jnp.int32)
     turned_coarse = jnp.swapaxes(weight_coarse, 1, 2).reshape(9, 192, 256)
 
-    pack = call(pack_kernel, (array(384, 256), array(384, 256)), [VMEM] * 2, limit=60)
-    lo, hi = swap_sides(*pack(inputs, cotangent), SP)
-    edge = call(edge_kernel, (array(256, 256), array(256, 256)), [VMEM] * 3)
-    low, high = edge(inputs, lo, hi)
-    ylo, yhi = swap_sides(high, low, FL)
+    pack = call(pack_kernel, (array(384, 256), array(384, 256)), [SMEM] + [VMEM] * 2, limit=60)
+    inner, outer = swap(*pack(place, inputs, cotangent), SP)
+    edge = call(edge_kernel, (array(256, 256), array(256, 256)), [SMEM] + [VMEM] * 3)
+    yinner, youter = swap(*edge(place, inputs, inner, outer), FL)
     partial, wide_cot = call(
         coarse_back_kernel,
         (array(512, 256), array(3, 34, 16, 192)),
-        [VMEM] * 4,
-    )(cotangent, lo, hi, turned_coarse)
-    blocks = (inputs, lo, hi, ylo, yhi)
+        [SMEM] + [VMEM] * 4,
+    )(place, cotangent, inner, outer, turned_coarse)
+    blocks = (inputs, inner, outer, yinner, youter)
     sent, slope, far = call(
         fine_forward_kernel,
         (array(8, 160, 256), array(640, 256, dtype=F32), array(768, 256)),
@@ -347,14 +381,13 @@
     )(place, *blocks, partial, weight_fine.reshape(9, 768, 256))
     far = lax.ppermute(far, "c", SWAP)
     got = lax.all_to_all(sent, FL, 0, 0, tiled=True)
-    grad, up, down, slab = call(
+    grad, slab = call(
         fine_grad_kernel,
-        (array(512, 256), array(320, 256), array(320, 256), array(512, 256)),
+        (array(640, 256), array(512, 256)),
         [SMEM] + [VMEM] * 2,
         [pltpu.VMEM((2, 192, 128), F32)],
     )(place, got, slope)
     other = lax.ppermute(grad, "c", SWAP)
-    lo, hi = swap_sides(up, down, SP)
     across = lax.ppermute(slab, "c", SWAP)
     terms = call(
         fine_weight_kernel,
@@ -367,7 +400,6 @@
         ],
         limit=24,
     )(place, *blocks, far, grad, other)
-    terms, lo, hi = lax.optimization_barrier((terms, lo, hi))
     spread = lax.all_to_all(terms, ("x", "yh", "z", "yl"), 0, 0, tiled=True)
 
     coarse_terms = call(
@@ -376,40 +408,46 @@
         [SMEM] + [VMEM] * 4,
         [pltpu.VMEM((34, 16, 192), BF), pltpu.VMEM((6912, 64), F32)],
     )(place, slab, across, wide_cot, far)
+    coarse_terms, other = lax.optimization_barrier((coarse_terms, other))
     coarse_terms = coarse_terms.reshape(4, 448, 128)
     arrived = [
         lax.ppermute(coarse_terms[step], "x", [(i, (i + step) % 4) for i in range(4)])
         for step in range(1, 4)
     ]
     coarse_terms = call(quad_kernel, array(448, 128), [VMEM] * 4)(coarse_terms[0], *arrived)
-    grad_input = call(
+    centre, inner, outer = call(
+        coarse_forward_kernel,
+        (array(512, 64, dtype=F32), array(128, 256), array(448, 256)),
+        [SMEM] + [VMEM] * 3,
+        [pltpu.VMEM((34, 16, 768), BF)],
+    )(place, slab, turned_coarse, grad)
+    inner, outer = swap(inner, outer, SP)
+    total, rest = call(
         fine_back_kernel,
-        array(512, 256),
-        [VMEM] * 5,
-        [pltpu.VMEM((4, 10, 32, 768), BF), pltpu.VMEM((512, 256), F32)],
+        (array(512, 256, dtype=F32), array(3, 256, 768)),
+        [SMEM] + [VMEM] * 3,
+        [pltpu.VMEM((4, 10, 32, 768), BF)],
         flops=2**31,
-    )(up, down, lo, hi, weight_fine.reshape(9, 3, 256, 256))
-    grad_input, coarse_terms = lax.optimization_barrier((grad_input, coarse_terms))
+    )(place, grad, other, weight_fine.reshape(9, 3, 256, 256))
+    coarse_terms, inner, outer, total = lax.optimization_barrier(
+        (coarse_terms, inner, outer, total)
+    )
+    grad_input = call(fine_rest_kernel, array(512, 256), [SMEM] + [VMEM] * 3, flops=2**30)(
+        place, total, outer, rest
+    )
     arrived = lax.ppermute(coarse_terms[224:], "yh", SWAP)
-    centre, up, down = call(
-        coarse_forward_kernel,
-        (array(512, 64, dtype=F32), array(128, 256), array(128, 256)),
-        [VMEM] * 2,
-        [pltpu.VMEM((34, 16, 768), BF)],
-    )(slab, turned_coarse)
-    lo, hi = swap_sides(up, down, SP)
-    coarse_out = call(coarse_out_kernel, array(512, 64), [VMEM] * 3)(centre, lo, hi)
+    coarse_out = call(coarse_out_kernel, array(512, 64), [VMEM] * 3)(centre, inner, outer)
+    grad_fine = call(
+        functools.partial(fine_sum_kernel, 1.0 / math.sqrt(cells)),
+        array(108, 128, dtype=F32),
+        [VMEM],
+    )(spread)
+    grad_fine, arrived = lax.optimization_barrier((grad_fine, arrived))
     grad_coarse = call(
         functools.partial(coarse_sum_kernel, 1.0 / math.sqrt(cells // 8)),
         array(64, 432, dtype=F32),
         [VMEM] * 2,
     )(coarse_terms, arrived)
-    grad_fine = call(
-        functools.partial(fine_sum_kernel, 1.0 / math.sqrt(cells)),
-        array(108, 128, dtype=F32),
-        [VMEM],
-        flops=2**31,
-    )(spread)
     return (
         coarse_out.reshape(1, 32, 16, 64),
         grad_input.reshape(2, 8, 32, 256),

time: 110 us -> 104 us (0.945)
  waiting for transfers between devices: 29.2 us -> 21.8 us
  starting transfers between devices: 49 us -> 44.1 us
  local copies, waits for them, and re-layouts: 8.44 us -> 12.9 us
  Pallas kernels: 21.3 us -> 23.2 us
    ppermute x8 -> x6, starting transfers between devices: 27.2 us -> 12.9 us  [the longest x3 10.7 us: swap(): lax.ppermute(outer, axis, pairs)]
    unnamed x30 -> x36, local copies, waits for them, and re-layouts: 8.4 us -> 12.9 us
    all_to_all x1, starting transfers between devices: 7.77 us -> 11.1 us  [body(): spread = lax.all_to_all(terms, ('x', 'yh', 'z', 'yl'), 0, 0, tiled=True)]
    ppermute x1, starting transfers between devices: 2.82 us -> 6.1 us  [body(): arrived = lax.ppermute(coarse_terms[224:], 'yh', SWAP)]
    ppermute x8 -> x6, waiting for transfers between devices: 9.43 us -> 6.37 us  [the longest x3 6.36 us: swap(): lax.ppermute(outer, axis, pairs)]
    ppermute x3, waiting for transfers between devices: 9.03 us -> 6.14 us  [body(): lax.ppermute(coarse_terms[step], 'x', [(i, (i + step) % 4) for i in range...]
    pallas_call x6 -> x7, Pallas kernels: 6.95 us -> 9.68 us  [the longest x1 2.64 us: body(): call(fine_back_kernel, (array(512, 256, dtype=F32), array(3, 256, 768)),...]
    all_to_all x1, starting transfers between devices: 6.65 us -> 8.18 us  [body(): got = lax.all_to_all(sent, FL, 0, 0, tiled=True)]
  transfers between devices with their start and end apart: 17 -> 15, of which waited for: 9 -> 5; matrix products, arithmetic and copies ran while one was open for 0% -> 0% of each run, Pallas kernels for 13% -> 12%
where the time goes in v5:
time: 104 us; the launch traced here: 103 us
  starting transfers between devices  44.1 us (42%)
  Pallas kernels  23.2 us (22%)
  waiting for transfers between devices  21.8 us (21%)
  local copies, waits for them, and re-layouts  12.9 us (12%)
    unnamed x36, local copies, waits for them, and re-layouts  12.9 us
    all_to_all x1, starting transfers between devices, body(): spread = lax.all_to_all(terms, ('x', 'yh', 'z', 'yl'), 0, 0, tiled=True)  11.1 us
    ppermute x3, starting transfers between devices, swap(): lax.ppermute(outer, axis, pairs)  10.7 us
    all_to_all x1, waiting for transfers between devices, body(): got = lax.all_to_all(sent, FL, 0, 0, tiled=True)  8.23 us
    all_to_all x1, starting transfers between devices, body(): got = lax.all_to_all(sent, FL, 0, 0, tiled=True)  8.18 us
    ppermute x3, waiting for transfers between devices, swap(): lax.ppermute(outer, axis, pairs)  6.36 us
    ppermute x3, waiting for transfers between devices, body(): lax.ppermute(coarse_terms[step], 'x', [(i, (i + step) % 4) for i in range...  6.14 us
    ppermute x1, starting transfers between devices, body(): arrived = lax.ppermute(coarse_terms[224:], 'yh', SWAP)  6.1 us
  transfers between devices with their start and end apart: 15, of which 5 were waited for; matrix products, arithmetic and copies ran while one was open for 0% of the time, Pallas kernels for 12%

profile of v5, /device:TPU:1, one launch (start us, length us, event | category | flops | bytes accessed | tf_op | source)
XLA Modules:
  0.0 103.4 jit_solution(1353296722769908148)
XLA Ops:
  1.3 1.8 %shard_map.75 = (bf16[384,256]{1,0:T(8,128)(2,1)}, bf16[384,256]{1,0:T(8,128)(2,1)}) custom-call(s32[4]{0:T(128)} %pad_add_fusion.place, bf16[2,8,32,256]{3,2,1,0:T(8,128)(2,1)} %own.7, bf16[1,32,16,64]{3,2,1,0:T(8,128)(2,1)} %cot.3), custom_call_target="tpu_custom_call" | custom-call | flops 1048576 | bytes 65536 | tf_op jit(solution)/shard_map/pallas_call | solution.py:362
  3.1 1.4 %collective-permute-start = (bf16[384,256]{1,0:T(8,128)(2,1)}, bf16[384,256]{1,0:T(8,128)(2,1)S(1)}, u32[]{:S(2)}, u32[]{:S(2)}) collective-permute-start(bf16[384,256]{1,0:T(8,128)(2,1)} %get-tuple-element.28), channel_id=1, source_target_pairs={{0,8},{8,0},{1,9},{9,1},{2,10},{10,2},{3,11},{11,3},{4,12},{12,4},... | collective-permute-start | bytes 589832 | tf_op jit(solution)/shard_map/ppermute | solution.py:352
  4.5 4.8 %collective-permute-start.1 = (bf16[384,256]{1,0:T(8,128)(2,1)}, bf16[384,256]{1,0:T(8,128)(2,1)S(1)}, u32[]{:S(2)}, u32[]{:S(2)}) collective-permute-start(bf16[384,256]{1,0:T(8,128)(2,1)} %get-tuple-element.29), channel_id=1, source_target_pairs={{8,16},{24,32},{40,48},{56,64},{72,80},{88,96},{104,112},{16,8},{3... | collective-permute-start | bytes 589832 | tf_op jit(solution)/shard_map/ppermute | solution.py:352
  9.3 6.4 %collective-permute-done.1.outer = bf16[384,256]{1,0:T(8,128)(2,1)S(1)} collective-permute-done((bf16[384,256]{1,0:T(8,128)(2,1)}, bf16[384,256]{1,0:T(8,128)(2,1)S(1)}, u32[]{:S(2)}, u32[]{:S(2)}) %collective-permute-start.1) | collective-permute-done | bytes 196640 | tf_op jit(solution)/shard_map/ppermute | solution.py:352
  19.3 1.2 %copy-done.5 = bf16[27,256,64]{1,2,0:T(8,128)(2,1)S(1)} copy-done((bf16[27,256,64]{1,2,0:T(8,128)(2,1)S(1)}, bf16[27,256,64]{1,2,0:T(8,128)(2,1)}, u32[]{:S(2)}) %copy-start.5) | copy-done | bytes 884760
  22.0 1.5 %shard_map.77 = (bf16[512,256]{1,0:T(8,128)(2,1)S(1)}, bf16[3,34,16,192]{3,2,1,0:T(8,128)(2,1)S(1)}) custom-call(s32[4]{0:T(128)S(1)} %copy-done.16, bf16[1,32,16,64]{3,2,1,0:T(8,128)(2,1)S(1)} %copy-done.12, bf16[384,256]{1,0:T(8,128)(2,1)S(1)} %collective-permute-done.inner, bf16[384,256]{1,0:T(8,128)(2,1)S(1)} %collective-permute-done.1.outer, ...), custom_call_target="tpu_custom_call" | custom-call | flops 1048576 | bytes 65536 | tf_op jit(solution)/shard_map/pallas_call | solution.py:365
  24.4 2.0 %copy-done.3 = bf16[27,256,256]{2,1,0:T(8,128)(2,1)S(1)} copy-done((bf16[27,256,256]{2,1,0:T(8,128)(2,1)S(1)}, bf16[27,256,256]{2,1,0:T(8,128)(2,1)}, u32[]{:S(2)}) %copy-start.3) | copy-done | bytes 3538968
  26.4 4.5 %shard_map.78 = (bf16[8,160,256]{2,1,0:T(8,128)(2,1)}, f32[640,256]{1,0:T(8,128)S(1)}, bf16[768,256]{1,0:T(8,128)(2,1)}) custom-call(s32[4]{0:T(128)S(1)} %copy-done.17, bf16[2,8,32,256]{3,2,1,0:T(8,128)(2,1)S(1)} %copy-done.2, bf16[384,256]{1,0:T(8,128)(2,1)S(1)} %collective-permute-done.inner, bf16[384,256]{1,0:T(8,128)(2,1)S(1)} %collective-permute-done.1.outer, ...), custom_call_target="tpu_custom_call" | custom-call | flops 1048576 | bytes 65536 | tf_op jit(solution)/shard_map/pallas_call | solution.py:371
  30.9 8.2 %all-to-all-start = ((bf16[8,160,256]{2,1,0:T(8,128)(2,1)}), bf16[8,160,256]{2,1,0:T(8,128)(2,1)S(1)}, u32[]{:S(2)}, u32[]{:S(2)}) async-start(bf16[8,160,256]{2,1,0:T(8,128)(2,1)} %get-tuple-element.33), calls=%async_computation | async-start | bytes 1310720 | tf_op jit(solution)/shard_map/all_to_all | solution.py:383
  39.1 8.2 %all-to-all-done.got = bf16[8,160,256]{2,1,0:T(8,128)(2,1)S(1)} async-done(((bf16[8,160,256]{2,1,0:T(8,128)(2,1)}), bf16[8,160,256]{2,1,0:T(8,128)(2,1)S(1)}, u32[]{:S(2)}, u32[]{:S(2)}) %all-to-all-start) | async-done | bytes 655392 | tf_op jit(solution)/shard_map/all_to_all | solution.py:383
  49.7 3.0 %shard_map.86 = bf16[64,54,256]{2,1,0:T(8,128)(2,1)S(1)} custom-call(s32[4]{0:T(128)S(1)} %copy-done.17, bf16[2,8,32,256]{3,2,1,0:T(8,128)(2,1)S(1)} %copy-done.2, bf16[384,256]{1,0:T(8,128)(2,1)S(1)} %collective-permute-done.inner, bf16[384,256]{1,0:T(8,128)(2,1)S(1)} %collective-permute-done.1.outer, bf16[256,256]{1,0:T(8,128)(2,1)S(1)} %collective-permute-done.2.yinner, ...), custom_call_target="tpu_custom_call" | custom-call | flops 1048576 | bytes 65536 | tf_op jit(solution)/shard_map/pallas_call | solution.py:392
  52.7 1.2 %copy-done = bf16[64,54,256]{2,1,0:T(8,128)(2,1)} copy-done((bf16[64,54,256]{2,1,0:T(8,128)(2,1)}, bf16[64,54,256]{2,1,0:T(8,128)(2,1)S(1)}, u32[]{:S(2)}) %copy-start) | copy-done | bytes 1769496
  54.7 11.1 %all-to-all-start.1 = ((bf16[64,54,256]{2,1,0:T(8,128)(2,1)}), bf16[64,54,256]{2,1,0:T(8,128)(2,1)S(1)}, u32[]{:S(2)}, u32[]{:S(2)}) async-start(bf16[64,54,256]{2,1,0:T(8,128)(2,1)} %copy-done), calls=%async_computation.1 | async-start | bytes 3670016 | tf_op jit(solution)/shard_map/all_to_all | solution.py:403
  67.4 1.8 %shard_map.80 = (f32[512,64]{1,0:T(8,128)S(1)}, bf16[128,256]{1,0:T(8,128)(2,1)S(1)}, bf16[448,256]{1,0:T(8,128)(2,1)S(1)}) custom-call(s32[4]{0:T(128)S(1)} %copy-done.17, bf16[512,256]{1,0:T(8,128)(2,1)S(1)} %copy-done.8, bf16[9,192,256]{2,1,0:T(8,128)(2,1)S(1)} %bitcast.20, bf16[640,256]{1,0:T(8,128)(2,1)S(1)} %get-tuple-element.36.grad), custom_call_target="tpu_custom_call" | custom-call | flops 1048576 | bytes 65536 | tf_op jit(solution)/shard_map/pallas_call | solution.py:418
  69.3 5.2 %collective-permute-start.11 = (bf16[448,256]{1,0:T(8,128)(2,1)S(1)}, bf16[448,256]{1,0:T(8,128)(2,1)S(1)}, u32[]{:S(2)}, u32[]{:S(2)}) collective-permute-start(bf16[448,256]{1,0:T(8,128)(2,1)S(1)} %get-tuple-element.42), channel_id=1, source_target_pairs={{8,16},{24,32},{40,48},{56,64},{72,80},{88,96},{104,112},{16,8},{3... | collective-permute-start | bytes 688136 | tf_op jit(solution)/shard_map/ppermute | solution.py:352
  75.5 1.1 %copy-done.11 = bf16[3,34,16,192]{3,2,1,0:T(8,128)(2,1)S(1)} copy-done((bf16[3,34,16,192]{3,2,1,0:T(8,128)(2,1)S(1)}, bf16[3,34,16,192]{3,2,1,0:T(8,128)(2,1)}, u32[]{:S(2)}) %copy-start.11) | copy-done | bytes 626712
  76.7 2.4 %shard_map.81 = bf16[8,224,128]{2,1,0:T(8,128)(2,1)S(1)} custom-call(s32[4]{0:T(128)S(1)} %copy-done.17, bf16[512,256]{1,0:T(8,128)(2,1)S(1)} %copy-done.9, bf16[512,256]{1,0:T(8,128)(2,1)S(1)} %collective-permute-done.4.other, bf16[3,34,16,192]{3,2,1,0:T(8,128)(2,1)S(1)} %copy-done.11, bf16[768,256]{1,0:T(8,128)(2,1)S(1)} %collective-permute-done.5.far), custom_call_target="tpu_custom_call" | custom-call | flops 1048576 | bytes 65536 | tf_op jit(solution)/shard_map/pallas_call | solution.py:405
  79.1 1.3 %collective-permute-start.7 = (bf16[448,128]{1,0:T(8,128)(2,1)S(1)}, bf16[448,128]{1,0:T(8,128)(2,1)S(1)}, u32[]{:S(2)}, u32[]{:S(2)}) collective-permute-start(bf16[448,128]{1,0:T(8,128)(2,1)S(1)} %bitcast.26), channel_id=1, source_target_pairs={{0,32},{32,64},{64,96},{96,0},{1,33},{33,65},{65,97},{97,1},{2,34}... | collective-permute-start | bytes 344072 | tf_op jit(solution)/shard_map/ppermute | solution.py:414
  80.4 2.6 %collective-permute-start.8 = (bf16[448,128]{1,0:T(8,128)(2,1)S(1)}, bf16[448,128]{1,0:T(8,128)(2,1)S(1)}, u32[]{:S(2)}, u32[]{:S(2)}) collective-permute-start(bf16[448,128]{1,0:T(8,128)(2,1)S(1)} %bitcast.25), channel_id=1, source_target_pairs={{0,64},{32,96},{64,0},{96,32},{1,65},{33,97},{65,1},{97,33},{2,66}... | collective-permute-start | bytes 344072 | tf_op jit(solution)/shard_map/ppermute | solution.py:414
  84.1 2.6 %shard_map.83 = (f32[512,256]{1,0:T(8,128)S(1)}, bf16[3,256,768]{2,1,0:T(8,128)(2,1)S(1)}) custom-call(s32[4]{0:T(128)S(1)} %copy-done.17, bf16[640,256]{1,0:T(8,128)(2,1)S(1)} %get-tuple-element.36.grad, bf16[640,256]{1,0:T(8,128)(2,1)S(1)} %copy-done.14, bf16[9,3,256,256]{3,2,1,0:T(8,128)(2,1)S(1)} %bitcast.18), custom_call_target="tpu_custom_call" | custom-call | flops 2147483648 | bytes 65536 | tf_op jit(solution)/shard_map/pallas_call | solution.py:425
  86.8 4.5 %collective-permute-done.7.first = bf16[448,128]{1,0:T(8,128)(2,1)S(1)} collective-permute-done((bf16[448,128]{1,0:T(8,128)(2,1)S(1)}, bf16[448,128]{1,0:T(8,128)(2,1)S(1)}, u32[]{:S(2)}, u32[]{:S(2)}) %collective-permute-start.7) | collective-permute-done | bytes 114720 | tf_op jit(solution)/shard_map/ppermute | solution.py:414
  91.3 1.6 %collective-permute-done.8.second = bf16[448,128]{1,0:T(8,128)(2,1)S(1)} collective-permute-done((bf16[448,128]{1,0:T(8,128)(2,1)S(1)}, bf16[448,128]{1,0:T(8,128)(2,1)S(1)}, u32[]{:S(2)}, u32[]{:S(2)}) %collective-permute-start.8) | collective-permute-done | bytes 114720 | tf_op jit(solution)/shard_map/ppermute | solution.py:414
  93.0 6.1 %collective-permute-start.12 = (bf16[224,128]{1,0:T(8,128)(2,1)S(1)}, bf16[224,128]{1,0:T(8,128)(2,1)S(1)}, u32[]{:S(2)}, u32[]{:S(2)}) collective-permute-start(bf16[224,128]{1,0:T(8,128)(2,1)S(1)} %slice.23), channel_id=1, source_target_pairs={{0,16},{16,0},{1,17},{17,1},{2,18},{18,2},{3,19},{19,3},{4,20},{20... | collective-permute-start | bytes 172040 | tf_op jit(solution)/shard_map/ppermute | solution.py:438
  99.9 1.8 %shard_map.85 = bf16[512,256]{1,0:T(8,128)(2,1)} custom-call(s32[4]{0:T(128)S(1)} %copy-done.17, f32[512,256]{1,0:T(8,128)S(1)} %get-tuple-element.47.total, bf16[448,256]{1,0:T(8,128)(2,1)S(1)} %collective-permute-done.11.outer, bf16[3,256,768]{2,1,0:T(8,128)(2,1)S(1)} %get-tuple-element.48.rest), custom_call_target="tpu_custom_call" | custom-call | flops 1073741824 | bytes 65536 | tf_op jit(solution)/shard_map/pallas_call | solution.py:435
  (59 shorter events, 16.2 us)
Async XLA Ops:
  0.6 23.7 %copy-start.2 = (bf16[2,8,32,256]{3,2,1,0:T(8,128)(2,1)S(1)}, bf16[2,8,32,256]{3,2,1,0:T(8,128)(2,1)}, u32[]{:S(2)}) copy-start(bf16[2,8,32,256]{3,2,1,0:T(8,128)(2,1)} %own.7) | copy-start | bytes 786436
  1.3 23.1 %copy-start.17 = (s32[4]{0:T(128)S(1)}, s32[4]{0:T(128)}, u32[]{:S(2)}) copy-start(s32[4]{0:T(128)} %pad_add_fusion.place) | copy-start | bytes 52
  3.1 6.2 %collective-permute-start = (bf16[384,256]{1,0:T(8,128)(2,1)}, bf16[384,256]{1,0:T(8,128)(2,1)S(1)}, u32[]{:S(2)}, u32[]{:S(2)}) collective-permute-start(bf16[384,256]{1,0:T(8,128)(2,1)} %get-tuple-element.28), channel_id=1, source_target_pairs={{0,8},{8,0},{1,9},{9,1},{2,10},{10,2},{3,11},{11,3},{4,12},{12,4},... | collective-permute-start | bytes 589832 | tf_op jit(solution)/shard_map/ppermute | solution.py:352
  4.5 11.2 %collective-permute-start.1 = (bf16[384,256]{1,0:T(8,128)(2,1)}, bf16[384,256]{1,0:T(8,128)(2,1)S(1)}, u32[]{:S(2)}, u32[]{:S(2)}) collective-permute-start(bf16[384,256]{1,0:T(8,128)(2,1)} %get-tuple-element.29), channel_id=1, source_target_pairs={{8,16},{24,32},{40,48},{56,64},{72,80},{88,96},{104,112},{16,8},{3... | collective-permute-start | bytes 589832 | tf_op jit(solution)/shard_map/ppermute | solution.py:352
  17.9 6.5 %collective-permute-start.2 = (bf16[256,256]{1,0:T(8,128)(2,1)S(1)}, bf16[256,256]{1,0:T(8,128)(2,1)S(1)}, u32[]{:S(2)}, u32[]{:S(2)}) collective-permute-start(bf16[256,256]{1,0:T(8,128)(2,1)S(1)} %get-tuple-element.30), channel_id=1, source_target_pairs={{0,1},{1,0},{2,3},{3,2},{4,5},{5,4},{6,7},{7,6},{8,9},{9,8},{10,11... | collective-permute-start | bytes 393224 | tf_op jit(solution)/shard_map/ppermute | solution.py:352
  18.6 5.8 %collective-permute-start.3 = (bf16[256,256]{1,0:T(8,128)(2,1)S(1)}, bf16[256,256]{1,0:T(8,128)(2,1)S(1)}, u32[]{:S(2)}, u32[]{:S(2)}) collective-permute-start(bf16[256,256]{1,0:T(8,128)(2,1)S(1)} %get-tuple-element.31), channel_id=1, source_target_pairs={{1,2},{3,4},{5,6},{2,1},{4,3},{6,5},{9,10},{11,12},{13,14},{10,9},... | collective-permute-start | bytes 393224 | tf_op jit(solution)/shard_map/ppermute | solution.py:352
  19.3 1.2 %copy-start.5 = (bf16[27,256,64]{1,2,0:T(8,128)(2,1)S(1)}, bf16[27,256,64]{1,2,0:T(8,128)(2,1)}, u32[]{:S(2)}) copy-start(bf16[27,256,64]{1,2,0:T(8,128)(2,1)} %param.6) | copy-start | bytes 2654212
  24.4 2.0 %copy-start.3 = (bf16[27,256,256]{2,1,0:T(8,128)(2,1)S(1)}, bf16[27,256,256]{2,1,0:T(8,128)(2,1)}, u32[]{:S(2)}) copy-start(bf16[27,256,256]{2,1,0:T(8,128)(2,1)} %param.5) | copy-start | bytes 10616836
  30.9 16.4 %all-to-all-start = ((bf16[8,160,256]{2,1,0:T(8,128)(2,1)}), bf16[8,160,256]{2,1,0:T(8,128)(2,1)S(1)}, u32[]{:S(2)}, u32[]{:S(2)}) async-start(bf16[8,160,256]{2,1,0:T(8,128)(2,1)} %get-tuple-element.33), calls=%async_computation | async-start | bytes 1310720 | tf_op jit(solution)/shard_map/all_to_all | solution.py:383
  39.0 9.0 %collective-permute-start.5 = (bf16[768,256]{1,0:T(8,128)(2,1)}, bf16[768,256]{1,0:T(8,128)(2,1)S(1)}, u32[]{:S(2)}, u32[]{:S(2)}) collective-permute-start(bf16[768,256]{1,0:T(8,128)(2,1)} %get-tuple-element.39), channel_id=1, source_target_pairs={{0,8},{8,0},{1,9},{9,1},{2,10},{10,2},{3,11},{11,3},{4,12},{12,4},... | collective-permute-start | bytes 1179656 | tf_op jit(solution)/shard_map/ppermute | solution.py:382
  48.0 1.7 %collective-permute-start.6 = (bf16[640,256]{1,0:T(8,128)(2,1)S(1)}, bf16[640,256]{1,0:T(8,128)(2,1)S(1)}, u32[]{:S(2)}, u32[]{:S(2)}) collective-permute-start(bf16[640,256]{1,0:T(8,128)(2,1)S(1)} %get-tuple-element.36.grad), channel_id=1, source_target_pairs={{0,8},{8,0},{1,9},{9,1},{2,10},{10,2},{3,11},{11,3},{4,12},{12,4},... | collective-permute-start | bytes 983048 | tf_op jit(solution)/shard_map/ppermute | solution.py:390
  52.7 1.3 %copy-start = (bf16[64,54,256]{2,1,0:T(8,128)(2,1)}, bf16[64,54,256]{2,1,0:T(8,128)(2,1)S(1)}, u32[]{:S(2)}) copy-start(bf16[64,54,256]{2,1,0:T(8,128)(2,1)S(1)} %shard_map.86) | copy-start | bytes 5308420
  54.7 11.8 %copy-start.6 = (bf16[27,256,64]{1,2,0:T(8,128)(2,1)S(1)}, bf16[27,256,64]{1,2,0:T(8,128)(2,1)}, u32[]{:S(2)}) copy-start(bf16[27,256,64]{1,2,0:T(8,128)(2,1)} %param.6) | copy-start | bytes 2654212
  54.7 47.0 %all-to-all-start.1 = ((bf16[64,54,256]{2,1,0:T(8,128)(2,1)}), bf16[64,54,256]{2,1,0:T(8,128)(2,1)S(1)}, u32[]{:S(2)}, u32[]{:S(2)}) async-start(bf16[64,54,256]{2,1,0:T(8,128)(2,1)} %copy-done), calls=%async_computation.1 | async-start | bytes 3670016 | tf_op jit(solution)/shard_map/all_to_all | solution.py:403
  65.8 8.8 %collective-permute-start.4 = (bf16[512,256]{1,0:T(8,128)(2,1)}, bf16[512,256]{1,0:T(8,128)(2,1)S(1)}, u32[]{:S(2)}, u32[]{:S(2)}) collective-permute-start(bf16[512,256]{1,0:T(8,128)(2,1)} %copy-done.7), channel_id=1, source_target_pairs={{0,8},{8,0},{1,9},{9,1},{2,10},{10,2},{3,11},{11,3},{4,12},{12,4},... | collective-permute-start | bytes 786440 | tf_op jit(solution)/shard_map/ppermute | solution.py:391
  67.4 16.7 %copy-start.4 = (bf16[27,256,256]{2,1,0:T(8,128)(2,1)S(1)}, bf16[27,256,256]{2,1,0:T(8,128)(2,1)}, u32[]{:S(2)}) copy-start(bf16[27,256,256]{2,1,0:T(8,128)(2,1)} %param.5) | copy-start | bytes 10616836
  69.2 23.8 %collective-permute-start.10 = (bf16[128,256]{1,0:T(8,128)(2,1)S(1)}, bf16[128,256]{1,0:T(8,128)(2,1)S(1)}, u32[]{:S(2)}, u32[]{:S(2)}) collective-permute-start(bf16[128,256]{1,0:T(8,128)(2,1)S(1)} %get-tuple-element.41), channel_id=1, source_target_pairs={{0,8},{8,0},{1,9},{9,1},{2,10},{10,2},{3,11},{11,3},{4,12},{12,4},... | collective-permute-start | bytes 196616 | tf_op jit(solution)/shard_map/ppermute | solution.py:352
  69.3 23.7 %collective-permute-start.11 = (bf16[448,256]{1,0:T(8,128)(2,1)S(1)}, bf16[448,256]{1,0:T(8,128)(2,1)S(1)}, u32[]{:S(2)}, u32[]{:S(2)}) collective-permute-start(bf16[448,256]{1,0:T(8,128)(2,1)S(1)} %get-tuple-element.42), channel_id=1, source_target_pairs={{8,16},{24,32},{40,48},{56,64},{72,80},{88,96},{104,112},{16,8},{3... | collective-permute-start | bytes 688136 | tf_op jit(solution)/shard_map/ppermute | solution.py:352
  75.5 1.1 %copy-start.11 = (bf16[3,34,16,192]{3,2,1,0:T(8,128)(2,1)S(1)}, bf16[3,34,16,192]{3,2,1,0:T(8,128)(2,1)}, u32[]{:S(2)}) copy-start(bf16[3,34,16,192]{3,2,1,0:T(8,128)(2,1)} %copy-done.10) | copy-start | bytes 1880068
  76.7 7.5 %copy-start.14 = (bf16[640,256]{1,0:T(8,128)(2,1)S(1)}, bf16[640,256]{1,0:T(8,128)(2,1)}, u32[]{:S(2)}) copy-start(bf16[640,256]{1,0:T(8,128)(2,1)} %copy-done.13) | copy-start | bytes 983044
  79.1 12.2 %collective-permute-start.7 = (bf16[448,128]{1,0:T(8,128)(2,1)S(1)}, bf16[448,128]{1,0:T(8,128)(2,1)S(1)}, u32[]{:S(2)}, u32[]{:S(2)}) collective-permute-start(bf16[448,128]{1,0:T(8,128)(2,1)S(1)} %bitcast.26), channel_id=1, source_target_pairs={{0,32},{32,64},{64,96},{96,0},{1,33},{33,65},{65,97},{97,1},{2,34}... | collective-permute-start | bytes 344072 | tf_op jit(solution)/shard_map/ppermute | solution.py:414
  80.4 12.5 %collective-permute-start.8 = (bf16[448,128]{1,0:T(8,128)(2,1)S(1)}, bf16[448,128]{1,0:T(8,128)(2,1)S(1)}, u32[]{:S(2)}, u32[]{:S(2)}) collective-permute-start(bf16[448,128]{1,0:T(8,128)(2,1)S(1)} %bitcast.25), channel_id=1, source_target_pairs={{0,64},{32,96},{64,0},{96,32},{1,65},{33,97},{65,1},{97,33},{2,66}... | collective-permute-start | bytes 344072 | tf_op jit(solution)/shard_map/ppermute | solution.py:414
  83.1 9.9 %collective-permute-start.9 = (bf16[448,128]{1,0:T(8,128)(2,1)S(1)}, bf16[448,128]{1,0:T(8,128)(2,1)S(1)}, u32[]{:S(2)}, u32[]{:S(2)}) collective-permute-start(bf16[448,128]{1,0:T(8,128)(2,1)S(1)} %bitcast.24), channel_id=1, source_target_pairs={{0,96},{32,0},{64,32},{96,64},{1,97},{33,1},{65,33},{97,65},{2,98}... | collective-permute-start | bytes 344072 | tf_op jit(solution)/shard_map/ppermute | solution.py:414
  93.0 9.6 %collective-permute-start.12 = (bf16[224,128]{1,0:T(8,128)(2,1)S(1)}, bf16[224,128]{1,0:T(8,128)(2,1)S(1)}, u32[]{:S(2)}, u32[]{:S(2)}) collective-permute-start(bf16[224,128]{1,0:T(8,128)(2,1)S(1)} %slice.23), channel_id=1, source_target_pairs={{0,16},{16,0},{1,17},{17,1},{2,18},{18,2},{3,19},{19,3},{4,20},{20... | collective-permute-start | bytes 172040 | tf_op jit(solution)/shard_map/ppermute | solution.py:438
  (9 other events, 7.4 us)

commit v6 on v5

--- a/solution.py
+++ b/solution.py
@@ -13,7 +13,7 @@
 BF = jnp.bfloat16
 F32 = jnp.float32
 VMEM = pl.BlockSpec(memory_space=pltpu.VMEM)
-SMEM = pl.BlockSpec(memory_space=pltpu.SMEM)
+ANY = pl.BlockSpec(memory_space=pl.ANY)
 SWAP = [(0, 1), (1, 0)]
 
 
@@ -58,11 +58,17 @@
     return jnp.concatenate([plane[128 * k : 128 * k + 128] for k in range(4)], axis=1)
 
 
+def position():
+    row = 2 * lax.axis_index("z") + lax.axis_index("yl")
+    return lax.axis_index("c"), lax.axis_index("yh"), lax.axis_index("x"), row
+
+
 def ordered(first, inner, outer):
     return jnp.where(first, outer, inner), jnp.where(first, inner, outer)
 
 
-def pack_kernel(place, own, cot, inner, outer):
+def pack_kernel(own, cot, inner, outer):
+    place = position()
     first = place[0] == 0
     low, high = own[0].reshape(256, 256), own[1].reshape(256, 256)
     inner[:256] = jnp.where(first, high, low)
@@ -72,12 +78,26 @@
     outer[256:] = packed(flat)
 
 
+def stage_kernel(token, w_hbm, wc_hbm, own_hbm, cot_hbm, w, wc, own, cot, sems):
+    copies = [pltpu.make_async_copy(w_hbm.at[k], w.at[k], sems.at[k]) for k in range(9)]
+    copies += [
+        pltpu.make_async_copy(wc_hbm, wc, sems.at[9]),
+        pltpu.make_async_copy(own_hbm, own, sems.at[10]),
+        pltpu.make_async_copy(cot_hbm, cot, sems.at[11]),
+    ]
+    for copy in copies:
+        copy.start()
+    for copy in copies:
+        copy.wait()
+
+
 def planes_of(place, own, inner, outer):
     lo, hi = ordered(place[0] == 0, inner[:256], outer[:256])
     return lo.reshape(8, 32, 256), own[0], own[1], hi.reshape(8, 32, 256)
 
 
-def edge_kernel(place, own, inner, outer, yinner, youter):
+def edge_kernel(own, inner, outer, yinner, youter):
+    place = position()
     first = lax.rem(place[3], 2) == 0
     for x, plane in enumerate(planes_of(place, own, inner, outer)):
         low, high = plane[:2].reshape(64, 256), plane[6:].reshape(64, 256)
@@ -93,7 +113,8 @@
     )
 
 
-def coarse_back_kernel(place, cot, inner, outer, w, partial, wide):
+def coarse_back_kernel(cot, inner, outer, w, partial, wide):
+    place = position()
     lo, hi = ordered(place[0] == 0, inner[256:], outer[256:])
     for x, plane in enumerate((unpacked(lo), cot[0], unpacked(hi))):
         wide[x] = along_depth(pad_rows(plane), -1)
@@ -107,9 +128,10 @@
 
 
 def fine_forward_kernel(
-    place, own, inner, outer, yinner, youter, partial, w,
+    own, inner, outer, yinner, youter, partial, w,
     sent, slope, far, wide, pre, sums, padded,
 ):
+    place = position()
     for x, plane in enumerate(planes_of(place, own, inner, outer)):
         plane = whole_plane(place, plane, yinner, youter, x)
         wide[x] = along_depth(plane, 1)
@@ -151,7 +173,8 @@
         sent[k, 64:] = padded[64 * k : 64 * k + 96]
 
 
-def fine_grad_kernel(place, got, slope, grad, slab, spread):
+def fine_grad_kernel(got, slope, grad, slab, spread):
+    place = position()
     for y in range(6):
         rows = slice(64 + 16 * y, 80 + 16 * y)
         total = got[0, rows].astype(F32)
@@ -178,8 +201,9 @@
 
 
 def fine_weight_kernel(
-    place, own, inner, outer, yinner, youter, far, grad, other, terms, wide, turned, total
+    own, inner, outer, yinner, youter, far, grad, other, terms, wide, turned, total
 ):
+    place = position()
     for core in range(2):
 
         @pl.when(place[0] == core)
@@ -228,7 +252,8 @@
                     terms[k * 8 + f] = total[k % 2, f * 54 : f * 54 + 54].astype(BF)
 
 
-def fine_back_kernel(place, grad, other, w, total, rest, wide):
+def fine_back_kernel(grad, other, w, total, rest, wide):
+    place = position()
     first = place[0] == 0
     none = jnp.zeros((320, 256), BF)
     planes = (
@@ -251,7 +276,8 @@
             rest[b, :, at] = jnp.where(first, w[6 + b, c], w[b, c])
 
 
-def fine_rest_kernel(place, total, outer, rest, out):
+def fine_rest_kernel(total, outer, rest, out):
+    place = position()
     wide = along_depth(outer[:320].reshape(10, 32, 256), -1)
     more = None
     for b in range(3):
@@ -265,7 +291,8 @@
     out[256:] = (total[256:] + jnp.where(first, 0.0, more)).astype(BF)
 
 
-def coarse_weight_kernel(place, slab, other, wide, far, terms, outer, total):
+def coarse_weight_kernel(slab, other, wide, far, terms, outer, total):
+    place = position()
     outer[...] = along_depth(pad_rows(unpacked(far[640:768])), -1)
     left = jnp.concatenate([slab[...].T, other[...].T], axis=1)
     for core in range(2):
@@ -295,7 +322,8 @@
                 terms[at] = jnp.concatenate([upper, lower], axis=1).astype(BF)
 
 
-def coarse_forward_kernel(place, slab, w, grad, own, inner, outer, wide):
+def coarse_forward_kernel(slab, w, grad, own, inner, outer, wide):
+    place = position()
     first = place[0] == 0
     outer[:320] = jnp.where(first, grad[:320], grad[320:])
     wide[...] = along_depth(pad_rows(slab[...].reshape(32, 16, 256)), 1)
@@ -354,60 +382,67 @@
 
 def body(inputs, weight_fine, weight_coarse, cotangent):
     cells = 65536
-    place = [lax.axis_index(name) for name in ("c", "yh", "x", FL)]
-    place = jnp.stack(place).astype(jnp.int32)
     turned_coarse = jnp.swapaxes(weight_coarse, 1, 2).reshape(9, 192, 256)
 
-    pack = call(pack_kernel, (array(384, 256), array(384, 256)), [SMEM] + [VMEM] * 2, limit=60)
-    inner, outer = swap(*pack(place, inputs, cotangent), SP)
-    edge = call(edge_kernel, (array(256, 256), array(256, 256)), [SMEM] + [VMEM] * 3)
-    yinner, youter = swap(*edge(place, inputs, inner, outer), FL)
+    pack = call(pack_kernel, (array(384, 256), array(384, 256)), [VMEM] * 2, limit=60)
+    inner, outer = pack(inputs, cotangent)
+    staged = call(
+        stage_kernel,
+        (array(9, 768, 256), array(9, 192, 256), array(2, 8, 32, 256), array(1, 32, 16, 64)),
+        [ANY] * 5,
+        [pltpu.SemaphoreType.DMA((12,))],
+    )(inner, weight_fine.reshape(9, 768, 256), turned_coarse, inputs, cotangent)
+    inner, outer = swap(inner, outer, SP)
+    inner, outer, staged = lax.optimization_barrier((inner, outer, staged))
+    near_fine, near_coarse, near_inputs, near_cotangent = staged
+    edge = call(edge_kernel, (array(256, 256), array(256, 256)), [VMEM] * 3)
+    yinner, youter = swap(*edge(near_inputs, inner, outer), FL)
     partial, wide_cot = call(
         coarse_back_kernel,
         (array(512, 256), array(3, 34, 16, 192)),
-        [SMEM] + [VMEM] * 4,
-    )(place, cotangent, inner, outer, turned_coarse)
+        [VMEM] * 4,
+    )(near_cotangent, inner, outer, near_coarse)
     blocks = (inputs, inner, outer, yinner, youter)
     sent, slope, far = call(
         fine_forward_kernel,
         (array(8, 160, 256), array(640, 256, dtype=F32), array(768, 256)),
-        [SMEM] + [VMEM] * 7,
+        [VMEM] * 7,
         [
             pltpu.VMEM((4, 12, 32, 768), BF),
             pltpu.VMEM((640, 256), F32),
             pltpu.VMEM((2, 128, 128), F32),
             pltpu.VMEM((544, 256), BF),
         ],
-    )(place, *blocks, partial, weight_fine.reshape(9, 768, 256))
+    )(near_inputs, *blocks[1:], partial, near_fine)
     far = lax.ppermute(far, "c", SWAP)
     got = lax.all_to_all(sent, FL, 0, 0, tiled=True)
     grad, slab = call(
         fine_grad_kernel,
         (array(640, 256), array(512, 256)),
-        [SMEM] + [VMEM] * 2,
+        [VMEM] * 2,
         [pltpu.VMEM((2, 192, 128), F32)],
-    )(place, got, slope)
+    )(got, slope)
     other = lax.ppermute(grad, "c", SWAP)
     across = lax.ppermute(slab, "c", SWAP)
     terms = call(
         fine_weight_kernel,
         array(64, 54, 256),
-        [SMEM] + [VMEM] * 8,
+        [VMEM] * 8,
         [
             pltpu.VMEM((6, 10, 32, 768), BF),
             pltpu.VMEM((9, 6, 256, 256), BF),
             pltpu.VMEM((2, 432, 256), F32),
         ],
         limit=24,
-    )(place, *blocks, far, grad, other)
+    )(*blocks, far, grad, other)
     spread = lax.all_to_all(terms, ("x", "yh", "z", "yl"), 0, 0, tiled=True)
 
     coarse_terms = call(
         coarse_weight_kernel,
         array(8, 224, 128),
-        [SMEM] + [VMEM] * 4,
+        [VMEM] * 4,
         [pltpu.VMEM((34, 16, 192), BF), pltpu.VMEM((6912, 64), F32)],
-    )(place, slab, across, wide_cot, far)
+    )(slab, across, wide_cot, far)
     coarse_terms, other = lax.optimization_barrier((coarse_terms, other))
     coarse_terms = coarse_terms.reshape(4, 448, 128)
     arrived = [
@@ -418,23 +453,21 @@
     centre, inner, outer = call(
         coarse_forward_kernel,
         (array(512, 64, dtype=F32), array(128, 256), array(448, 256)),
-        [SMEM] + [VMEM] * 3,
+        [VMEM] * 3,
         [pltpu.VMEM((34, 16, 768), BF)],
-    )(place, slab, turned_coarse, grad)
+    )(slab, turned_coarse, grad)
     inner, outer = swap(inner, outer, SP)
     total, rest = call(
         fine_back_kernel,
         (array(512, 256, dtype=F32), array(3, 256, 768)),
-        [SMEM] + [VMEM] * 3,
+        [VMEM] * 3,
         [pltpu.VMEM((4, 10, 32, 768), BF)],
         flops=2**31,
-    )(place, grad, other, weight_fine.reshape(9, 3, 256, 256))
+    )(grad, other, weight_fine.reshape(9, 3, 256, 256))
     coarse_terms, inner, outer, total = lax.optimization_barrier(
         (coarse_terms, inner, outer, total)
     )
-    grad_input = call(fine_rest_kernel, array(512, 256), [SMEM] + [VMEM] * 3, flops=2**30)(
-        place, total, outer, rest
-    )
+    grad_input = call(fine_rest_kernel, array(512, 256), [VMEM] * 3, flops=2**30)(total, outer, rest)
     arrived = lax.ppermute(coarse_terms[224:], "yh", SWAP)
     coarse_out = call(coarse_out_kernel, array(512, 64), [VMEM] * 3)(centre, inner, outer)
     grad_fine = call(

time: 104 us -> 96.1 us (0.924)
  Pallas kernels: 23.2 us -> 20.5 us
  waiting for transfers between devices: 21.8 us -> 19.3 us
  local copies, waits for them, and re-layouts: 12.9 us -> 11.2 us
    ppermute x3, waiting for transfers between devices: 6.36 us -> 0.01 us  [swap(): lax.ppermute(outer, axis, pairs)]
    all_to_all x1, starting transfers between devices: 11.1 us -> 7.7 us  [body(): spread = lax.all_to_all(terms, ('x', 'yh', 'z', 'yl'), 0, 0, tiled=True)]
    ppermute x1, starting transfers between devices: 0.09 us -> 2.93 us  [body(): other = lax.ppermute(grad, 'c', SWAP)]
    ppermute x3, waiting for transfers between devices: 6.14 us -> 8.74 us  [body(): lax.ppermute(coarse_terms[step], 'x', [(i, (i + step) % 4) for i in range...]
    ppermute x1, starting transfers between devices: 0.01 us -> 1.93 us  [body(): far = lax.ppermute(far, 'c', SWAP)]
    unnamed x36 -> x32, local copies, waits for them, and re-layouts: 12.9 us -> 11.2 us
    ppermute x3, waiting for transfers between devices: 0.01 us -> 1.68 us  [swap(): lax.ppermute(inner, partner, SWAP)]
    ppermute x1, starting transfers between devices: 6.1 us -> 4.45 us  [body(): arrived = lax.ppermute(coarse_terms[224:], 'yh', SWAP)]
  transfers between devices with their start and end apart: 15 -> 15, of which waited for: 5 -> 6; matrix products, arithmetic and copies ran while one was open for 0% -> 0% of each run, Pallas kernels for 12% -> 12%
where the time goes in v6:
time: 96.1 us; the launch traced here: 95.5 us
  starting transfers between devices  43.6 us (45%)
  Pallas kernels  20.5 us (21%)
  waiting for transfers between devices  19.3 us (20%)
  local copies, waits for them, and re-layouts  11.2 us (12%)
    ppermute x3, starting transfers between devices, swap(): lax.ppermute(outer, axis, pairs)  11.9 us
    unnamed x32, local copies, waits for them, and re-layouts  11.2 us
    ppermute x3, waiting for transfers between devices, body(): lax.ppermute(coarse_terms[step], 'x', [(i, (i + step) % 4) for i in range...  8.74 us
    all_to_all x1, starting transfers between devices, body(): got = lax.all_to_all(sent, FL, 0, 0, tiled=True)  8.68 us
    all_to_all x1, starting transfers between devices, body(): spread = lax.all_to_all(terms, ('x', 'yh', 'z', 'yl'), 0, 0, tiled=True)  7.7 us
    all_to_all x1, waiting for transfers between devices, body(): got = lax.all_to_all(sent, FL, 0, 0, tiled=True)  7.66 us
    ppermute x1, starting transfers between devices, body(): arrived = lax.ppermute(coarse_terms[224:], 'yh', SWAP)  4.45 us
    ppermute x3, starting transfers between devices, body(): lax.ppermute(coarse_terms[step], 'x', [(i, (i + step) % 4) for i in range...  4.39 us
  transfers between devices with their start and end apart: 15, of which 6 were waited for; matrix products, arithmetic and copies ran while one was open for 0% of the time, Pallas kernels for 12%

profile of v6, /device:TPU:1, one launch (start us, length us, event | category | flops | bytes accessed | tf_op | source)
XLA Modules:
  0.0 95.5 jit_solution(906829847631255937)
XLA Ops:
  0.6 1.8 %shard_map.75 = (bf16[384,256]{1,0:T(8,128)(2,1)}, bf16[384,256]{1,0:T(8,128)(2,1)}) custom-call(bf16[2,8,32,256]{3,2,1,0:T(8,128)(2,1)} %own.3, bf16[1,32,16,64]{3,2,1,0:T(8,128)(2,1)} %cot_hbm.1), custom_call_target="tpu_custom_call" | custom-call | flops 1048576 | bytes 65536 | tf_op jit(solution)/shard_map/pallas_call | solution.py:388
  2.4 6.2 %collective-permute-start.1 = (bf16[384,256]{1,0:T(8,128)(2,1)}, bf16[384,256]{1,0:T(8,128)(2,1)S(1)}, u32[]{:S(2)}, u32[]{:S(2)}) collective-permute-start(bf16[384,256]{1,0:T(8,128)(2,1)} %get-tuple-element.39), channel_id=1, source_target_pairs={{8,16},{24,32},{40,48},{56,64},{72,80},{88,96},{104,112},{16,8},{3... | collective-permute-start | bytes 589832 | tf_op jit(solution)/shard_map/ppermute | solution.py:380
  8.7 2.0 %copy-done.1 = bf16[27,256,256]{2,1,0:T(8,128)(2,1)S(1)} copy-done((bf16[27,256,256]{2,1,0:T(8,128)(2,1)S(1)}, bf16[27,256,256]{2,1,0:T(8,128)(2,1)}, u32[]{:S(2)}) %copy-start.1) | copy-done | bytes 3538968
  10.7 1.2 %copy-done.3 = bf16[27,256,64]{1,2,0:T(8,128)(2,1)S(1)} copy-done((bf16[27,256,64]{1,2,0:T(8,128)(2,1)S(1)}, bf16[27,256,64]{1,2,0:T(8,128)(2,1)}, u32[]{:S(2)}) %copy-start.3) | copy-done | bytes 884760
  14.7 2.2 %shard_map.76 = (bf16[9,768,256]{2,1,0:T(8,128)(2,1)S(1)}, bf16[9,192,256]{2,1,0:T(8,128)(2,1)S(1)}, bf16[2,8,32,256]{3,2,1,0:T(8,128)(2,1)S(1)}, bf16[1,32,16,64]{3,2,1,0:T(8,128)(2,1)S(1)}) custom-call(bf16[384,256]{1,0:T(8,128)(2,1)S(1)} %copy-done.15, bf16[9,768,256]{2,1,0:T(8,128)(2,1)S(1)} %bitcast.13, bf16[9,192,256]{2,1,0:T(8,128)(2,1)S(1)} %bitcast.15, ...), custom_call_target="tpu_custom_call" | custom-call | flops 1048576 | bytes 65536 | tf_op jit(solution)/shard_map/pallas_call | solution.py:389
  19.9 1.7 %collective-permute-done.2.yinner = bf16[256,256]{1,0:T(8,128)(2,1)S(1)} collective-permute-done((bf16[256,256]{1,0:T(8,128)(2,1)S(1)}, bf16[256,256]{1,0:T(8,128)(2,1)S(1)}, u32[]{:S(2)}, u32[]{:S(2)}) %collective-permute-start.2) | collective-permute-done | bytes 131104 | tf_op jit(solution)/shard_map/ppermute | solution.py:380
  21.6 4.0 %shard_map.79 = (bf16[8,160,256]{2,1,0:T(8,128)(2,1)}, f32[640,256]{1,0:T(8,128)S(1)}, bf16[768,256]{1,0:T(8,128)(2,1)}) custom-call(bf16[2,8,32,256]{3,2,1,0:T(8,128)(2,1)S(1)} %get-tuple-element.44.own, bf16[384,256]{1,0:T(8,128)(2,1)S(1)} %collective-permute-done.inner, bf16[384,256]{1,0:T(8,128)(2,1)S(1)} %collective-permute-done.1.outer, ...), custom_call_target="tpu_custom_call" | custom-call | flops 1048576 | bytes 65536 | tf_op jit(solution)/shard_map/pallas_call | solution.py:406
  25.6 8.7 %all-to-all-start = ((bf16[8,160,256]{2,1,0:T(8,128)(2,1)}), bf16[8,160,256]{2,1,0:T(8,128)(2,1)S(1)}, u32[]{:S(2)}, u32[]{:S(2)}) async-start(bf16[8,160,256]{2,1,0:T(8,128)(2,1)} %get-tuple-element.53), calls=%async_computation | async-start | bytes 1310720 | tf_op jit(solution)/shard_map/all_to_all | solution.py:418
  34.2 1.9 %collective-permute-start.5 = (bf16[768,256]{1,0:T(8,128)(2,1)}, bf16[768,256]{1,0:T(8,128)(2,1)S(1)}, u32[]{:S(2)}, u32[]{:S(2)}) collective-permute-start(bf16[768,256]{1,0:T(8,128)(2,1)} %get-tuple-element.59), channel_id=1, source_target_pairs={{0,8},{8,0},{1,9},{9,1},{2,10},{10,2},{3,11},{11,3},{4,12},{12,4},... | collective-permute-start | bytes 1179656 | tf_op jit(solution)/shard_map/ppermute | solution.py:417
  36.2 7.7 %all-to-all-done.got = bf16[8,160,256]{2,1,0:T(8,128)(2,1)S(1)} async-done(((bf16[8,160,256]{2,1,0:T(8,128)(2,1)}), bf16[8,160,256]{2,1,0:T(8,128)(2,1)S(1)}, u32[]{:S(2)}, u32[]{:S(2)}) %all-to-all-start) | async-done | bytes 655392 | tf_op jit(solution)/shard_map/all_to_all | solution.py:418
  43.9 2.9 %collective-permute-start.6 = (bf16[640,256]{1,0:T(8,128)(2,1)S(1)}, bf16[640,256]{1,0:T(8,128)(2,1)S(1)}, u32[]{:S(2)}, u32[]{:S(2)}) collective-permute-start(bf16[640,256]{1,0:T(8,128)(2,1)S(1)} %get-tuple-element.56.grad), channel_id=1, source_target_pairs={{0,8},{8,0},{1,9},{9,1},{2,10},{10,2},{3,11},{11,3},{4,12},{12,4},... | collective-permute-start | bytes 983048 | tf_op jit(solution)/shard_map/ppermute | solution.py:425
  46.9 1.3 %collective-permute-done.6.other = bf16[640,256]{1,0:T(8,128)(2,1)S(1)} collective-permute-done((bf16[640,256]{1,0:T(8,128)(2,1)S(1)}, bf16[640,256]{1,0:T(8,128)(2,1)S(1)}, u32[]{:S(2)}, u32[]{:S(2)}) %collective-permute-start.6) | collective-permute-done | bytes 327712 | tf_op jit(solution)/shard_map/ppermute | solution.py:425
  48.1 2.5 %shard_map.87 = bf16[64,54,256]{2,1,0:T(8,128)(2,1)S(1)} custom-call(bf16[2,8,32,256]{3,2,1,0:T(8,128)(2,1)S(1)} %copy-done.6, bf16[384,256]{1,0:T(8,128)(2,1)S(1)} %collective-permute-done.inner, bf16[384,256]{1,0:T(8,128)(2,1)S(1)} %collective-permute-done.1.outer, bf16[256,256]{1,0:T(8,128)(2,1)S(1)} %collective-permute-done.2.yinner, ...), custom_call_target="tpu_custom_call" | custom-call | flops 1048576 | bytes 65536 | tf_op jit(solution)/shard_map/pallas_call | solution.py:427
  50.6 1.2 %copy-done = bf16[64,54,256]{2,1,0:T(8,128)(2,1)} copy-done((bf16[64,54,256]{2,1,0:T(8,128)(2,1)}, bf16[64,54,256]{2,1,0:T(8,128)(2,1)S(1)}, u32[]{:S(2)}) %copy-start) | copy-done | bytes 1769496
  51.9 7.7 %all-to-all-start.1 = ((bf16[64,54,256]{2,1,0:T(8,128)(2,1)}), bf16[64,54,256]{2,1,0:T(8,128)(2,1)S(1)}, u32[]{:S(2)}, u32[]{:S(2)}) async-start(bf16[64,54,256]{2,1,0:T(8,128)(2,1)} %copy-done), calls=%async_computation.1 | async-start | bytes 3670016 | tf_op jit(solution)/shard_map/all_to_all | solution.py:438
  61.3 1.2 %shard_map.81 = (f32[512,64]{1,0:T(8,128)S(1)}, bf16[128,256]{1,0:T(8,128)(2,1)S(1)}, bf16[448,256]{1,0:T(8,128)(2,1)S(1)}) custom-call(bf16[512,256]{1,0:T(8,128)(2,1)S(1)} %copy-done.8, bf16[9,192,256]{2,1,0:T(8,128)(2,1)S(1)} %bitcast.16, bf16[640,256]{1,0:T(8,128)(2,1)S(1)} %get-tuple-element.56.grad), custom_call_target="tpu_custom_call" | custom-call | flops 1048576 | bytes 65536 | tf_op jit(solution)/shard_map/pallas_call | solution.py:453
  62.8 5.1 %collective-permute-start.11 = (bf16[448,256]{1,0:T(8,128)(2,1)S(1)}, bf16[448,256]{1,0:T(8,128)(2,1)S(1)}, u32[]{:S(2)}, u32[]{:S(2)}) collective-permute-start(bf16[448,256]{1,0:T(8,128)(2,1)S(1)} %get-tuple-element.62), channel_id=1, source_target_pairs={{8,16},{24,32},{40,48},{56,64},{72,80},{88,96},{104,112},{16,8},{3... | collective-permute-start | bytes 688136 | tf_op jit(solution)/shard_map/ppermute | solution.py:380
  70.0 1.9 %shard_map.82 = bf16[8,224,128]{2,1,0:T(8,128)(2,1)S(1)} custom-call(bf16[512,256]{1,0:T(8,128)(2,1)S(1)} %copy-done.9, bf16[512,256]{1,0:T(8,128)(2,1)S(1)} %collective-permute-done.4.other, bf16[3,34,16,192]{3,2,1,0:T(8,128)(2,1)S(1)} %copy-done.11, bf16[768,256]{1,0:T(8,128)(2,1)S(1)} %collective-permute-done.5.far), custom_call_target="tpu_custom_call" | custom-call | flops 1048576 | bytes 65536 | tf_op jit(solution)/shard_map/pallas_call | solution.py:440
  71.9 2.9 %collective-permute-start.8 = (bf16[448,128]{1,0:T(8,128)(2,1)S(1)}, bf16[448,128]{1,0:T(8,128)(2,1)S(1)}, u32[]{:S(2)}, u32[]{:S(2)}) collective-permute-start(bf16[448,128]{1,0:T(8,128)(2,1)S(1)} %bitcast.22), channel_id=1, source_target_pairs={{0,64},{32,96},{64,0},{96,32},{1,65},{33,97},{65,1},{97,33},{2,66}... | collective-permute-start | bytes 344072 | tf_op jit(solution)/shard_map/ppermute | solution.py:449
  76.3 2.1 %shard_map.84 = (f32[512,256]{1,0:T(8,128)S(1)}, bf16[3,256,768]{2,1,0:T(8,128)(2,1)S(1)}) custom-call(bf16[640,256]{1,0:T(8,128)(2,1)S(1)} %get-tuple-element.56.grad, bf16[640,256]{1,0:T(8,128)(2,1)S(1)} %copy-done.14, bf16[9,3,256,256]{3,2,1,0:T(8,128)(2,1)S(1)} %bitcast.14), custom_call_target="tpu_custom_call" | custom-call | flops 2147483648 | bytes 65536 | tf_op jit(solution)/shard_map/pallas_call | solution.py:460
  78.4 5.9 %collective-permute-done.8.second = bf16[448,128]{1,0:T(8,128)(2,1)S(1)} collective-permute-done((bf16[448,128]{1,0:T(8,128)(2,1)S(1)}, bf16[448,128]{1,0:T(8,128)(2,1)S(1)}, u32[]{:S(2)}, u32[]{:S(2)}) %collective-permute-start.8) | collective-permute-done | bytes 114720 | tf_op jit(solution)/shard_map/ppermute | solution.py:449
  85.1 2.0 %collective-permute-done.7.first = bf16[448,128]{1,0:T(8,128)(2,1)S(1)} collective-permute-done((bf16[448,128]{1,0:T(8,128)(2,1)S(1)}, bf16[448,128]{1,0:T(8,128)(2,1)S(1)}, u32[]{:S(2)}, u32[]{:S(2)}) %collective-permute-start.7) | collective-permute-done | bytes 114720 | tf_op jit(solution)/shard_map/ppermute | solution.py:449
  87.3 4.5 %collective-permute-start.12 = (bf16[224,128]{1,0:T(8,128)(2,1)S(1)}, bf16[224,128]{1,0:T(8,128)(2,1)S(1)}, u32[]{:S(2)}, u32[]{:S(2)}) collective-permute-start(bf16[224,128]{1,0:T(8,128)(2,1)S(1)} %slice.23), channel_id=1, source_target_pairs={{0,16},{16,0},{1,17},{17,1},{2,18},{18,2},{3,19},{19,3},{4,20},{20... | collective-permute-start | bytes 172040 | tf_op jit(solution)/shard_map/ppermute | solution.py:471
  92.5 1.2 %shard_map.86 = bf16[512,256]{1,0:T(8,128)(2,1)} custom-call(f32[512,256]{1,0:T(8,128)S(1)} %get-tuple-element.67.total, bf16[448,256]{1,0:T(8,128)(2,1)S(1)} %collective-permute-done.11.outer, bf16[3,256,768]{2,1,0:T(8,128)(2,1)S(1)} %get-tuple-element.68.rest), custom_call_target="tpu_custom_call" | custom-call | flops 1073741824 | bytes 65536 | tf_op jit(solution)/shard_map/pallas_call | solution.py:470
  (55 shorter events, 15.0 us)
Async XLA Ops:
  2.4 14.4 %collective-permute-start.1 = (bf16[384,256]{1,0:T(8,128)(2,1)}, bf16[384,256]{1,0:T(8,128)(2,1)S(1)}, u32[]{:S(2)}, u32[]{:S(2)}) collective-permute-start(bf16[384,256]{1,0:T(8,128)(2,1)} %get-tuple-element.39), channel_id=1, source_target_pairs={{8,16},{24,32},{40,48},{56,64},{72,80},{88,96},{104,112},{16,8},{3... | collective-permute-start | bytes 589832 | tf_op jit(solution)/shard_map/ppermute | solution.py:380
  8.6 8.2 %collective-permute-start = (bf16[384,256]{1,0:T(8,128)(2,1)}, bf16[384,256]{1,0:T(8,128)(2,1)S(1)}, u32[]{:S(2)}, u32[]{:S(2)}) collective-permute-start(bf16[384,256]{1,0:T(8,128)(2,1)} %get-tuple-element.38.token), channel_id=1, source_target_pairs={{0,8},{8,0},{1,9},{9,1},{2,10},{10,2},{3,11},{11,3},{4,12},{12,4},... | collective-permute-start | bytes 589832 | tf_op jit(solution)/shard_map/ppermute | solution.py:380
  8.7 2.0 %copy-start.1 = (bf16[27,256,256]{2,1,0:T(8,128)(2,1)S(1)}, bf16[27,256,256]{2,1,0:T(8,128)(2,1)}, u32[]{:S(2)}) copy-start(bf16[27,256,256]{2,1,0:T(8,128)(2,1)} %param.5) | copy-start | bytes 10616836
  10.7 1.2 %copy-start.3 = (bf16[27,256,64]{1,2,0:T(8,128)(2,1)S(1)}, bf16[27,256,64]{1,2,0:T(8,128)(2,1)}, u32[]{:S(2)}) copy-start(bf16[27,256,64]{1,2,0:T(8,128)(2,1)} %param.6) | copy-start | bytes 2654212
  16.9 4.7 %collective-permute-start.2 = (bf16[256,256]{1,0:T(8,128)(2,1)S(1)}, bf16[256,256]{1,0:T(8,128)(2,1)S(1)}, u32[]{:S(2)}, u32[]{:S(2)}) collective-permute-start(bf16[256,256]{1,0:T(8,128)(2,1)S(1)} %get-tuple-element.47), channel_id=1, source_target_pairs={{0,1},{1,0},{2,3},{3,2},{4,5},{5,4},{6,7},{7,6},{8,9},{9,8},{10,11... | collective-permute-start | bytes 393224 | tf_op jit(solution)/shard_map/ppermute | solution.py:380
  17.4 4.2 %collective-permute-start.3 = (bf16[256,256]{1,0:T(8,128)(2,1)S(1)}, bf16[256,256]{1,0:T(8,128)(2,1)S(1)}, u32[]{:S(2)}, u32[]{:S(2)}) collective-permute-start(bf16[256,256]{1,0:T(8,128)(2,1)S(1)} %get-tuple-element.48), channel_id=1, source_target_pairs={{1,2},{3,4},{5,6},{2,1},{4,3},{6,5},{9,10},{11,12},{13,14},{10,9},... | collective-permute-start | bytes 393224 | tf_op jit(solution)/shard_map/ppermute | solution.py:380
  25.5 22.6 %copy-start.6 = (bf16[2,8,32,256]{3,2,1,0:T(8,128)(2,1)S(1)}, bf16[2,8,32,256]{3,2,1,0:T(8,128)(2,1)}, u32[]{:S(2)}) copy-start(bf16[2,8,32,256]{3,2,1,0:T(8,128)(2,1)} %own.3) | copy-start | bytes 786436
  25.6 18.3 %all-to-all-start = ((bf16[8,160,256]{2,1,0:T(8,128)(2,1)}), bf16[8,160,256]{2,1,0:T(8,128)(2,1)S(1)}, u32[]{:S(2)}, u32[]{:S(2)}) async-start(bf16[8,160,256]{2,1,0:T(8,128)(2,1)} %get-tuple-element.53), calls=%async_computation | async-start | bytes 1310720 | tf_op jit(solution)/shard_map/all_to_all | solution.py:418
  34.2 12.7 %collective-permute-start.5 = (bf16[768,256]{1,0:T(8,128)(2,1)}, bf16[768,256]{1,0:T(8,128)(2,1)S(1)}, u32[]{:S(2)}, u32[]{:S(2)}) collective-permute-start(bf16[768,256]{1,0:T(8,128)(2,1)} %get-tuple-element.59), channel_id=1, source_target_pairs={{0,8},{8,0},{1,9},{9,1},{2,10},{10,2},{3,11},{11,3},{4,12},{12,4},... | collective-permute-start | bytes 1179656 | tf_op jit(solution)/shard_map/ppermute | solution.py:417
  43.9 6.7 %copy-start.7 = (bf16[512,256]{1,0:T(8,128)(2,1)}, bf16[512,256]{1,0:T(8,128)(2,1)S(1)}, u32[]{:S(2)}) copy-start(bf16[512,256]{1,0:T(8,128)(2,1)S(1)} %get-tuple-element.55.slab) | copy-start | bytes 786436
  43.9 4.2 %collective-permute-start.6 = (bf16[640,256]{1,0:T(8,128)(2,1)S(1)}, bf16[640,256]{1,0:T(8,128)(2,1)S(1)}, u32[]{:S(2)}, u32[]{:S(2)}) collective-permute-start(bf16[640,256]{1,0:T(8,128)(2,1)S(1)} %get-tuple-element.56.grad), channel_id=1, source_target_pairs={{0,8},{8,0},{1,9},{9,1},{2,10},{10,2},{3,11},{11,3},{4,12},{12,4},... | collective-permute-start | bytes 983048 | tf_op jit(solution)/shard_map/ppermute | solution.py:425
  48.1 2.5 %copy-start.13 = (bf16[640,256]{1,0:T(8,128)(2,1)}, bf16[640,256]{1,0:T(8,128)(2,1)S(1)}, u32[]{:S(2)}) copy-start(bf16[640,256]{1,0:T(8,128)(2,1)S(1)} %collective-permute-done.6.other) | copy-start | bytes 983044
  50.6 1.3 %copy-start = (bf16[64,54,256]{2,1,0:T(8,128)(2,1)}, bf16[64,54,256]{2,1,0:T(8,128)(2,1)S(1)}, u32[]{:S(2)}) copy-start(bf16[64,54,256]{2,1,0:T(8,128)(2,1)S(1)} %shard_map.87) | copy-start | bytes 5308420
  51.9 8.4 %copy-start.4 = (bf16[27,256,64]{1,2,0:T(8,128)(2,1)S(1)}, bf16[27,256,64]{1,2,0:T(8,128)(2,1)}, u32[]{:S(2)}) copy-start(bf16[27,256,64]{1,2,0:T(8,128)(2,1)} %param.6) | copy-start | bytes 2654212
  51.9 41.9 %all-to-all-start.1 = ((bf16[64,54,256]{2,1,0:T(8,128)(2,1)}), bf16[64,54,256]{2,1,0:T(8,128)(2,1)S(1)}, u32[]{:S(2)}, u32[]{:S(2)}) async-start(bf16[64,54,256]{2,1,0:T(8,128)(2,1)} %copy-done), calls=%async_computation.1 | async-start | bytes 3670016 | tf_op jit(solution)/shard_map/all_to_all | solution.py:438
  59.6 8.3 %collective-permute-start.4 = (bf16[512,256]{1,0:T(8,128)(2,1)}, bf16[512,256]{1,0:T(8,128)(2,1)S(1)}, u32[]{:S(2)}, u32[]{:S(2)}) collective-permute-start(bf16[512,256]{1,0:T(8,128)(2,1)} %copy-done.7), channel_id=1, source_target_pairs={{0,8},{8,0},{1,9},{9,1},{2,10},{10,2},{3,11},{11,3},{4,12},{12,4},... | collective-permute-start | bytes 786440 | tf_op jit(solution)/shard_map/ppermute | solution.py:426
  61.3 15.1 %copy-start.2 = (bf16[27,256,256]{2,1,0:T(8,128)(2,1)S(1)}, bf16[27,256,256]{2,1,0:T(8,128)(2,1)}, u32[]{:S(2)}) copy-start(bf16[27,256,256]{2,1,0:T(8,128)(2,1)} %param.5) | copy-start | bytes 10616836
  62.5 24.8 %collective-permute-start.10 = (bf16[128,256]{1,0:T(8,128)(2,1)S(1)}, bf16[128,256]{1,0:T(8,128)(2,1)S(1)}, u32[]{:S(2)}, u32[]{:S(2)}) collective-permute-start(bf16[128,256]{1,0:T(8,128)(2,1)S(1)} %get-tuple-element.61), channel_id=1, source_target_pairs={{0,8},{8,0},{1,9},{9,1},{2,10},{10,2},{3,11},{11,3},{4,12},{12,4},... | collective-permute-start | bytes 196616 | tf_op jit(solution)/shard_map/ppermute | solution.py:380
  62.8 24.5 %collective-permute-start.11 = (bf16[448,256]{1,0:T(8,128)(2,1)S(1)}, bf16[448,256]{1,0:T(8,128)(2,1)S(1)}, u32[]{:S(2)}, u32[]{:S(2)}) collective-permute-start(bf16[448,256]{1,0:T(8,128)(2,1)S(1)} %get-tuple-element.62), channel_id=1, source_target_pairs={{8,16},{24,32},{40,48},{56,64},{72,80},{88,96},{104,112},{16,8},{3... | collective-permute-start | bytes 688136 | tf_op jit(solution)/shard_map/ppermute | solution.py:380
  70.0 6.4 %copy-start.14 = (bf16[640,256]{1,0:T(8,128)(2,1)S(1)}, bf16[640,256]{1,0:T(8,128)(2,1)}, u32[]{:S(2)}) copy-start(bf16[640,256]{1,0:T(8,128)(2,1)} %copy-done.13) | copy-start | bytes 983044
  71.9 12.4 %collective-permute-start.8 = (bf16[448,128]{1,0:T(8,128)(2,1)S(1)}, bf16[448,128]{1,0:T(8,128)(2,1)S(1)}, u32[]{:S(2)}, u32[]{:S(2)}) collective-permute-start(bf16[448,128]{1,0:T(8,128)(2,1)S(1)} %bitcast.22), channel_id=1, source_target_pairs={{0,64},{32,96},{64,0},{96,32},{1,65},{33,97},{65,1},{97,33},{2,66}... | collective-permute-start | bytes 344072 | tf_op jit(solution)/shard_map/ppermute | solution.py:449
  74.9 10.3 %collective-permute-start.9 = (bf16[448,128]{1,0:T(8,128)(2,1)S(1)}, bf16[448,128]{1,0:T(8,128)(2,1)S(1)}, u32[]{:S(2)}, u32[]{:S(2)}) collective-permute-start(bf16[448,128]{1,0:T(8,128)(2,1)S(1)} %bitcast.21), channel_id=1, source_target_pairs={{0,96},{32,0},{64,32},{96,64},{1,97},{33,1},{65,33},{97,65},{2,98}... | collective-permute-start | bytes 344072 | tf_op jit(solution)/shard_map/ppermute | solution.py:449
  75.6 11.6 %collective-permute-start.7 = (bf16[448,128]{1,0:T(8,128)(2,1)S(1)}, bf16[448,128]{1,0:T(8,128)(2,1)S(1)}, u32[]{:S(2)}, u32[]{:S(2)}) collective-permute-start(bf16[448,128]{1,0:T(8,128)(2,1)S(1)} %bitcast.20), channel_id=1, source_target_pairs={{0,32},{32,64},{64,96},{96,0},{1,33},{33,65},{65,97},{97,1},{2,34}... | collective-permute-start | bytes 344072 | tf_op jit(solution)/shard_map/ppermute | solution.py:449
  87.3 7.4 %collective-permute-start.12 = (bf16[224,128]{1,0:T(8,128)(2,1)S(1)}, bf16[224,128]{1,0:T(8,128)(2,1)S(1)}, u32[]{:S(2)}, u32[]{:S(2)}) collective-permute-start(bf16[224,128]{1,0:T(8,128)(2,1)S(1)} %slice.23), channel_id=1, source_target_pairs={{0,16},{16,0},{1,17},{17,1},{2,18},{18,2},{3,19},{19,3},{4,20},{20... | collective-permute-start | bytes 172040 | tf_op jit(solution)/shard_map/ppermute | solution.py:471
  (7 other events, 6.7 us)

commit v7 on v6

--- a/solution.py
+++ b/solution.py
@@ -78,13 +78,9 @@
     outer[256:] = packed(flat)
 
 
-def stage_kernel(token, w_hbm, wc_hbm, own_hbm, cot_hbm, w, wc, own, cot, sems):
-    copies = [pltpu.make_async_copy(w_hbm.at[k], w.at[k], sems.at[k]) for k in range(9)]
-    copies += [
-        pltpu.make_async_copy(wc_hbm, wc, sems.at[9]),
-        pltpu.make_async_copy(own_hbm, own, sems.at[10]),
-        pltpu.make_async_copy(cot_hbm, cot, sems.at[11]),
-    ]
+def stage_kernel(token, wc_hbm, own_hbm, cot_hbm, wc, own, cot, sems):
+    pairs = ((wc_hbm, wc), (own_hbm, own), (cot_hbm, cot))
+    copies = [pltpu.make_async_copy(*pair, sems.at[k]) for k, pair in enumerate(pairs)]
     for copy in copies:
         copy.start()
     for copy in copies:
@@ -113,7 +109,7 @@
     )
 
 
-def coarse_back_kernel(cot, inner, outer, w, partial, wide):
+def coarse_back_kernel(cot, inner, outer, w, partial, wide, padded):
     place = position()
     lo, hi = ordered(place[0] == 0, inner[256:], outer[256:])
     for x, plane in enumerate((unpacked(lo), cot[0], unpacked(hi))):
@@ -124,12 +120,15 @@
         window = wide[2 - a, 2 - b : 34 - b].reshape(512, 192)
         term = jnp.dot(window, w[k], preferred_element_type=F32)
         total = term if k == 0 else total + term
-    partial[...] = total.astype(BF)
+    padded[:16] = jnp.zeros((16, 256), BF)
+    padded[16:528] = total.astype(BF)
+    padded[528:] = jnp.zeros((16, 256), BF)
+    for k in range(8):
+        partial[k] = padded[64 * k : 64 * k + 96]
 
 
 def fine_forward_kernel(
-    own, inner, outer, yinner, youter, partial, w,
-    sent, slope, far, wide, pre, sums, padded,
+    own, inner, outer, yinner, youter, w, sent, slope, far, wide, pre, sums,
 ):
     place = position()
     for x, plane in enumerate(planes_of(place, own, inner, outer)):
@@ -165,21 +164,17 @@
         odd = sums[side, pl.ds(1, 64, stride=2)]
         pooled.append(((even + odd) * 0.125).astype(BF))
     pooled = jnp.concatenate(pooled, axis=1)
-    padded[:16] = jnp.zeros((16, 256), BF)
-    padded[16:528] = partial[...]
-    padded[528:] = jnp.zeros((16, 256), BF)
     for k in range(8):
-        sent[k, :64] = pooled
-        sent[k, 64:] = padded[64 * k : 64 * k + 96]
-
-
-def fine_grad_kernel(got, slope, grad, slab, spread):
+        sent[k] = pooled
+
+
+def fine_grad_kernel(parts, slope, grad, spread):
     place = position()
     for y in range(6):
-        rows = slice(64 + 16 * y, 80 + 16 * y)
-        total = got[0, rows].astype(F32)
+        rows = slice(16 * y, 16 * y + 16)
+        total = parts[0, rows].astype(F32)
         for k in range(1, 8):
-            total = total + got[k, rows].astype(F32)
+            total = total + parts[k, rows].astype(F32)
         total = total.astype(BF).astype(F32)
         if y == 0:
             total = jnp.where(place[3] > 0, total, 0.0)
@@ -196,8 +191,6 @@
                 if 0 <= row < 10:
                     at = x * 320 + row * 32
                     grad[at : at + 32] = (wide * slope[at : at + 32]).astype(BF)
-    for k in range(8):
-        slab[64 * k : 64 * k + 64] = got[k, :64]
 
 
 def fine_weight_kernel(
@@ -388,42 +381,44 @@
     inner, outer = pack(inputs, cotangent)
     staged = call(
         stage_kernel,
-        (array(9, 768, 256), array(9, 192, 256), array(2, 8, 32, 256), array(1, 32, 16, 64)),
-        [ANY] * 5,
-        [pltpu.SemaphoreType.DMA((12,))],
-    )(inner, weight_fine.reshape(9, 768, 256), turned_coarse, inputs, cotangent)
+        (array(9, 192, 256), array(2, 8, 32, 256), array(1, 32, 16, 64)),
+        [ANY] * 4,
+        [pltpu.SemaphoreType.DMA((3,))],
+    )(inner, turned_coarse, inputs, cotangent)
     inner, outer = swap(inner, outer, SP)
     inner, outer, staged = lax.optimization_barrier((inner, outer, staged))
-    near_fine, near_coarse, near_inputs, near_cotangent = staged
+    near_coarse, near_inputs, near_cotangent = staged
     edge = call(edge_kernel, (array(256, 256), array(256, 256)), [VMEM] * 3)
     yinner, youter = swap(*edge(near_inputs, inner, outer), FL)
     partial, wide_cot = call(
         coarse_back_kernel,
-        (array(512, 256), array(3, 34, 16, 192)),
+        (array(8, 96, 256), array(3, 34, 16, 192)),
         [VMEM] * 4,
+        [pltpu.VMEM((544, 256), BF)],
     )(near_cotangent, inner, outer, near_coarse)
+    partial, yinner, youter = lax.optimization_barrier((partial, yinner, youter))
+    parts = lax.all_to_all(partial, FL, 0, 0, tiled=True)
     blocks = (inputs, inner, outer, yinner, youter)
     sent, slope, far = call(
         fine_forward_kernel,
-        (array(8, 160, 256), array(640, 256, dtype=F32), array(768, 256)),
-        [VMEM] * 7,
+        (array(8, 64, 256), array(640, 256, dtype=F32), array(768, 256)),
+        [VMEM] * 6,
         [
             pltpu.VMEM((4, 12, 32, 768), BF),
             pltpu.VMEM((640, 256), F32),
             pltpu.VMEM((2, 128, 128), F32),
-            pltpu.VMEM((544, 256), BF),
         ],
-    )(near_inputs, *blocks[1:], partial, near_fine)
+    )(*blocks, weight_fine.reshape(9, 768, 256))
     far = lax.ppermute(far, "c", SWAP)
     got = lax.all_to_all(sent, FL, 0, 0, tiled=True)
-    grad, slab = call(
+    slab = got.reshape(512, 256)
+    grad = call(
         fine_grad_kernel,
-        (array(640, 256), array(512, 256)),
+        array(640, 256),
         [VMEM] * 2,
         [pltpu.VMEM((2, 192, 128), F32)],
-    )(got, slope)
+    )(parts, slope)
     other = lax.ppermute(grad, "c", SWAP)
-    across = lax.ppermute(slab, "c", SWAP)
     terms = call(
         fine_weight_kernel,
         array(64, 54, 256),
@@ -435,8 +430,10 @@
         ],
         limit=24,
     )(*blocks, far, grad, other)
+    terms, slab = lax.optimization_barrier((terms, slab))
     spread = lax.all_to_all(terms, ("x", "yh", "z", "yl"), 0, 0, tiled=True)
 
+    across = lax.ppermute(slab, "c", SWAP)
     coarse_terms = call(
         coarse_weight_kernel,
         array(8, 224, 128),

time: 96.1 us -> 94.4 us (0.982)
  starting transfers between devices: 43.6 us -> 46.9 us
  waiting for transfers between devices: 19.3 us -> 16.3 us
  local copies, waits for them, and re-layouts: 11.2 us -> 9.04 us
    all_to_all x0 -> x1, starting transfers between devices: none -> 7.83 us  [body(): parts = lax.all_to_all(partial, FL, 0, 0, tiled=True)]
    all_to_all x1, starting transfers between devices: 8.68 us -> 3.41 us  [body(): got = lax.all_to_all(sent, FL, 0, 0, tiled=True)]
    all_to_all x1, waiting for transfers between devices: 7.66 us -> 3.33 us  [body(): got = lax.all_to_all(sent, FL, 0, 0, tiled=True)]
    all_to_all x0 -> x1, waiting for transfers between devices: none -> 3.5 us  [body(): parts = lax.all_to_all(partial, FL, 0, 0, tiled=True)]
    ppermute x1, starting transfers between devices: 2.93 us -> 0.5 us  [body(): other = lax.ppermute(grad, 'c', SWAP)]
    ppermute x1, starting transfers between devices: 4.45 us -> 6.65 us  [body(): arrived = lax.ppermute(coarse_terms[224:], 'yh', SWAP)]
    unnamed x32 -> x28, local copies, waits for them, and re-layouts: 11.2 us -> 9 us
    ppermute x1, starting transfers between devices: 1.93 us -> 0.01 us  [body(): far = lax.ppermute(far, 'c', SWAP)]
  transfers between devices with their start and end apart: 15 -> 16, of which waited for: 6 -> 7; matrix products, arithmetic and copies ran while one was open for 0% -> 0% of each run, Pallas kernels for 12% -> 19%
where the time goes in v7:
time: 94.4 us; the launch traced here: 93.6 us
  starting transfers between devices  46.9 us (50%)
  Pallas kernels  20.5 us (22%)
  waiting for transfers between devices  16.3 us (17%)
  local copies, waits for them, and re-layouts  9.04 us (10%)
    ppermute x3, starting transfers between devices, swap(): lax.ppermute(outer, axis, pairs)  10.5 us
    all_to_all x1, starting transfers between devices, body(): spread = lax.all_to_all(terms, ('x', 'yh', 'z', 'yl'), 0, 0, tiled=True)  9.37 us
    unnamed x28, local copies, waits for them, and re-layouts  9 us
    all_to_all x1, starting transfers between devices, body(): parts = lax.all_to_all(partial, FL, 0, 0, tiled=True)  7.83 us
    ppermute x3, waiting for transfers between devices, body(): lax.ppermute(coarse_terms[step], 'x', [(i, (i + step) % 4) for i in range...  7 us
    ppermute x1, starting transfers between devices, body(): arrived = lax.ppermute(coarse_terms[224:], 'yh', SWAP)  6.65 us
    ppermute x3, starting transfers between devices, body(): lax.ppermute(coarse_terms[step], 'x', [(i, (i + step) % 4) for i in range...  4.98 us
    pallas_call x1, Pallas kernels, body(): call(fine_weight_kernel, array(64, 54, 256), [VMEM] * 8, [pltpu.VMEM((6,...  3.75 us
  transfers between devices with their start and end apart: 16, of which 7 were waited for; matrix products, arithmetic and copies ran while one was open for 0% of the time, Pallas kernels for 19%

profile of v7, /device:TPU:1, one launch (start us, length us, event | category | flops | bytes accessed | tf_op | source)
XLA Modules:
  0.0 93.6 jit_solution(15401737853673341513)
XLA Ops:
  0.6 1.8 %shard_map.75 = (bf16[384,256]{1,0:T(8,128)(2,1)}, bf16[384,256]{1,0:T(8,128)(2,1)}) custom-call(bf16[2,8,32,256]{3,2,1,0:T(8,128)(2,1)} %own.5, bf16[1,32,16,64]{3,2,1,0:T(8,128)(2,1)} %cot_hbm.1), custom_call_target="tpu_custom_call" | custom-call | flops 1048576 | bytes 65536 | tf_op jit(solution)/shard_map/pallas_call | solution.py:381
  2.4 1.4 %collective-permute-start = (bf16[384,256]{1,0:T(8,128)(2,1)}, bf16[384,256]{1,0:T(8,128)(2,1)S(1)}, u32[]{:S(2)}, u32[]{:S(2)}) collective-permute-start(bf16[384,256]{1,0:T(8,128)(2,1)} %get-tuple-element.39.token), channel_id=1, source_target_pairs={{0,8},{8,0},{1,9},{9,1},{2,10},{10,2},{3,11},{11,3},{4,12},{12,4},... | collective-permute-start | bytes 589832 | tf_op jit(solution)/shard_map/ppermute | solution.py:373
  3.9 4.8 %collective-permute-start.1 = (bf16[384,256]{1,0:T(8,128)(2,1)}, bf16[384,256]{1,0:T(8,128)(2,1)S(1)}, u32[]{:S(2)}, u32[]{:S(2)}) collective-permute-start(bf16[384,256]{1,0:T(8,128)(2,1)} %get-tuple-element.40), channel_id=1, source_target_pairs={{8,16},{24,32},{40,48},{56,64},{72,80},{88,96},{104,112},{16,8},{3... | collective-permute-start | bytes 589832 | tf_op jit(solution)/shard_map/ppermute | solution.py:373
  9.6 1.2 %copy-done.4 = bf16[27,256,64]{1,2,0:T(8,128)(2,1)S(1)} copy-done((bf16[27,256,64]{1,2,0:T(8,128)(2,1)S(1)}, bf16[27,256,64]{1,2,0:T(8,128)(2,1)}, u32[]{:S(2)}) %copy-start.4) | copy-done | bytes 884760
  15.1 1.7 %shard_map.77 = (bf16[8,96,256]{2,1,0:T(8,128)(2,1)}, bf16[3,34,16,192]{3,2,1,0:T(8,128)(2,1)S(1)}) custom-call(bf16[1,32,16,64]{3,2,1,0:T(8,128)(2,1)S(1)} %get-tuple-element.46.cot, bf16[384,256]{1,0:T(8,128)(2,1)S(1)} %collective-permute-done.inner, bf16[384,256]{1,0:T(8,128)(2,1)S(1)} %collective-permute-done.1.outer, ...), custom_call_target="tpu_custom_call" | custom-call | flops 1048576 | bytes 65536 | tf_op jit(solution)/shard_map/pallas_call | solution.py:393
  17.6 1.3 %collective-permute-done.2.yinner = bf16[256,256]{1,0:T(8,128)(2,1)S(1)} collective-permute-done((bf16[256,256]{1,0:T(8,128)(2,1)S(1)}, bf16[256,256]{1,0:T(8,128)(2,1)S(1)}, u32[]{:S(2)}, u32[]{:S(2)}) %collective-permute-start.2) | collective-permute-done | bytes 131104 | tf_op jit(solution)/shard_map/ppermute | solution.py:373
  18.9 7.8 %all-to-all-start = ((bf16[8,96,256]{2,1,0:T(8,128)(2,1)}), bf16[8,96,256]{2,1,0:T(8,128)(2,1)S(1)}, u32[]{:S(2)}, u32[]{:S(2)}) async-start(bf16[8,96,256]{2,1,0:T(8,128)(2,1)} %get-tuple-element.55), calls=%async_computation | async-start | bytes 786432 | tf_op jit(solution)/shard_map/all_to_all | solution.py:400
  26.8 2.0 %copy-done.2 = bf16[27,256,256]{2,1,0:T(8,128)(2,1)S(1)} copy-done((bf16[27,256,256]{2,1,0:T(8,128)(2,1)S(1)}, bf16[27,256,256]{2,1,0:T(8,128)(2,1)}, u32[]{:S(2)}) %copy-start.2) | copy-done | bytes 3538968
  28.7 3.7 %shard_map.79 = (bf16[8,64,256]{2,1,0:T(8,128)(2,1)}, f32[640,256]{1,0:T(8,128)S(1)}, bf16[768,256]{1,0:T(8,128)(2,1)S(1)}) custom-call(bf16[2,8,32,256]{3,2,1,0:T(8,128)(2,1)S(1)} %copy-done.1, bf16[384,256]{1,0:T(8,128)(2,1)S(1)} %collective-permute-done.inner, bf16[384,256]{1,0:T(8,128)(2,1)S(1)} %collective-permute-done.1.outer, ...), custom_call_target="tpu_custom_call" | custom-call | flops 1048576 | bytes 65536 | tf_op jit(solution)/shard_map/pallas_call | solution.py:402
  32.5 3.5 %all-to-all-done.parts = bf16[8,96,256]{2,1,0:T(8,128)(2,1)S(1)} async-done(((bf16[8,96,256]{2,1,0:T(8,128)(2,1)}), bf16[8,96,256]{2,1,0:T(8,128)(2,1)S(1)}, u32[]{:S(2)}, u32[]{:S(2)}) %all-to-all-start) | async-done | bytes 393248 | tf_op jit(solution)/shard_map/all_to_all | solution.py:400
  36.6 3.4 %all-to-all-start.1 = ((bf16[8,64,256]{2,1,0:T(8,128)(2,1)}), bf16[8,64,256]{2,1,0:T(8,128)(2,1)S(1)}, u32[]{:S(2)}, u32[]{:S(2)}) async-start(bf16[8,64,256]{2,1,0:T(8,128)(2,1)} %get-tuple-element.57), calls=%async_computation.1 | async-start | bytes 524288 | tf_op jit(solution)/shard_map/all_to_all | solution.py:413
  40.1 3.7 %shard_map.81 = bf16[64,54,256]{2,1,0:T(8,128)(2,1)} custom-call(bf16[2,8,32,256]{3,2,1,0:T(8,128)(2,1)S(1)} %copy-done.1, bf16[384,256]{1,0:T(8,128)(2,1)S(1)} %collective-permute-done.inner, bf16[384,256]{1,0:T(8,128)(2,1)S(1)} %collective-permute-done.1.outer, bf16[256,256]{1,0:T(8,128)(2,1)S(1)} %collective-permute-done.2.yinner, ...), custom_call_target="tpu_custom_call" | custom-call | flops 1048576 | bytes 65536 | tf_op jit(solution)/shard_map/pallas_call | solution.py:422
  43.8 3.3 %all-to-all-done.1 = bf16[8,64,256]{2,1,0:T(8,128)(2,1)S(1)} async-done(((bf16[8,64,256]{2,1,0:T(8,128)(2,1)}), bf16[8,64,256]{2,1,0:T(8,128)(2,1)S(1)}, u32[]{:S(2)}, u32[]{:S(2)}) %all-to-all-start.1) | async-done | bytes 262176 | tf_op jit(solution)/shard_map/all_to_all | solution.py:413
  47.2 9.4 %all-to-all-start.2 = ((bf16[64,54,256]{2,1,0:T(8,128)(2,1)}), bf16[64,54,256]{2,1,0:T(8,128)(2,1)S(1)}, u32[]{:S(2)}, u32[]{:S(2)}) async-start(bf16[64,54,256]{2,1,0:T(8,128)(2,1)} %shard_map.81), calls=%async_computation.2 | async-start | bytes 3670016 | tf_op jit(solution)/shard_map/all_to_all | solution.py:434
  56.5 1.5 %collective-permute-start.6 = (bf16[512,256]{1,0:T(8,128)(2,1)S(1)}, bf16[512,256]{1,0:T(8,128)(2,1)S(1)}, u32[]{:S(2)}, u32[]{:S(2)}) collective-permute-start(bf16[512,256]{1,0:T(8,128)(2,1)S(1)} %bitcast.18), channel_id=1, source_target_pairs={{0,8},{8,0},{1,9},{9,1},{2,10},{10,2},{3,11},{11,3},{4,12},{12,4},... | collective-permute-start | bytes 786440 | tf_op jit(solution)/shard_map/ppermute | solution.py:436
  58.1 1.2 %shard_map.82 = (f32[512,64]{1,0:T(8,128)S(1)}, bf16[128,256]{1,0:T(8,128)(2,1)S(1)}, bf16[448,256]{1,0:T(8,128)(2,1)S(1)}) custom-call(bf16[512,256]{1,0:T(8,128)(2,1)S(1)} %bitcast.19, bf16[9,192,256]{2,1,0:T(8,128)(2,1)S(1)} %bitcast.17, bf16[640,256]{1,0:T(8,128)(2,1)S(1)} %shard_map.80.grad), custom_call_target="tpu_custom_call" | custom-call | flops 1048576 | bytes 65536 | tf_op jit(solution)/shard_map/pallas_call | solution.py:450
  59.6 5.1 %collective-permute-start.11 = (bf16[448,256]{1,0:T(8,128)(2,1)S(1)}, bf16[448,256]{1,0:T(8,128)(2,1)S(1)}, u32[]{:S(2)}, u32[]{:S(2)}) collective-permute-start(bf16[448,256]{1,0:T(8,128)(2,1)S(1)} %get-tuple-element.63), channel_id=1, source_target_pairs={{8,16},{24,32},{40,48},{56,64},{72,80},{88,96},{104,112},{16,8},{3... | collective-permute-start | bytes 688136 | tf_op jit(solution)/shard_map/ppermute | solution.py:373
  66.8 1.9 %shard_map.83 = bf16[8,224,128]{2,1,0:T(8,128)(2,1)S(1)} custom-call(bf16[512,256]{1,0:T(8,128)(2,1)S(1)} %bitcast.20, bf16[512,256]{1,0:T(8,128)(2,1)S(1)} %collective-permute-done.6.other, bf16[3,34,16,192]{3,2,1,0:T(8,128)(2,1)S(1)} %copy-done.9, bf16[768,256]{1,0:T(8,128)(2,1)S(1)} %copy-done.7), custom_call_target="tpu_custom_call" | custom-call | flops 1048576 | bytes 65536 | tf_op jit(solution)/shard_map/pallas_call | solution.py:437
  68.8 1.3 %collective-permute-start.7 = (bf16[448,128]{1,0:T(8,128)(2,1)S(1)}, bf16[448,128]{1,0:T(8,128)(2,1)S(1)}, u32[]{:S(2)}, u32[]{:S(2)}) collective-permute-start(bf16[448,128]{1,0:T(8,128)(2,1)S(1)} %bitcast.26), channel_id=1, source_target_pairs={{0,32},{32,64},{64,96},{96,0},{1,33},{33,65},{65,97},{97,1},{2,34}... | collective-permute-start | bytes 344072 | tf_op jit(solution)/shard_map/ppermute | solution.py:446
  70.0 2.6 %collective-permute-start.8 = (bf16[448,128]{1,0:T(8,128)(2,1)S(1)}, bf16[448,128]{1,0:T(8,128)(2,1)S(1)}, u32[]{:S(2)}, u32[]{:S(2)}) collective-permute-start(bf16[448,128]{1,0:T(8,128)(2,1)S(1)} %bitcast.25), channel_id=1, source_target_pairs={{0,64},{32,96},{64,0},{96,32},{1,65},{33,97},{65,1},{97,33},{2,66}... | collective-permute-start | bytes 344072 | tf_op jit(solution)/shard_map/ppermute | solution.py:446
  73.7 2.1 %shard_map.85 = (f32[512,256]{1,0:T(8,128)S(1)}, bf16[3,256,768]{2,1,0:T(8,128)(2,1)S(1)}) custom-call(bf16[640,256]{1,0:T(8,128)(2,1)S(1)} %shard_map.80.grad, bf16[640,256]{1,0:T(8,128)(2,1)S(1)} %copy-done.12, bf16[9,3,256,256]{3,2,1,0:T(8,128)(2,1)S(1)} %bitcast.15), custom_call_target="tpu_custom_call" | custom-call | flops 2147483648 | bytes 65536 | tf_op jit(solution)/shard_map/pallas_call | solution.py:457
  75.9 6.4 %collective-permute-done.7.first = bf16[448,128]{1,0:T(8,128)(2,1)S(1)} collective-permute-done((bf16[448,128]{1,0:T(8,128)(2,1)S(1)}, bf16[448,128]{1,0:T(8,128)(2,1)S(1)}, u32[]{:S(2)}, u32[]{:S(2)}) %collective-permute-start.7) | collective-permute-done | bytes 114720 | tf_op jit(solution)/shard_map/ppermute | solution.py:446
  83.3 6.6 %collective-permute-start.12 = (bf16[224,128]{1,0:T(8,128)(2,1)S(1)}, bf16[224,128]{1,0:T(8,128)(2,1)S(1)}, u32[]{:S(2)}, u32[]{:S(2)}) collective-permute-start(bf16[224,128]{1,0:T(8,128)(2,1)S(1)} %slice.23), channel_id=1, source_target_pairs={{0,16},{16,0},{1,17},{17,1},{2,18},{18,2},{3,19},{19,3},{4,20},{20... | collective-permute-start | bytes 172040 | tf_op jit(solution)/shard_map/ppermute | solution.py:468
  90.7 1.2 %shard_map.87 = bf16[512,256]{1,0:T(8,128)(2,1)} custom-call(f32[512,256]{1,0:T(8,128)S(1)} %get-tuple-element.68.total, bf16[448,256]{1,0:T(8,128)(2,1)S(1)} %collective-permute-done.11.outer, bf16[3,256,768]{2,1,0:T(8,128)(2,1)S(1)} %get-tuple-element.69.rest), custom_call_target="tpu_custom_call" | custom-call | flops 1073741824 | bytes 65536 | tf_op jit(solution)/shard_map/pallas_call | solution.py:467
  (53 shorter events, 13.8 us)
Async XLA Ops:
  2.4 10.6 %collective-permute-start = (bf16[384,256]{1,0:T(8,128)(2,1)}, bf16[384,256]{1,0:T(8,128)(2,1)S(1)}, u32[]{:S(2)}, u32[]{:S(2)}) collective-permute-start(bf16[384,256]{1,0:T(8,128)(2,1)} %get-tuple-element.39.token), channel_id=1, source_target_pairs={{0,8},{8,0},{1,9},{9,1},{2,10},{10,2},{3,11},{11,3},{4,12},{12,4},... | collective-permute-start | bytes 589832 | tf_op jit(solution)/shard_map/ppermute | solution.py:373
  3.9 10.0 %collective-permute-start.1 = (bf16[384,256]{1,0:T(8,128)(2,1)}, bf16[384,256]{1,0:T(8,128)(2,1)S(1)}, u32[]{:S(2)}, u32[]{:S(2)}) collective-permute-start(bf16[384,256]{1,0:T(8,128)(2,1)} %get-tuple-element.40), channel_id=1, source_target_pairs={{8,16},{24,32},{40,48},{56,64},{72,80},{88,96},{104,112},{16,8},{3... | collective-permute-start | bytes 589832 | tf_op jit(solution)/shard_map/ppermute | solution.py:373
  9.6 1.2 %copy-start.4 = (bf16[27,256,64]{1,2,0:T(8,128)(2,1)S(1)}, bf16[27,256,64]{1,2,0:T(8,128)(2,1)}, u32[]{:S(2)}) copy-start(bf16[27,256,64]{1,2,0:T(8,128)(2,1)} %param.6) | copy-start | bytes 2654212
  12.6 14.1 %copy-start.1 = (bf16[2,8,32,256]{3,2,1,0:T(8,128)(2,1)S(1)}, bf16[2,8,32,256]{3,2,1,0:T(8,128)(2,1)}, u32[]{:S(2)}) copy-start(bf16[2,8,32,256]{3,2,1,0:T(8,128)(2,1)} %own.5) | copy-start | bytes 786436
  13.9 5.0 %collective-permute-start.2 = (bf16[256,256]{1,0:T(8,128)(2,1)S(1)}, bf16[256,256]{1,0:T(8,128)(2,1)S(1)}, u32[]{:S(2)}, u32[]{:S(2)}) collective-permute-start(bf16[256,256]{1,0:T(8,128)(2,1)S(1)} %get-tuple-element.50), channel_id=1, source_target_pairs={{0,1},{1,0},{2,3},{3,2},{4,5},{5,4},{6,7},{7,6},{8,9},{9,8},{10,11... | collective-permute-start | bytes 393224 | tf_op jit(solution)/shard_map/ppermute | solution.py:373
  14.4 4.5 %collective-permute-start.3 = (bf16[256,256]{1,0:T(8,128)(2,1)S(1)}, bf16[256,256]{1,0:T(8,128)(2,1)S(1)}, u32[]{:S(2)}, u32[]{:S(2)}) collective-permute-start(bf16[256,256]{1,0:T(8,128)(2,1)S(1)} %get-tuple-element.51), channel_id=1, source_target_pairs={{1,2},{3,4},{5,6},{2,1},{4,3},{6,5},{9,10},{11,12},{13,14},{10,9},... | collective-permute-start | bytes 393224 | tf_op jit(solution)/shard_map/ppermute | solution.py:373
  18.9 17.1 %all-to-all-start = ((bf16[8,96,256]{2,1,0:T(8,128)(2,1)}), bf16[8,96,256]{2,1,0:T(8,128)(2,1)S(1)}, u32[]{:S(2)}, u32[]{:S(2)}) async-start(bf16[8,96,256]{2,1,0:T(8,128)(2,1)} %get-tuple-element.55), calls=%async_computation | async-start | bytes 786432 | tf_op jit(solution)/shard_map/all_to_all | solution.py:400
  26.7 2.0 %copy-start.2 = (bf16[27,256,256]{2,1,0:T(8,128)(2,1)S(1)}, bf16[27,256,256]{2,1,0:T(8,128)(2,1)}, u32[]{:S(2)}) copy-start(bf16[27,256,256]{2,1,0:T(8,128)(2,1)} %param.5) | copy-start | bytes 10616836
  32.5 7.5 %collective-permute-start.4 = (bf16[768,256]{1,0:T(8,128)(2,1)S(1)}, bf16[768,256]{1,0:T(8,128)(2,1)S(1)}, u32[]{:S(2)}, u32[]{:S(2)}) collective-permute-start(bf16[768,256]{1,0:T(8,128)(2,1)S(1)} %get-tuple-element.54), channel_id=1, source_target_pairs={{0,8},{8,0},{1,9},{9,1},{2,10},{10,2},{3,11},{11,3},{4,12},{12,4},... | collective-permute-start | bytes 1179656 | tf_op jit(solution)/shard_map/ppermute | solution.py:412
  36.1 3.9 %collective-permute-start.5 = (bf16[640,256]{1,0:T(8,128)(2,1)S(1)}, bf16[640,256]{1,0:T(8,128)(2,1)S(1)}, u32[]{:S(2)}, u32[]{:S(2)}) collective-permute-start(bf16[640,256]{1,0:T(8,128)(2,1)S(1)} %shard_map.80.grad), channel_id=1, source_target_pairs={{0,8},{8,0},{1,9},{9,1},{2,10},{10,2},{3,11},{11,3},{4,12},{12,4},... | collective-permute-start | bytes 983048 | tf_op jit(solution)/shard_map/ppermute | solution.py:421
  36.6 10.5 %all-to-all-start.1 = ((bf16[8,64,256]{2,1,0:T(8,128)(2,1)}), bf16[8,64,256]{2,1,0:T(8,128)(2,1)S(1)}, u32[]{:S(2)}, u32[]{:S(2)}) async-start(bf16[8,64,256]{2,1,0:T(8,128)(2,1)} %get-tuple-element.57), calls=%async_computation.1 | async-start | bytes 524288 | tf_op jit(solution)/shard_map/all_to_all | solution.py:413
  40.0 3.8 %copy-start.6 = (bf16[768,256]{1,0:T(8,128)(2,1)}, bf16[768,256]{1,0:T(8,128)(2,1)S(1)}, u32[]{:S(2)}) copy-start(bf16[768,256]{1,0:T(8,128)(2,1)S(1)} %collective-permute-done.4.far) | copy-start | bytes 1179652
  40.1 3.8 %copy-start.11 = (bf16[640,256]{1,0:T(8,128)(2,1)}, bf16[640,256]{1,0:T(8,128)(2,1)S(1)}, u32[]{:S(2)}) copy-start(bf16[640,256]{1,0:T(8,128)(2,1)S(1)} %collective-permute-done.5.other) | copy-start | bytes 983044
  47.1 10.9 %copy-start.5 = (bf16[27,256,64]{1,2,0:T(8,128)(2,1)S(1)}, bf16[27,256,64]{1,2,0:T(8,128)(2,1)}, u32[]{:S(2)}) copy-start(bf16[27,256,64]{1,2,0:T(8,128)(2,1)} %param.6) | copy-start | bytes 2654212
  47.2 44.8 %all-to-all-start.2 = ((bf16[64,54,256]{2,1,0:T(8,128)(2,1)}), bf16[64,54,256]{2,1,0:T(8,128)(2,1)S(1)}, u32[]{:S(2)}, u32[]{:S(2)}) async-start(bf16[64,54,256]{2,1,0:T(8,128)(2,1)} %shard_map.81), calls=%async_computation.2 | async-start | bytes 3670016 | tf_op jit(solution)/shard_map/all_to_all | solution.py:434
  56.5 8.1 %collective-permute-start.6 = (bf16[512,256]{1,0:T(8,128)(2,1)S(1)}, bf16[512,256]{1,0:T(8,128)(2,1)S(1)}, u32[]{:S(2)}, u32[]{:S(2)}) collective-permute-start(bf16[512,256]{1,0:T(8,128)(2,1)S(1)} %bitcast.18), channel_id=1, source_target_pairs={{0,8},{8,0},{1,9},{9,1},{2,10},{10,2},{3,11},{11,3},{4,12},{12,4},... | collective-permute-start | bytes 786440 | tf_op jit(solution)/shard_map/ppermute | solution.py:436
  58.0 15.7 %copy-start.3 = (bf16[27,256,256]{2,1,0:T(8,128)(2,1)S(1)}, bf16[27,256,256]{2,1,0:T(8,128)(2,1)}, u32[]{:S(2)}) copy-start(bf16[27,256,256]{2,1,0:T(8,128)(2,1)} %param.5) | copy-start | bytes 10616836
  59.3 23.6 %collective-permute-start.10 = (bf16[128,256]{1,0:T(8,128)(2,1)S(1)}, bf16[128,256]{1,0:T(8,128)(2,1)S(1)}, u32[]{:S(2)}, u32[]{:S(2)}) collective-permute-start(bf16[128,256]{1,0:T(8,128)(2,1)S(1)} %get-tuple-element.62), channel_id=1, source_target_pairs={{0,8},{8,0},{1,9},{9,1},{2,10},{10,2},{3,11},{11,3},{4,12},{12,4},... | collective-permute-start | bytes 196616 | tf_op jit(solution)/shard_map/ppermute | solution.py:373
  59.6 23.7 %collective-permute-start.11 = (bf16[448,256]{1,0:T(8,128)(2,1)S(1)}, bf16[448,256]{1,0:T(8,128)(2,1)S(1)}, u32[]{:S(2)}, u32[]{:S(2)}) collective-permute-start(bf16[448,256]{1,0:T(8,128)(2,1)S(1)} %get-tuple-element.63), channel_id=1, source_target_pairs={{8,16},{24,32},{40,48},{56,64},{72,80},{88,96},{104,112},{16,8},{3... | collective-permute-start | bytes 688136 | tf_op jit(solution)/shard_map/ppermute | solution.py:373
  66.8 6.9 %copy-start.12 = (bf16[640,256]{1,0:T(8,128)(2,1)S(1)}, bf16[640,256]{1,0:T(8,128)(2,1)}, u32[]{:S(2)}) copy-start(bf16[640,256]{1,0:T(8,128)(2,1)} %copy-done.11) | copy-start | bytes 983044
  68.8 13.4 %collective-permute-start.7 = (bf16[448,128]{1,0:T(8,128)(2,1)S(1)}, bf16[448,128]{1,0:T(8,128)(2,1)S(1)}, u32[]{:S(2)}, u32[]{:S(2)}) collective-permute-start(bf16[448,128]{1,0:T(8,128)(2,1)S(1)} %bitcast.26), channel_id=1, source_target_pairs={{0,32},{32,64},{64,96},{96,0},{1,33},{33,65},{65,97},{97,1},{2,34}... | collective-permute-start | bytes 344072 | tf_op jit(solution)/shard_map/ppermute | solution.py:446
  70.0 12.8 %collective-permute-start.8 = (bf16[448,128]{1,0:T(8,128)(2,1)S(1)}, bf16[448,128]{1,0:T(8,128)(2,1)S(1)}, u32[]{:S(2)}, u32[]{:S(2)}) collective-permute-start(bf16[448,128]{1,0:T(8,128)(2,1)S(1)} %bitcast.25), channel_id=1, source_target_pairs={{0,64},{32,96},{64,0},{96,32},{1,65},{33,97},{65,1},{97,33},{2,66}... | collective-permute-start | bytes 344072 | tf_op jit(solution)/shard_map/ppermute | solution.py:446
  72.7 10.2 %collective-permute-start.9 = (bf16[448,128]{1,0:T(8,128)(2,1)S(1)}, bf16[448,128]{1,0:T(8,128)(2,1)S(1)}, u32[]{:S(2)}, u32[]{:S(2)}) collective-permute-start(bf16[448,128]{1,0:T(8,128)(2,1)S(1)} %bitcast.24), channel_id=1, source_target_pairs={{0,96},{32,0},{64,32},{96,64},{1,97},{33,1},{65,33},{97,65},{2,98}... | collective-permute-start | bytes 344072 | tf_op jit(solution)/shard_map/ppermute | solution.py:446
  83.3 9.6 %collective-permute-start.12 = (bf16[224,128]{1,0:T(8,128)(2,1)S(1)}, bf16[224,128]{1,0:T(8,128)(2,1)S(1)}, u32[]{:S(2)}, u32[]{:S(2)}) collective-permute-start(bf16[224,128]{1,0:T(8,128)(2,1)S(1)} %slice.23), channel_id=1, source_target_pairs={{0,16},{16,0},{1,17},{17,1},{2,18},{18,2},{3,19},{19,3},{4,20},{20... | collective-permute-start | bytes 172040 | tf_op jit(solution)/shard_map/ppermute | solution.py:468
  (6 other events, 5.8 us)

commit v8 on v7

--- a/solution.py
+++ b/solution.py
@@ -304,15 +304,15 @@
                 for c in range(3):
                     row = (3 * k + c) * 256
                     total[row : row + 256] = term[:, c * 64 : c * 64 + 64]
-            for block in range(8):
-                x, yh = divmod(block, 2)
-                row = (2 * block + core) * 432
-                upper = total[row : row + 224]
-                lower = jnp.concatenate(
-                    [total[row + 224 : row + 432], jnp.zeros((16, 64), F32)], axis=0
-                )
-                at = lax.rem(4 + x - place[2], 4) * 2 + lax.rem(place[1] + yh, 2)
-                terms[at] = jnp.concatenate([upper, lower], axis=1).astype(BF)
+    for step in range(4):
+        for c in range(2):
+            block = lax.rem(place[2] + step, 4) * 4 + lax.rem(place[1] + place[0], 2) * 2 + c
+            row = pl.multiple_of(block * 432, 16)
+            upper = total[pl.ds(row, 224)]
+            lower = total[pl.ds(pl.multiple_of(row + 224, 16), 208)]
+            lower = jnp.concatenate([lower, jnp.zeros((16, 64), F32)], axis=0)
+            both = jnp.concatenate([upper, lower], axis=1).astype(BF)
+            terms[step, 224 * c : 224 * c + 224] = both
 
 
 def coarse_forward_kernel(slab, w, grad, own, inner, outer, wide):
@@ -354,14 +354,16 @@
     out[pl.ds(1, 54, stride=2)] = total[:, 128:]
 
 
-def quad_kernel(own, first, second, third, out):
-    total = own[...].astype(F32) + first[...].astype(F32)
-    total = total + second[...].astype(F32) + third[...].astype(F32)
-    out[...] = total.astype(BF)
+def quad_kernel(own, beside, first, second, third, held, sent):
+    core = lax.axis_index("c")
+    total = jnp.where(core == 0, own[...], beside[...]).astype(F32)
+    total = total + first[...].astype(F32) + second[...].astype(F32) + third[...].astype(F32)
+    held[...] = jnp.where(core == 0, total[:224], total[224:]).astype(BF)
+    sent[...] = jnp.where(core == 0, total[224:], total[:224]).astype(BF)
 
 
 def coarse_sum_kernel(scale, own, other, out):
-    total = own[:224].astype(F32) + other[...].astype(F32)
+    total = own[...].astype(F32) + other[...].astype(F32)
     total = total * scale
     out[...] = jnp.concatenate([total[:, :64], total[:208, 64:]], axis=0).T
 
@@ -436,17 +438,11 @@
     across = lax.ppermute(slab, "c", SWAP)
     coarse_terms = call(
         coarse_weight_kernel,
-        array(8, 224, 128),
+        array(4, 448, 128),
         [VMEM] * 4,
         [pltpu.VMEM((34, 16, 192), BF), pltpu.VMEM((6912, 64), F32)],
     )(slab, across, wide_cot, far)
     coarse_terms, other = lax.optimization_barrier((coarse_terms, other))
-    coarse_terms = coarse_terms.reshape(4, 448, 128)
-    arrived = [
-        lax.ppermute(coarse_terms[step], "x", [(i, (i + step) % 4) for i in range(4)])
-        for step in range(1, 4)
-    ]
-    coarse_terms = call(quad_kernel, array(448, 128), [VMEM] * 4)(coarse_terms[0], *arrived)
     centre, inner, outer = call(
         coarse_forward_kernel,
         (array(512, 64, dtype=F32), array(128, 256), array(448, 256)),
@@ -454,6 +450,23 @@
         [pltpu.VMEM((34, 16, 768), BF)],
     )(slab, turned_coarse, grad)
     inner, outer = swap(inner, outer, SP)
+    coarse_terms, inner = lax.optimization_barrier((coarse_terms, inner))
+    arrived = []
+    for step in range(4):
+        pairs = [(4 * x + 2 * y, (4 * x + 4 * step) % 16 + 2 * y) for x in range(4) for y in range(2)]
+        pairs = [pair for pair in pairs if step > 0]
+        for x in range(4):
+            pairs += [(4 * x + 2 * y + 1, (4 * x + 4 * step) % 16 + 3 - 2 * y) for y in range(2)]
+        arrived.append(lax.ppermute(coarse_terms[step], SP, pairs))
+    grad_fine = call(
+        functools.partial(fine_sum_kernel, 1.0 / math.sqrt(cells)),
+        array(108, 128, dtype=F32),
+        [VMEM],
+    )(spread)
+    grad_fine, arrived = lax.optimization_barrier((grad_fine, arrived))
+    held, sent = call(quad_kernel, (array(224, 128), array(224, 128)), [VMEM] * 5)(
+        coarse_terms[0], *arrived
+    )
     total, rest = call(
         fine_back_kernel,
         (array(512, 256, dtype=F32), array(3, 256, 768)),
@@ -461,23 +474,15 @@
         [pltpu.VMEM((4, 10, 32, 768), BF)],
         flops=2**31,
     )(grad, other, weight_fine.reshape(9, 3, 256, 256))
-    coarse_terms, inner, outer, total = lax.optimization_barrier(
-        (coarse_terms, inner, outer, total)
-    )
+    _, inner, outer, total = lax.optimization_barrier((sent, inner, outer, total))
     grad_input = call(fine_rest_kernel, array(512, 256), [VMEM] * 3, flops=2**30)(total, outer, rest)
-    arrived = lax.ppermute(coarse_terms[224:], "yh", SWAP)
+    arrived = lax.ppermute(sent, "c", SWAP)
     coarse_out = call(coarse_out_kernel, array(512, 64), [VMEM] * 3)(centre, inner, outer)
-    grad_fine = call(
-        functools.partial(fine_sum_kernel, 1.0 / math.sqrt(cells)),
-        array(108, 128, dtype=F32),
-        [VMEM],
-    )(spread)
-    grad_fine, arrived = lax.optimization_barrier((grad_fine, arrived))
     grad_coarse = call(
         functools.partial(coarse_sum_kernel, 1.0 / math.sqrt(cells // 8)),
         array(64, 432, dtype=F32),
         [VMEM] * 2,
-    )(coarse_terms, arrived)
+    )(held, arrived)
     return (
         coarse_out.reshape(1, 32, 16, 64),
         grad_input.reshape(2, 8, 32, 256),

time: 94.4 us -> 93.7 us (level)
  waiting for transfers between devices: 16.3 us -> 12.3 us
  local copies, waits for them, and re-layouts: 9.04 us -> 10.9 us
    ppermute x4 -> x5, waiting for transfers between devices: 7 us -> 3.38 us  [the longest x4 3.38 us: body(): arrived.append(lax.ppermute(coarse_terms[step], SP, pairs))]
    unnamed x28 -> x40, local copies, waits for them, and re-layouts: 9 us -> 10.8 us
    ppermute x4 -> x5, starting transfers between devices: 11.6 us -> 12.6 us  [the longest x4 12 us: body(): arrived.append(lax.ppermute(coarse_terms[step], SP, pairs))]
  transfers between devices with their start and end apart: 16 -> 17, of which waited for: 7 -> 6; matrix products, arithmetic and copies ran while one was open for 0% -> 0% of each run, Pallas kernels for 19% -> 20%
where the time goes in v8:
time: 93.7 us; the launch traced here: 93 us
  starting transfers between devices  47.6 us (51%)
  Pallas kernels  21.3 us (23%)
  waiting for transfers between devices  12.3 us (13%)
  local copies, waits for them, and re-layouts  10.9 us (12%)
    ppermute x4, starting transfers between devices, body(): arrived.append(lax.ppermute(coarse_terms[step], SP, pairs))  12 us
    unnamed x40, local copies, waits for them, and re-layouts  10.8 us
    ppermute x3, starting transfers between devices, swap(): lax.ppermute(outer, axis, pairs)  10.5 us
    all_to_all x1, starting transfers between devices, body(): spread = lax.all_to_all(terms, ('x', 'yh', 'z', 'yl'), 0, 0, tiled=True)  9.37 us
    all_to_all x1, starting transfers between devices, body(): parts = lax.all_to_all(partial, FL, 0, 0, tiled=True)  7.83 us
    pallas_call x1, Pallas kernels, body(): call(fine_weight_kernel, array(64, 54, 256), [VMEM] * 8, [pltpu.VMEM((6,...  3.78 us
    pallas_call x1, Pallas kernels, body(): call(fine_forward_kernel, (array(8, 64, 256), array(640, 256, dtype=F32),...  3.74 us
    all_to_all x1, waiting for transfers between devices, body(): parts = lax.all_to_all(partial, FL, 0, 0, tiled=True)  3.5 us
  transfers between devices with their start and end apart: 17, of which 6 were waited for; matrix products, arithmetic and copies ran while one was open for 0% of the time, Pallas kernels for 20%

profile of v8, /device:TPU:1, one launch (start us, length us, event | category | flops | bytes accessed | tf_op | source)
XLA Modules:
  0.0 93.0 jit_solution(12636010745819333743)
XLA Ops:
  0.6 1.8 %shard_map.75 = (bf16[384,256]{1,0:T(8,128)(2,1)}, bf16[384,256]{1,0:T(8,128)(2,1)}) custom-call(bf16[2,8,32,256]{3,2,1,0:T(8,128)(2,1)} %own.5, bf16[1,32,16,64]{3,2,1,0:T(8,128)(2,1)} %cot_hbm.1), custom_call_target="tpu_custom_call" | custom-call | flops 1048576 | bytes 65536 | tf_op jit(solution)/shard_map/pallas_call | solution.py:383
  2.4 1.4 %collective-permute-start = (bf16[384,256]{1,0:T(8,128)(2,1)}, bf16[384,256]{1,0:T(8,128)(2,1)S(1)}, u32[]{:S(2)}, u32[]{:S(2)}) collective-permute-start(bf16[384,256]{1,0:T(8,128)(2,1)} %get-tuple-element.45.token), channel_id=1, source_target_pairs={{0,8},{8,0},{1,9},{9,1},{2,10},{10,2},{3,11},{11,3},{4,12},{12,4},... | collective-permute-start | bytes 589832 | tf_op jit(solution)/shard_map/ppermute | solution.py:375
  3.9 4.8 %collective-permute-start.1 = (bf16[384,256]{1,0:T(8,128)(2,1)}, bf16[384,256]{1,0:T(8,128)(2,1)S(1)}, u32[]{:S(2)}, u32[]{:S(2)}) collective-permute-start(bf16[384,256]{1,0:T(8,128)(2,1)} %get-tuple-element.46), channel_id=1, source_target_pairs={{8,16},{24,32},{40,48},{56,64},{72,80},{88,96},{104,112},{16,8},{3... | collective-permute-start | bytes 589832 | tf_op jit(solution)/shard_map/ppermute | solution.py:375
  15.1 1.7 %shard_map.77 = (bf16[8,96,256]{2,1,0:T(8,128)(2,1)}, bf16[3,34,16,192]{3,2,1,0:T(8,128)(2,1)S(1)}) custom-call(bf16[1,32,16,64]{3,2,1,0:T(8,128)(2,1)S(1)} %get-tuple-element.52.cot, bf16[384,256]{1,0:T(8,128)(2,1)S(1)} %collective-permute-done.inner, bf16[384,256]{1,0:T(8,128)(2,1)S(1)} %collective-permute-done.1.outer, ...), custom_call_target="tpu_custom_call" | custom-call | flops 1048576 | bytes 65536 | tf_op jit(solution)/shard_map/pallas_call | solution.py:395
  17.6 1.3 %collective-permute-done.2.yinner = bf16[256,256]{1,0:T(8,128)(2,1)S(1)} collective-permute-done((bf16[256,256]{1,0:T(8,128)(2,1)S(1)}, bf16[256,256]{1,0:T(8,128)(2,1)S(1)}, u32[]{:S(2)}, u32[]{:S(2)}) %collective-permute-start.2) | collective-permute-done | bytes 131104 | tf_op jit(solution)/shard_map/ppermute | solution.py:375
  18.9 7.8 %all-to-all-start = ((bf16[8,96,256]{2,1,0:T(8,128)(2,1)}), bf16[8,96,256]{2,1,0:T(8,128)(2,1)S(1)}, u32[]{:S(2)}, u32[]{:S(2)}) async-start(bf16[8,96,256]{2,1,0:T(8,128)(2,1)} %get-tuple-element.61), calls=%async_computation | async-start | bytes 786432 | tf_op jit(solution)/shard_map/all_to_all | solution.py:402
  26.7 2.0 %copy-done.2 = bf16[27,256,256]{2,1,0:T(8,128)(2,1)S(1)} copy-done((bf16[27,256,256]{2,1,0:T(8,128)(2,1)S(1)}, bf16[27,256,256]{2,1,0:T(8,128)(2,1)}, u32[]{:S(2)}) %copy-start.2) | copy-done | bytes 3538968
  28.7 3.7 %shard_map.79 = (bf16[8,64,256]{2,1,0:T(8,128)(2,1)}, f32[640,256]{1,0:T(8,128)S(1)}, bf16[768,256]{1,0:T(8,128)(2,1)S(1)}) custom-call(bf16[2,8,32,256]{3,2,1,0:T(8,128)(2,1)S(1)} %copy-done.1, bf16[384,256]{1,0:T(8,128)(2,1)S(1)} %collective-permute-done.inner, bf16[384,256]{1,0:T(8,128)(2,1)S(1)} %collective-permute-done.1.outer, ...), custom_call_target="tpu_custom_call" | custom-call | flops 1048576 | bytes 65536 | tf_op jit(solution)/shard_map/pallas_call | solution.py:404
  32.5 3.5 %all-to-all-done.parts = bf16[8,96,256]{2,1,0:T(8,128)(2,1)S(1)} async-done(((bf16[8,96,256]{2,1,0:T(8,128)(2,1)}), bf16[8,96,256]{2,1,0:T(8,128)(2,1)S(1)}, u32[]{:S(2)}, u32[]{:S(2)}) %all-to-all-start) | async-done | bytes 393248 | tf_op jit(solution)/shard_map/all_to_all | solution.py:402
  36.6 3.4 %all-to-all-start.1 = ((bf16[8,64,256]{2,1,0:T(8,128)(2,1)}), bf16[8,64,256]{2,1,0:T(8,128)(2,1)S(1)}, u32[]{:S(2)}, u32[]{:S(2)}) async-start(bf16[8,64,256]{2,1,0:T(8,128)(2,1)} %get-tuple-element.63), calls=%async_computation.1 | async-start | bytes 524288 | tf_op jit(solution)/shard_map/all_to_all | solution.py:415
  40.1 3.8 %shard_map.81 = bf16[64,54,256]{2,1,0:T(8,128)(2,1)} custom-call(bf16[2,8,32,256]{3,2,1,0:T(8,128)(2,1)S(1)} %copy-done.1, bf16[384,256]{1,0:T(8,128)(2,1)S(1)} %collective-permute-done.inner, bf16[384,256]{1,0:T(8,128)(2,1)S(1)} %collective-permute-done.1.outer, bf16[256,256]{1,0:T(8,128)(2,1)S(1)} %collective-permute-done.2.yinner, ...), custom_call_target="tpu_custom_call" | custom-call | flops 1048576 | bytes 65536 | tf_op jit(solution)/shard_map/pallas_call | solution.py:424
  43.8 3.3 %all-to-all-done.1 = bf16[8,64,256]{2,1,0:T(8,128)(2,1)S(1)} async-done(((bf16[8,64,256]{2,1,0:T(8,128)(2,1)}), bf16[8,64,256]{2,1,0:T(8,128)(2,1)S(1)}, u32[]{:S(2)}, u32[]{:S(2)}) %all-to-all-start.1) | async-done | bytes 262176 | tf_op jit(solution)/shard_map/all_to_all | solution.py:415
  47.1 9.4 %all-to-all-start.2 = ((bf16[64,54,256]{2,1,0:T(8,128)(2,1)}), bf16[64,54,256]{2,1,0:T(8,128)(2,1)S(1)}, u32[]{:S(2)}, u32[]{:S(2)}) async-start(bf16[64,54,256]{2,1,0:T(8,128)(2,1)} %shard_map.81), calls=%async_computation.2 | async-start | bytes 3670016 | tf_op jit(solution)/shard_map/all_to_all | solution.py:436
  56.5 1.5 %collective-permute-start.6 = (bf16[512,256]{1,0:T(8,128)(2,1)S(1)}, bf16[512,256]{1,0:T(8,128)(2,1)S(1)}, u32[]{:S(2)}, u32[]{:S(2)}) collective-permute-start(bf16[512,256]{1,0:T(8,128)(2,1)S(1)} %bitcast.22), channel_id=1, source_target_pairs={{0,8},{8,0},{1,9},{9,1},{2,10},{10,2},{3,11},{11,3},{4,12},{12,4},... | collective-permute-start | bytes 786440 | tf_op jit(solution)/shard_map/ppermute | solution.py:438
  58.0 1.9 %shard_map.82 = (f32[512,64]{1,0:T(8,128)S(1)}, bf16[128,256]{1,0:T(8,128)(2,1)S(1)}, bf16[448,256]{1,0:T(8,128)(2,1)}) custom-call(bf16[512,256]{1,0:T(8,128)(2,1)S(1)} %bitcast.23, bf16[9,192,256]{2,1,0:T(8,128)(2,1)S(1)} %bitcast.21, bf16[640,256]{1,0:T(8,128)(2,1)S(1)} %shard_map.80.grad), custom_call_target="tpu_custom_call" | custom-call | flops 1048576 | bytes 65536 | tf_op jit(solution)/shard_map/pallas_call | solution.py:446
  60.0 5.1 %collective-permute-start.12 = (bf16[448,256]{1,0:T(8,128)(2,1)}, bf16[448,256]{1,0:T(8,128)(2,1)S(1)}, u32[]{:S(2)}, u32[]{:S(2)}) collective-permute-start(bf16[448,256]{1,0:T(8,128)(2,1)} %get-tuple-element.77), channel_id=1, source_target_pairs={{8,16},{24,32},{40,48},{56,64},{72,80},{88,96},{104,112},{16,8},{3... | collective-permute-start | bytes 688136 | tf_op jit(solution)/shard_map/ppermute | solution.py:375
  67.2 1.9 %shard_map.83 = bf16[4,448,128]{2,1,0:T(8,128)(2,1)S(1)} custom-call(bf16[512,256]{1,0:T(8,128)(2,1)S(1)} %bitcast.24, bf16[512,256]{1,0:T(8,128)(2,1)S(1)} %collective-permute-done.6.other, bf16[3,34,16,192]{3,2,1,0:T(8,128)(2,1)S(1)} %copy-done.9, bf16[768,256]{1,0:T(8,128)(2,1)S(1)} %copy-done.7), custom_call_target="tpu_custom_call" | custom-call | flops 1048576 | bytes 65536 | tf_op jit(solution)/shard_map/pallas_call | solution.py:439
  69.2 3.1 %collective-permute-start.8 = (bf16[448,128]{1,0:T(8,128)(2,1)S(1)}, bf16[448,128]{1,0:T(8,128)(2,1)S(1)}, u32[]{:S(2)}, u32[]{:S(2)}) collective-permute-start(bf16[448,128]{1,0:T(8,128)(2,1)S(1)} %get-tuple-element.89.own), channel_id=1, source_target_pairs={{8,24},{24,8},{40,56},{56,40},{72,88},{88,72},{104,120},{120,104},... | collective-permute-start | bytes 344072 | tf_op jit(solution)/shard_map/ppermute | solution.py:460
  72.3 2.8 %collective-permute-start.9 = (bf16[448,128]{1,0:T(8,128)(2,1)S(1)}, bf16[448,128]{1,0:T(8,128)(2,1)S(1)}, u32[]{:S(2)}, u32[]{:S(2)}) collective-permute-start(bf16[448,128]{1,0:T(8,128)(2,1)S(1)} %get-tuple-element.88), channel_id=1, source_target_pairs={{0,32},{16,48},{32,64},{48,80},{64,96},{80,112},{96,0},{112,16},{8... | collective-permute-start | bytes 344072 | tf_op jit(solution)/shard_map/ppermute | solution.py:460
  75.1 2.3 %collective-permute-start.10 = (bf16[448,128]{1,0:T(8,128)(2,1)S(1)}, bf16[448,128]{1,0:T(8,128)(2,1)S(1)}, u32[]{:S(2)}, u32[]{:S(2)}) collective-permute-start(bf16[448,128]{1,0:T(8,128)(2,1)S(1)} %get-tuple-element.87), channel_id=1, source_target_pairs={{0,64},{16,80},{32,96},{48,112},{64,0},{80,16},{96,32},{112,48},{8... | collective-permute-start | bytes 344072 | tf_op jit(solution)/shard_map/ppermute | solution.py:460
  77.5 3.7 %collective-permute-start.11 = (bf16[448,128]{1,0:T(8,128)(2,1)S(1)}, bf16[448,128]{1,0:T(8,128)(2,1)S(1)}, u32[]{:S(2)}, u32[]{:S(2)}) collective-permute-start(bf16[448,128]{1,0:T(8,128)(2,1)S(1)} %get-tuple-element.86), channel_id=1, source_target_pairs={{0,96},{16,112},{32,0},{48,16},{64,32},{80,48},{96,64},{112,80},{8... | collective-permute-start | bytes 344072 | tf_op jit(solution)/shard_map/ppermute | solution.py:460
  81.2 2.1 %shard_map.86 = (f32[512,256]{1,0:T(8,128)S(1)}, bf16[3,256,768]{2,1,0:T(8,128)(2,1)S(1)}) custom-call(bf16[640,256]{1,0:T(8,128)(2,1)S(1)} %shard_map.80.grad, bf16[640,256]{1,0:T(8,128)(2,1)S(1)} %copy-done.12, bf16[9,3,256,256]{3,2,1,0:T(8,128)(2,1)S(1)} %bitcast.19), custom_call_target="tpu_custom_call" | custom-call | flops 2147483648 | bytes 65536 | tf_op jit(solution)/shard_map/pallas_call | solution.py:470
  86.9 2.5 %collective-permute-done.10.second = bf16[448,128]{1,0:T(8,128)(2,1)S(1)} collective-permute-done((bf16[448,128]{1,0:T(8,128)(2,1)S(1)}, bf16[448,128]{1,0:T(8,128)(2,1)S(1)}, u32[]{:S(2)}, u32[]{:S(2)}) %collective-permute-start.10) | collective-permute-done | bytes 114720 | tf_op jit(solution)/shard_map/ppermute | solution.py:460
  90.9 1.2 %shard_map.88 = bf16[512,256]{1,0:T(8,128)(2,1)} custom-call(f32[512,256]{1,0:T(8,128)S(1)} %copy-done.19, bf16[448,256]{1,0:T(8,128)(2,1)S(1)} %collective-permute-done.12.outer, bf16[3,256,768]{2,1,0:T(8,128)(2,1)S(1)} %copy-done.17), custom_call_target="tpu_custom_call" | custom-call | flops 1073741824 | bytes 65536 | tf_op jit(solution)/shard_map/pallas_call | solution.py:478
  (66 shorter events, 16.0 us)
Async XLA Ops:
  2.4 10.6 %collective-permute-start = (bf16[384,256]{1,0:T(8,128)(2,1)}, bf16[384,256]{1,0:T(8,128)(2,1)S(1)}, u32[]{:S(2)}, u32[]{:S(2)}) collective-permute-start(bf16[384,256]{1,0:T(8,128)(2,1)} %get-tuple-element.45.token), channel_id=1, source_target_pairs={{0,8},{8,0},{1,9},{9,1},{2,10},{10,2},{3,11},{11,3},{4,12},{12,4},... | collective-permute-start | bytes 589832 | tf_op jit(solution)/shard_map/ppermute | solution.py:375
  3.9 10.0 %collective-permute-start.1 = (bf16[384,256]{1,0:T(8,128)(2,1)}, bf16[384,256]{1,0:T(8,128)(2,1)S(1)}, u32[]{:S(2)}, u32[]{:S(2)}) collective-permute-start(bf16[384,256]{1,0:T(8,128)(2,1)} %get-tuple-element.46), channel_id=1, source_target_pairs={{8,16},{24,32},{40,48},{56,64},{72,80},{88,96},{104,112},{16,8},{3... | collective-permute-start | bytes 589832 | tf_op jit(solution)/shard_map/ppermute | solution.py:375
  12.6 14.1 %copy-start.1 = (bf16[2,8,32,256]{3,2,1,0:T(8,128)(2,1)S(1)}, bf16[2,8,32,256]{3,2,1,0:T(8,128)(2,1)}, u32[]{:S(2)}) copy-start(bf16[2,8,32,256]{3,2,1,0:T(8,128)(2,1)} %own.5) | copy-start | bytes 786436
  13.9 5.0 %collective-permute-start.2 = (bf16[256,256]{1,0:T(8,128)(2,1)S(1)}, bf16[256,256]{1,0:T(8,128)(2,1)S(1)}, u32[]{:S(2)}, u32[]{:S(2)}) collective-permute-start(bf16[256,256]{1,0:T(8,128)(2,1)S(1)} %get-tuple-element.56), channel_id=1, source_target_pairs={{0,1},{1,0},{2,3},{3,2},{4,5},{5,4},{6,7},{7,6},{8,9},{9,8},{10,11... | collective-permute-start | bytes 393224 | tf_op jit(solution)/shard_map/ppermute | solution.py:375
  14.4 4.5 %collective-permute-start.3 = (bf16[256,256]{1,0:T(8,128)(2,1)S(1)}, bf16[256,256]{1,0:T(8,128)(2,1)S(1)}, u32[]{:S(2)}, u32[]{:S(2)}) collective-permute-start(bf16[256,256]{1,0:T(8,128)(2,1)S(1)} %get-tuple-element.57), channel_id=1, source_target_pairs={{1,2},{3,4},{5,6},{2,1},{4,3},{6,5},{9,10},{11,12},{13,14},{10,9},... | collective-permute-start | bytes 393224 | tf_op jit(solution)/shard_map/ppermute | solution.py:375
  18.9 17.1 %all-to-all-start = ((bf16[8,96,256]{2,1,0:T(8,128)(2,1)}), bf16[8,96,256]{2,1,0:T(8,128)(2,1)S(1)}, u32[]{:S(2)}, u32[]{:S(2)}) async-start(bf16[8,96,256]{2,1,0:T(8,128)(2,1)} %get-tuple-element.61), calls=%async_computation | async-start | bytes 786432 | tf_op jit(solution)/shard_map/all_to_all | solution.py:402
  32.5 7.5 %collective-permute-start.4 = (bf16[768,256]{1,0:T(8,128)(2,1)S(1)}, bf16[768,256]{1,0:T(8,128)(2,1)S(1)}, u32[]{:S(2)}, u32[]{:S(2)}) collective-permute-start(bf16[768,256]{1,0:T(8,128)(2,1)S(1)} %get-tuple-element.60), channel_id=1, source_target_pairs={{0,8},{8,0},{1,9},{9,1},{2,10},{10,2},{3,11},{11,3},{4,12},{12,4},... | collective-permute-start | bytes 1179656 | tf_op jit(solution)/shard_map/ppermute | solution.py:414
  36.1 3.9 %collective-permute-start.5 = (bf16[640,256]{1,0:T(8,128)(2,1)S(1)}, bf16[640,256]{1,0:T(8,128)(2,1)S(1)}, u32[]{:S(2)}, u32[]{:S(2)}) collective-permute-start(bf16[640,256]{1,0:T(8,128)(2,1)S(1)} %shard_map.80.grad), channel_id=1, source_target_pairs={{0,8},{8,0},{1,9},{9,1},{2,10},{10,2},{3,11},{11,3},{4,12},{12,4},... | collective-permute-start | bytes 983048 | tf_op jit(solution)/shard_map/ppermute | solution.py:423
  36.6 10.5 %all-to-all-start.1 = ((bf16[8,64,256]{2,1,0:T(8,128)(2,1)}), bf16[8,64,256]{2,1,0:T(8,128)(2,1)S(1)}, u32[]{:S(2)}, u32[]{:S(2)}) async-start(bf16[8,64,256]{2,1,0:T(8,128)(2,1)} %get-tuple-element.63), calls=%async_computation.1 | async-start | bytes 524288 | tf_op jit(solution)/shard_map/all_to_all | solution.py:415
  47.1 10.9 %copy-start.5 = (bf16[27,256,64]{1,2,0:T(8,128)(2,1)S(1)}, bf16[27,256,64]{1,2,0:T(8,128)(2,1)}, u32[]{:S(2)}) copy-start(bf16[27,256,64]{1,2,0:T(8,128)(2,1)} %param.6) | copy-start | bytes 2654212
  47.1 38.0 %all-to-all-start.2 = ((bf16[64,54,256]{2,1,0:T(8,128)(2,1)}), bf16[64,54,256]{2,1,0:T(8,128)(2,1)S(1)}, u32[]{:S(2)}, u32[]{:S(2)}) async-start(bf16[64,54,256]{2,1,0:T(8,128)(2,1)} %shard_map.81), calls=%async_computation.2 | async-start | bytes 3670016 | tf_op jit(solution)/shard_map/all_to_all | solution.py:436
  56.5 8.5 %collective-permute-start.6 = (bf16[512,256]{1,0:T(8,128)(2,1)S(1)}, bf16[512,256]{1,0:T(8,128)(2,1)S(1)}, u32[]{:S(2)}, u32[]{:S(2)}) collective-permute-start(bf16[512,256]{1,0:T(8,128)(2,1)S(1)} %bitcast.22), channel_id=1, source_target_pairs={{0,8},{8,0},{1,9},{9,1},{2,10},{10,2},{3,11},{11,3},{4,12},{12,4},... | collective-permute-start | bytes 786440 | tf_op jit(solution)/shard_map/ppermute | solution.py:438
  58.0 23.2 %copy-start.3 = (bf16[27,256,256]{2,1,0:T(8,128)(2,1)S(1)}, bf16[27,256,256]{2,1,0:T(8,128)(2,1)}, u32[]{:S(2)}) copy-start(bf16[27,256,256]{2,1,0:T(8,128)(2,1)} %param.5) | copy-start | bytes 10616836
  60.0 21.2 %copy-start.13 = (f32[512,64]{1,0:T(8,128)}, f32[512,64]{1,0:T(8,128)S(1)}, u32[]{:S(2)}) copy-start(f32[512,64]{1,0:T(8,128)S(1)} %get-tuple-element.65.own) | copy-start | bytes 393220
  60.0 9.2 %collective-permute-start.7 = (bf16[128,256]{1,0:T(8,128)(2,1)S(1)}, bf16[128,256]{1,0:T(8,128)(2,1)S(1)}, u32[]{:S(2)}, u32[]{:S(2)}) collective-permute-start(bf16[128,256]{1,0:T(8,128)(2,1)S(1)} %get-tuple-element.68), channel_id=1, source_target_pairs={{0,8},{8,0},{1,9},{9,1},{2,10},{10,2},{3,11},{11,3},{4,12},{12,4},... | collective-permute-start | bytes 196616 | tf_op jit(solution)/shard_map/ppermute | solution.py:375
  60.0 30.1 %collective-permute-start.12 = (bf16[448,256]{1,0:T(8,128)(2,1)}, bf16[448,256]{1,0:T(8,128)(2,1)S(1)}, u32[]{:S(2)}, u32[]{:S(2)}) collective-permute-start(bf16[448,256]{1,0:T(8,128)(2,1)} %get-tuple-element.77), channel_id=1, source_target_pairs={{8,16},{24,32},{40,48},{56,64},{72,80},{88,96},{104,112},{16,8},{3... | collective-permute-start | bytes 688136 | tf_op jit(solution)/shard_map/ppermute | solution.py:375
  67.2 14.0 %copy-start.12 = (bf16[640,256]{1,0:T(8,128)(2,1)S(1)}, bf16[640,256]{1,0:T(8,128)(2,1)}, u32[]{:S(2)}) copy-start(bf16[640,256]{1,0:T(8,128)(2,1)} %copy-done.11) | copy-start | bytes 983044
  69.2 17.7 %collective-permute-start.8 = (bf16[448,128]{1,0:T(8,128)(2,1)S(1)}, bf16[448,128]{1,0:T(8,128)(2,1)S(1)}, u32[]{:S(2)}, u32[]{:S(2)}) collective-permute-start(bf16[448,128]{1,0:T(8,128)(2,1)S(1)} %get-tuple-element.89.own), channel_id=1, source_target_pairs={{8,24},{24,8},{40,56},{56,40},{72,88},{88,72},{104,120},{120,104},... | collective-permute-start | bytes 344072 | tf_op jit(solution)/shard_map/ppermute | solution.py:460
  72.3 14.6 %collective-permute-start.9 = (bf16[448,128]{1,0:T(8,128)(2,1)S(1)}, bf16[448,128]{1,0:T(8,128)(2,1)S(1)}, u32[]{:S(2)}, u32[]{:S(2)}) collective-permute-start(bf16[448,128]{1,0:T(8,128)(2,1)S(1)} %get-tuple-element.88), channel_id=1, source_target_pairs={{0,32},{16,48},{32,64},{48,80},{64,96},{80,112},{96,0},{112,16},{8... | collective-permute-start | bytes 344072 | tf_op jit(solution)/shard_map/ppermute | solution.py:460
  75.1 14.3 %collective-permute-start.10 = (bf16[448,128]{1,0:T(8,128)(2,1)S(1)}, bf16[448,128]{1,0:T(8,128)(2,1)S(1)}, u32[]{:S(2)}, u32[]{:S(2)}) collective-permute-start(bf16[448,128]{1,0:T(8,128)(2,1)S(1)} %get-tuple-element.87), channel_id=1, source_target_pairs={{0,64},{16,80},{32,96},{48,112},{64,0},{80,16},{96,32},{112,48},{8... | collective-permute-start | bytes 344072 | tf_op jit(solution)/shard_map/ppermute | solution.py:460
  77.5 12.0 %collective-permute-start.11 = (bf16[448,128]{1,0:T(8,128)(2,1)S(1)}, bf16[448,128]{1,0:T(8,128)(2,1)S(1)}, u32[]{:S(2)}, u32[]{:S(2)}) collective-permute-start(bf16[448,128]{1,0:T(8,128)(2,1)S(1)} %get-tuple-element.86), channel_id=1, source_target_pairs={{0,96},{16,112},{32,0},{48,16},{64,32},{80,48},{96,64},{112,80},{8... | collective-permute-start | bytes 344072 | tf_op jit(solution)/shard_map/ppermute | solution.py:460
  85.1 5.8 %copy-start.17 = (bf16[3,256,768]{2,1,0:T(8,128)(2,1)S(1)}, bf16[3,256,768]{2,1,0:T(8,128)(2,1)}, u32[]{:S(2)}) copy-start(bf16[3,256,768]{2,1,0:T(8,128)(2,1)} %copy-done.16) | copy-start | bytes 3538948
  85.1 5.8 %copy-start.19 = (f32[512,256]{1,0:T(8,128)S(1)}, f32[512,256]{1,0:T(8,128)}, u32[]{:S(2)}) copy-start(f32[512,256]{1,0:T(8,128)} %copy-done.18) | copy-start | bytes 1572868
  89.5 2.6 %collective-permute-start.13 = (bf16[224,128]{1,0:T(8,128)(2,1)S(1)}, bf16[224,128]{1,0:T(8,128)(2,1)S(1)}, u32[]{:S(2)}, u32[]{:S(2)}) collective-permute-start(bf16[224,128]{1,0:T(8,128)(2,1)S(1)} %get-tuple-element.75), channel_id=1, source_target_pairs={{0,8},{8,0},{1,9},{9,1},{2,10},{10,2},{3,11},{11,3},{4,12},{12,4},... | collective-permute-start | bytes 172040 | tf_op jit(solution)/shard_map/ppermute | solution.py:479
  (13 other events, 23.4 us)

commit v9 on v8

--- a/solution.py
+++ b/solution.py
@@ -269,7 +269,7 @@
             rest[b, :, at] = jnp.where(first, w[6 + b, c], w[b, c])
 
 
-def fine_rest_kernel(total, outer, rest, out):
+def last_kernel(scale, total, outer, rest, centre, inner, parts, out, coarse, fine):
     place = position()
     wide = along_depth(outer[:320].reshape(10, 32, 256), -1)
     more = None
@@ -282,6 +282,16 @@
     first = place[0] == 0
     out[:256] = (total[:256] + jnp.where(first, more, 0.0)).astype(BF)
     out[256:] = (total[256:] + jnp.where(first, 0.0, more)).astype(BF)
+    for k in range(4):
+        rows, columns = slice(128 * k, 128 * k + 128), slice(64 * k, 64 * k + 64)
+        plane = centre[rows] + inner[:, columns].astype(F32) + outer[320:, columns].astype(F32)
+        coarse[rows] = plane.astype(BF)
+    terms = parts[0].astype(F32)
+    for k in range(1, 64):
+        terms = terms + parts[k].astype(F32)
+    terms = terms * scale
+    fine[pl.ds(0, 54, stride=2)] = terms[:, :128]
+    fine[pl.ds(1, 54, stride=2)] = terms[:, 128:]
 
 
 def coarse_weight_kernel(slab, other, wide, far, terms, outer, total):
@@ -336,22 +346,6 @@
     up, down = packed(total[:, :64]).astype(BF), packed(total[:, 128:]).astype(BF)
     inner[...] = jnp.where(first, up, down)
     outer[320:] = jnp.where(first, down, up)
-
-
-def coarse_out_kernel(own, inner, outer, out):
-    for k in range(4):
-        rows, columns = slice(128 * k, 128 * k + 128), slice(64 * k, 64 * k + 64)
-        total = own[rows] + inner[:, columns].astype(F32) + outer[320:, columns].astype(F32)
-        out[rows] = total.astype(BF)
-
-
-def fine_sum_kernel(scale, parts, out):
-    total = parts[0].astype(F32)
-    for k in range(1, 64):
-        total = total + parts[k].astype(F32)
-    total = total * scale
-    out[pl.ds(0, 54, stride=2)] = total[:, :128]
-    out[pl.ds(1, 54, stride=2)] = total[:, 128:]
 
 
 def quad_kernel(own, beside, first, second, third, held, sent):
@@ -458,15 +452,6 @@
         for x in range(4):
             pairs += [(4 * x + 2 * y + 1, (4 * x + 4 * step) % 16 + 3 - 2 * y) for y in range(2)]
         arrived.append(lax.ppermute(coarse_terms[step], SP, pairs))
-    grad_fine = call(
-        functools.partial(fine_sum_kernel, 1.0 / math.sqrt(cells)),
-        array(108, 128, dtype=F32),
-        [VMEM],
-    )(spread)
-    grad_fine, arrived = lax.optimization_barrier((grad_fine, arrived))
-    held, sent = call(quad_kernel, (array(224, 128), array(224, 128)), [VMEM] * 5)(
-        coarse_terms[0], *arrived
-    )
     total, rest = call(
         fine_back_kernel,
         (array(512, 256, dtype=F32), array(3, 256, 768)),
@@ -474,10 +459,20 @@
         [pltpu.VMEM((4, 10, 32, 768), BF)],
         flops=2**31,
     )(grad, other, weight_fine.reshape(9, 3, 256, 256))
-    _, inner, outer, total = lax.optimization_barrier((sent, inner, outer, total))
-    grad_input = call(fine_rest_kernel, array(512, 256), [VMEM] * 3, flops=2**30)(total, outer, rest)
+    total, rest, arrived = lax.optimization_barrier((total, rest, arrived))
+    held, sent = call(quad_kernel, (array(224, 128), array(224, 128)), [VMEM] * 5)(
+        coarse_terms[0], *arrived
+    )
+    _, inner, outer, total, spread = lax.optimization_barrier(
+        (sent, inner, outer, total, spread)
+    )
+    grad_input, coarse_out, grad_fine = call(
+        functools.partial(last_kernel, 1.0 / math.sqrt(cells)),
+        (array(512, 256), array(512, 64), array(108, 128, dtype=F32)),
+        [VMEM] * 6,
+        flops=2**30,
+    )(total, outer, rest, centre, inner, spread)
     arrived = lax.ppermute(sent, "c", SWAP)
-    coarse_out = call(coarse_out_kernel, array(512, 64), [VMEM] * 3)(centre, inner, outer)
     grad_coarse = call(
         functools.partial(coarse_sum_kernel, 1.0 / math.sqrt(cells // 8)),
         array(64, 432, dtype=F32),

time: 93.7 us -> 92.9 us (level)
  Pallas kernels: 21.3 us -> 19.1 us
  starting transfers between devices: 47.6 us -> 49.1 us
  waiting for transfers between devices: 12.3 us -> 11.1 us
  local copies, waits for them, and re-layouts: 10.9 us -> 12 us
    all_to_all x1, waiting for transfers between devices: 3.5 us -> 0.34 us  [body(): parts = lax.all_to_all(partial, FL, 0, 0, tiled=True)]
    ppermute x1, starting transfers between devices: 0.5 us -> 2.31 us  [body(): other = lax.ppermute(grad, 'c', SWAP)]
    pallas_call x3 -> x1, Pallas kernels: 2.9 us -> 1.36 us  [body(): call(functools.partial(last_kernel, 1.0 / math.sqrt(cells)), (array(512,...]
    ppermute x3, starting transfers between devices: 10.5 us -> 11.9 us  [swap(): lax.ppermute(outer, axis, pairs)]
    ppermute x3, starting transfers between devices: 1.93 us -> 0.59 us  [swap(): lax.ppermute(inner, partner, SWAP)]
    ppermute x1, starting transfers between devices: 0.01 us -> 1.31 us  [body(): far = lax.ppermute(far, 'c', SWAP)]
    ppermute x1, waiting for transfers between devices: 0.01 us -> 1.23 us  [body(): arrived = lax.ppermute(sent, 'c', SWAP)]
    ppermute x4, starting transfers between devices: 12 us -> 10.8 us  [body(): arrived.append(lax.ppermute(coarse_terms[step], SP, pairs))]
  transfers between devices with their start and end apart: 17 -> 17, of which waited for: 6 -> 6; matrix products, arithmetic and copies ran while one was open for 0% -> 0% of each run, Pallas kernels for 20% -> 17%
where the time goes in v9:
time: 92.9 us; the launch traced here: 92.1 us
  starting transfers between devices  49.1 us (53%)
  Pallas kernels  19.1 us (21%)
  local copies, waits for them, and re-layouts  12 us (13%)
  waiting for transfers between devices  11.1 us (12%)
    unnamed x36, local copies, waits for them, and re-layouts  12 us
    ppermute x3, starting transfers between devices, swap(): lax.ppermute(outer, axis, pairs)  11.9 us
    ppermute x4, starting transfers between devices, body(): arrived.append(lax.ppermute(coarse_terms[step], SP, pairs))  10.8 us
    all_to_all x1, starting transfers between devices, body(): parts = lax.all_to_all(partial, FL, 0, 0, tiled=True)  8.55 us
    all_to_all x1, starting transfers between devices, body(): spread = lax.all_to_all(terms, ('x', 'yh', 'z', 'yl'), 0, 0, tiled=True)  8.5 us
    ppermute x4, waiting for transfers between devices, body(): arrived.append(lax.ppermute(coarse_terms[step], SP, pairs))  4.12 us
    pallas_call x1, Pallas kernels, body(): call(fine_weight_kernel, array(64, 54, 256), [VMEM] * 8, [pltpu.VMEM((6,...  3.77 us
    pallas_call x1, Pallas kernels, body(): call(fine_forward_kernel, (array(8, 64, 256), array(640, 256, dtype=F32),...  3.74 us
  transfers between devices with their start and end apart: 17, of which 6 were waited for; matrix products, arithmetic and copies ran while one was open for 0% of the time, Pallas kernels for 17%

profile of v9, /device:TPU:1, one launch (start us, length us, event | category | flops | bytes accessed | tf_op | source)
XLA Modules:
  0.0 92.1 jit_solution(2171958603222643431)
XLA Ops:
  0.6 1.8 %shard_map.75 = (bf16[384,256]{1,0:T(8,128)(2,1)}, bf16[384,256]{1,0:T(8,128)(2,1)}) custom-call(bf16[2,8,32,256]{3,2,1,0:T(8,128)(2,1)} %own.5, bf16[1,32,16,64]{3,2,1,0:T(8,128)(2,1)} %cot_hbm.1), custom_call_target="tpu_custom_call" | custom-call | flops 1048576 | bytes 65536 | tf_op jit(solution)/shard_map/pallas_call | solution.py:377
  2.4 6.2 %collective-permute-start.1 = (bf16[384,256]{1,0:T(8,128)(2,1)}, bf16[384,256]{1,0:T(8,128)(2,1)S(1)}, u32[]{:S(2)}, u32[]{:S(2)}) collective-permute-start(bf16[384,256]{1,0:T(8,128)(2,1)} %get-tuple-element.51), channel_id=1, source_target_pairs={{8,16},{24,32},{40,48},{56,64},{72,80},{88,96},{104,112},{16,8},{3... | collective-permute-start | bytes 589832 | tf_op jit(solution)/shard_map/ppermute | solution.py:369
  14.8 1.7 %shard_map.77 = (bf16[8,96,256]{2,1,0:T(8,128)(2,1)}, bf16[3,34,16,192]{3,2,1,0:T(8,128)(2,1)S(1)}) custom-call(bf16[1,32,16,64]{3,2,1,0:T(8,128)(2,1)S(1)} %get-tuple-element.57.cot, bf16[384,256]{1,0:T(8,128)(2,1)S(1)} %collective-permute-done.inner, bf16[384,256]{1,0:T(8,128)(2,1)S(1)} %collective-permute-done.1.outer, ...), custom_call_target="tpu_custom_call" | custom-call | flops 1048576 | bytes 65536 | tf_op jit(solution)/shard_map/pallas_call | solution.py:389
  17.4 1.6 %collective-permute-done.2.yinner = bf16[256,256]{1,0:T(8,128)(2,1)S(1)} collective-permute-done((bf16[256,256]{1,0:T(8,128)(2,1)S(1)}, bf16[256,256]{1,0:T(8,128)(2,1)S(1)}, u32[]{:S(2)}, u32[]{:S(2)}) %collective-permute-start.2) | collective-permute-done | bytes 131104 | tf_op jit(solution)/shard_map/ppermute | solution.py:369
  19.0 8.6 %all-to-all-start = ((bf16[8,96,256]{2,1,0:T(8,128)(2,1)}), bf16[8,96,256]{2,1,0:T(8,128)(2,1)S(1)}, u32[]{:S(2)}, u32[]{:S(2)}) async-start(bf16[8,96,256]{2,1,0:T(8,128)(2,1)} %get-tuple-element.66), calls=%async_computation | async-start | bytes 786432 | tf_op jit(solution)/shard_map/all_to_all | solution.py:396
  27.5 2.0 %copy-done.2 = bf16[27,256,256]{2,1,0:T(8,128)(2,1)S(1)} copy-done((bf16[27,256,256]{2,1,0:T(8,128)(2,1)S(1)}, bf16[27,256,256]{2,1,0:T(8,128)(2,1)}, u32[]{:S(2)}) %copy-start.2) | copy-done | bytes 3538968
  29.5 3.7 %shard_map.79 = (bf16[8,64,256]{2,1,0:T(8,128)(2,1)}, f32[640,256]{1,0:T(8,128)S(1)}, bf16[768,256]{1,0:T(8,128)(2,1)S(1)}) custom-call(bf16[2,8,32,256]{3,2,1,0:T(8,128)(2,1)S(1)} %copy-done.1, bf16[384,256]{1,0:T(8,128)(2,1)S(1)} %collective-permute-done.inner, bf16[384,256]{1,0:T(8,128)(2,1)S(1)} %collective-permute-done.1.outer, ...), custom_call_target="tpu_custom_call" | custom-call | flops 1048576 | bytes 65536 | tf_op jit(solution)/shard_map/pallas_call | solution.py:398
  33.3 1.3 %collective-permute-start.4 = (bf16[768,256]{1,0:T(8,128)(2,1)S(1)}, bf16[768,256]{1,0:T(8,128)(2,1)S(1)}, u32[]{:S(2)}, u32[]{:S(2)}) collective-permute-start(bf16[768,256]{1,0:T(8,128)(2,1)S(1)} %get-tuple-element.65), channel_id=1, source_target_pairs={{0,8},{8,0},{1,9},{9,1},{2,10},{10,2},{3,11},{11,3},{4,12},{12,4},... | collective-permute-start | bytes 1179656 | tf_op jit(solution)/shard_map/ppermute | solution.py:408
  35.0 2.3 %collective-permute-start.5 = (bf16[640,256]{1,0:T(8,128)(2,1)S(1)}, bf16[640,256]{1,0:T(8,128)(2,1)S(1)}, u32[]{:S(2)}, u32[]{:S(2)}) collective-permute-start(bf16[640,256]{1,0:T(8,128)(2,1)S(1)} %shard_map.80.grad), channel_id=1, source_target_pairs={{0,8},{8,0},{1,9},{9,1},{2,10},{10,2},{3,11},{11,3},{4,12},{12,4},... | collective-permute-start | bytes 983048 | tf_op jit(solution)/shard_map/ppermute | solution.py:417
  37.4 3.4 %all-to-all-start.1 = ((bf16[8,64,256]{2,1,0:T(8,128)(2,1)}), bf16[8,64,256]{2,1,0:T(8,128)(2,1)S(1)}, u32[]{:S(2)}, u32[]{:S(2)}) async-start(bf16[8,64,256]{2,1,0:T(8,128)(2,1)} %get-tuple-element.68), calls=%async_computation.1 | async-start | bytes 524288 | tf_op jit(solution)/shard_map/all_to_all | solution.py:409
  40.8 3.8 %shard_map.81 = bf16[64,54,256]{2,1,0:T(8,128)(2,1)} custom-call(bf16[2,8,32,256]{3,2,1,0:T(8,128)(2,1)S(1)} %copy-done.1, bf16[384,256]{1,0:T(8,128)(2,1)S(1)} %collective-permute-done.inner, bf16[384,256]{1,0:T(8,128)(2,1)S(1)} %collective-permute-done.1.outer, bf16[256,256]{1,0:T(8,128)(2,1)S(1)} %collective-permute-done.2.yinner, ...), custom_call_target="tpu_custom_call" | custom-call | flops 1048576 | bytes 65536 | tf_op jit(solution)/shard_map/pallas_call | solution.py:418
  44.6 3.2 %all-to-all-done.1 = bf16[8,64,256]{2,1,0:T(8,128)(2,1)S(1)} async-done(((bf16[8,64,256]{2,1,0:T(8,128)(2,1)}), bf16[8,64,256]{2,1,0:T(8,128)(2,1)S(1)}, u32[]{:S(2)}, u32[]{:S(2)}) %all-to-all-start.1) | async-done | bytes 262176 | tf_op jit(solution)/shard_map/all_to_all | solution.py:409
  47.8 8.5 %all-to-all-start.2 = ((bf16[64,54,256]{2,1,0:T(8,128)(2,1)}), bf16[64,54,256]{2,1,0:T(8,128)(2,1)S(1)}, u32[]{:S(2)}, u32[]{:S(2)}) async-start(bf16[64,54,256]{2,1,0:T(8,128)(2,1)} %shard_map.81), calls=%async_computation.2 | async-start | bytes 3670016 | tf_op jit(solution)/shard_map/all_to_all | solution.py:430
  56.3 1.6 %collective-permute-start.6 = (bf16[512,256]{1,0:T(8,128)(2,1)S(1)}, bf16[512,256]{1,0:T(8,128)(2,1)S(1)}, u32[]{:S(2)}, u32[]{:S(2)}) collective-permute-start(bf16[512,256]{1,0:T(8,128)(2,1)S(1)} %bitcast.22), channel_id=1, source_target_pairs={{0,8},{8,0},{1,9},{9,1},{2,10},{10,2},{3,11},{11,3},{4,12},{12,4},... | collective-permute-start | bytes 786440 | tf_op jit(solution)/shard_map/ppermute | solution.py:432
  60.0 5.1 %collective-permute-start.12 = (bf16[448,256]{1,0:T(8,128)(2,1)S(1)}, bf16[448,256]{1,0:T(8,128)(2,1)S(1)}, u32[]{:S(2)}, u32[]{:S(2)}) collective-permute-start(bf16[448,256]{1,0:T(8,128)(2,1)S(1)} %get-tuple-element.83), channel_id=1, source_target_pairs={{8,16},{24,32},{40,48},{56,64},{72,80},{88,96},{104,112},{16,8},{3... | collective-permute-start | bytes 688136 | tf_op jit(solution)/shard_map/ppermute | solution.py:369
  67.2 1.9 %shard_map.82 = bf16[4,448,128]{2,1,0:T(8,128)(2,1)S(1)} custom-call(bf16[512,256]{1,0:T(8,128)(2,1)S(1)} %bitcast.24, bf16[512,256]{1,0:T(8,128)(2,1)S(1)} %collective-permute-done.6.other, bf16[3,34,16,192]{3,2,1,0:T(8,128)(2,1)S(1)} %copy-done.11, bf16[768,256]{1,0:T(8,128)(2,1)S(1)} %copy-done.7), custom_call_target="tpu_custom_call" | custom-call | flops 1048576 | bytes 65536 | tf_op jit(solution)/shard_map/pallas_call | solution.py:433
  70.0 4.6 %collective-permute-start.10 = (bf16[448,128]{1,0:T(8,128)(2,1)S(1)}, bf16[448,128]{1,0:T(8,128)(2,1)S(1)}, u32[]{:S(2)}, u32[]{:S(2)}) collective-permute-start(bf16[448,128]{1,0:T(8,128)(2,1)S(1)} %get-tuple-element.97), channel_id=1, source_target_pairs={{0,64},{16,80},{32,96},{48,112},{64,0},{80,16},{96,32},{112,48},{8... | collective-permute-start | bytes 344072 | tf_op jit(solution)/shard_map/ppermute | solution.py:454
  74.7 1.3 %collective-permute-start.9 = (bf16[448,128]{1,0:T(8,128)(2,1)S(1)}, bf16[448,128]{1,0:T(8,128)(2,1)S(1)}, u32[]{:S(2)}, u32[]{:S(2)}) collective-permute-start(bf16[448,128]{1,0:T(8,128)(2,1)S(1)} %get-tuple-element.98), channel_id=1, source_target_pairs={{0,32},{16,48},{32,64},{48,80},{64,96},{80,112},{96,0},{112,16},{8... | collective-permute-start | bytes 344072 | tf_op jit(solution)/shard_map/ppermute | solution.py:454
  76.0 3.9 %collective-permute-start.8 = (bf16[448,128]{1,0:T(8,128)(2,1)S(1)}, bf16[448,128]{1,0:T(8,128)(2,1)S(1)}, u32[]{:S(2)}, u32[]{:S(2)}) collective-permute-start(bf16[448,128]{1,0:T(8,128)(2,1)S(1)} %get-tuple-element.99.own), channel_id=1, source_target_pairs={{8,24},{24,8},{40,56},{56,40},{72,88},{88,72},{104,120},{120,104},... | collective-permute-start | bytes 344072 | tf_op jit(solution)/shard_map/ppermute | solution.py:454
  80.0 2.1 %shard_map.84 = (f32[512,256]{1,0:T(8,128)S(1)}, bf16[3,256,768]{2,1,0:T(8,128)(2,1)S(1)}) custom-call(bf16[640,256]{1,0:T(8,128)(2,1)S(1)} %shard_map.80.grad, bf16[640,256]{1,0:T(8,128)(2,1)S(1)} %copy-done.14, bf16[9,3,256,256]{3,2,1,0:T(8,128)(2,1)S(1)} %bitcast.19), custom_call_target="tpu_custom_call" | custom-call | flops 2147483648 | bytes 65536 | tf_op jit(solution)/shard_map/pallas_call | solution.py:455
  83.1 4.1 %collective-permute-done.10.second = bf16[448,128]{1,0:T(8,128)(2,1)S(1)} collective-permute-done((bf16[448,128]{1,0:T(8,128)(2,1)S(1)}, bf16[448,128]{1,0:T(8,128)(2,1)S(1)}, u32[]{:S(2)}, u32[]{:S(2)}) %collective-permute-start.10) | collective-permute-done | bytes 114720 | tf_op jit(solution)/shard_map/ppermute | solution.py:454
  87.4 1.2 %collective-permute-done.13.other = bf16[224,128]{1,0:T(8,128)(2,1)S(1)} collective-permute-done((bf16[224,128]{1,0:T(8,128)(2,1)S(1)}, bf16[224,128]{1,0:T(8,128)(2,1)S(1)}, u32[]{:S(2)}, u32[]{:S(2)}) %collective-permute-start.13) | collective-permute-done | bytes 57376 | tf_op jit(solution)/shard_map/ppermute | solution.py:475
  89.5 1.3 %copy-done.9 = bf16[3,256,768]{2,1,0:T(8,128)(2,1)S(1)} copy-done((bf16[3,256,768]{2,1,0:T(8,128)(2,1)S(1)}, bf16[3,256,768]{2,1,0:T(8,128)(2,1)}, u32[]{:S(2)}) %copy-start.9) | copy-done | bytes 1179672
  90.8 1.4 %shard_map.86 = (bf16[512,256]{1,0:T(8,128)(2,1)}, bf16[512,64]{1,0:T(8,128)(2,1)}, f32[108,128]{1,0:T(8,128)}) custom-call(f32[512,256]{1,0:T(8,128)S(1)} %get-tuple-element.86.total, bf16[448,256]{1,0:T(8,128)(2,1)S(1)} %collective-permute-done.12.outer, bf16[3,256,768]{2,1,0:T(8,128)(2,1)S(1)} %copy-done.9, f32[512,64]{1,0:T(8,128)S(1)} %copy-done.16, ...), custom_call_target="tpu_custom_call" | custom-call | flops 1073741824 | bytes 65536 | tf_op jit(solution)/shard_map/pallas_call | solution.py:469
  (60 shorter events, 14.5 us)
Async XLA Ops:
  2.4 11.2 %collective-permute-start.1 = (bf16[384,256]{1,0:T(8,128)(2,1)}, bf16[384,256]{1,0:T(8,128)(2,1)S(1)}, u32[]{:S(2)}, u32[]{:S(2)}) collective-permute-start(bf16[384,256]{1,0:T(8,128)(2,1)} %get-tuple-element.51), channel_id=1, source_target_pairs={{8,16},{24,32},{40,48},{56,64},{72,80},{88,96},{104,112},{16,8},{3... | collective-permute-start | bytes 589832 | tf_op jit(solution)/shard_map/ppermute | solution.py:369
  8.6 5.0 %collective-permute-start = (bf16[384,256]{1,0:T(8,128)(2,1)}, bf16[384,256]{1,0:T(8,128)(2,1)S(1)}, u32[]{:S(2)}, u32[]{:S(2)}) collective-permute-start(bf16[384,256]{1,0:T(8,128)(2,1)} %get-tuple-element.50.token), channel_id=1, source_target_pairs={{0,8},{8,0},{1,9},{9,1},{2,10},{10,2},{3,11},{11,3},{4,12},{12,4},... | collective-permute-start | bytes 589832 | tf_op jit(solution)/shard_map/ppermute | solution.py:369
  12.7 14.8 %copy-start.1 = (bf16[2,8,32,256]{3,2,1,0:T(8,128)(2,1)S(1)}, bf16[2,8,32,256]{3,2,1,0:T(8,128)(2,1)}, u32[]{:S(2)}) copy-start(bf16[2,8,32,256]{3,2,1,0:T(8,128)(2,1)} %own.5) | copy-start | bytes 786436
  13.7 5.3 %collective-permute-start.2 = (bf16[256,256]{1,0:T(8,128)(2,1)S(1)}, bf16[256,256]{1,0:T(8,128)(2,1)S(1)}, u32[]{:S(2)}, u32[]{:S(2)}) collective-permute-start(bf16[256,256]{1,0:T(8,128)(2,1)S(1)} %get-tuple-element.61), channel_id=1, source_target_pairs={{0,1},{1,0},{2,3},{3,2},{4,5},{5,4},{6,7},{7,6},{8,9},{9,8},{10,11... | collective-permute-start | bytes 393224 | tf_op jit(solution)/shard_map/ppermute | solution.py:369
  14.2 4.8 %collective-permute-start.3 = (bf16[256,256]{1,0:T(8,128)(2,1)S(1)}, bf16[256,256]{1,0:T(8,128)(2,1)S(1)}, u32[]{:S(2)}, u32[]{:S(2)}) collective-permute-start(bf16[256,256]{1,0:T(8,128)(2,1)S(1)} %get-tuple-element.62), channel_id=1, source_target_pairs={{1,2},{3,4},{5,6},{2,1},{4,3},{6,5},{9,10},{11,12},{13,14},{10,9},... | collective-permute-start | bytes 393224 | tf_op jit(solution)/shard_map/ppermute | solution.py:369
  19.0 16.0 %all-to-all-start = ((bf16[8,96,256]{2,1,0:T(8,128)(2,1)}), bf16[8,96,256]{2,1,0:T(8,128)(2,1)S(1)}, u32[]{:S(2)}, u32[]{:S(2)}) async-start(bf16[8,96,256]{2,1,0:T(8,128)(2,1)} %get-tuple-element.66), calls=%async_computation | async-start | bytes 786432 | tf_op jit(solution)/shard_map/all_to_all | solution.py:396
  33.3 7.5 %collective-permute-start.4 = (bf16[768,256]{1,0:T(8,128)(2,1)S(1)}, bf16[768,256]{1,0:T(8,128)(2,1)S(1)}, u32[]{:S(2)}, u32[]{:S(2)}) collective-permute-start(bf16[768,256]{1,0:T(8,128)(2,1)S(1)} %get-tuple-element.65), channel_id=1, source_target_pairs={{0,8},{8,0},{1,9},{9,1},{2,10},{10,2},{3,11},{11,3},{4,12},{12,4},... | collective-permute-start | bytes 1179656 | tf_op jit(solution)/shard_map/ppermute | solution.py:408
  35.0 5.8 %collective-permute-start.5 = (bf16[640,256]{1,0:T(8,128)(2,1)S(1)}, bf16[640,256]{1,0:T(8,128)(2,1)S(1)}, u32[]{:S(2)}, u32[]{:S(2)}) collective-permute-start(bf16[640,256]{1,0:T(8,128)(2,1)S(1)} %shard_map.80.grad), channel_id=1, source_target_pairs={{0,8},{8,0},{1,9},{9,1},{2,10},{10,2},{3,11},{11,3},{4,12},{12,4},... | collective-permute-start | bytes 983048 | tf_op jit(solution)/shard_map/ppermute | solution.py:417
  37.4 10.5 %all-to-all-start.1 = ((bf16[8,64,256]{2,1,0:T(8,128)(2,1)}), bf16[8,64,256]{2,1,0:T(8,128)(2,1)S(1)}, u32[]{:S(2)}, u32[]{:S(2)}) async-start(bf16[8,64,256]{2,1,0:T(8,128)(2,1)} %get-tuple-element.68), calls=%async_computation.1 | async-start | bytes 524288 | tf_op jit(solution)/shard_map/all_to_all | solution.py:409
  40.8 3.8 %copy-start.6 = (bf16[768,256]{1,0:T(8,128)(2,1)}, bf16[768,256]{1,0:T(8,128)(2,1)S(1)}, u32[]{:S(2)}) copy-start(bf16[768,256]{1,0:T(8,128)(2,1)S(1)} %collective-permute-done.4.far) | copy-start | bytes 1179652
  40.8 3.8 %copy-start.13 = (bf16[640,256]{1,0:T(8,128)(2,1)}, bf16[640,256]{1,0:T(8,128)(2,1)S(1)}, u32[]{:S(2)}) copy-start(bf16[640,256]{1,0:T(8,128)(2,1)S(1)} %collective-permute-done.5.other) | copy-start | bytes 983044
  47.8 10.2 %copy-start.5 = (bf16[27,256,64]{1,2,0:T(8,128)(2,1)S(1)}, bf16[27,256,64]{1,2,0:T(8,128)(2,1)}, u32[]{:S(2)}) copy-start(bf16[27,256,64]{1,2,0:T(8,128)(2,1)} %param.6) | copy-start | bytes 2654212
  47.8 41.6 %all-to-all-start.2 = ((bf16[64,54,256]{2,1,0:T(8,128)(2,1)}), bf16[64,54,256]{2,1,0:T(8,128)(2,1)S(1)}, u32[]{:S(2)}, u32[]{:S(2)}) async-start(bf16[64,54,256]{2,1,0:T(8,128)(2,1)} %shard_map.81), calls=%async_computation.2 | async-start | bytes 3670016 | tf_op jit(solution)/shard_map/all_to_all | solution.py:430
  56.3 8.7 %collective-permute-start.6 = (bf16[512,256]{1,0:T(8,128)(2,1)S(1)}, bf16[512,256]{1,0:T(8,128)(2,1)S(1)}, u32[]{:S(2)}, u32[]{:S(2)}) collective-permute-start(bf16[512,256]{1,0:T(8,128)(2,1)S(1)} %bitcast.22), channel_id=1, source_target_pairs={{0,8},{8,0},{1,9},{9,1},{2,10},{10,2},{3,11},{11,3},{4,12},{12,4},... | collective-permute-start | bytes 786440 | tf_op jit(solution)/shard_map/ppermute | solution.py:432
  58.0 21.9 %copy-start.3 = (bf16[27,256,256]{2,1,0:T(8,128)(2,1)S(1)}, bf16[27,256,256]{2,1,0:T(8,128)(2,1)}, u32[]{:S(2)}) copy-start(bf16[27,256,256]{2,1,0:T(8,128)(2,1)} %param.5) | copy-start | bytes 10616836
  59.9 9.2 %collective-permute-start.7 = (bf16[128,256]{1,0:T(8,128)(2,1)S(1)}, bf16[128,256]{1,0:T(8,128)(2,1)S(1)}, u32[]{:S(2)}, u32[]{:S(2)}) collective-permute-start(bf16[128,256]{1,0:T(8,128)(2,1)S(1)} %get-tuple-element.72), channel_id=1, source_target_pairs={{0,8},{8,0},{1,9},{9,1},{2,10},{10,2},{3,11},{11,3},{4,12},{12,4},... | collective-permute-start | bytes 196616 | tf_op jit(solution)/shard_map/ppermute | solution.py:369
  60.0 29.5 %collective-permute-start.12 = (bf16[448,256]{1,0:T(8,128)(2,1)S(1)}, bf16[448,256]{1,0:T(8,128)(2,1)S(1)}, u32[]{:S(2)}, u32[]{:S(2)}) collective-permute-start(bf16[448,256]{1,0:T(8,128)(2,1)S(1)} %get-tuple-element.83), channel_id=1, source_target_pairs={{8,16},{24,32},{40,48},{56,64},{72,80},{88,96},{104,112},{16,8},{3... | collective-permute-start | bytes 688136 | tf_op jit(solution)/shard_map/ppermute | solution.py:369
  67.2 12.8 %copy-start.14 = (bf16[640,256]{1,0:T(8,128)(2,1)S(1)}, bf16[640,256]{1,0:T(8,128)(2,1)}, u32[]{:S(2)}) copy-start(bf16[640,256]{1,0:T(8,128)(2,1)} %copy-done.13) | copy-start | bytes 983044
  69.2 13.9 %collective-permute-start.11 = (bf16[448,128]{1,0:T(8,128)(2,1)S(1)}, bf16[448,128]{1,0:T(8,128)(2,1)S(1)}, u32[]{:S(2)}, u32[]{:S(2)}) collective-permute-start(bf16[448,128]{1,0:T(8,128)(2,1)S(1)} %get-tuple-element.96), channel_id=1, source_target_pairs={{0,96},{16,112},{32,0},{48,16},{64,32},{80,48},{96,64},{112,80},{8... | collective-permute-start | bytes 344072 | tf_op jit(solution)/shard_map/ppermute | solution.py:454
  70.0 17.2 %collective-permute-start.10 = (bf16[448,128]{1,0:T(8,128)(2,1)S(1)}, bf16[448,128]{1,0:T(8,128)(2,1)S(1)}, u32[]{:S(2)}, u32[]{:S(2)}) collective-permute-start(bf16[448,128]{1,0:T(8,128)(2,1)S(1)} %get-tuple-element.97), channel_id=1, source_target_pairs={{0,64},{16,80},{32,96},{48,112},{64,0},{80,16},{96,32},{112,48},{8... | collective-permute-start | bytes 344072 | tf_op jit(solution)/shard_map/ppermute | solution.py:454
  74.7 12.6 %collective-permute-start.9 = (bf16[448,128]{1,0:T(8,128)(2,1)S(1)}, bf16[448,128]{1,0:T(8,128)(2,1)S(1)}, u32[]{:S(2)}, u32[]{:S(2)}) collective-permute-start(bf16[448,128]{1,0:T(8,128)(2,1)S(1)} %get-tuple-element.98), channel_id=1, source_target_pairs={{0,32},{16,48},{32,64},{48,80},{64,96},{80,112},{96,0},{112,16},{8... | collective-permute-start | bytes 344072 | tf_op jit(solution)/shard_map/ppermute | solution.py:454
  76.0 11.2 %collective-permute-start.8 = (bf16[448,128]{1,0:T(8,128)(2,1)S(1)}, bf16[448,128]{1,0:T(8,128)(2,1)S(1)}, u32[]{:S(2)}, u32[]{:S(2)}) collective-permute-start(bf16[448,128]{1,0:T(8,128)(2,1)S(1)} %get-tuple-element.99.own), channel_id=1, source_target_pairs={{8,24},{24,8},{40,56},{56,40},{72,88},{88,72},{104,120},{120,104},... | collective-permute-start | bytes 344072 | tf_op jit(solution)/shard_map/ppermute | solution.py:454
  80.0 9.5 %copy-start.16 = (f32[512,64]{1,0:T(8,128)S(1)}, f32[512,64]{1,0:T(8,128)}, u32[]{:S(2)}) copy-start(f32[512,64]{1,0:T(8,128)} %copy-done.15) | copy-start | bytes 393220
  87.3 1.3 %collective-permute-start.13 = (bf16[224,128]{1,0:T(8,128)(2,1)S(1)}, bf16[224,128]{1,0:T(8,128)(2,1)S(1)}, u32[]{:S(2)}, u32[]{:S(2)}) collective-permute-start(bf16[224,128]{1,0:T(8,128)(2,1)S(1)} %get-tuple-element.81), channel_id=1, source_target_pairs={{0,8},{8,0},{1,9},{9,1},{2,10},{10,2},{3,11},{11,3},{4,12},{12,4},... | collective-permute-start | bytes 172040 | tf_op jit(solution)/shard_map/ppermute | solution.py:475
  (11 other events, 12.0 us)

commit v10 on v9

--- a/solution.py
+++ b/solution.py
@@ -473,6 +473,7 @@
         flops=2**30,
     )(total, outer, rest, centre, inner, spread)
     arrived = lax.ppermute(sent, "c", SWAP)
+    grad_fine, arrived = lax.optimization_barrier((grad_fine, arrived))
     grad_coarse = call(
         functools.partial(coarse_sum_kernel, 1.0 / math.sqrt(cells // 8)),
         array(64, 432, dtype=F32),

time: 92.9 us -> 93.1 us (level)
    ppermute x1, waiting for transfers between devices: 1.23 us -> 0.01 us  [body(): arrived = lax.ppermute(sent, 'c', SWAP)]
  transfers between devices with their start and end apart: 17 -> 17, of which waited for: 6 -> 6; matrix products, arithmetic and copies ran while one was open for 0% -> 0% of each run, Pallas kernels for 17% -> 18%
where the time goes in v10:
time: 93.1 us; the launch traced here: 91.5 us
  starting transfers between devices  49.1 us (53%)
  Pallas kernels  19.1 us (21%)
  local copies, waits for them, and re-layouts  12 us (13%)
  waiting for transfers between devices  10.5 us (11%)
    unnamed x36, local copies, waits for them, and re-layouts  12 us
    ppermute x3, starting transfers between devices, swap(): lax.ppermute(outer, axis, pairs)  11.9 us
    ppermute x4, starting transfers between devices, body(): arrived.append(lax.ppermute(coarse_terms[step], SP, pairs))  10.8 us
    all_to_all x1, starting transfers between devices, body(): parts = lax.all_to_all(partial, FL, 0, 0, tiled=True)  8.55 us
    all_to_all x1, starting transfers between devices, body(): spread = lax.all_to_all(terms, ('x', 'yh', 'z', 'yl'), 0, 0, tiled=True)  8.5 us
    ppermute x4, waiting for transfers between devices, body(): arrived.append(lax.ppermute(coarse_terms[step], SP, pairs))  4.12 us
    pallas_call x1, Pallas kernels, body(): call(fine_weight_kernel, array(64, 54, 256), [VMEM] * 8, [pltpu.VMEM((6,...  3.77 us
    pallas_call x1, Pallas kernels, body(): call(fine_forward_kernel, (array(8, 64, 256), array(640, 256, dtype=F32),...  3.74 us
  transfers between devices with their start and end apart: 17, of which 6 were waited for; matrix products, arithmetic and copies ran while one was open for 0% of the time, Pallas kernels for 18%

profile of v10, /device:TPU:1, one launch (start us, length us, event | category | flops | bytes accessed | tf_op | source)
XLA Modules:
  0.0 91.5 jit_solution(3862764364244193696)
XLA Ops:
  0.6 1.8 %shard_map.75 = (bf16[384,256]{1,0:T(8,128)(2,1)}, bf16[384,256]{1,0:T(8,128)(2,1)}) custom-call(bf16[2,8,32,256]{3,2,1,0:T(8,128)(2,1)} %own.5, bf16[1,32,16,64]{3,2,1,0:T(8,128)(2,1)} %cot_hbm.1), custom_call_target="tpu_custom_call" | custom-call | flops 1048576 | bytes 65536 | tf_op jit(solution)/shard_map/pallas_call | solution.py:377
  2.4 6.2 %collective-permute-start.1 = (bf16[384,256]{1,0:T(8,128)(2,1)}, bf16[384,256]{1,0:T(8,128)(2,1)S(1)}, u32[]{:S(2)}, u32[]{:S(2)}) collective-permute-start(bf16[384,256]{1,0:T(8,128)(2,1)} %get-tuple-element.53), channel_id=1, source_target_pairs={{8,16},{24,32},{40,48},{56,64},{72,80},{88,96},{104,112},{16,8},{3... | collective-permute-start | bytes 589832 | tf_op jit(solution)/shard_map/ppermute | solution.py:369
  14.8 1.7 %shard_map.77 = (bf16[8,96,256]{2,1,0:T(8,128)(2,1)}, bf16[3,34,16,192]{3,2,1,0:T(8,128)(2,1)S(1)}) custom-call(bf16[1,32,16,64]{3,2,1,0:T(8,128)(2,1)S(1)} %get-tuple-element.59.cot, bf16[384,256]{1,0:T(8,128)(2,1)S(1)} %collective-permute-done.inner, bf16[384,256]{1,0:T(8,128)(2,1)S(1)} %collective-permute-done.1.outer, ...), custom_call_target="tpu_custom_call" | custom-call | flops 1048576 | bytes 65536 | tf_op jit(solution)/shard_map/pallas_call | solution.py:389
  17.4 1.6 %collective-permute-done.2.yinner = bf16[256,256]{1,0:T(8,128)(2,1)S(1)} collective-permute-done((bf16[256,256]{1,0:T(8,128)(2,1)S(1)}, bf16[256,256]{1,0:T(8,128)(2,1)S(1)}, u32[]{:S(2)}, u32[]{:S(2)}) %collective-permute-start.2) | collective-permute-done | bytes 131104 | tf_op jit(solution)/shard_map/ppermute | solution.py:369
  19.0 8.6 %all-to-all-start = ((bf16[8,96,256]{2,1,0:T(8,128)(2,1)}), bf16[8,96,256]{2,1,0:T(8,128)(2,1)S(1)}, u32[]{:S(2)}, u32[]{:S(2)}) async-start(bf16[8,96,256]{2,1,0:T(8,128)(2,1)} %get-tuple-element.68), calls=%async_computation | async-start | bytes 786432 | tf_op jit(solution)/shard_map/all_to_all | solution.py:396
  27.5 2.0 %copy-done.2 = bf16[27,256,256]{2,1,0:T(8,128)(2,1)S(1)} copy-done((bf16[27,256,256]{2,1,0:T(8,128)(2,1)S(1)}, bf16[27,256,256]{2,1,0:T(8,128)(2,1)}, u32[]{:S(2)}) %copy-start.2) | copy-done | bytes 3538968
  29.5 3.7 %shard_map.79 = (bf16[8,64,256]{2,1,0:T(8,128)(2,1)}, f32[640,256]{1,0:T(8,128)S(1)}, bf16[768,256]{1,0:T(8,128)(2,1)S(1)}) custom-call(bf16[2,8,32,256]{3,2,1,0:T(8,128)(2,1)S(1)} %copy-done.1, bf16[384,256]{1,0:T(8,128)(2,1)S(1)} %collective-permute-done.inner, bf16[384,256]{1,0:T(8,128)(2,1)S(1)} %collective-permute-done.1.outer, ...), custom_call_target="tpu_custom_call" | custom-call | flops 1048576 | bytes 65536 | tf_op jit(solution)/shard_map/pallas_call | solution.py:398
  33.3 1.3 %collective-permute-start.4 = (bf16[768,256]{1,0:T(8,128)(2,1)S(1)}, bf16[768,256]{1,0:T(8,128)(2,1)S(1)}, u32[]{:S(2)}, u32[]{:S(2)}) collective-permute-start(bf16[768,256]{1,0:T(8,128)(2,1)S(1)} %get-tuple-element.67), channel_id=1, source_target_pairs={{0,8},{8,0},{1,9},{9,1},{2,10},{10,2},{3,11},{11,3},{4,12},{12,4},... | collective-permute-start | bytes 1179656 | tf_op jit(solution)/shard_map/ppermute | solution.py:408
  35.0 2.3 %collective-permute-start.5 = (bf16[640,256]{1,0:T(8,128)(2,1)S(1)}, bf16[640,256]{1,0:T(8,128)(2,1)S(1)}, u32[]{:S(2)}, u32[]{:S(2)}) collective-permute-start(bf16[640,256]{1,0:T(8,128)(2,1)S(1)} %shard_map.80.grad), channel_id=1, source_target_pairs={{0,8},{8,0},{1,9},{9,1},{2,10},{10,2},{3,11},{11,3},{4,12},{12,4},... | collective-permute-start | bytes 983048 | tf_op jit(solution)/shard_map/ppermute | solution.py:417
  37.4 3.4 %all-to-all-start.1 = ((bf16[8,64,256]{2,1,0:T(8,128)(2,1)}), bf16[8,64,256]{2,1,0:T(8,128)(2,1)S(1)}, u32[]{:S(2)}, u32[]{:S(2)}) async-start(bf16[8,64,256]{2,1,0:T(8,128)(2,1)} %get-tuple-element.70), calls=%async_computation.1 | async-start | bytes 524288 | tf_op jit(solution)/shard_map/all_to_all | solution.py:409
  40.8 3.8 %shard_map.81 = bf16[64,54,256]{2,1,0:T(8,128)(2,1)} custom-call(bf16[2,8,32,256]{3,2,1,0:T(8,128)(2,1)S(1)} %copy-done.1, bf16[384,256]{1,0:T(8,128)(2,1)S(1)} %collective-permute-done.inner, bf16[384,256]{1,0:T(8,128)(2,1)S(1)} %collective-permute-done.1.outer, bf16[256,256]{1,0:T(8,128)(2,1)S(1)} %collective-permute-done.2.yinner, ...), custom_call_target="tpu_custom_call" | custom-call | flops 1048576 | bytes 65536 | tf_op jit(solution)/shard_map/pallas_call | solution.py:418
  44.6 3.2 %all-to-all-done.1 = bf16[8,64,256]{2,1,0:T(8,128)(2,1)S(1)} async-done(((bf16[8,64,256]{2,1,0:T(8,128)(2,1)}), bf16[8,64,256]{2,1,0:T(8,128)(2,1)S(1)}, u32[]{:S(2)}, u32[]{:S(2)}) %all-to-all-start.1) | async-done | bytes 262176 | tf_op jit(solution)/shard_map/all_to_all | solution.py:409
  47.8 8.5 %all-to-all-start.2 = ((bf16[64,54,256]{2,1,0:T(8,128)(2,1)}), bf16[64,54,256]{2,1,0:T(8,128)(2,1)S(1)}, u32[]{:S(2)}, u32[]{:S(2)}) async-start(bf16[64,54,256]{2,1,0:T(8,128)(2,1)} %shard_map.81), calls=%async_computation.2 | async-start | bytes 3670016 | tf_op jit(solution)/shard_map/all_to_all | solution.py:430
  56.3 1.6 %collective-permute-start.6 = (bf16[512,256]{1,0:T(8,128)(2,1)S(1)}, bf16[512,256]{1,0:T(8,128)(2,1)S(1)}, u32[]{:S(2)}, u32[]{:S(2)}) collective-permute-start(bf16[512,256]{1,0:T(8,128)(2,1)S(1)} %bitcast.22), channel_id=1, source_target_pairs={{0,8},{8,0},{1,9},{9,1},{2,10},{10,2},{3,11},{11,3},{4,12},{12,4},... | collective-permute-start | bytes 786440 | tf_op jit(solution)/shard_map/ppermute | solution.py:432
  58.0 1.2 %shard_map.83 = (f32[512,64]{1,0:T(8,128)S(1)}, bf16[128,256]{1,0:T(8,128)(2,1)S(1)}, bf16[448,256]{1,0:T(8,128)(2,1)S(1)}) custom-call(bf16[512,256]{1,0:T(8,128)(2,1)S(1)} %bitcast.23, bf16[9,192,256]{2,1,0:T(8,128)(2,1)S(1)} %bitcast.21, bf16[640,256]{1,0:T(8,128)(2,1)S(1)} %shard_map.80.grad), custom_call_target="tpu_custom_call" | custom-call | flops 1048576 | bytes 65536 | tf_op jit(solution)/shard_map/pallas_call | solution.py:440
  60.0 5.1 %collective-permute-start.12 = (bf16[448,256]{1,0:T(8,128)(2,1)S(1)}, bf16[448,256]{1,0:T(8,128)(2,1)S(1)}, u32[]{:S(2)}, u32[]{:S(2)}) collective-permute-start(bf16[448,256]{1,0:T(8,128)(2,1)S(1)} %get-tuple-element.85), channel_id=1, source_target_pairs={{8,16},{24,32},{40,48},{56,64},{72,80},{88,96},{104,112},{16,8},{3... | collective-permute-start | bytes 688136 | tf_op jit(solution)/shard_map/ppermute | solution.py:369
  67.2 1.9 %shard_map.82 = bf16[4,448,128]{2,1,0:T(8,128)(2,1)S(1)} custom-call(bf16[512,256]{1,0:T(8,128)(2,1)S(1)} %bitcast.24, bf16[512,256]{1,0:T(8,128)(2,1)S(1)} %collective-permute-done.6.other, bf16[3,34,16,192]{3,2,1,0:T(8,128)(2,1)S(1)} %copy-done.11, bf16[768,256]{1,0:T(8,128)(2,1)S(1)} %copy-done.7), custom_call_target="tpu_custom_call" | custom-call | flops 1048576 | bytes 65536 | tf_op jit(solution)/shard_map/pallas_call | solution.py:433
  70.0 4.6 %collective-permute-start.10 = (bf16[448,128]{1,0:T(8,128)(2,1)S(1)}, bf16[448,128]{1,0:T(8,128)(2,1)S(1)}, u32[]{:S(2)}, u32[]{:S(2)}) collective-permute-start(bf16[448,128]{1,0:T(8,128)(2,1)S(1)} %get-tuple-element.101), channel_id=1, source_target_pairs={{0,64},{16,80},{32,96},{48,112},{64,0},{80,16},{96,32},{112,48},{8... | collective-permute-start | bytes 344072 | tf_op jit(solution)/shard_map/ppermute | solution.py:454
  74.7 1.3 %collective-permute-start.9 = (bf16[448,128]{1,0:T(8,128)(2,1)S(1)}, bf16[448,128]{1,0:T(8,128)(2,1)S(1)}, u32[]{:S(2)}, u32[]{:S(2)}) collective-permute-start(bf16[448,128]{1,0:T(8,128)(2,1)S(1)} %get-tuple-element.102), channel_id=1, source_target_pairs={{0,32},{16,48},{32,64},{48,80},{64,96},{80,112},{96,0},{112,16},{8... | collective-permute-start | bytes 344072 | tf_op jit(solution)/shard_map/ppermute | solution.py:454
  76.0 3.9 %collective-permute-start.8 = (bf16[448,128]{1,0:T(8,128)(2,1)S(1)}, bf16[448,128]{1,0:T(8,128)(2,1)S(1)}, u32[]{:S(2)}, u32[]{:S(2)}) collective-permute-start(bf16[448,128]{1,0:T(8,128)(2,1)S(1)} %get-tuple-element.103.own), channel_id=1, source_target_pairs={{8,24},{24,8},{40,56},{56,40},{72,88},{88,72},{104,120},{120,104},... | collective-permute-start | bytes 344072 | tf_op jit(solution)/shard_map/ppermute | solution.py:454
  80.0 2.1 %shard_map.84 = (f32[512,256]{1,0:T(8,128)S(1)}, bf16[3,256,768]{2,1,0:T(8,128)(2,1)S(1)}) custom-call(bf16[640,256]{1,0:T(8,128)(2,1)S(1)} %shard_map.80.grad, bf16[640,256]{1,0:T(8,128)(2,1)S(1)} %copy-done.14, bf16[9,3,256,256]{3,2,1,0:T(8,128)(2,1)S(1)} %bitcast.19), custom_call_target="tpu_custom_call" | custom-call | flops 2147483648 | bytes 65536 | tf_op jit(solution)/shard_map/pallas_call | solution.py:455
  83.1 4.1 %collective-permute-done.10.second = bf16[448,128]{1,0:T(8,128)(2,1)S(1)} collective-permute-done((bf16[448,128]{1,0:T(8,128)(2,1)S(1)}, bf16[448,128]{1,0:T(8,128)(2,1)S(1)}, u32[]{:S(2)}, u32[]{:S(2)}) %collective-permute-start.10) | collective-permute-done | bytes 114720 | tf_op jit(solution)/shard_map/ppermute | solution.py:454
  88.1 1.3 %copy-done.9 = bf16[3,256,768]{2,1,0:T(8,128)(2,1)S(1)} copy-done((bf16[3,256,768]{2,1,0:T(8,128)(2,1)S(1)}, bf16[3,256,768]{2,1,0:T(8,128)(2,1)}, u32[]{:S(2)}) %copy-start.9) | copy-done | bytes 1179672
  89.3 1.4 %shard_map.86 = (bf16[512,256]{1,0:T(8,128)(2,1)}, bf16[512,64]{1,0:T(8,128)(2,1)}, f32[108,128]{1,0:T(8,128)}) custom-call(f32[512,256]{1,0:T(8,128)S(1)} %get-tuple-element.88.total, bf16[448,256]{1,0:T(8,128)(2,1)S(1)} %collective-permute-done.12.outer, bf16[3,256,768]{2,1,0:T(8,128)(2,1)S(1)} %copy-done.9, f32[512,64]{1,0:T(8,128)S(1)} %copy-done.16, ...), custom_call_target="tpu_custom_call" | custom-call | flops 1073741824 | bytes 65536 | tf_op jit(solution)/shard_map/pallas_call | solution.py:469
  (60 shorter events, 14.0 us)
Async XLA Ops:
  2.4 11.2 %collective-permute-start.1 = (bf16[384,256]{1,0:T(8,128)(2,1)}, bf16[384,256]{1,0:T(8,128)(2,1)S(1)}, u32[]{:S(2)}, u32[]{:S(2)}) collective-permute-start(bf16[384,256]{1,0:T(8,128)(2,1)} %get-tuple-element.53), channel_id=1, source_target_pairs={{8,16},{24,32},{40,48},{56,64},{72,80},{88,96},{104,112},{16,8},{3... | collective-permute-start | bytes 589832 | tf_op jit(solution)/shard_map/ppermute | solution.py:369
  8.6 5.0 %collective-permute-start = (bf16[384,256]{1,0:T(8,128)(2,1)}, bf16[384,256]{1,0:T(8,128)(2,1)S(1)}, u32[]{:S(2)}, u32[]{:S(2)}) collective-permute-start(bf16[384,256]{1,0:T(8,128)(2,1)} %get-tuple-element.52.token), channel_id=1, source_target_pairs={{0,8},{8,0},{1,9},{9,1},{2,10},{10,2},{3,11},{11,3},{4,12},{12,4},... | collective-permute-start | bytes 589832 | tf_op jit(solution)/shard_map/ppermute | solution.py:369
  12.7 14.8 %copy-start.1 = (bf16[2,8,32,256]{3,2,1,0:T(8,128)(2,1)S(1)}, bf16[2,8,32,256]{3,2,1,0:T(8,128)(2,1)}, u32[]{:S(2)}) copy-start(bf16[2,8,32,256]{3,2,1,0:T(8,128)(2,1)} %own.5) | copy-start | bytes 786436
  13.7 5.3 %collective-permute-start.2 = (bf16[256,256]{1,0:T(8,128)(2,1)S(1)}, bf16[256,256]{1,0:T(8,128)(2,1)S(1)}, u32[]{:S(2)}, u32[]{:S(2)}) collective-permute-start(bf16[256,256]{1,0:T(8,128)(2,1)S(1)} %get-tuple-element.63), channel_id=1, source_target_pairs={{0,1},{1,0},{2,3},{3,2},{4,5},{5,4},{6,7},{7,6},{8,9},{9,8},{10,11... | collective-permute-start | bytes 393224 | tf_op jit(solution)/shard_map/ppermute | solution.py:369
  14.2 4.8 %collective-permute-start.3 = (bf16[256,256]{1,0:T(8,128)(2,1)S(1)}, bf16[256,256]{1,0:T(8,128)(2,1)S(1)}, u32[]{:S(2)}, u32[]{:S(2)}) collective-permute-start(bf16[256,256]{1,0:T(8,128)(2,1)S(1)} %get-tuple-element.64), channel_id=1, source_target_pairs={{1,2},{3,4},{5,6},{2,1},{4,3},{6,5},{9,10},{11,12},{13,14},{10,9},... | collective-permute-start | bytes 393224 | tf_op jit(solution)/shard_map/ppermute | solution.py:369
  19.0 16.0 %all-to-all-start = ((bf16[8,96,256]{2,1,0:T(8,128)(2,1)}), bf16[8,96,256]{2,1,0:T(8,128)(2,1)S(1)}, u32[]{:S(2)}, u32[]{:S(2)}) async-start(bf16[8,96,256]{2,1,0:T(8,128)(2,1)} %get-tuple-element.68), calls=%async_computation | async-start | bytes 786432 | tf_op jit(solution)/shard_map/all_to_all | solution.py:396
  33.3 7.5 %collective-permute-start.4 = (bf16[768,256]{1,0:T(8,128)(2,1)S(1)}, bf16[768,256]{1,0:T(8,128)(2,1)S(1)}, u32[]{:S(2)}, u32[]{:S(2)}) collective-permute-start(bf16[768,256]{1,0:T(8,128)(2,1)S(1)} %get-tuple-element.67), channel_id=1, source_target_pairs={{0,8},{8,0},{1,9},{9,1},{2,10},{10,2},{3,11},{11,3},{4,12},{12,4},... | collective-permute-start | bytes 1179656 | tf_op jit(solution)/shard_map/ppermute | solution.py:408
  35.0 5.8 %collective-permute-start.5 = (bf16[640,256]{1,0:T(8,128)(2,1)S(1)}, bf16[640,256]{1,0:T(8,128)(2,1)S(1)}, u32[]{:S(2)}, u32[]{:S(2)}) collective-permute-start(bf16[640,256]{1,0:T(8,128)(2,1)S(1)} %shard_map.80.grad), channel_id=1, source_target_pairs={{0,8},{8,0},{1,9},{9,1},{2,10},{10,2},{3,11},{11,3},{4,12},{12,4},... | collective-permute-start | bytes 983048 | tf_op jit(solution)/shard_map/ppermute | solution.py:417
  37.4 10.5 %all-to-all-start.1 = ((bf16[8,64,256]{2,1,0:T(8,128)(2,1)}), bf16[8,64,256]{2,1,0:T(8,128)(2,1)S(1)}, u32[]{:S(2)}, u32[]{:S(2)}) async-start(bf16[8,64,256]{2,1,0:T(8,128)(2,1)} %get-tuple-element.70), calls=%async_computation.1 | async-start | bytes 524288 | tf_op jit(solution)/shard_map/all_to_all | solution.py:409
  40.8 3.8 %copy-start.6 = (bf16[768,256]{1,0:T(8,128)(2,1)}, bf16[768,256]{1,0:T(8,128)(2,1)S(1)}, u32[]{:S(2)}) copy-start(bf16[768,256]{1,0:T(8,128)(2,1)S(1)} %collective-permute-done.4.far) | copy-start | bytes 1179652
  40.8 3.8 %copy-start.13 = (bf16[640,256]{1,0:T(8,128)(2,1)}, bf16[640,256]{1,0:T(8,128)(2,1)S(1)}, u32[]{:S(2)}) copy-start(bf16[640,256]{1,0:T(8,128)(2,1)S(1)} %collective-permute-done.5.other) | copy-start | bytes 983044
  47.8 10.2 %copy-start.5 = (bf16[27,256,64]{1,2,0:T(8,128)(2,1)S(1)}, bf16[27,256,64]{1,2,0:T(8,128)(2,1)}, u32[]{:S(2)}) copy-start(bf16[27,256,64]{1,2,0:T(8,128)(2,1)} %param.6) | copy-start | bytes 2654212
  47.8 40.2 %all-to-all-start.2 = ((bf16[64,54,256]{2,1,0:T(8,128)(2,1)}), bf16[64,54,256]{2,1,0:T(8,128)(2,1)S(1)}, u32[]{:S(2)}, u32[]{:S(2)}) async-start(bf16[64,54,256]{2,1,0:T(8,128)(2,1)} %shard_map.81), calls=%async_computation.2 | async-start | bytes 3670016 | tf_op jit(solution)/shard_map/all_to_all | solution.py:430
  56.3 8.7 %collective-permute-start.6 = (bf16[512,256]{1,0:T(8,128)(2,1)S(1)}, bf16[512,256]{1,0:T(8,128)(2,1)S(1)}, u32[]{:S(2)}, u32[]{:S(2)}) collective-permute-start(bf16[512,256]{1,0:T(8,128)(2,1)S(1)} %bitcast.22), channel_id=1, source_target_pairs={{0,8},{8,0},{1,9},{9,1},{2,10},{10,2},{3,11},{11,3},{4,12},{12,4},... | collective-permute-start | bytes 786440 | tf_op jit(solution)/shard_map/ppermute | solution.py:432
  58.0 21.9 %copy-start.3 = (bf16[27,256,256]{2,1,0:T(8,128)(2,1)S(1)}, bf16[27,256,256]{2,1,0:T(8,128)(2,1)}, u32[]{:S(2)}) copy-start(bf16[27,256,256]{2,1,0:T(8,128)(2,1)} %param.5) | copy-start | bytes 10616836
  59.9 9.2 %collective-permute-start.7 = (bf16[128,256]{1,0:T(8,128)(2,1)S(1)}, bf16[128,256]{1,0:T(8,128)(2,1)S(1)}, u32[]{:S(2)}, u32[]{:S(2)}) collective-permute-start(bf16[128,256]{1,0:T(8,128)(2,1)S(1)} %get-tuple-element.74), channel_id=1, source_target_pairs={{0,8},{8,0},{1,9},{9,1},{2,10},{10,2},{3,11},{11,3},{4,12},{12,4},... | collective-permute-start | bytes 196616 | tf_op jit(solution)/shard_map/ppermute | solution.py:369
  60.0 28.1 %collective-permute-start.12 = (bf16[448,256]{1,0:T(8,128)(2,1)S(1)}, bf16[448,256]{1,0:T(8,128)(2,1)S(1)}, u32[]{:S(2)}, u32[]{:S(2)}) collective-permute-start(bf16[448,256]{1,0:T(8,128)(2,1)S(1)} %get-tuple-element.85), channel_id=1, source_target_pairs={{8,16},{24,32},{40,48},{56,64},{72,80},{88,96},{104,112},{16,8},{3... | collective-permute-start | bytes 688136 | tf_op jit(solution)/shard_map/ppermute | solution.py:369
  67.2 12.8 %copy-start.14 = (bf16[640,256]{1,0:T(8,128)(2,1)S(1)}, bf16[640,256]{1,0:T(8,128)(2,1)}, u32[]{:S(2)}) copy-start(bf16[640,256]{1,0:T(8,128)(2,1)} %copy-done.13) | copy-start | bytes 983044
  69.2 13.9 %collective-permute-start.11 = (bf16[448,128]{1,0:T(8,128)(2,1)S(1)}, bf16[448,128]{1,0:T(8,128)(2,1)S(1)}, u32[]{:S(2)}, u32[]{:S(2)}) collective-permute-start(bf16[448,128]{1,0:T(8,128)(2,1)S(1)} %get-tuple-element.100), channel_id=1, source_target_pairs={{0,96},{16,112},{32,0},{48,16},{64,32},{80,48},{96,64},{112,80},{8... | collective-permute-start | bytes 344072 | tf_op jit(solution)/shard_map/ppermute | solution.py:454
  70.0 17.2 %collective-permute-start.10 = (bf16[448,128]{1,0:T(8,128)(2,1)S(1)}, bf16[448,128]{1,0:T(8,128)(2,1)S(1)}, u32[]{:S(2)}, u32[]{:S(2)}) collective-permute-start(bf16[448,128]{1,0:T(8,128)(2,1)S(1)} %get-tuple-element.101), channel_id=1, source_target_pairs={{0,64},{16,80},{32,96},{48,112},{64,0},{80,16},{96,32},{112,48},{8... | collective-permute-start | bytes 344072 | tf_op jit(solution)/shard_map/ppermute | solution.py:454
  74.7 12.6 %collective-permute-start.9 = (bf16[448,128]{1,0:T(8,128)(2,1)S(1)}, bf16[448,128]{1,0:T(8,128)(2,1)S(1)}, u32[]{:S(2)}, u32[]{:S(2)}) collective-permute-start(bf16[448,128]{1,0:T(8,128)(2,1)S(1)} %get-tuple-element.102), channel_id=1, source_target_pairs={{0,32},{16,48},{32,64},{48,80},{64,96},{80,112},{96,0},{112,16},{8... | collective-permute-start | bytes 344072 | tf_op jit(solution)/shard_map/ppermute | solution.py:454
  76.0 11.2 %collective-permute-start.8 = (bf16[448,128]{1,0:T(8,128)(2,1)S(1)}, bf16[448,128]{1,0:T(8,128)(2,1)S(1)}, u32[]{:S(2)}, u32[]{:S(2)}) collective-permute-start(bf16[448,128]{1,0:T(8,128)(2,1)S(1)} %get-tuple-element.103.own), channel_id=1, source_target_pairs={{8,24},{24,8},{40,56},{56,40},{72,88},{88,72},{104,120},{120,104},... | collective-permute-start | bytes 344072 | tf_op jit(solution)/shard_map/ppermute | solution.py:454
  80.0 8.1 %copy-start.16 = (f32[512,64]{1,0:T(8,128)S(1)}, f32[512,64]{1,0:T(8,128)}, u32[]{:S(2)}) copy-start(f32[512,64]{1,0:T(8,128)} %copy-done.15) | copy-start | bytes 393220
  87.3 3.4 %collective-permute-start.13 = (bf16[224,128]{1,0:T(8,128)(2,1)S(1)}, bf16[224,128]{1,0:T(8,128)(2,1)S(1)}, u32[]{:S(2)}, u32[]{:S(2)}) collective-permute-start(bf16[224,128]{1,0:T(8,128)(2,1)S(1)} %get-tuple-element.83), channel_id=1, source_target_pairs={{0,8},{8,0},{1,9},{9,1},{2,10},{10,2},{3,11},{11,3},{4,12},{12,4},... | collective-permute-start | bytes 172040 | tf_op jit(solution)/shard_map/ppermute | solution.py:475
  (11 other events, 12.0 us)

commit v11 on v9

--- a/solution.py
+++ b/solution.py
@@ -470,6 +470,7 @@
         functools.partial(last_kernel, 1.0 / math.sqrt(cells)),
         (array(512, 256), array(512, 64), array(108, 128, dtype=F32)),
         [VMEM] * 6,
+        limit=60,
         flops=2**30,
     )(total, outer, rest, centre, inner, spread)
     arrived = lax.ppermute(sent, "c", SWAP)

time: 92.9 us -> 94.8 us (1.020)
  Pallas kernels: 19.1 us -> 21.2 us
  local copies, waits for them, and re-layouts: 12 us -> 10.1 us
  starting transfers between devices: 49.1 us -> 50.2 us
    pallas_call x1, Pallas kernels: 1.36 us -> 3.61 us  [body(): call(functools.partial(last_kernel, 1.0 / math.sqrt(cells)), (array(512,...]
    unnamed x36 -> x32, local copies, waits for them, and re-layouts: 12 us -> 10.1 us
    ppermute x4, waiting for transfers between devices: 4.12 us -> 5.51 us  [body(): arrived.append(lax.ppermute(coarse_terms[step], SP, pairs))]
    all_to_all x1, waiting for transfers between devices: 3.25 us -> 1.96 us  [body(): got = lax.all_to_all(sent, FL, 0, 0, tiled=True)]
where the time goes in v11:
time: 94.8 us; the launch traced here: 94.1 us
  starting transfers between devices  50.2 us (53%)
  Pallas kernels  21.2 us (22%)
  waiting for transfers between devices  11.7 us (12%)
  local copies, waits for them, and re-layouts  10.1 us (11%)
    ppermute x3, starting transfers between devices, swap(): lax.ppermute(outer, axis, pairs)  11.8 us
    ppermute x4, starting transfers between devices, body(): arrived.append(lax.ppermute(coarse_terms[step], SP, pairs))  10.8 us
    unnamed x32, local copies, waits for them, and re-layouts  10.1 us
    all_to_all x1, starting transfers between devices, body(): spread = lax.all_to_all(terms, ('x', 'yh', 'z', 'yl'), 0, 0, tiled=True)  9.44 us
    all_to_all x1, starting transfers between devices, body(): parts = lax.all_to_all(partial, FL, 0, 0, tiled=True)  8.55 us
    ppermute x4, waiting for transfers between devices, body(): arrived.append(lax.ppermute(coarse_terms[step], SP, pairs))  5.51 us
    pallas_call x1, Pallas kernels, body(): call(fine_forward_kernel, (array(8, 64, 256), array(640, 256, dtype=F32),...  3.73 us
    pallas_call x1, Pallas kernels, body(): call(fine_weight_kernel, array(64, 54, 256), [VMEM] * 8, [pltpu.VMEM((6,...  3.7 us
  transfers between devices with their start and end apart: 17, of which 6 were waited for; matrix products, arithmetic and copies ran while one was open for 0% of the time, Pallas kernels for 17%

profile of v11, /device:TPU:1, one launch (start us, length us, event | category | flops | bytes accessed | tf_op | source)
XLA Modules:
  0.0 94.1 jit_solution(13458637522364257676)
XLA Ops:
  0.6 1.8 %shard_map.75 = (bf16[384,256]{1,0:T(8,128)(2,1)}, bf16[384,256]{1,0:T(8,128)(2,1)}) custom-call(bf16[2,8,32,256]{3,2,1,0:T(8,128)(2,1)} %own.5, bf16[1,32,16,64]{3,2,1,0:T(8,128)(2,1)} %cot_hbm.1), custom_call_target="tpu_custom_call" | custom-call | flops 1048576 | bytes 65536 | tf_op jit(solution)/shard_map/pallas_call | solution.py:377
  2.4 6.2 %collective-permute-start.1 = (bf16[384,256]{1,0:T(8,128)(2,1)}, bf16[384,256]{1,0:T(8,128)(2,1)S(1)}, u32[]{:S(2)}, u32[]{:S(2)}) collective-permute-start(bf16[384,256]{1,0:T(8,128)(2,1)} %get-tuple-element.51), channel_id=1, source_target_pairs={{8,16},{24,32},{40,48},{56,64},{72,80},{88,96},{104,112},{16,8},{3... | collective-permute-start | bytes 589832 | tf_op jit(solution)/shard_map/ppermute | solution.py:369
  14.9 1.7 %shard_map.77 = (bf16[8,96,256]{2,1,0:T(8,128)(2,1)}, bf16[3,34,16,192]{3,2,1,0:T(8,128)(2,1)S(1)}) custom-call(bf16[1,32,16,64]{3,2,1,0:T(8,128)(2,1)S(1)} %get-tuple-element.57.cot, bf16[384,256]{1,0:T(8,128)(2,1)S(1)} %collective-permute-done.inner, bf16[384,256]{1,0:T(8,128)(2,1)S(1)} %collective-permute-done.1.outer, ...), custom_call_target="tpu_custom_call" | custom-call | flops 1048576 | bytes 65536 | tf_op jit(solution)/shard_map/pallas_call | solution.py:389
  16.5 2.5 %collective-permute-done.2.yinner = bf16[256,256]{1,0:T(8,128)(2,1)S(1)} collective-permute-done((bf16[256,256]{1,0:T(8,128)(2,1)S(1)}, bf16[256,256]{1,0:T(8,128)(2,1)S(1)}, u32[]{:S(2)}, u32[]{:S(2)}) %collective-permute-start.2) | collective-permute-done | bytes 131104 | tf_op jit(solution)/shard_map/ppermute | solution.py:369
  19.0 8.6 %all-to-all-start = ((bf16[8,96,256]{2,1,0:T(8,128)(2,1)}), bf16[8,96,256]{2,1,0:T(8,128)(2,1)S(1)}, u32[]{:S(2)}, u32[]{:S(2)}) async-start(bf16[8,96,256]{2,1,0:T(8,128)(2,1)} %get-tuple-element.66), calls=%async_computation | async-start | bytes 786432 | tf_op jit(solution)/shard_map/all_to_all | solution.py:396
  27.6 2.0 %copy-done.2 = bf16[27,256,256]{2,1,0:T(8,128)(2,1)S(1)} copy-done((bf16[27,256,256]{2,1,0:T(8,128)(2,1)S(1)}, bf16[27,256,256]{2,1,0:T(8,128)(2,1)}, u32[]{:S(2)}) %copy-start.2) | copy-done | bytes 3538968
  29.5 3.7 %shard_map.79 = (bf16[8,64,256]{2,1,0:T(8,128)(2,1)S(1)}, f32[640,256]{1,0:T(8,128)S(1)}, bf16[768,256]{1,0:T(8,128)(2,1)}) custom-call(bf16[2,8,32,256]{3,2,1,0:T(8,128)(2,1)S(1)} %copy-done.1, bf16[384,256]{1,0:T(8,128)(2,1)S(1)} %collective-permute-done.inner, bf16[384,256]{1,0:T(8,128)(2,1)S(1)} %collective-permute-done.1.outer, ...), custom_call_target="tpu_custom_call" | custom-call | flops 1048576 | bytes 65536 | tf_op jit(solution)/shard_map/pallas_call | solution.py:398
  34.0 1.3 %collective-permute-start.4 = (bf16[768,256]{1,0:T(8,128)(2,1)}, bf16[768,256]{1,0:T(8,128)(2,1)S(1)}, u32[]{:S(2)}, u32[]{:S(2)}) collective-permute-start(bf16[768,256]{1,0:T(8,128)(2,1)} %get-tuple-element.65), channel_id=1, source_target_pairs={{0,8},{8,0},{1,9},{9,1},{2,10},{10,2},{3,11},{11,3},{4,12},{12,4},... | collective-permute-start | bytes 1179656 | tf_op jit(solution)/shard_map/ppermute | solution.py:408
  35.4 2.0 %collective-permute-start.5 = (bf16[640,256]{1,0:T(8,128)(2,1)S(1)}, bf16[640,256]{1,0:T(8,128)(2,1)S(1)}, u32[]{:S(2)}, u32[]{:S(2)}) collective-permute-start(bf16[640,256]{1,0:T(8,128)(2,1)S(1)} %shard_map.80.grad), channel_id=1, source_target_pairs={{0,8},{8,0},{1,9},{9,1},{2,10},{10,2},{3,11},{11,3},{4,12},{12,4},... | collective-permute-start | bytes 983048 | tf_op jit(solution)/shard_map/ppermute | solution.py:417
  37.4 3.6 %all-to-all-start.1 = ((bf16[8,64,256]{2,1,0:T(8,128)(2,1)}), bf16[8,64,256]{2,1,0:T(8,128)(2,1)S(1)}, u32[]{:S(2)}, u32[]{:S(2)}) async-start(bf16[8,64,256]{2,1,0:T(8,128)(2,1)} %copy-done.12), calls=%async_computation.1 | async-start | bytes 524288 | tf_op jit(solution)/shard_map/all_to_all | solution.py:409
  41.9 3.7 %shard_map.81 = bf16[64,54,256]{2,1,0:T(8,128)(2,1)} custom-call(bf16[2,8,32,256]{3,2,1,0:T(8,128)(2,1)S(1)} %copy-done.1, bf16[384,256]{1,0:T(8,128)(2,1)S(1)} %collective-permute-done.inner, bf16[384,256]{1,0:T(8,128)(2,1)S(1)} %collective-permute-done.1.outer, bf16[256,256]{1,0:T(8,128)(2,1)S(1)} %collective-permute-done.2.yinner, ...), custom_call_target="tpu_custom_call" | custom-call | flops 1048576 | bytes 65536 | tf_op jit(solution)/shard_map/pallas_call | solution.py:418
  45.5 2.0 %all-to-all-done.1 = bf16[8,64,256]{2,1,0:T(8,128)(2,1)S(1)} async-done(((bf16[8,64,256]{2,1,0:T(8,128)(2,1)}), bf16[8,64,256]{2,1,0:T(8,128)(2,1)S(1)}, u32[]{:S(2)}, u32[]{:S(2)}) %all-to-all-start.1) | async-done | bytes 262176 | tf_op jit(solution)/shard_map/all_to_all | solution.py:409
  47.5 9.4 %all-to-all-start.2 = ((bf16[64,54,256]{2,1,0:T(8,128)(2,1)}), bf16[64,54,256]{2,1,0:T(8,128)(2,1)}, u32[]{:S(2)}, u32[]{:S(2)}) async-start(bf16[64,54,256]{2,1,0:T(8,128)(2,1)} %shard_map.81), calls=%async_computation.2 | async-start | bytes 3670016 | tf_op jit(solution)/shard_map/all_to_all | solution.py:430
  57.0 1.8 %collective-permute-start.6 = (bf16[512,256]{1,0:T(8,128)(2,1)S(1)}, bf16[512,256]{1,0:T(8,128)(2,1)S(1)}, u32[]{:S(2)}, u32[]{:S(2)}) collective-permute-start(bf16[512,256]{1,0:T(8,128)(2,1)S(1)} %bitcast.22), channel_id=1, source_target_pairs={{0,8},{8,0},{1,9},{9,1},{2,10},{10,2},{3,11},{11,3},{4,12},{12,4},... | collective-permute-start | bytes 786440 | tf_op jit(solution)/shard_map/ppermute | solution.py:432
  58.8 1.2 %shard_map.83 = (f32[512,64]{1,0:T(8,128)S(1)}, bf16[128,256]{1,0:T(8,128)(2,1)S(1)}, bf16[448,256]{1,0:T(8,128)(2,1)S(1)}) custom-call(bf16[512,256]{1,0:T(8,128)(2,1)S(1)} %bitcast.23, bf16[9,192,256]{2,1,0:T(8,128)(2,1)S(1)} %bitcast.21, bf16[640,256]{1,0:T(8,128)(2,1)S(1)} %shard_map.80.grad), custom_call_target="tpu_custom_call" | custom-call | flops 1048576 | bytes 65536 | tf_op jit(solution)/shard_map/pallas_call | solution.py:440
  60.3 5.0 %collective-permute-start.12 = (bf16[448,256]{1,0:T(8,128)(2,1)S(1)}, bf16[448,256]{1,0:T(8,128)(2,1)S(1)}, u32[]{:S(2)}, u32[]{:S(2)}) collective-permute-start(bf16[448,256]{1,0:T(8,128)(2,1)S(1)} %get-tuple-element.83), channel_id=1, source_target_pairs={{8,16},{24,32},{40,48},{56,64},{72,80},{88,96},{104,112},{16,8},{3... | collective-permute-start | bytes 688136 | tf_op jit(solution)/shard_map/ppermute | solution.py:369
  65.3 1.9 %shard_map.82 = bf16[4,448,128]{2,1,0:T(8,128)(2,1)S(1)} custom-call(bf16[512,256]{1,0:T(8,128)(2,1)S(1)} %bitcast.24, bf16[512,256]{1,0:T(8,128)(2,1)S(1)} %collective-permute-done.6.other, bf16[3,34,16,192]{3,2,1,0:T(8,128)(2,1)S(1)} %get-tuple-element.70.wide, bf16[768,256]{1,0:T(8,128)(2,1)S(1)} %collective-permute-done.4.far), custom_call_target="tpu_custom_call" | custom-call | flops 1048576 | bytes 65536 | tf_op jit(solution)/shard_map/pallas_call | solution.py:433
  68.2 4.6 %collective-permute-start.10 = (bf16[448,128]{1,0:T(8,128)(2,1)S(1)}, bf16[448,128]{1,0:T(8,128)(2,1)S(1)}, u32[]{:S(2)}, u32[]{:S(2)}) collective-permute-start(bf16[448,128]{1,0:T(8,128)(2,1)S(1)} %get-tuple-element.97), channel_id=1, source_target_pairs={{0,64},{16,80},{32,96},{48,112},{64,0},{80,16},{96,32},{112,48},{8... | collective-permute-start | bytes 344072 | tf_op jit(solution)/shard_map/ppermute | solution.py:454
  72.8 1.3 %collective-permute-start.9 = (bf16[448,128]{1,0:T(8,128)(2,1)S(1)}, bf16[448,128]{1,0:T(8,128)(2,1)S(1)}, u32[]{:S(2)}, u32[]{:S(2)}) collective-permute-start(bf16[448,128]{1,0:T(8,128)(2,1)S(1)} %get-tuple-element.98), channel_id=1, source_target_pairs={{0,32},{16,48},{32,64},{48,80},{64,96},{80,112},{96,0},{112,16},{8... | collective-permute-start | bytes 344072 | tf_op jit(solution)/shard_map/ppermute | solution.py:454
  74.2 3.9 %collective-permute-start.8 = (bf16[448,128]{1,0:T(8,128)(2,1)S(1)}, bf16[448,128]{1,0:T(8,128)(2,1)S(1)}, u32[]{:S(2)}, u32[]{:S(2)}) collective-permute-start(bf16[448,128]{1,0:T(8,128)(2,1)S(1)} %get-tuple-element.99.own), channel_id=1, source_target_pairs={{8,24},{24,8},{40,56},{56,40},{72,88},{88,72},{104,120},{120,104},... | collective-permute-start | bytes 344072 | tf_op jit(solution)/shard_map/ppermute | solution.py:454
  78.1 2.1 %shard_map.84 = (f32[512,256]{1,0:T(8,128)S(1)}, bf16[3,256,768]{2,1,0:T(8,128)(2,1)S(1)}) custom-call(bf16[640,256]{1,0:T(8,128)(2,1)S(1)} %shard_map.80.grad, bf16[640,256]{1,0:T(8,128)(2,1)S(1)} %collective-permute-done.5.other, bf16[9,3,256,256]{3,2,1,0:T(8,128)(2,1)S(1)} %bitcast.19), custom_call_target="tpu_custom_call" | custom-call | flops 2147483648 | bytes 65536 | tf_op jit(solution)/shard_map/pallas_call | solution.py:455
  82.5 5.1 %collective-permute-done.10.second = bf16[448,128]{1,0:T(8,128)(2,1)S(1)} collective-permute-done((bf16[448,128]{1,0:T(8,128)(2,1)S(1)}, bf16[448,128]{1,0:T(8,128)(2,1)S(1)}, u32[]{:S(2)}, u32[]{:S(2)}) %collective-permute-start.10) | collective-permute-done | bytes 114720 | tf_op jit(solution)/shard_map/ppermute | solution.py:454
  87.7 1.2 %collective-permute-done.13.other = bf16[224,128]{1,0:T(8,128)(2,1)S(1)} collective-permute-done((bf16[224,128]{1,0:T(8,128)(2,1)S(1)}, bf16[224,128]{1,0:T(8,128)(2,1)S(1)}, u32[]{:S(2)}, u32[]{:S(2)}) %collective-permute-start.13) | collective-permute-done | bytes 57376 | tf_op jit(solution)/shard_map/ppermute | solution.py:476
  90.5 3.6 %shard_map.86 = (bf16[512,256]{1,0:T(8,128)(2,1)}, bf16[512,64]{1,0:T(8,128)(2,1)}, f32[108,128]{1,0:T(8,128)}) custom-call(f32[512,256]{1,0:T(8,128)} %copy-done.8, bf16[448,256]{1,0:T(8,128)(2,1)} %copy-done.14, bf16[3,256,768]{2,1,0:T(8,128)(2,1)} %copy-done.6, f32[512,64]{1,0:T(8,128)} %copy-done.11, bf16[128,256]{1,0:T(8,128)(2,1)} %copy-done.15, ...), custom_call_target="tpu_custom_call" | custom-call | flops 1073741824 | bytes 65536 | tf_op jit(solution)/shard_map/pallas_call | solution.py:469
  (56 shorter events, 13.0 us)
Async XLA Ops:
  2.4 11.2 %collective-permute-start.1 = (bf16[384,256]{1,0:T(8,128)(2,1)}, bf16[384,256]{1,0:T(8,128)(2,1)S(1)}, u32[]{:S(2)}, u32[]{:S(2)}) collective-permute-start(bf16[384,256]{1,0:T(8,128)(2,1)} %get-tuple-element.51), channel_id=1, source_target_pairs={{8,16},{24,32},{40,48},{56,64},{72,80},{88,96},{104,112},{16,8},{3... | collective-permute-start | bytes 589832 | tf_op jit(solution)/shard_map/ppermute | solution.py:369
  8.7 5.0 %collective-permute-start = (bf16[384,256]{1,0:T(8,128)(2,1)}, bf16[384,256]{1,0:T(8,128)(2,1)S(1)}, u32[]{:S(2)}, u32[]{:S(2)}) collective-permute-start(bf16[384,256]{1,0:T(8,128)(2,1)} %get-tuple-element.50.token), channel_id=1, source_target_pairs={{0,8},{8,0},{1,9},{9,1},{2,10},{10,2},{3,11},{11,3},{4,12},{12,4},... | collective-permute-start | bytes 589832 | tf_op jit(solution)/shard_map/ppermute | solution.py:369
  12.7 14.8 %copy-start.1 = (bf16[2,8,32,256]{3,2,1,0:T(8,128)(2,1)S(1)}, bf16[2,8,32,256]{3,2,1,0:T(8,128)(2,1)}, u32[]{:S(2)}) copy-start(bf16[2,8,32,256]{3,2,1,0:T(8,128)(2,1)} %own.5) | copy-start | bytes 786436
  13.7 5.3 %collective-permute-start.2 = (bf16[256,256]{1,0:T(8,128)(2,1)S(1)}, bf16[256,256]{1,0:T(8,128)(2,1)S(1)}, u32[]{:S(2)}, u32[]{:S(2)}) collective-permute-start(bf16[256,256]{1,0:T(8,128)(2,1)S(1)} %get-tuple-element.61), channel_id=1, source_target_pairs={{0,1},{1,0},{2,3},{3,2},{4,5},{5,4},{6,7},{7,6},{8,9},{9,8},{10,11... | collective-permute-start | bytes 393224 | tf_op jit(solution)/shard_map/ppermute | solution.py:369
  14.2 4.8 %collective-permute-start.3 = (bf16[256,256]{1,0:T(8,128)(2,1)S(1)}, bf16[256,256]{1,0:T(8,128)(2,1)S(1)}, u32[]{:S(2)}, u32[]{:S(2)}) collective-permute-start(bf16[256,256]{1,0:T(8,128)(2,1)S(1)} %get-tuple-element.62), channel_id=1, source_target_pairs={{1,2},{3,4},{5,6},{2,1},{4,3},{6,5},{9,10},{11,12},{13,14},{10,9},... | collective-permute-start | bytes 393224 | tf_op jit(solution)/shard_map/ppermute | solution.py:369
  19.0 14.3 %copy-start.9 = (bf16[256,256]{1,0:T(8,128)(2,1)}, bf16[256,256]{1,0:T(8,128)(2,1)S(1)}, u32[]{:S(2)}) copy-start(bf16[256,256]{1,0:T(8,128)(2,1)S(1)} %collective-permute-done.3.youter) | copy-start | bytes 393220
  19.0 16.3 %all-to-all-start = ((bf16[8,96,256]{2,1,0:T(8,128)(2,1)}), bf16[8,96,256]{2,1,0:T(8,128)(2,1)S(1)}, u32[]{:S(2)}, u32[]{:S(2)}) async-start(bf16[8,96,256]{2,1,0:T(8,128)(2,1)} %get-tuple-element.66), calls=%async_computation | async-start | bytes 786432 | tf_op jit(solution)/shard_map/all_to_all | solution.py:396
  27.5 2.0 %copy-start.2 = (bf16[27,256,256]{2,1,0:T(8,128)(2,1)S(1)}, bf16[27,256,256]{2,1,0:T(8,128)(2,1)}, u32[]{:S(2)}) copy-start(bf16[27,256,256]{2,1,0:T(8,128)(2,1)} %param.5) | copy-start | bytes 10616836
  34.0 6.9 %collective-permute-start.4 = (bf16[768,256]{1,0:T(8,128)(2,1)}, bf16[768,256]{1,0:T(8,128)(2,1)S(1)}, u32[]{:S(2)}, u32[]{:S(2)}) collective-permute-start(bf16[768,256]{1,0:T(8,128)(2,1)} %get-tuple-element.65), channel_id=1, source_target_pairs={{0,8},{8,0},{1,9},{9,1},{2,10},{10,2},{3,11},{11,3},{4,12},{12,4},... | collective-permute-start | bytes 1179656 | tf_op jit(solution)/shard_map/ppermute | solution.py:408
  35.4 5.5 %collective-permute-start.5 = (bf16[640,256]{1,0:T(8,128)(2,1)S(1)}, bf16[640,256]{1,0:T(8,128)(2,1)S(1)}, u32[]{:S(2)}, u32[]{:S(2)}) collective-permute-start(bf16[640,256]{1,0:T(8,128)(2,1)S(1)} %shard_map.80.grad), channel_id=1, source_target_pairs={{0,8},{8,0},{1,9},{9,1},{2,10},{10,2},{3,11},{11,3},{4,12},{12,4},... | collective-permute-start | bytes 983048 | tf_op jit(solution)/shard_map/ppermute | solution.py:417
  37.4 10.1 %all-to-all-start.1 = ((bf16[8,64,256]{2,1,0:T(8,128)(2,1)}), bf16[8,64,256]{2,1,0:T(8,128)(2,1)S(1)}, u32[]{:S(2)}, u32[]{:S(2)}) async-start(bf16[8,64,256]{2,1,0:T(8,128)(2,1)} %copy-done.12), calls=%async_computation.1 | async-start | bytes 524288 | tf_op jit(solution)/shard_map/all_to_all | solution.py:409
  47.5 11.3 %copy-start.5 = (bf16[27,256,64]{1,2,0:T(8,128)(2,1)S(1)}, bf16[27,256,64]{1,2,0:T(8,128)(2,1)}, u32[]{:S(2)}) copy-start(bf16[27,256,64]{1,2,0:T(8,128)(2,1)} %param.6) | copy-start | bytes 2654212
  47.5 42.3 %all-to-all-start.2 = ((bf16[64,54,256]{2,1,0:T(8,128)(2,1)}), bf16[64,54,256]{2,1,0:T(8,128)(2,1)}, u32[]{:S(2)}, u32[]{:S(2)}) async-start(bf16[64,54,256]{2,1,0:T(8,128)(2,1)} %shard_map.81), calls=%async_computation.2 | async-start | bytes 3670016 | tf_op jit(solution)/shard_map/all_to_all | solution.py:430
  57.0 8.4 %collective-permute-start.6 = (bf16[512,256]{1,0:T(8,128)(2,1)S(1)}, bf16[512,256]{1,0:T(8,128)(2,1)S(1)}, u32[]{:S(2)}, u32[]{:S(2)}) collective-permute-start(bf16[512,256]{1,0:T(8,128)(2,1)S(1)} %bitcast.22), channel_id=1, source_target_pairs={{0,8},{8,0},{1,9},{9,1},{2,10},{10,2},{3,11},{11,3},{4,12},{12,4},... | collective-permute-start | bytes 786440 | tf_op jit(solution)/shard_map/ppermute | solution.py:432
  58.8 19.3 %copy-start.3 = (bf16[27,256,256]{2,1,0:T(8,128)(2,1)S(1)}, bf16[27,256,256]{2,1,0:T(8,128)(2,1)}, u32[]{:S(2)}) copy-start(bf16[27,256,256]{2,1,0:T(8,128)(2,1)} %param.5) | copy-start | bytes 10616836
  60.0 7.3 %copy-start.11 = (f32[512,64]{1,0:T(8,128)}, f32[512,64]{1,0:T(8,128)S(1)}, u32[]{:S(2)}) copy-start(f32[512,64]{1,0:T(8,128)S(1)} %get-tuple-element.89.centre) | copy-start | bytes 393220
  60.0 7.3 %collective-permute-start.7 = (bf16[128,256]{1,0:T(8,128)(2,1)S(1)}, bf16[128,256]{1,0:T(8,128)(2,1)S(1)}, u32[]{:S(2)}, u32[]{:S(2)}) collective-permute-start(bf16[128,256]{1,0:T(8,128)(2,1)S(1)} %get-tuple-element.72), channel_id=1, source_target_pairs={{0,8},{8,0},{1,9},{9,1},{2,10},{10,2},{3,11},{11,3},{4,12},{12,4},... | collective-permute-start | bytes 196616 | tf_op jit(solution)/shard_map/ppermute | solution.py:369
  60.3 29.5 %collective-permute-start.12 = (bf16[448,256]{1,0:T(8,128)(2,1)S(1)}, bf16[448,256]{1,0:T(8,128)(2,1)S(1)}, u32[]{:S(2)}, u32[]{:S(2)}) collective-permute-start(bf16[448,256]{1,0:T(8,128)(2,1)S(1)} %get-tuple-element.83), channel_id=1, source_target_pairs={{8,16},{24,32},{40,48},{56,64},{72,80},{88,96},{104,112},{16,8},{3... | collective-permute-start | bytes 688136 | tf_op jit(solution)/shard_map/ppermute | solution.py:369
  67.3 12.9 %copy-start.15 = (bf16[128,256]{1,0:T(8,128)(2,1)}, bf16[128,256]{1,0:T(8,128)(2,1)S(1)}, u32[]{:S(2)}) copy-start(bf16[128,256]{1,0:T(8,128)(2,1)S(1)} %collective-permute-done.7.inner) | copy-start | bytes 196612
  67.3 15.1 %collective-permute-start.11 = (bf16[448,128]{1,0:T(8,128)(2,1)S(1)}, bf16[448,128]{1,0:T(8,128)(2,1)S(1)}, u32[]{:S(2)}, u32[]{:S(2)}) collective-permute-start(bf16[448,128]{1,0:T(8,128)(2,1)S(1)} %get-tuple-element.96), channel_id=1, source_target_pairs={{0,96},{16,112},{32,0},{48,16},{64,32},{80,48},{96,64},{112,80},{8... | collective-permute-start | bytes 344072 | tf_op jit(solution)/shard_map/ppermute | solution.py:454
  68.2 19.4 %collective-permute-start.10 = (bf16[448,128]{1,0:T(8,128)(2,1)S(1)}, bf16[448,128]{1,0:T(8,128)(2,1)S(1)}, u32[]{:S(2)}, u32[]{:S(2)}) collective-permute-start(bf16[448,128]{1,0:T(8,128)(2,1)S(1)} %get-tuple-element.97), channel_id=1, source_target_pairs={{0,64},{16,80},{32,96},{48,112},{64,0},{80,16},{96,32},{112,48},{8... | collective-permute-start | bytes 344072 | tf_op jit(solution)/shard_map/ppermute | solution.py:454
  72.8 14.7 %collective-permute-start.9 = (bf16[448,128]{1,0:T(8,128)(2,1)S(1)}, bf16[448,128]{1,0:T(8,128)(2,1)S(1)}, u32[]{:S(2)}, u32[]{:S(2)}) collective-permute-start(bf16[448,128]{1,0:T(8,128)(2,1)S(1)} %get-tuple-element.98), channel_id=1, source_target_pairs={{0,32},{16,48},{32,64},{48,80},{64,96},{80,112},{96,0},{112,16},{8... | collective-permute-start | bytes 344072 | tf_op jit(solution)/shard_map/ppermute | solution.py:454
  74.2 13.4 %collective-permute-start.8 = (bf16[448,128]{1,0:T(8,128)(2,1)S(1)}, bf16[448,128]{1,0:T(8,128)(2,1)S(1)}, u32[]{:S(2)}, u32[]{:S(2)}) collective-permute-start(bf16[448,128]{1,0:T(8,128)(2,1)S(1)} %get-tuple-element.99.own), channel_id=1, source_target_pairs={{8,24},{24,8},{40,56},{56,40},{72,88},{88,72},{104,120},{120,104},... | collective-permute-start | bytes 344072 | tf_op jit(solution)/shard_map/ppermute | solution.py:454
  87.6 1.3 %collective-permute-start.13 = (bf16[224,128]{1,0:T(8,128)(2,1)S(1)}, bf16[224,128]{1,0:T(8,128)(2,1)S(1)}, u32[]{:S(2)}, u32[]{:S(2)}) collective-permute-start(bf16[224,128]{1,0:T(8,128)(2,1)S(1)} %get-tuple-element.81), channel_id=1, source_target_pairs={{0,8},{8,0},{1,9},{9,1},{2,10},{10,2},{3,11},{11,3},{4,12},{12,4},... | collective-permute-start | bytes 172040 | tf_op jit(solution)/shard_map/ppermute | solution.py:476
  (9 other events, 8.1 us)
